TPU v7x, 32 devices: a whole 2x2x4 slice. The times are simulated.
32 devices in a mesh: gx: 8 (over z, core), gy: 4 (over y, x).
Axes of the slice: x: 2, y: 2, z: 4, core: 2. Of those that a mesh axis runs over, the one named last changes fastest.
Arguments:
- currents: bfloat16 [256, 128, 2, 128], P('gx', 'gy'), may hold values from -6 to 6
- box_count: int32 [256, 128], P('gx', 'gy'), may hold values from 0 to 128, as said below
- aggregate: bfloat16 [256, 256], replicated, may hold values from -0.375 to 0.375
- near_blocks: bfloat16 [9, 256, 256], replicated, may hold values from -0.125 to 0.125
- low_translator: float32 [16, 2, 128], replicated, may hold values from -1.5 to 1.5
- child_to_parent: bfloat16 [4, 256, 512], replicated, may hold values from -0.1875 to 0.1875
- coarse_list: int32 [128, 64, 16], P('gx', 'gy'), may hold values from 0 to 1023
- coarse_kind: int32 [128, 64, 16], P('gx', 'gy'), may hold values from 0 to 63
- coarse_count: int32 [128, 64], P('gx', 'gy'), may hold values from 1 to 16, as said below
- up_translator: float32 [64, 2, 256], replicated, may hold values from -1.5 to 1.5
- parent_to_child: bfloat16 [4, 512, 256], replicated, may hold values from -0.25 to 0.25
- receive_map: bfloat16 [256, 256], replicated, may hold values from -0.375 to 0.375
Outputs:
- field: float32 [256, 128, 2, 128], P('gx', 'gy')
Inputs may be any that keep to these rules, and one draw needn't show every extreme that they name: `box_count`: ground clutter makes some boxes full and most sparse; some box holds 128 unknowns and some none. `coarse_count`: some list uses all 16 entries.
All inputs are finite; a program needn't handle non-finite values.
Results may differ from a plain program's by a relative error of at most 0.0041.
Values may be sent and summed in bfloat16 or wider, within the bound.
No kernel may reach another device: no remote copies, remote signals or barrier semaphores. Data moves between devices by JAX's collectives and lax.ppermute only.
A program may use at most 128 MiB of HBM per device.

v0:
```python
import jax
import jax.numpy as jnp
from jax import lax
from jax.sharding import PartitionSpec as P


def extended(cells, sides, width):
    for axis, dim in sides:
        count = lax.axis_size(axis)
        ends = count - 1
        head = lax.slice_in_dim(cells, 0, width, axis=dim)
        tail = lax.slice_in_dim(cells, cells.shape[dim] - width, cells.shape[dim], axis=dim)
        cells = jnp.concatenate(
            [
                lax.ppermute(tail, axis, [(i, (i + 1) % count) for i in range(ends)]),
                cells,
                lax.ppermute(head, axis, [((i + 1) % count, i) for i in range(ends)]),
            ],
            axis=dim,
        )
    return cells


def complex_flat(table, pattern, half):
    real_part = pattern[..., :half].astype(jnp.float32)
    imag_part = pattern[..., half:].astype(jnp.float32)
    first = table[..., :half] * real_part - table[..., half:] * imag_part
    second = table[..., :half] * imag_part + table[..., half:] * real_part
    return jnp.concatenate([first, second], axis=-1)


def make_patterns(block, aggregate):
    size_a, size_b = (block.shape[0], block.shape[1])
    flat_block = block.reshape(size_a * size_b, block.shape[2] * block.shape[3])
    result = jnp.dot(flat_block, aggregate, preferred_element_type=jnp.float32)
    return result.astype(jnp.bfloat16).reshape(size_a, size_b, aggregate.shape[1])


def translate_group(flat_group, lists, kinds, counts, table):
    rows_a, rows_b, slots = lists.shape
    kind_total, width_two = table.shape
    half = width_two // 2
    kind_ids = jnp.arange(kind_total, dtype=jnp.int32)[None, :]

    def accumulate(slot, total):
        index = lists[:, :, slot].reshape(rows_a * rows_b)
        source = jnp.take(flat_group, index, axis=0)
        choose = (kinds[:, :, slot].reshape(rows_a * rows_b)[:, None] == kind_ids).astype(
            jnp.float32
        )
        factors = jnp.dot(
            choose, table, precision=lax.Precision.HIGHEST, preferred_element_type=jnp.float32
        )
        term = complex_flat(factors, source, half)
        keep = (slot < counts).reshape(rows_a * rows_b)
        return total + jnp.where(keep[:, None], term, jnp.zeros_like(term))

    start = jnp.zeros((rows_a * rows_b, width_two), jnp.float32)
    result = lax.fori_loop(0, slots, accumulate, start)
    return result.astype(jnp.bfloat16).reshape(rows_a, rows_b, width_two)


def body(
    currents,
    box_count,
    aggregate,
    near_blocks,
    low_translator,
    child_to_parent,
    coarse_list,
    coarse_kind,
    coarse_count,
    up_translator,
    parent_to_child,
    receive_map,
):
    tile_x, tile_y = box_count.shape
    unknowns = currents.shape[-1]
    samples = low_translator.shape[-1]
    parent_samples = up_translator.shape[-1]
    kind_total = up_translator.shape[0]
    low_flat = low_translator.reshape(low_translator.shape[0], 2 * samples)
    mask = jnp.arange(unknowns, dtype=jnp.int32)[None, None, :] < box_count[:, :, None]
    live = jnp.where(mask[:, :, None, :], currents, jnp.zeros_like(currents))
    near_pad = extended(live, (("gx", 0), ("gy", 1)), 1)
    pattern = make_patterns(live, aggregate)
    pattern_pad = extended(pattern, (("gx", 0), ("gy", 1)), 2)
    lower_in = jnp.zeros((tile_x, tile_y, 2 * samples), jnp.float32)
    offset = 0
    for shift_x in range(-2, 3):
        for shift_y in range(-2, 3):
            if max(abs(shift_x), abs(shift_y)) < 2:
                continue
            source = pattern_pad[
                2 + shift_x : 2 + shift_x + tile_x, 2 + shift_y : 2 + shift_y + tile_y
            ]
            lower_in = lower_in + complex_flat(low_flat[offset], source, samples)
            offset += 1
    parents_x, parents_y = (tile_x // 2, tile_y // 2)
    children = pattern.reshape(parents_x, 2, parents_y, 2, 2 * samples)
    coarse_sum = jnp.zeros((parents_x * parents_y, 2 * parent_samples), jnp.float32)
    for half_x in range(2):
        for half_y in range(2):
            child = children[:, half_x, :, half_y].reshape(parents_x * parents_y, 2 * samples)
            coarse_sum = coarse_sum + jnp.dot(
                child, child_to_parent[2 * half_x + half_y], preferred_element_type=jnp.float32
            )
    coarse = coarse_sum.astype(jnp.bfloat16).reshape(parents_x, parents_y, 2 * parent_samples)
    group = lax.all_gather(coarse, "gy", axis=1, tiled=True)
    flat_group = group.reshape(group.shape[0] * group.shape[1], 2 * parent_samples)
    table = up_translator.reshape(kind_total, 2 * parent_samples)
    coarse_in = translate_group(flat_group, coarse_list, coarse_kind, coarse_count, table)
    coarse_flat = coarse_in.reshape(parents_x * parents_y, 2 * parent_samples)
    pieces = [
        jnp.dot(coarse_flat, parent_to_child[child_id], preferred_element_type=jnp.float32).reshape(
            parents_x, parents_y, 2 * samples
        )
        for child_id in range(4)
    ]
    rows_first = jnp.stack([pieces[0], pieces[1]], axis=2)
    rows_second = jnp.stack([pieces[2], pieces[3]], axis=2)
    from_parent = jnp.stack([rows_first, rows_second], axis=1).reshape(tile_x, tile_y, 2 * samples)
    incoming = (lower_in + from_parent).astype(jnp.bfloat16)
    field = jnp.dot(
        incoming.reshape(tile_x * tile_y, 2 * samples),
        receive_map,
        preferred_element_type=jnp.float32,
    )
    for shift_x in range(-1, 2):
        for shift_y in range(-1, 2):
            source = near_pad[
                1 + shift_x : 1 + shift_x + tile_x, 1 + shift_y : 1 + shift_y + tile_y
            ].reshape(tile_x * tile_y, 2 * unknowns)
            field = field + jnp.dot(
                source,
                near_blocks[3 * (shift_x + 1) + shift_y + 1],
                preferred_element_type=jnp.float32,
            )
    return field.reshape(tile_x, tile_y, 2, unknowns) * mask[:, :, None, :].astype(jnp.float32)


def solution(mesh):
    in_specs = (
        P("gx", "gy", None, None),
        P("gx", "gy"),
        P(),
        P(),
        P(),
        P(),
        P("gx", "gy", None),
        P("gx", "gy", None),
        P("gx", "gy"),
        P(),
        P(),
        P(),
    )
    out_specs = P("gx", "gy", None, None)
    return jax.shard_map(body, mesh=mesh, in_specs=in_specs, out_specs=out_specs, check_vma=False)
```

profile of v0, /device:TPU:5, one launch (start us, length us, event | category | flops | bytes accessed | tf_op | source)
XLA Modules:
  0.0 151.0 jit_solution(11352619582034095496)
XLA Ops:
  6.5 1.7 %fusion.114 = (f32[32,32,128]{2,1,0:T(8,128)}, pred[32,32,128]{2,1,0:T(8,128)(4,1)S(1)}) fusion(s32[32,32]{1,0:T(8,128)} %param.15), kind=kLoop, calls=%fused_computation.263 | loop fusion | flops 262144 | bytes 659456 | tf_op jit(solution)/shard_map/convert_element_type | solution.py:139
  8.3 1.9 %broadcast_select_fusion.1 = bf16[32,32,2,128]{3,2,1,0:T(2,128)(2,1)S(1)} fusion(bf16[32,32,2,128]{3,2,1,0:T(2,128)(2,1)} %param.14, pred[32,32,128]{2,1,0:T(8,128)(4,1)S(1)} %get-tuple-element.269), kind=kLoop, calls=%fused_computation.56 | loop fusion | flops 262144 | bytes 1179648 | tf_op jit(solution)/shard_map/jit(_where)/select_n | solution.py:84
  10.5 3.8 %collective-permute-start = (bf16[2,32,256]{2,1,0:T(8,128)(2,1)S(1)}, bf16[2,32,256]{2,1,0:T(8,128)(2,1)S(1)}, u32[]{:S(2)}, u32[]{:S(2)}) collective-permute-start(bf16[2,32,256]{2,1,0:T(8,128)(2,1)S(1)} %bitcast.304), channel_id=1, source_target_pairs={{0,4},{4,8},{8,12},{12,16},{16,20},{20,24},{24,28},{1,5},{5,9},{9,... | collective-permute-start | bytes 98312 | tf_op jit(solution)/shard_map/ppermute | solution.py:15
  14.3 1.9 %collective-permute-start.1 = (bf16[2,32,256]{2,1,0:T(8,128)(2,1)S(1)}, bf16[2,32,256]{2,1,0:T(8,128)(2,1)S(1)}, u32[]{:S(2)}, u32[]{:S(2)}) collective-permute-start(bf16[2,32,256]{2,1,0:T(8,128)(2,1)S(1)} %bitcast.303), channel_id=1, source_target_pairs={{4,0},{8,4},{12,8},{16,12},{20,16},{24,20},{28,24},{5,1},{9,5},{13... | collective-permute-start | bytes 98312 | tf_op jit(solution)/shard_map/ppermute | solution.py:17
  16.4 1.1 fusion.119
  17.7 1.1 copy-done.13
  19.5 0.9 fusion.7
  20.5 3.7 %collective-permute-start.4 = (bf16[1,32,2,128]{3,2,1,0:T(2,128)(2,1)S(1)}, bf16[1,32,2,128]{3,2,1,0:T(2,128)(2,1)S(1)}, u32[]{:S(2)}, u32[]{:S(2)}) collective-permute-start(bf16[1,32,2,128]{3,2,1,0:T(2,128)(2,1)S(1)} %get-tuple-element.260), channel_id=1, source_target_pairs={{0,4},{4,8},{8,12},{12,16},{16,20},{20,24},{24,28},{1,5},{5,9},{9,... | collective-permute-start | bytes 49160 | tf_op jit(solution)/shard_map/ppermute | solution.py:15
  24.2 1.9 %collective-permute-start.5 = (bf16[1,32,2,128]{3,2,1,0:T(2,128)(2,1)S(1)}, bf16[1,32,2,128]{3,2,1,0:T(2,128)(2,1)S(1)}, u32[]{:S(2)}, u32[]{:S(2)}) collective-permute-start(bf16[1,32,2,128]{3,2,1,0:T(2,128)(2,1)S(1)} %get-tuple-element.261), channel_id=1, source_target_pairs={{4,0},{8,4},{12,8},{16,12},{20,16},{24,20},{28,24},{5,1},{9,5},{13... | collective-permute-start | bytes 49160 | tf_op jit(solution)/shard_map/ppermute | solution.py:17
  26.5 2.8 %collective-permute-done.5 = bf16[1,32,2,128]{3,2,1,0:T(2,128)(2,1)S(1)} collective-permute-done((bf16[1,32,2,128]{3,2,1,0:T(2,128)(2,1)S(1)}, bf16[1,32,2,128]{3,2,1,0:T(2,128)(2,1)S(1)}, u32[]{:S(2)}, u32[]{:S(2)}) %collective-permute-start.5) | collective-permute-done | bytes 16416 | tf_op jit(solution)/shard_map/ppermute | solution.py:17
  29.3 3.1 %collective-permute-start.6 = (bf16[34,1,2,128]{3,2,1,0:T(2,128)(2,1)S(1)}, bf16[34,1,2,128]{3,2,1,0:T(2,128)(2,1)S(1)}, u32[]{:S(2)}, u32[]{:S(2)}) collective-permute-start(bf16[34,1,2,128]{3,2,1,0:T(2,128)(2,1)S(1)} %get-tuple-element.257), channel_id=1, source_target_pairs={{0,1},{1,2},{2,3},{4,5},{5,6},{6,7},{8,9},{9,10},{10,11},{12,13},{... | collective-permute-start | bytes 52232 | tf_op jit(solution)/shard_map/ppermute | solution.py:15
  32.4 3.1 %collective-permute-start.7 = (bf16[34,1,2,128]{3,2,1,0:T(2,128)(2,1)S(1)}, bf16[34,1,2,128]{3,2,1,0:T(2,128)(2,1)S(1)}, u32[]{:S(2)}, u32[]{:S(2)}) collective-permute-start(bf16[34,1,2,128]{3,2,1,0:T(2,128)(2,1)S(1)} %get-tuple-element.256), channel_id=1, source_target_pairs={{1,0},{2,1},{3,2},{5,4},{6,5},{7,6},{9,8},{10,9},{11,10},{13,12},{... | collective-permute-start | bytes 52232 | tf_op jit(solution)/shard_map/ppermute | solution.py:17
  35.5 2.4 %pad_maximum_fusion.3 = (bf16[32,32,2,128]{3,2,1,0:T(2,128)(2,1)}, bf16[32,32,2,128]{3,2,1,0:T(2,128)(2,1)}) fusion(bf16[1,32,2,128]{3,2,1,0:T(2,128)(2,1)S(1)} %collective-permute-done.5, bf16[32,32,2,128]{3,2,1,0:T(2,128)(2,1)S(1)} %broadcast_select_fusion.1, bf16[1,32,2,128]{3,2,1,0:T(2,128)(2,1)S(1)} %collective-permute-done.4), kind=kLoop, calls=%fused_computation.176 | loop fusion | flops 524288 | bytes 1605632 | tf_op jit(solution)/shard_map/concatenate | solution.py:13
  37.9 2.2 %collective-permute-start.2 = (bf16[36,2,256]{2,1,0:T(2,128)(2,1)S(1)}, bf16[36,2,256]{2,1,0:T(2,128)(2,1)S(1)}, u32[]{:S(2)}, u32[]{:S(2)}) collective-permute-start(bf16[36,2,256]{2,1,0:T(2,128)(2,1)S(1)} %get-tuple-element.242), channel_id=1, source_target_pairs={{0,1},{1,2},{2,3},{4,5},{5,6},{6,7},{8,9},{9,10},{10,11},{12,13},{... | collective-permute-start | bytes 110600 | tf_op jit(solution)/shard_map/ppermute | solution.py:15
  40.2 4.0 %collective-permute-start.3 = (bf16[36,2,256]{2,1,0:T(2,128)(2,1)S(1)}, bf16[36,2,256]{2,1,0:T(2,128)(2,1)S(1)}, u32[]{:S(2)}, u32[]{:S(2)}) collective-permute-start(bf16[36,2,256]{2,1,0:T(2,128)(2,1)S(1)} %get-tuple-element.243), channel_id=1, source_target_pairs={{1,0},{2,1},{3,2},{5,4},{6,5},{7,6},{9,8},{10,9},{11,10},{13,12},{... | collective-permute-start | bytes 110600 | tf_op jit(solution)/shard_map/ppermute | solution.py:17
  44.1 1.2 fusion.50
  45.3 1.1 fusion.28
  46.5 2.2 %pad_maximum_fusion.2 = (bf16[34,33,2,128]{3,2,1,0:T(2,128)(2,1)S(1)}, bf16[34,33,2,128]{3,2,1,0:T(2,128)(2,1)S(1)}) fusion(bf16[34,1,2,128]{3,2,1,0:T(2,128)(2,1)S(1)} %collective-permute-done.7, bf16[1,32,2,128]{3,2,1,0:T(2,128)(2,1)S(1)} %collective-permute-done.5, bf16[32,32,2,128]{3,2,1,0:T(2,128)(2,1)S(1)} %broadcast_select_fusion.1, ...), kind=kLoop, calls=%fused_computation.125 | loop fusion | flops 1723392 | bytes 1740800 | tf_op jit(solution)/shard_map/concatenate | solution.py:13
  48.7 4.3 %fusion.115 = (bf16[32,32,2,128]{3,2,1,0:T(2,128)(2,1)}, bf16[32,32,2,128]{3,2,1,0:T(2,128)(2,1)}, bf16[32,32,2,128]{3,2,1,0:T(2,128)(2,1)}, bf16[32,32,2,128]{3...) fusion(bf16[34,33,2,128]{3,2,1,0:T(2,128)(2,1)S(1)} %get-tuple-element.254, ...), kind=kLoop, calls=%fused_computation.264 | loop fusion | bytes 6291456 | tf_op jit(solution)/shard_map/slice | solution.py:131
  53.0 0.5 maximum_maximum_fusion
  53.5 1.7 %fusion.34 = (f32[32,32,128]{2,1,0:T(8,128)}, f32[32,32,128]{2,1,0:T(8,128)}, f32[32,32,128]{2,1,0:T(8,128)}, f32[32,32,128]{2,1,0:T(8,128)}) fusion(f32[128]{0:T(128)S(1)} %get-tuple-element.290, f32[128]{0:T(128)S(1)} %get-tuple-element.291, bf16[36,34,256]{2,1,0:T(8,128)(2,1)S(1)} %get-tuple-element.240, bf16[36,34,256]{2,1,0:T(8,128)(2,1)S(1)} %get-tuple-element.241, ...), kind=kLoop, calls=%fused_computation.136 | loop fusion | flops 2097152 | bytes 3147776 | tf_op jit(solution)/shard_map/sub | solution.py:27
  55.2 2.1 %fusion.24 = (f32[32,32,128]{2,1,0:T(8,128)}, f32[32,32,128]{2,1,0:T(8,128)}, f32[32,32,128]{2,1,0:T(8,128)}, f32[32,32,128]{2,1,0:T(8,128)}, f32[32,32,128]{2,1,0:T(8,128)}, /*index=5*/f32[32,32,128]{2,1,0:T(8,128)}) fusion(f32[128]{0:T(128)S(1)} %get-tuple-element.289, f32[128]{0:T(128)S(1)} %get-tuple-element.270, ...), kind=kLoop, calls=%fused_computation.126 | loop fusion | flops 3145728 | bytes 4721664 | tf_op jit(solution)/shard_map/sub | solution.py:27
  57.3 2.1 %fusion.26 = (f32[32,32,128]{2,1,0:T(8,128)}, f32[32,32,128]{2,1,0:T(8,128)}, f32[32,32,128]{2,1,0:T(8,128)}, f32[32,32,128]{2,1,0:T(8,128)}, f32[32,32,128]{2,1,0:T(8,128)}, /*index=5*/f32[32,32,128]{2,1,0:T(8,128)}) fusion(f32[128]{0:T(128)S(1)} %get-tuple-element.298, f32[128]{0:T(128)S(1)} %get-tuple-element.299, ...), kind=kLoop, calls=%fused_computation.128 | loop fusion | flops 3145728 | bytes 4721664 | tf_op jit(solution)/shard_map/sub | solution.py:27
  59.4 2.4 %fusion.32 = (f32[32,32,128]{2,1,0:T(8,128)}, f32[32,32,128]{2,1,0:T(8,128)}, f32[32,32,128]{2,1,0:T(8,128)}, f32[32,32,128]{2,1,0:T(8,128)}, f32[32,32,128]{2,1,0:T(8,128)}, /*index=5*/f32[32,32,128]{2,1,0:T(8,128)}) fusion(f32[128]{0:T(128)S(1)} %get-tuple-element.292, f32[128]{0:T(128)S(1)} %get-tuple-element.293, ...), kind=kLoop, calls=%fused_computation.134 | loop fusion | flops 3145728 | bytes 4721664 | tf_op jit(solution)/shard_map/sub | solution.py:27
  61.9 2.5 %fusion.30 = (f32[32,32,128]{2,1,0:T(8,128)}, f32[32,32,128]{2,1,0:T(8,128)}, f32[32,32,128]{2,1,0:T(8,128)}, f32[32,32,128]{2,1,0:T(8,128)}, f32[32,32,128]{2,1,0:T(8,128)}, /*index=5*/f32[32,32,128]{2,1,0:T(8,128)}) fusion(f32[128]{0:T(128)S(1)} %get-tuple-element.294, f32[128]{0:T(128)S(1)} %get-tuple-element.295, ...), kind=kLoop, calls=%fused_computation.132 | loop fusion | flops 3145728 | bytes 4721664 | tf_op jit(solution)/shard_map/sub | solution.py:27
  64.4 59.7 %while.14 = (s32[]{:T(128)}, f32[256,512]{1,0:T(8,128)S(1)}, s32[16,16]{1,0:T(8,128)S(1)}, s32[16,16,16]{1,0,2:T(8,128)S(1)}, f32[64,512]{1,0:T(8,128)S(1)}, /*i...) while((s32[]{:T(128)}, f32[256,512]{1,0:T(8,128)S(1)}, ...), condition=%wide.region_1.2_spmd.clone, body=%wide.region_0.1_spmd.clone.sunk | while | flops 101862912 | bytes 4610671 | solution.py:59
  64.5 2.6 %gather_fusion = bf16[256,512]{1,0:T(8,128)(2,1)S(1)} fusion(bf16[1024,512]{1,0:T(8,128)(2,1)} %get-tuple-element.384, s32[1024]{0:T(1024)S(1)} %pad_clamp_fusion.2), kind=kCustom, calls=%fused_computation.clone.clone.1 | custom fusion | bytes 525312 | tf_op jit(solution)/shard_map/while/body/eval_jaxpr/jit(_take)/gather | solution.py:47
  67.4 0.4 fusion.136
  68.3 2.6 %gather_fusion = bf16[256,512]{1,0:T(8,128)(2,1)S(1)} fusion(bf16[1024,512]{1,0:T(8,128)(2,1)} %get-tuple-element.384, s32[1024]{0:T(1024)S(1)} %pad_clamp_fusion.2), kind=kCustom, calls=%fused_computation.clone.clone.1 | custom fusion | bytes 525312 | tf_op jit(solution)/shard_map/while/body/eval_jaxpr/jit(_take)/gather | solution.py:47
  72.0 2.6 %gather_fusion = bf16[256,512]{1,0:T(8,128)(2,1)S(1)} fusion(bf16[1024,512]{1,0:T(8,128)(2,1)} %get-tuple-element.384, s32[1024]{0:T(1024)S(1)} %pad_clamp_fusion.2), kind=kCustom, calls=%fused_computation.clone.clone.1 | custom fusion | bytes 525312 | tf_op jit(solution)/shard_map/while/body/eval_jaxpr/jit(_take)/gather | solution.py:47
  74.9 0.4 fusion.136
  75.7 2.6 %gather_fusion = bf16[256,512]{1,0:T(8,128)(2,1)S(1)} fusion(bf16[1024,512]{1,0:T(8,128)(2,1)} %get-tuple-element.384, s32[1024]{0:T(1024)S(1)} %pad_clamp_fusion.2), kind=kCustom, calls=%fused_computation.clone.clone.1 | custom fusion | bytes 525312 | tf_op jit(solution)/shard_map/while/body/eval_jaxpr/jit(_take)/gather | solution.py:47
  78.6 0.4 fusion.136
  79.4 2.6 %gather_fusion = bf16[256,512]{1,0:T(8,128)(2,1)S(1)} fusion(bf16[1024,512]{1,0:T(8,128)(2,1)} %get-tuple-element.384, s32[1024]{0:T(1024)S(1)} %pad_clamp_fusion.2), kind=kCustom, calls=%fused_computation.clone.clone.1 | custom fusion | bytes 525312 | tf_op jit(solution)/shard_map/while/body/eval_jaxpr/jit(_take)/gather | solution.py:47
  82.3 0.4 fusion.136
  83.2 2.6 %gather_fusion = bf16[256,512]{1,0:T(8,128)(2,1)S(1)} fusion(bf16[1024,512]{1,0:T(8,128)(2,1)} %get-tuple-element.384, s32[1024]{0:T(1024)S(1)} %pad_clamp_fusion.2), kind=kCustom, calls=%fused_computation.clone.clone.1 | custom fusion | bytes 525312 | tf_op jit(solution)/shard_map/while/body/eval_jaxpr/jit(_take)/gather | solution.py:47
  86.9 2.6 %gather_fusion = bf16[256,512]{1,0:T(8,128)(2,1)S(1)} fusion(bf16[1024,512]{1,0:T(8,128)(2,1)} %get-tuple-element.384, s32[1024]{0:T(1024)S(1)} %pad_clamp_fusion.2), kind=kCustom, calls=%fused_computation.clone.clone.1 | custom fusion | bytes 525312 | tf_op jit(solution)/shard_map/while/body/eval_jaxpr/jit(_take)/gather | solution.py:47
  89.8 0.4 fusion.136
  90.6 2.6 %gather_fusion = bf16[256,512]{1,0:T(8,128)(2,1)S(1)} fusion(bf16[1024,512]{1,0:T(8,128)(2,1)} %get-tuple-element.384, s32[1024]{0:T(1024)S(1)} %pad_clamp_fusion.2), kind=kCustom, calls=%fused_computation.clone.clone.1 | custom fusion | bytes 525312 | tf_op jit(solution)/shard_map/while/body/eval_jaxpr/jit(_take)/gather | solution.py:47
  93.5 0.4 fusion.136
  94.3 2.6 %gather_fusion = bf16[256,512]{1,0:T(8,128)(2,1)S(1)} fusion(bf16[1024,512]{1,0:T(8,128)(2,1)} %get-tuple-element.384, s32[1024]{0:T(1024)S(1)} %pad_clamp_fusion.2), kind=kCustom, calls=%fused_computation.clone.clone.1 | custom fusion | bytes 525312 | tf_op jit(solution)/shard_map/while/body/eval_jaxpr/jit(_take)/gather | solution.py:47
  98.1 2.6 %gather_fusion = bf16[256,512]{1,0:T(8,128)(2,1)S(1)} fusion(bf16[1024,512]{1,0:T(8,128)(2,1)} %get-tuple-element.384, s32[1024]{0:T(1024)S(1)} %pad_clamp_fusion.2), kind=kCustom, calls=%fused_computation.clone.clone.1 | custom fusion | bytes 525312 | tf_op jit(solution)/shard_map/while/body/eval_jaxpr/jit(_take)/gather | solution.py:47
  101.8 2.6 %gather_fusion = bf16[256,512]{1,0:T(8,128)(2,1)S(1)} fusion(bf16[1024,512]{1,0:T(8,128)(2,1)} %get-tuple-element.384, s32[1024]{0:T(1024)S(1)} %pad_clamp_fusion.2), kind=kCustom, calls=%fused_computation.clone.clone.1 | custom fusion | bytes 525312 | tf_op jit(solution)/shard_map/while/body/eval_jaxpr/jit(_take)/gather | solution.py:47
  104.7 0.4 fusion.136
  105.5 2.6 %gather_fusion = bf16[256,512]{1,0:T(8,128)(2,1)S(1)} fusion(bf16[1024,512]{1,0:T(8,128)(2,1)} %get-tuple-element.384, s32[1024]{0:T(1024)S(1)} %pad_clamp_fusion.2), kind=kCustom, calls=%fused_computation.clone.clone.1 | custom fusion | bytes 525312 | tf_op jit(solution)/shard_map/while/body/eval_jaxpr/jit(_take)/gather | solution.py:47
  109.2 2.6 %gather_fusion = bf16[256,512]{1,0:T(8,128)(2,1)S(1)} fusion(bf16[1024,512]{1,0:T(8,128)(2,1)} %get-tuple-element.384, s32[1024]{0:T(1024)S(1)} %pad_clamp_fusion.2), kind=kCustom, calls=%fused_computation.clone.clone.1 | custom fusion | bytes 525312 | tf_op jit(solution)/shard_map/while/body/eval_jaxpr/jit(_take)/gather | solution.py:47
  113.0 2.6 %gather_fusion = bf16[256,512]{1,0:T(8,128)(2,1)S(1)} fusion(bf16[1024,512]{1,0:T(8,128)(2,1)} %get-tuple-element.384, s32[1024]{0:T(1024)S(1)} %pad_clamp_fusion.2), kind=kCustom, calls=%fused_computation.clone.clone.1 | custom fusion | bytes 525312 | tf_op jit(solution)/shard_map/while/body/eval_jaxpr/jit(_take)/gather | solution.py:47
  116.7 2.6 %gather_fusion = bf16[256,512]{1,0:T(8,128)(2,1)S(1)} fusion(bf16[1024,512]{1,0:T(8,128)(2,1)} %get-tuple-element.384, s32[1024]{0:T(1024)S(1)} %pad_clamp_fusion.2), kind=kCustom, calls=%fused_computation.clone.clone.1 | custom fusion | bytes 525312 | tf_op jit(solution)/shard_map/while/body/eval_jaxpr/jit(_take)/gather | solution.py:47
  119.5 0.4 fusion.136
  120.4 2.6 %gather_fusion = bf16[256,512]{1,0:T(8,128)(2,1)S(1)} fusion(bf16[1024,512]{1,0:T(8,128)(2,1)} %get-tuple-element.384, s32[1024]{0:T(1024)S(1)} %pad_clamp_fusion.2), kind=kCustom, calls=%fused_computation.clone.clone.1 | custom fusion | bytes 525312 | tf_op jit(solution)/shard_map/while/body/eval_jaxpr/jit(_take)/gather | solution.py:47
  123.3 0.4 fusion.136
  125.2 0.8 copy.19
  126.0 0.7 reshape.262
  127.1 6.5 %fusion.74 = f32[1024,256]{1,0:T(8,128)S(1)} fusion(bf16[256,256]{1,0:T(8,128)(2,1)S(1)} %copy-done.15, f32[1024,256]{1,0:T(8,128)S(1)} %reshape.262, f32[1024,128]{1,0:T(8,128)} %bitcast.276, f32[1024,128]{1,0:T(8,128)} %bitcast.277, f32[1024,128]{1,0:T(8,128)} %bitcast.278, f32[1024,128]{1,0:T(8,128)} %bitcast.279, f32[1024,128]{1,0:T(8,128)} %bitcast.289, ...), kind=kOutput, calls=%fused_computation.182 | convolution fusion | flops 142868480 | bytes 19005440 | tf_op jit(solution)/shard_map/dot_general | solution.py:124
  133.9 0.7 copy-done.4
  135.0 0.7 copy-done.9
  136.0 0.7 copy-done.8
  137.4 0.7 copy-done.7
  138.4 0.7 copy-done.6
  139.5 0.7 copy-done.3
  140.5 0.7 copy-done.5
  141.5 0.5 reshape.271
  142.1 0.5 copy-done.2
  142.6 1.5 %broadcast_multiply_fusion = f32[32,32,2,128]{3,2,1,0:T(2,128)} fusion(f32[32,32,2,128]{3,2,1,0:T(2,128)S(1)} %reshape.271, f32[32,32,128]{2,1,0:T(8,128)S(1)} %copy-done.2), kind=kLoop, calls=%fused_computation.180 | loop fusion | flops 262144 | bytes 2621440 | tf_op jit(solution)/shard_map/mul | solution.py:139
  (275 shorter events, 19.6 us)
Async XLA Ops:
  6.5 3.7 %copy-start = (bf16[256,256]{1,0:T(8,128)(2,1)S(1)}, bf16[256,256]{1,0:T(8,128)(2,1)}, u32[]{:S(2)}) copy-start(bf16[256,256]{1,0:T(8,128)(2,1)} %param.16) | copy-start | bytes 393220
  6.5 57.8 %all-gather.2.cloned.1.call-start = ((), (), s32[]{:S(2)}) async-start(), calls=%async_computation | async-start | bytes 1310720 | tf_op jit(solution)/shard_map/all_gather | solution.py:109
  10.5 27.3 %collective-permute-start = (bf16[2,32,256]{2,1,0:T(8,128)(2,1)S(1)}, bf16[2,32,256]{2,1,0:T(8,128)(2,1)S(1)}, u32[]{:S(2)}, u32[]{:S(2)}) collective-permute-start(bf16[2,32,256]{2,1,0:T(8,128)(2,1)S(1)} %bitcast.304), channel_id=1, source_target_pairs={{0,4},{4,8},{8,12},{12,16},{16,20},{20,24},{24,28},{1,5},{5,9},{9,... | collective-permute-start | bytes 98312 | tf_op jit(solution)/shard_map/ppermute | solution.py:15
  14.3 23.6 %collective-permute-start.1 = (bf16[2,32,256]{2,1,0:T(8,128)(2,1)S(1)}, bf16[2,32,256]{2,1,0:T(8,128)(2,1)S(1)}, u32[]{:S(2)}, u32[]{:S(2)}) collective-permute-start(bf16[2,32,256]{2,1,0:T(8,128)(2,1)S(1)} %bitcast.303), channel_id=1, source_target_pairs={{4,0},{8,4},{12,8},{16,12},{20,16},{24,20},{28,24},{5,1},{9,5},{13... | collective-permute-start | bytes 98312 | tf_op jit(solution)/shard_map/ppermute | solution.py:17
  17.6 1.2 copy-start.13
  19.3 6.9 %copy-start.19 = (f32[16,2,128]{2,1,0:T(2,128)S(1)}, f32[16,2,128]{2,1,0:T(2,128)}, u32[]{:S(2)}) copy-start(f32[16,2,128]{2,1,0:T(2,128)} %param.18) | copy-start | bytes 49156
  19.3 6.9 %copy-start.16 = (f32[64,2,256]{2,1,0:T(2,128)S(1)}, f32[64,2,256]{2,1,0:T(2,128)}, u32[]{:S(2)}) copy-start(f32[64,2,256]{2,1,0:T(2,128)} %param.23) | copy-start | bytes 393220
  19.5 6.7 %copy-start.17 = (s32[16,16,16]{2,1,0:T(8,128)S(1)}, s32[16,16,16]{2,1,0:T(8,128)}, u32[]{:S(2)}) copy-start(s32[16,16,16]{2,1,0:T(8,128)} %param.21) | copy-start | bytes 49156
  19.5 6.8 %copy-start.18 = (s32[16,16,16]{2,1,0:T(8,128)S(1)}, s32[16,16,16]{2,1,0:T(8,128)}, u32[]{:S(2)}) copy-start(s32[16,16,16]{2,1,0:T(8,128)} %param.20) | copy-start | bytes 49156
  20.5 5.9 %collective-permute-start.4 = (bf16[1,32,2,128]{3,2,1,0:T(2,128)(2,1)S(1)}, bf16[1,32,2,128]{3,2,1,0:T(2,128)(2,1)S(1)}, u32[]{:S(2)}, u32[]{:S(2)}) collective-permute-start(bf16[1,32,2,128]{3,2,1,0:T(2,128)(2,1)S(1)} %get-tuple-element.260), channel_id=1, source_target_pairs={{0,4},{4,8},{8,12},{12,16},{16,20},{20,24},{24,28},{1,5},{5,9},{9,... | collective-permute-start | bytes 49160 | tf_op jit(solution)/shard_map/ppermute | solution.py:15
  24.2 5.1 %collective-permute-start.5 = (bf16[1,32,2,128]{3,2,1,0:T(2,128)(2,1)S(1)}, bf16[1,32,2,128]{3,2,1,0:T(2,128)(2,1)S(1)}, u32[]{:S(2)}, u32[]{:S(2)}) collective-permute-start(bf16[1,32,2,128]{3,2,1,0:T(2,128)(2,1)S(1)} %get-tuple-element.261), channel_id=1, source_target_pairs={{4,0},{8,4},{12,8},{16,12},{20,16},{24,20},{28,24},{5,1},{9,5},{13... | collective-permute-start | bytes 49160 | tf_op jit(solution)/shard_map/ppermute | solution.py:17
  29.3 17.2 %collective-permute-start.6 = (bf16[34,1,2,128]{3,2,1,0:T(2,128)(2,1)S(1)}, bf16[34,1,2,128]{3,2,1,0:T(2,128)(2,1)S(1)}, u32[]{:S(2)}, u32[]{:S(2)}) collective-permute-start(bf16[34,1,2,128]{3,2,1,0:T(2,128)(2,1)S(1)} %get-tuple-element.257), channel_id=1, source_target_pairs={{0,1},{1,2},{2,3},{4,5},{5,6},{6,7},{8,9},{9,10},{10,11},{12,13},{... | collective-permute-start | bytes 52232 | tf_op jit(solution)/shard_map/ppermute | solution.py:15
  32.4 14.0 %collective-permute-start.7 = (bf16[34,1,2,128]{3,2,1,0:T(2,128)(2,1)S(1)}, bf16[34,1,2,128]{3,2,1,0:T(2,128)(2,1)S(1)}, u32[]{:S(2)}, u32[]{:S(2)}) collective-permute-start(bf16[34,1,2,128]{3,2,1,0:T(2,128)(2,1)S(1)} %get-tuple-element.256), channel_id=1, source_target_pairs={{1,0},{2,1},{3,2},{5,4},{6,5},{7,6},{9,8},{10,9},{11,10},{13,12},{... | collective-permute-start | bytes 52232 | tf_op jit(solution)/shard_map/ppermute | solution.py:17
  37.9 15.1 %collective-permute-start.2 = (bf16[36,2,256]{2,1,0:T(2,128)(2,1)S(1)}, bf16[36,2,256]{2,1,0:T(2,128)(2,1)S(1)}, u32[]{:S(2)}, u32[]{:S(2)}) collective-permute-start(bf16[36,2,256]{2,1,0:T(2,128)(2,1)S(1)} %get-tuple-element.242), channel_id=1, source_target_pairs={{0,1},{1,2},{2,3},{4,5},{5,6},{6,7},{8,9},{9,10},{10,11},{12,13},{... | collective-permute-start | bytes 110600 | tf_op jit(solution)/shard_map/ppermute | solution.py:15
  40.2 12.9 %collective-permute-start.3 = (bf16[36,2,256]{2,1,0:T(2,128)(2,1)S(1)}, bf16[36,2,256]{2,1,0:T(2,128)(2,1)S(1)}, u32[]{:S(2)}, u32[]{:S(2)}) collective-permute-start(bf16[36,2,256]{2,1,0:T(2,128)(2,1)S(1)} %get-tuple-element.243), channel_id=1, source_target_pairs={{1,0},{2,1},{3,2},{5,4},{6,5},{7,6},{9,8},{10,9},{11,10},{13,12},{... | collective-permute-start | bytes 110600 | tf_op jit(solution)/shard_map/ppermute | solution.py:17
  61.9 2.5 %copy-start.14 = (s32[16,16]{1,0:T(8,128)S(1)}, s32[16,16]{1,0:T(8,128)}, u32[]{:S(2)}) copy-start(s32[16,16]{1,0:T(8,128)} %param.22) | copy-start | bytes 3076
  64.4 59.7 %copy-start.12 = (bf16[4,512,256]{2,1,0:T(8,128)(2,1)S(1)}, bf16[4,512,256]{2,1,0:T(8,128)(2,1)}, u32[]{:S(2)}) copy-start(bf16[4,512,256]{2,1,0:T(8,128)(2,1)} %param.24) | copy-start | bytes 3145732
  126.0 1.0 copy-start.1
  126.0 1.1 copy-start.15
  127.1 6.5 %copy-start.10 = (bf16[32,32,2,128]{3,2,1,0:T(2,128)(2,1)S(1)}, bf16[32,32,2,128]{3,2,1,0:T(2,128)(2,1)}, u32[]{:S(2)}) copy-start(bf16[32,32,2,128]{3,2,1,0:T(2,128)(2,1)} %get-tuple-element.302) | copy-start | bytes 1572868
  127.1 6.5 %copy-start.11 = (bf16[9,256,256]{2,1,0:T(8,128)(2,1)S(1)}, bf16[9,256,256]{2,1,0:T(8,128)(2,1)}, u32[]{:S(2)}) copy-start(bf16[9,256,256]{2,1,0:T(8,128)(2,1)} %param.17) | copy-start | bytes 3538948
  133.6 1.0 copy-start.4
  134.7 1.0 copy-start.9
  135.7 1.0 copy-start.8
  137.1 1.0 copy-start.7
  138.1 1.0 copy-start.6
  139.1 1.0 copy-start.3
  140.2 1.0 copy-start.5
  141.5 1.0 copy-start.2
Sparse Core Ops, SparseCore 0:
  20.6 28.7 all-gather.1
where the time goes:
time: 152 us; the launch traced here: 151 us
  local copies, waits for them, and re-layouts  61.8 us (41%)
  other arithmetic  29.2 us (19%)
  starting transfers between devices  23.6 us (16%)
  matrix products  18.5 us (12%)
  between operations  13.9 us (9%)
  waiting for transfers between devices  2.81 us (2%)
    gather x16, local copies, waits for them, and re-layouts, accumulate(): source = jnp.take(flat_group, index, axis=0)  41.2 us
    sub x23, other arithmetic, complex_flat(): first = table[..., :half] * real_part - table[..., half:] * imag_part  14.4 us
    ppermute x4, starting transfers between devices, extended(): lax.ppermute(tail, axis, [(i, (i + 1) % count) for i in range(ends)])  12.7 us
    ppermute x4, starting transfers between devices, extended(): lax.ppermute(head, axis, [((i + 1) % count, i) for i in range(ends)])  10.9 us
    unnamed x47, local copies, waits for them, and re-layouts  7.43 us
    dot_general x16, matrix products, accumulate(): jnp.dot(choose, table, precision=lax.Precision.HIGHEST, preferred_element...  6.53 us
    dot_general x1, matrix products, body(): jnp.dot(incoming.reshape(tile_x * tile_y, 2 * samples), receive_map, pref...  6.53 us
    concatenate x4, other arithmetic, extended(): jnp.concatenate([lax.ppermute(tail, axis, [(i, (i + 1) % count) for i in...  5.13 us
  transfers between devices with their start and end apart: 9, of which 1 were waited for; matrix products, arithmetic and copies ran while one was open for 17% of the time, Pallas kernels for 0%

commit v1 on v0

v1 whole, which is shorter than its diff:
```python
import functools

import jax
import jax.numpy as jnp
from jax import lax
from jax.experimental import pallas as pl
from jax.experimental.pallas import tpu as pltpu
from jax.sharding import PartitionSpec as P

F32 = jnp.float32
BF16 = jnp.bfloat16
MIB = 1 << 20


def vmem(count):
    return [pl.BlockSpec(memory_space=pltpu.VMEM)] * count


def params(mib):
    return pltpu.CompilerParams(vmem_limit_bytes=mib * MIB)


def cost(macs, moved):
    return pl.CostEstimate(flops=2 * macs, bytes_accessed=moved, transcendentals=0)


def mm(left, right):
    return jnp.dot(left, right, preferred_element_type=F32)


def count_rows(counts_ref, tile_x, tile_y, lanes):
    eye = lax.broadcasted_iota(jnp.int32, (tile_y, tile_y), 0) == lax.broadcasted_iota(
        jnp.int32, (tile_y, tile_y), 1
    )
    counts = counts_ref[...].astype(F32)
    diag = [
        jnp.where(eye, jnp.broadcast_to(counts[i : i + 1], (tile_y, tile_y)), 0.0) for i in range(tile_x)
    ]
    return mm(jnp.concatenate(diag, axis=0).astype(BF16), jnp.ones((tile_y, lanes), BF16))


def parents_kernel(tile_x, tile_y, cur_ref, counts_ref, agg_ref, up_ref, live_ref, coarse_ref, wide, pats):
    lanes = cur_ref.shape[1]
    wide[...] = cur_ref[...].astype(F32)
    boxes = tile_x * tile_y
    keep = lax.broadcasted_iota(jnp.int32, (boxes, lanes), 1).astype(F32) < count_rows(
        counts_ref, tile_x, tile_y, lanes
    )
    for part in range(2):
        live = jnp.where(keep, wide[pl.ds(part, boxes, stride=2), :], 0.0)
        live_ref[:, part * lanes : (part + 1) * lanes] = live.astype(BF16)
    pattern = mm(live_ref[...], agg_ref[...])
    half = pattern.shape[1] // 2
    pats[0] = pattern[:, :half]
    pats[1] = pattern[:, half:]
    children = []
    for side_x in range(2):
        for side_y in range(2):
            for part in range(2):
                rows = [
                    pats[part, pl.ds((2 * p + side_x) * tile_y + side_y, tile_y // 2, stride=2), :]
                    for p in range(tile_x // 2)
                ]
                children.append(jnp.concatenate(rows, axis=0).astype(BF16))
    coarse_ref[...] = mm(jnp.concatenate(children, axis=1), up_ref[...]).astype(BF16)


LEFT = 8


def local_kernel(
    tile_x, tile_y, live_ref, top_ref, bottom_ref, left_ref, right_ref, agg_ref, near_ref, low_ref,
    lower_ref, field_ref, cells, sides, packed, pats, shifted,
):
    lanes = lower_ref.shape[2]
    width = tile_y + 2 * LEFT
    rows_x = tile_x + 4
    for part in range(2):
        cols = slice(part * lanes, (part + 1) * lanes)
        sides[0] = left_ref[:, cols].astype(F32)
        sides[1] = right_ref[:, cols].astype(F32)
        for i in range(rows_x):
            if i < 2:
                row = top_ref[i * tile_y : (i + 1) * tile_y, cols]
            elif i < tile_x + 2:
                row = live_ref[(i - 2) * tile_y : (i - 1) * tile_y, cols]
            else:
                row = bottom_ref[(i - tile_x - 2) * tile_y : (i - tile_x - 1) * tile_y, cols]
            base = i * width + LEFT
            cells[part, base : base + tile_y, :] = row.astype(F32)
            cells[part, base - 2 : base, :] = sides[0, 2 * i : 2 * i + 2, :]
            cells[part, base + tile_y : base + tile_y + 2, :] = sides[1, 2 * i : 2 * i + 2, :]
        packed[:, cols] = cells[part].astype(BF16)
        for i in range(tile_x + 2):
            for shift in range(-1, 2):
                base = (i + 1) * width + LEFT + shift
                place = (2 * (shift + 1) + part) * lanes
                shifted[i * tile_y : (i + 1) * tile_y, place : place + lanes] = cells[
                    part, base : base + tile_y, :
                ].astype(BF16)
    pattern = mm(packed[...], agg_ref[...]).astype(BF16).astype(F32)
    pats[0] = pattern[:, :lanes]
    pats[1] = pattern[:, lanes:]

    offsets = [
        (dx, dy) for dx in range(-2, 3) for dy in range(-2, 3) if max(abs(dx), abs(dy)) == 2
    ]

    def lower_row(i, carry):
        first = jnp.zeros((tile_y, lanes), F32)
        second = jnp.zeros((tile_y, lanes), F32)
        for k, (dx, dy) in enumerate(offsets):
            start = (i + 2 + dx) * width + (LEFT + dy)
            real = pats[0, pl.ds(start, tile_y), :]
            imag = pats[1, pl.ds(start, tile_y), :]
            t_real = low_ref[2 * k : 2 * k + 1, :]
            t_imag = low_ref[2 * k + 1 : 2 * k + 2, :]
            first = first + (t_real * real - t_imag * imag)
            second = second + (t_real * imag + t_imag * real)
        lower_ref[0, pl.ds(pl.multiple_of(i * tile_y, tile_y), tile_y), :] = first
        lower_ref[1, pl.ds(pl.multiple_of(i * tile_y, tile_y), tile_y), :] = second
        return carry

    lax.fori_loop(0, tile_x, lower_row, 0)
    depth = near_ref.shape[1]
    for block in range(4):
        size = tile_x * tile_y // 4
        total = None
        for shift in range(3):
            start = block * size + shift * tile_y
            term = mm(shifted[start : start + size, :], near_ref[shift])
            total = term if total is None else total + term
        field_ref[0, block * size : (block + 1) * size, :] = total[:, :lanes]
        field_ref[1, block * size : (block + 1) * size, :] = total[:, lanes:]


STEP = 2


def lists_kernel(chunks, tile_x, tile_y, *refs):
    sources = refs[:chunks]
    (codes_ref, kinds_ref, table_ref, counts_ref, lower_ref, near_ref, down_ref, recv_ref, out_ref,
     group, pieces, picks, kind_picks, incoming, kept) = refs[chunks:]
    parents_x, parents_y = tile_x // 2, tile_y // 2
    parents = parents_x * parents_y
    slots = codes_ref.shape[1]
    kinds, wide = table_ref.shape
    half = wide // 2
    lanes = lower_ref.shape[2]
    for c in range(chunks):
        group[c * parents : (c + 1) * parents, :] = sources[c][...]
    table = table_ref[...]
    high = table.astype(BF16)
    middle = (table - high.astype(F32)).astype(BF16)
    low = (table - high.astype(F32) - middle.astype(F32)).astype(BF16)
    pieces[0:kinds, :] = high
    pieces[kinds : 2 * kinds, :] = middle
    pieces[2 * kinds : 3 * kinds, :] = low
    lane = lax.broadcasted_iota(jnp.int32, (parents_y, 128), 1)
    kind_of = lax.rem(lane, kinds)

    def step(n, carry):
        for k in range(STEP):
            start = pl.multiple_of((n * STEP + k) * parents_y, parents_y)
            codes = codes_ref[pl.ds(start, parents_y), :]
            kind = kinds_ref[pl.ds(start, parents_y), :]
            for s in range(slots):
                row = (k * slots + s) * parents_y
                code = jnp.broadcast_to(codes[:, s : s + 1], (parents_y, 128))
                for c in range(chunks * parents // 128):
                    picks[row : row + parents_y, c * 128 : (c + 1) * 128] = jnp.where(
                        code == lane + c * 128, 1.0, 0.0
                    ).astype(BF16)
                which = jnp.broadcast_to(kind[:, s : s + 1], (parents_y, 128))
                hit = jnp.where(which == kind_of, 1.0, 0.0).astype(BF16)
                kind_picks[row : row + parents_y, 0:128] = hit
                kind_picks[row : row + parents_y, 128 : 3 * kinds] = hit[:, : 3 * kinds - 128]
        gathered = mm(picks[...], group[...])
        factors = mm(kind_picks[...], pieces[...])
        for k in range(STEP):
            first = jnp.zeros((parents_y, half), F32)
            second = jnp.zeros((parents_y, half), F32)
            for s in range(slots):
                row = slice((k * slots + s) * parents_y, (k * slots + s + 1) * parents_y)
                t_real, t_imag = factors[row, :half], factors[row, half:]
                real, imag = gathered[row, :half], gathered[row, half:]
                first = first + (t_real * real - t_imag * imag)
                second = second + (t_real * imag + t_imag * real)
            start = pl.multiple_of((n * STEP + k) * parents_y, parents_y)
            incoming[pl.ds(start, parents_y), :half] = first.astype(BF16)
            incoming[pl.ds(start, parents_y), half:] = second.astype(BF16)
        return carry

    lax.fori_loop(0, parents_x // STEP, step, 0)

    limits = count_rows(counts_ref, tile_x, tile_y, lanes)
    kept[...] = jnp.where(
        lax.broadcasted_iota(jnp.int32, limits.shape, 1).astype(F32) < limits, 1.0, 0.0
    )
    for side_x in range(2):
        for side_y in range(2):
            down = mm(incoming[...], down_ref[2 * side_x + side_y])
            starts = [(2 * p + side_x) * tile_y + side_y for p in range(parents_x)]

            def rows_of(ref, part):
                return jnp.concatenate(
                    [ref[part, pl.ds(start, parents_y, stride=2), :] for start in starts], axis=0
                )

            total = jnp.concatenate(
                [down[:, part * lanes : (part + 1) * lanes] + rows_of(lower_ref, part) for part in range(2)],
                axis=1,
            )
            field = mm(total.astype(BF16), recv_ref[...])
            mask = jnp.concatenate(
                [kept[pl.ds(start, parents_y, stride=2), :] for start in starts], axis=0
            )
            for part in range(2):
                value = (field[:, part * lanes : (part + 1) * lanes] + rows_of(near_ref, part)) * mask
                for p, start in enumerate(starts):
                    out_ref[pl.ds(2 * start + part, parents_y, stride=4), :] = value[
                        p * parents_y : (p + 1) * parents_y
                    ]


def shifts_of(count):
    up = [(i, i + 1) for i in range(count - 1)]
    return up, [(b, a) for a, b in up]


def body(
    currents, box_count, aggregate, near_blocks, low_translator, child_to_parent, coarse_list,
    coarse_kind, coarse_count, up_translator, parent_to_child, receive_map,
):
    tile_x, tile_y = box_count.shape
    boxes = tile_x * tile_y
    lanes = currents.shape[-1]
    parents_x, parents_y, slots = coarse_list.shape
    parents = parents_x * parents_y
    kinds, _, half = up_translator.shape
    wide = 2 * half
    chunks = lax.axis_size("gy")

    live, coarse = pl.pallas_call(
        functools.partial(parents_kernel, tile_x, tile_y),
        name="parents",
        out_shape=[
            jax.ShapeDtypeStruct((boxes, 2 * lanes), BF16),
            jax.ShapeDtypeStruct((parents, wide), BF16),
        ],
        in_specs=vmem(4),
        out_specs=vmem(2),
        scratch_shapes=[pltpu.VMEM((2 * boxes, lanes), F32), pltpu.VMEM((2, boxes, lanes), F32)],
        compiler_params=params(32),
        cost_estimate=cost(200 * MIB, 3 * MIB),
    )(
        currents.reshape(2 * boxes, lanes),
        box_count,
        aggregate,
        child_to_parent.reshape(8 * lanes, wide),
    )

    sources = [coarse] + [
        lax.ppermute(coarse, "gy", [(i, i ^ d) for i in range(chunks)]) for d in range(1, chunks)
    ]
    up, down = shifts_of(lax.axis_size("gx"))
    top = lax.ppermute(live[boxes - 2 * tile_y :], "gx", up)
    bottom = lax.ppermute(live[: 2 * tile_y], "gx", down)
    tall = jnp.concatenate([top, live, bottom], axis=0).reshape(tile_x + 4, tile_y, 2 * lanes)

    def edge(cells):
        cells = cells.reshape(2 * (tile_x + 4), 2 * lanes)
        return jnp.pad(cells, ((0, -cells.shape[0] % 16), (0, 0)))

    up, down = shifts_of(chunks)
    left = lax.ppermute(edge(tall[:, tile_y - 2 :]), "gy", up)
    right = lax.ppermute(edge(tall[:, :2]), "gy", down)

    width = tile_y + 2 * LEFT
    lower, near = pl.pallas_call(
        functools.partial(local_kernel, tile_x, tile_y),
        name="local",
        out_shape=[
            jax.ShapeDtypeStruct((2, boxes, lanes), F32),
            jax.ShapeDtypeStruct((2, boxes, lanes), F32),
        ],
        in_specs=vmem(8),
        out_specs=vmem(2),
        scratch_shapes=[
            pltpu.VMEM((2, (tile_x + 4) * width, lanes), F32),
            pltpu.VMEM((2,) + (left.shape[0], lanes), F32),
            pltpu.VMEM(((tile_x + 4) * width, 2 * lanes), BF16),
            pltpu.VMEM((2, (tile_x + 4) * width, lanes), F32),
            pltpu.VMEM(((tile_x + 2) * tile_y, 6 * lanes), BF16),
        ],
        compiler_params=params(48),
        cost_estimate=cost(2000 * MIB, 5 * MIB),
    )(
        live, top, bottom, left, right, aggregate,
        near_blocks.reshape(3, 6 * lanes, 2 * lanes),
        low_translator.reshape(-1, lanes),
    )

    me = lax.axis_index("gy")
    across = parents_y * chunks
    row, column = coarse_list // across, coarse_list % across
    place = (column // parents_y) ^ me
    codes = place * parents + row * parents_y + column % parents_y
    used = lax.broadcasted_iota(jnp.int32, codes.shape, 2) < coarse_count[:, :, None]
    codes = jnp.where(used, codes, -1).reshape(parents, slots)

    out = pl.pallas_call(
        functools.partial(lists_kernel, chunks, tile_x, tile_y),
        name="lists",
        out_shape=jax.ShapeDtypeStruct((2 * boxes, lanes), F32),
        in_specs=vmem(chunks + 8),
        out_specs=pl.BlockSpec(memory_space=pltpu.VMEM),
        scratch_shapes=[
            pltpu.VMEM((chunks * parents, wide), BF16),
            pltpu.VMEM((3 * kinds, wide), BF16),
            pltpu.VMEM((STEP * slots * parents_y, chunks * parents), BF16),
            pltpu.VMEM((STEP * slots * parents_y, 3 * kinds), BF16),
            pltpu.VMEM((parents, wide), BF16),
            pltpu.VMEM((boxes, lanes), F32),
        ],
        compiler_params=params(56),
        cost_estimate=cost(3000 * MIB, 8 * MIB),
    )(
        *sources, codes, coarse_kind.reshape(parents, slots),
        up_translator.reshape(kinds, wide), box_count, lower, near, parent_to_child, receive_map,
    )
    return out.reshape(tile_x, tile_y, 2, lanes)


def solution(mesh):
    tiles = P("gx", "gy")
    in_specs = (tiles, tiles, P(), P(), P(), P(), tiles, tiles, tiles, P(), P(), P())
    return jax.shard_map(body, mesh=mesh, in_specs=in_specs, out_specs=tiles, check_vma=False)
```

time: 152 us -> 49.4 us (0.33)
  the two profiles are of different devices: /device:TPU:5 before, /device:TPU:0 now
where the time goes in v1:
time: 49.4 us; the launch traced here: 49 us
  Pallas kernels  18.8 us (38%)
  starting transfers between devices  14.2 us (29%)
  local copies, waits for them, and re-layouts  7.57 us (15%)
  waiting for transfers between devices  7.33 us (15%)
  other arithmetic  0.95 us (2%)
    pallas_call x1, Pallas kernels, body(): pl.pallas_call(functools.partial(lists_kernel, chunks, tile_x, tile_y), n...  12.8 us
    unnamed x33, local copies, waits for them, and re-layouts  7.45 us
    ppermute x1, waiting for transfers between devices, body(): left = lax.ppermute(edge(tall[:, tile_y - 2:]), 'gy', up)  5.45 us
    pallas_call x1, Pallas kernels, body(): pl.pallas_call(functools.partial(local_kernel, tile_x, tile_y), name='loc...  5.1 us
    ppermute x3, starting transfers between devices, body(): lax.ppermute(coarse, 'gy', [(i, i ^ d) for i in range(chunks)])  4.6 us
    ppermute x1, starting transfers between devices, body(): left = lax.ppermute(edge(tall[:, tile_y - 2:]), 'gy', up)  3.81 us
    ppermute x1, starting transfers between devices, body(): top = lax.ppermute(live[boxes - 2 * tile_y:], 'gx', up)  3.03 us
    ppermute x1, waiting for transfers between devices, body(): right = lax.ppermute(edge(tall[:, :2]), 'gy', down)  1.86 us
  transfers between devices with their start and end apart: 7, of which 2 were waited for; matrix products, arithmetic and copies ran while one was open for 4% of the time, Pallas kernels for 10%

profile of v1, /device:TPU:0, one launch (start us, length us, event | category | flops | bytes accessed | tf_op | source)
XLA Modules:
  0.0 49.0 jit_solution(2266502933634628736)
XLA Ops:
  0.0 0.0 copy-start
  0.0 1.2 %copy-done = bf16[4,256,512]{2,1,0:T(8,128)(2,1)S(1)} copy-done((bf16[4,256,512]{2,1,0:T(8,128)(2,1)S(1)}, bf16[4,256,512]{2,1,0:T(8,128)(2,1)}, u32[]{:S(2)}) %copy-start) | copy-done | bytes 1048600
  1.2 0.0 copy-start.1
  1.2 1.0 %copy-done.1 = bf16[32,32,2,128]{3,2,1,0:T(2,128)(2,1)S(1)} copy-done((bf16[32,32,2,128]{3,2,1,0:T(2,128)(2,1)S(1)}, bf16[32,32,2,128]{3,2,1,0:T(2,128)(2,1)}, u32[]{:S(2)}) %copy-start.1) | copy-done | bytes 524312
  2.3 0.0 copy-start.2
  2.3 0.9 %copy-done.2 = bf16[256,256]{1,0:T(8,128)(2,1)S(1)} copy-done((bf16[256,256]{1,0:T(8,128)(2,1)S(1)}, bf16[256,256]{1,0:T(8,128)(2,1)}, u32[]{:S(2)}) %copy-start.2) | copy-done | bytes 131096
  3.2 0.0 copy-start.4
  3.2 0.7 %copy-done.4 = s32[32,32]{1,0:T(8,128)S(1)} copy-done((s32[32,32]{1,0:T(8,128)S(1)}, s32[32,32]{1,0:T(8,128)}, u32[]{:S(2)}) %copy-start.4) | copy-done | bytes 4120
  3.9 0.9 %parents.1 = (bf16[1024,256]{1,0:T(8,128)(2,1)S(1)}, bf16[256,512]{1,0:T(8,128)(2,1)S(1)}) custom-call(bf16[2048,128]{1,0:T(8,128)(2,1)S(1)} %bitcast.11, s32[32,32]{1,0:T(8,128)S(1)} %copy-done.4, bf16[256,256]{1,0:T(8,128)(2,1)S(1)} %copy-done.2, bf16[1024,512]{1,0:T(8,128)(2,1)S(1)} %bitcast.10), custom_call_target="tpu_custom_call" | custom-call | flops 419430400 | bytes 3145728 | tf_op jit(solution)/shard_map/parents/pallas_call | solution.py:244
  4.8 0.0 copy-start.6
  4.8 0.0 copy-start.10
  4.8 0.0 copy-start.12
  4.8 0.0 copy-start.11
  4.8 0.0 copy-start.3
  4.8 0.0 copy-start.5
  4.8 0.0 copy-start.7
  4.9 1.4 %collective-permute-start.4 = (bf16[64,256]{1,0:T(8,128)(2,1)S(1)}, bf16[64,256]{1,0:T(8,128)(2,1)S(1)}, u32[]{:S(2)}, u32[]{:S(2)}) collective-permute-start(bf16[64,256]{1,0:T(8,128)(2,1)S(1)} %get-tuple-element.15), channel_id=1, source_target_pairs={{4,0},{8,4},{12,8},{16,12},{20,16},{24,20},{28,24},{5,1},{9,5},{13... | collective-permute-start | bytes 98312 | tf_op jit(solution)/shard_map/ppermute | solution.py:268
  6.3 3.0 %collective-permute-start.3 = (bf16[64,256]{1,0:T(8,128)(2,1)S(1)}, bf16[64,256]{1,0:T(8,128)(2,1)S(1)}, u32[]{:S(2)}, u32[]{:S(2)}) collective-permute-start(bf16[64,256]{1,0:T(8,128)(2,1)S(1)} %get-tuple-element.16), channel_id=1, source_target_pairs={{0,4},{4,8},{8,12},{12,16},{16,20},{20,24},{24,28},{1,5},{5,9},{9,... | collective-permute-start | bytes 98312 | tf_op jit(solution)/shard_map/ppermute | solution.py:267
  9.3 4.0 %collective-permute-start.2 = (bf16[256,512]{1,0:T(8,128)(2,1)S(1)}, bf16[256,512]{1,0:T(8,128)(2,1)S(1)}, u32[]{:S(2)}, u32[]{:S(2)}) collective-permute-start(bf16[256,512]{1,0:T(8,128)(2,1)S(1)} %get-tuple-element.9.refs_0_), channel_id=1, source_target_pairs={{0,3},{1,2},{2,1},{3,0},{4,7},{5,6},{6,5},{7,4},{8,11},{9,10},{10,... | collective-permute-start | bytes 786440 | tf_op jit(solution)/shard_map/ppermute | solution.py:264
  13.3 0.5 %collective-permute-start.1 = (bf16[256,512]{1,0:T(8,128)(2,1)S(1)}, bf16[256,512]{1,0:T(8,128)(2,1)S(1)}, u32[]{:S(2)}, u32[]{:S(2)}) collective-permute-start(bf16[256,512]{1,0:T(8,128)(2,1)S(1)} %get-tuple-element.9.refs_0_), channel_id=1, source_target_pairs={{0,2},{1,3},{2,0},{3,1},{4,6},{5,7},{6,4},{7,5},{8,10},{9,11},{10,... | collective-permute-start | bytes 786440 | tf_op jit(solution)/shard_map/ppermute | solution.py:264
  13.8 0.1 collective-permute-start
  13.9 0.0 collective-permute-done.4.bottom_ref
  13.9 0.0 collective-permute-done.3.top_ref
  14.0 0.1 fusion.12
  14.1 3.8 %collective-permute-start.5 = (bf16[80,256]{1,0:T(8,128)(2,1)S(1)}, bf16[80,256]{1,0:T(8,128)(2,1)S(1)}, u32[]{:S(2)}, u32[]{:S(2)}) collective-permute-start(bf16[80,256]{1,0:T(8,128)(2,1)S(1)} %pad.7), channel_id=1, source_target_pairs={{0,1},{1,2},{2,3},{4,5},{5,6},{6,7},{8,9},{9,10},{10,11},{12,13},{... | collective-permute-start | bytes 122888 | tf_op jit(solution)/shard_map/ppermute | solution.py:276
  18.0 1.3 %collective-permute-start.6 = (bf16[80,256]{1,0:T(8,128)(2,1)S(1)}, bf16[80,256]{1,0:T(8,128)(2,1)S(1)}, u32[]{:S(2)}, u32[]{:S(2)}) collective-permute-start(bf16[80,256]{1,0:T(8,128)(2,1)S(1)} %pad.8), channel_id=1, source_target_pairs={{1,0},{2,1},{3,2},{5,4},{6,5},{7,6},{9,8},{10,9},{11,10},{13,12},{... | collective-permute-start | bytes 122888 | tf_op jit(solution)/shard_map/ppermute | solution.py:277
  19.3 0.0 copy-done.10
  19.3 0.0 copy-done.12
  19.3 0.9 %fusion.4 = s32[16,16,16]{2,1,0:T(8,128)} fusion(s32[16,16,16]{2,1,0:T(8,128)S(1)} %copy-done.10, s32[]{:T(128)S(6)} %axis_index.12, s32[16,16]{1,0:T(8,128)S(1)} %copy-done.12), kind=kLoop, calls=%fused_computation.15 | loop fusion | flops 184320 | bytes 33796 | tf_op jit(solution)/shard_map/jit(_where)/select_n | solution.py:310
  20.2 0.0 copy-done.11
  20.2 0.7 %copy.13 = f32[8,8,2,256]{3,1,2,0:T(8,128)} copy(f32[8,8,2,256]{3,2,1,0:T(2,128)S(1)} %bitcast.15) | data formatting | bytes 262144
  20.8 5.5 %collective-permute-done.5.left_ref = bf16[80,256]{1,0:T(8,128)(2,1)S(1)} collective-permute-done((bf16[80,256]{1,0:T(8,128)(2,1)S(1)}, bf16[80,256]{1,0:T(8,128)(2,1)S(1)}, u32[]{:S(2)}, u32[]{:S(2)}) %collective-permute-start.5) | collective-permute-done | bytes 40992 | tf_op jit(solution)/shard_map/ppermute | solution.py:276
  26.3 1.9 %collective-permute-done.6.right_ref = bf16[80,256]{1,0:T(8,128)(2,1)S(1)} collective-permute-done((bf16[80,256]{1,0:T(8,128)(2,1)S(1)}, bf16[80,256]{1,0:T(8,128)(2,1)S(1)}, u32[]{:S(2)}, u32[]{:S(2)}) %collective-permute-start.6) | collective-permute-done | bytes 40992 | tf_op jit(solution)/shard_map/ppermute | solution.py:277
  28.2 0.0 copy-done.3
  28.2 0.0 copy-done.5
  28.2 0.0 copy-done.7
  28.2 5.1 %local.1 = (f32[2,1024,128]{2,1,0:T(8,128)S(1)}, f32[2,1024,128]{2,1,0:T(8,128)S(1)}) custom-call(bf16[1024,256]{1,0:T(8,128)(2,1)S(1)} %get-tuple-element.10.live_ref, bf16[64,256]{1,0:T(8,128)(2,1)S(1)} %collective-permute-done.3.top_ref, bf16[64,256]{1,0:T(8,128)(2,1)S(1)} %collective-permute-done.4.bottom_ref, ...), custom_call_target="tpu_custom_call" | custom-call | flops 4194304000 | bytes 5242880 | tf_op jit(solution)/shard_map/local/pallas_call | solution.py:280
  33.3 0.0 copy-done.6
  33.3 0.0 copy-start.8
  33.3 1.0 %copy-done.8 = f32[2,1024,128]{2,1,0:T(8,128)} copy-done((f32[2,1024,128]{2,1,0:T(8,128)}, f32[2,1024,128]{2,1,0:T(8,128)S(1)}, u32[]{:S(2)}) %copy-start.8) | copy-done | bytes 1048600
  34.3 0.0 copy-start.9
  34.3 1.0 %copy-done.9 = f32[2,1024,128]{2,1,0:T(8,128)} copy-done((f32[2,1024,128]{2,1,0:T(8,128)}, f32[2,1024,128]{2,1,0:T(8,128)S(1)}, u32[]{:S(2)}) %copy-start.9) | copy-done | bytes 1048600
  35.3 0.0 collective-permute-done.2.refs_3_
  35.3 0.0 copy-start.13
  35.3 0.0 collective-permute-done.1.refs_2_
  35.3 0.0 copy-start.14
  35.3 0.0 collective-permute-done.refs_1_
  35.3 0.0 copy-start.15
  35.3 0.7 %copy-done.13 = bf16[256,512]{1,0:T(8,128)(2,1)} copy-done((bf16[256,512]{1,0:T(8,128)(2,1)}, bf16[256,512]{1,0:T(8,128)(2,1)S(1)}, u32[]{:S(2)}) %copy-start.13) | copy-done | bytes 262168
  36.0 0.1 copy-done.14
  36.1 0.1 copy-done.15
  36.2 12.8 %lists.1 = f32[2048,128]{1,0:T(8,128)} custom-call(bf16[256,512]{1,0:T(8,128)(2,1)} %copy-done.6, bf16[256,512]{1,0:T(8,128)(2,1)} %copy-done.15, bf16[256,512]{1,0:T(8,128)(2,1)} %copy-done.14, bf16[256,512]{1,0:T(8,128)(2,1)} %copy-done.13, s32[256,16]{1,0:T(8,128)} %bitcast.16, s32[256,16]{1,0:T(8,128)} %bitcast.18, f32[64,512]{1,0:T(8,128)} %bitcast.17, ...), custom_call_target="tpu_custom_call" | custom-call | flops 6291456000 | bytes 8388608 | tf_op jit(solution)/shard_map/lists/pallas_call | solution.py:312
  (6 shorter events, 0.1 us)
Async XLA Ops:
  0.0 1.2 %copy-start = (bf16[4,256,512]{2,1,0:T(8,128)(2,1)S(1)}, bf16[4,256,512]{2,1,0:T(8,128)(2,1)}, u32[]{:S(2)}) copy-start(bf16[4,256,512]{2,1,0:T(8,128)(2,1)} %param.17) | copy-start | bytes 3145732
  1.2 1.0 %copy-start.1 = (bf16[32,32,2,128]{3,2,1,0:T(2,128)(2,1)S(1)}, bf16[32,32,2,128]{3,2,1,0:T(2,128)(2,1)}, u32[]{:S(2)}) copy-start(bf16[32,32,2,128]{3,2,1,0:T(2,128)(2,1)} %param.12) | copy-start | bytes 1572868
  2.3 0.9 %copy-start.2 = (bf16[256,256]{1,0:T(8,128)(2,1)S(1)}, bf16[256,256]{1,0:T(8,128)(2,1)}, u32[]{:S(2)}) copy-start(bf16[256,256]{1,0:T(8,128)(2,1)} %agg_ref.3) | copy-start | bytes 393220
  3.2 0.7 %copy-start.4 = (s32[32,32]{1,0:T(8,128)S(1)}, s32[32,32]{1,0:T(8,128)}, u32[]{:S(2)}) copy-start(s32[32,32]{1,0:T(8,128)} %refs_7_.1) | copy-start | bytes 12292
  4.8 28.5 %copy-start.6 = (bf16[256,512]{1,0:T(8,128)(2,1)}, bf16[256,512]{1,0:T(8,128)(2,1)S(1)}, u32[]{:S(2)}) copy-start(bf16[256,512]{1,0:T(8,128)(2,1)S(1)} %get-tuple-element.9.refs_0_) | copy-start | bytes 786436
  4.8 14.5 %copy-start.10 = (s32[16,16,16]{2,1,0:T(8,128)S(1)}, s32[16,16,16]{2,1,0:T(8,128)}, u32[]{:S(2)}) copy-start(s32[16,16,16]{2,1,0:T(8,128)} %param.18) | copy-start | bytes 49156
  4.8 14.5 %copy-start.12 = (s32[16,16]{1,0:T(8,128)S(1)}, s32[16,16]{1,0:T(8,128)}, u32[]{:S(2)}) copy-start(s32[16,16]{1,0:T(8,128)} %param.20) | copy-start | bytes 3076
  4.8 15.4 %copy-start.11 = (f32[64,2,256]{2,1,0:T(2,128)S(1)}, f32[64,2,256]{2,1,0:T(2,128)}, u32[]{:S(2)}) copy-start(f32[64,2,256]{2,1,0:T(2,128)} %param.21) | copy-start | bytes 393220
  4.8 23.4 %copy-start.3 = (bf16[256,256]{1,0:T(8,128)(2,1)S(1)}, bf16[256,256]{1,0:T(8,128)(2,1)}, u32[]{:S(2)}) copy-start(bf16[256,256]{1,0:T(8,128)(2,1)} %agg_ref.3) | copy-start | bytes 393220
  4.8 23.4 %copy-start.5 = (bf16[9,256,256]{2,1,0:T(8,128)(2,1)S(1)}, bf16[9,256,256]{2,1,0:T(8,128)(2,1)}, u32[]{:S(2)}) copy-start(bf16[9,256,256]{2,1,0:T(8,128)(2,1)} %param.15) | copy-start | bytes 3538948
  4.8 23.3 %copy-start.7 = (f32[16,2,128]{2,1,0:T(2,128)S(1)}, f32[16,2,128]{2,1,0:T(2,128)}, u32[]{:S(2)}) copy-start(f32[16,2,128]{2,1,0:T(2,128)} %param.16) | copy-start | bytes 49156
  4.9 9.1 %collective-permute-start.4 = (bf16[64,256]{1,0:T(8,128)(2,1)S(1)}, bf16[64,256]{1,0:T(8,128)(2,1)S(1)}, u32[]{:S(2)}, u32[]{:S(2)}) collective-permute-start(bf16[64,256]{1,0:T(8,128)(2,1)S(1)} %get-tuple-element.15), channel_id=1, source_target_pairs={{4,0},{8,4},{12,8},{16,12},{20,16},{24,20},{28,24},{5,1},{9,5},{13... | collective-permute-start | bytes 98312 | tf_op jit(solution)/shard_map/ppermute | solution.py:268
  6.3 7.6 %collective-permute-start.3 = (bf16[64,256]{1,0:T(8,128)(2,1)S(1)}, bf16[64,256]{1,0:T(8,128)(2,1)S(1)}, u32[]{:S(2)}, u32[]{:S(2)}) collective-permute-start(bf16[64,256]{1,0:T(8,128)(2,1)S(1)} %get-tuple-element.16), channel_id=1, source_target_pairs={{0,4},{4,8},{8,12},{12,16},{16,20},{20,24},{24,28},{1,5},{5,9},{9,... | collective-permute-start | bytes 98312 | tf_op jit(solution)/shard_map/ppermute | solution.py:267
  9.3 26.0 %collective-permute-start.2 = (bf16[256,512]{1,0:T(8,128)(2,1)S(1)}, bf16[256,512]{1,0:T(8,128)(2,1)S(1)}, u32[]{:S(2)}, u32[]{:S(2)}) collective-permute-start(bf16[256,512]{1,0:T(8,128)(2,1)S(1)} %get-tuple-element.9.refs_0_), channel_id=1, source_target_pairs={{0,3},{1,2},{2,1},{3,0},{4,7},{5,6},{6,5},{7,4},{8,11},{9,10},{10,... | collective-permute-start | bytes 786440 | tf_op jit(solution)/shard_map/ppermute | solution.py:264
  13.3 22.0 %collective-permute-start.1 = (bf16[256,512]{1,0:T(8,128)(2,1)S(1)}, bf16[256,512]{1,0:T(8,128)(2,1)S(1)}, u32[]{:S(2)}, u32[]{:S(2)}) collective-permute-start(bf16[256,512]{1,0:T(8,128)(2,1)S(1)} %get-tuple-element.9.refs_0_), channel_id=1, source_target_pairs={{0,2},{1,3},{2,0},{3,1},{4,6},{5,7},{6,4},{7,5},{8,10},{9,11},{10,... | collective-permute-start | bytes 786440 | tf_op jit(solution)/shard_map/ppermute | solution.py:264
  13.8 21.5 %collective-permute-start = (bf16[256,512]{1,0:T(8,128)(2,1)S(1)}, bf16[256,512]{1,0:T(8,128)(2,1)S(1)}, u32[]{:S(2)}, u32[]{:S(2)}) collective-permute-start(bf16[256,512]{1,0:T(8,128)(2,1)S(1)} %get-tuple-element.9.refs_0_), channel_id=1, source_target_pairs={{0,1},{1,0},{2,3},{3,2},{4,5},{5,4},{6,7},{7,6},{8,9},{9,8},{10,11... | collective-permute-start | bytes 786440 | tf_op jit(solution)/shard_map/ppermute | solution.py:264
  14.1 12.2 %collective-permute-start.5 = (bf16[80,256]{1,0:T(8,128)(2,1)S(1)}, bf16[80,256]{1,0:T(8,128)(2,1)S(1)}, u32[]{:S(2)}, u32[]{:S(2)}) collective-permute-start(bf16[80,256]{1,0:T(8,128)(2,1)S(1)} %pad.7), channel_id=1, source_target_pairs={{0,1},{1,2},{2,3},{4,5},{5,6},{6,7},{8,9},{9,10},{10,11},{12,13},{... | collective-permute-start | bytes 122888 | tf_op jit(solution)/shard_map/ppermute | solution.py:276
  18.0 10.2 %collective-permute-start.6 = (bf16[80,256]{1,0:T(8,128)(2,1)S(1)}, bf16[80,256]{1,0:T(8,128)(2,1)S(1)}, u32[]{:S(2)}, u32[]{:S(2)}) collective-permute-start(bf16[80,256]{1,0:T(8,128)(2,1)S(1)} %pad.8), channel_id=1, source_target_pairs={{1,0},{2,1},{3,2},{5,4},{6,5},{7,6},{9,8},{10,9},{11,10},{13,12},{... | collective-permute-start | bytes 122888 | tf_op jit(solution)/shard_map/ppermute | solution.py:277
  33.3 1.0 %copy-start.8 = (f32[2,1024,128]{2,1,0:T(8,128)}, f32[2,1024,128]{2,1,0:T(8,128)S(1)}, u32[]{:S(2)}) copy-start(f32[2,1024,128]{2,1,0:T(8,128)S(1)} %get-tuple-element.11.refs_8_) | copy-start | bytes 3145732
  34.3 1.0 %copy-start.9 = (f32[2,1024,128]{2,1,0:T(8,128)}, f32[2,1024,128]{2,1,0:T(8,128)S(1)}, u32[]{:S(2)}) copy-start(f32[2,1024,128]{2,1,0:T(8,128)S(1)} %get-tuple-element.12.refs_9_) | copy-start | bytes 3145732
  35.3 0.7 %copy-start.13 = (bf16[256,512]{1,0:T(8,128)(2,1)}, bf16[256,512]{1,0:T(8,128)(2,1)S(1)}, u32[]{:S(2)}) copy-start(bf16[256,512]{1,0:T(8,128)(2,1)S(1)} %collective-permute-done.2.refs_3_) | copy-start | bytes 786436
  35.3 0.8 %copy-start.14 = (bf16[256,512]{1,0:T(8,128)(2,1)}, bf16[256,512]{1,0:T(8,128)(2,1)S(1)}, u32[]{:S(2)}) copy-start(bf16[256,512]{1,0:T(8,128)(2,1)S(1)} %collective-permute-done.1.refs_2_) | copy-start | bytes 786436
  35.3 0.9 %copy-start.15 = (bf16[256,512]{1,0:T(8,128)(2,1)}, bf16[256,512]{1,0:T(8,128)(2,1)S(1)}, u32[]{:S(2)}) copy-start(bf16[256,512]{1,0:T(8,128)(2,1)S(1)} %collective-permute-done.refs_1_) | copy-start | bytes 786436

commit v2 on v1

v2 whole, which is shorter than its diff:
```python
import functools

import jax
import jax.numpy as jnp
from jax import lax
from jax.experimental import pallas as pl
from jax.experimental.pallas import tpu as pltpu
from jax.sharding import PartitionSpec as P

F32 = jnp.float32
BF16 = jnp.bfloat16
MIB = 1 << 20


def vmem(count):
    return [pl.BlockSpec(memory_space=pltpu.VMEM)] * count


def hbm(array):
    return pltpu.with_memory_space_constraint(array, pltpu.HBM)


def params(mib):
    return pltpu.CompilerParams(vmem_limit_bytes=mib * MIB)


def cost(macs, moved):
    return pl.CostEstimate(flops=2 * macs, bytes_accessed=moved, transcendentals=0)


def mm(left, right):
    return jnp.dot(left, right, preferred_element_type=F32)


def count_rows(counts_ref, tile_x, tile_y, lanes):
    eye = lax.broadcasted_iota(jnp.int32, (tile_y, tile_y), 0) == lax.broadcasted_iota(
        jnp.int32, (tile_y, tile_y), 1
    )
    counts = counts_ref[...].astype(F32)
    diag = [
        jnp.where(eye, jnp.broadcast_to(counts[i : i + 1], (tile_y, tile_y)), 0.0) for i in range(tile_x)
    ]
    return mm(jnp.concatenate(diag, axis=0).astype(BF16), jnp.ones((tile_y, lanes), BF16))


def parents_kernel(
    tile_x, tile_y, cur_hbm, counts_hbm, agg_hbm, up_hbm, live_ref, coarse_ref,
    cur_ref, counts_ref, agg_ref, up_ref, wide, pats, rows4, sems,
):
    loads = [
        pltpu.make_async_copy(source, target, sems.at[k])
        for k, (source, target) in enumerate(
            [(counts_hbm, counts_ref), (cur_hbm, cur_ref), (agg_hbm, agg_ref), (up_hbm, up_ref)]
        )
    ]
    for load in loads:
        load.start()
    lanes = cur_ref.shape[1]
    boxes = tile_x * tile_y
    loads[0].wait()
    keep = lax.broadcasted_iota(jnp.int32, (boxes, lanes), 1).astype(F32) < count_rows(
        counts_ref, tile_x, tile_y, lanes
    )
    loads[1].wait()
    wide[...] = cur_ref[...].astype(F32)
    for part in range(2):
        live = jnp.where(keep, wide[pl.ds(part, boxes, stride=2), :], 0.0)
        live_ref[:, part * lanes : (part + 1) * lanes] = live.astype(BF16)
    loads[2].wait()
    pattern = mm(live_ref[...], agg_ref[...])
    pats[0] = pattern[:, :lanes]
    pats[1] = pattern[:, lanes:]
    children = []
    for side_x in range(2):
        for side_y in range(2):
            for part in range(2):
                rows = [
                    pats[part, pl.ds((2 * p + side_x) * tile_y + side_y, tile_y // 2, stride=2), :]
                    for p in range(tile_x // 2)
                ]
                children.append(jnp.concatenate(rows, axis=0).astype(BF16))
    loads[3].wait()
    coarse = mm(jnp.concatenate(children, axis=1), up_ref[...])
    for place, column in enumerate((0, 2, 1, 3)):
        rows4[pl.ds(place, coarse.shape[0], stride=4), :] = coarse[:, column * 128 : (column + 1) * 128]
    coarse_ref[...] = rows4[...].astype(BF16)


LEFT = 8
OFFSETS = [(dx, dy) for dx in range(-2, 3) for dy in range(-2, 3) if max(abs(dx), abs(dy)) == 2]
BLOCK = 8


def local_kernel(
    tile_x, tile_y, live_ref, top_ref, bottom_ref, agg_ref, near_ref, low_ref,
    lower_ref, field_ref, cells, packed, pats, shifted, tables,
):
    lanes = lower_ref.shape[2]
    width = tile_y + 2 * LEFT
    none = jnp.zeros((LEFT, lanes), F32)
    for part in range(2):
        cols = slice(part * lanes, (part + 1) * lanes)
        for i in range(tile_x + 4):
            if i < 2:
                row = top_ref[i * tile_y : (i + 1) * tile_y, cols]
            elif i < tile_x + 2:
                row = live_ref[(i - 2) * tile_y : (i - 1) * tile_y, cols]
            else:
                row = bottom_ref[(i - tile_x - 2) * tile_y : (i - tile_x - 1) * tile_y, cols]
            base = i * width
            cells[part, base : base + LEFT, :] = none
            cells[part, base + LEFT : base + LEFT + tile_y, :] = row.astype(F32)
            cells[part, base + LEFT + tile_y : base + width, :] = none
        packed[:, cols] = cells[part].astype(BF16)
        for i in range(tile_x + 2):
            for shift in range(-1, 2):
                base = (i + 1) * width + LEFT + shift
                place = (2 * (shift + 1) + part) * lanes
                shifted[i * tile_y : (i + 1) * tile_y, place : place + lanes] = cells[
                    part, base : base + tile_y, :
                ].astype(BF16)
    pattern = mm(packed[...], agg_ref[...]).astype(BF16).astype(F32)
    pats[0] = pattern[:, :lanes]
    pats[1] = pattern[:, lanes:]
    pats[2] = pattern[:, :lanes] + pattern[:, lanes:]
    for k in range(len(OFFSETS)):
        t_real, t_imag = low_ref[2 * k : 2 * k + 1, :], low_ref[2 * k + 1 : 2 * k + 2, :]
        tables[3 * k : 3 * k + 1, :] = t_real
        tables[3 * k + 1 : 3 * k + 2, :] = t_imag - t_real
        tables[3 * k + 2 : 3 * k + 3, :] = t_imag + t_real

    def rows_block(block, carry):
        total = None
        size = BLOCK * tile_y
        for shift in range(3):
            start = pl.multiple_of(block * size + shift * tile_y, tile_y)
            term = mm(shifted[pl.ds(start, size), :], near_ref[shift])
            total = term if total is None else total + term
        start = pl.multiple_of(block * size, size)
        field_ref[0, pl.ds(start, size), :] = total[:, :lanes]
        field_ref[1, pl.ds(start, size), :] = total[:, lanes:]
        origin = pl.multiple_of(block * (BLOCK * width), 8)
        for i in range(BLOCK):
            both = jnp.zeros((tile_y, lanes), F32)
            first = jnp.zeros((tile_y, lanes), F32)
            second = jnp.zeros((tile_y, lanes), F32)
            for k, (dx, dy) in enumerate(OFFSETS):
                rows = pl.ds(origin + ((i + 2 + dx) * width + LEFT + dy), tile_y)
                both = both + tables[3 * k : 3 * k + 1, :] * pats[2, rows, :]
                first = first + tables[3 * k + 1 : 3 * k + 2, :] * pats[0, rows, :]
                second = second + tables[3 * k + 2 : 3 * k + 3, :] * pats[1, rows, :]
            place = pl.ds(pl.multiple_of(start + i * tile_y, tile_y), tile_y)
            lower_ref[0, place, :] = both - second
            lower_ref[1, place, :] = both + first
        return carry

    lax.fori_loop(0, tile_x // BLOCK, rows_block, 0)


def columns_kernel(
    tile_x, tile_y, left_ref, right_ref, agg_ref, near_ref, low_ref, lower_in, field_in,
    lower_ref, field_ref, cells, pats,
):
    lanes = lower_ref.shape[2]
    lower_ref[...] = lower_in[...]
    field_ref[...] = field_in[...]
    for side, ref in enumerate((left_ref, right_ref)):
        pattern = mm(ref[...], agg_ref[...]).astype(BF16).astype(F32)
        for part in range(2):
            cols = slice(part * lanes, (part + 1) * lanes)
            cells[part] = ref[:, cols].astype(F32)
            pats[part] = pattern[:, cols]

        def column(store, part, place, dx):
            return store[part, pl.ds(2 * (2 + dx) + place, tile_x, stride=2), :]

        pairs = [(0, 0, -2), (0, 1, -1), (1, 1, -2)]
        if side:
            pairs = [(tile_y - 1, 1, 2), (tile_y - 1, 0, 1), (tile_y - 2, 0, 2)]
        sums = {}
        for box, place, dy in pairs:
            for dx in range(-2, 3):
                if (dx, dy) not in OFFSETS:
                    continue
                k = OFFSETS.index((dx, dy))
                t_real, t_imag = low_ref[2 * k : 2 * k + 1, :], low_ref[2 * k + 1 : 2 * k + 2, :]
                real, imag = column(pats, 0, place, dx), column(pats, 1, place, dx)
                first, second = sums.get(box, (0.0, 0.0))
                sums[box] = (
                    first + (t_real * real - t_imag * imag), second + (t_real * imag + t_imag * real)
                )
        for box, values in sums.items():
            for part in range(2):
                rows = pl.ds(box, tile_x, stride=tile_y)
                lower_ref[part, rows, :] = lower_ref[part, rows, :] + values[part]
        place, box = (0, tile_y - 1) if side else (1, 0)
        total = None
        for dx in range(-1, 2):
            source = jnp.concatenate([column(cells, part, place, dx) for part in range(2)], axis=1)
            start = 4 * lanes if side else 0
            term = mm(source.astype(BF16), near_ref[dx + 1, start : start + 2 * lanes, :])
            total = term if total is None else total + term
        for part in range(2):
            rows = pl.ds(box, tile_x, stride=tile_y)
            field_ref[part, rows, :] = field_ref[part, rows, :] + total[:, part * lanes : (part + 1) * lanes]


GROUP = 8


def lists_kernel(chunks, tile_x, tile_y, *refs):
    sources = refs[:chunks]
    (source_rows, table_rows, table_ref, counts_ref, lower_ref, near_ref, down_ref, recv_ref, out_ref,
     cells, table8, sums, kept) = refs[chunks:]
    parents_x, parents_y = tile_x // 2, tile_y // 2
    parents = parents_x * parents_y
    slots = source_rows.shape[0] // parents
    kinds = table_ref.shape[0] // 4
    lanes = lower_ref.shape[2]
    for place, row in enumerate((0, 0, 2, 2, 1, 1, 3, 3)):
        table8[pl.ds(place, kinds, stride=8), :] = table_ref[pl.ds(row, kinds, stride=4), :]
    table8[8 * kinds : 8 * kinds + 8, :] = jnp.zeros((8, lanes), F32)
    for c in range(chunks):
        rows = sources[c][...].astype(F32).reshape(parents // 2, 8, lanes)
        for half in range(2):
            own = rows[:, 4 * half : 4 * half + 4, :]
            cells[c * (parents // 2) : (c + 1) * (parents // 2), half] = jnp.concatenate([own, own], axis=1)

    def step(n, carry):
        for k in range(GROUP):
            first = n * (GROUP * slots) + k * slots
            total = [None, None]
            for s in range(slots):
                source = source_rows[first + s]
                kind = pl.multiple_of(table_rows[first + s], 8)
                term = cells_flat[pl.ds(pl.multiple_of(source, 8), 8), :] * table8[pl.ds(kind, 8), :]
                total[s % 2] = term if total[s % 2] is None else total[s % 2] + term
            sums[pl.ds(pl.multiple_of((n * GROUP + k) * 8, 8), 8), :] = total[0] + total[1]
        return carry

    cells_flat = cells.reshape(chunks * parents * 8, lanes)
    lax.fori_loop(0, parents // GROUP, step, 0)

    def row(place):
        return sums[pl.ds(place, parents, stride=8), :]

    incoming = jnp.concatenate(
        [row(0) - row(5), row(2) - row(7), row(1) + row(4), row(3) + row(6)], axis=1
    ).astype(BF16)
    limits = count_rows(counts_ref, tile_x, tile_y, lanes)
    kept[...] = jnp.where(
        lax.broadcasted_iota(jnp.int32, limits.shape, 1).astype(F32) < limits, 1.0, 0.0
    )
    for side_x in range(2):
        for side_y in range(2):
            down = mm(incoming, down_ref[2 * side_x + side_y])
            starts = [(2 * p + side_x) * tile_y + side_y for p in range(parents_x)]

            def rows_of(ref, part):
                return jnp.concatenate(
                    [ref[part, pl.ds(start, parents_y, stride=2), :] for start in starts], axis=0
                )

            total = jnp.concatenate(
                [down[:, part * lanes : (part + 1) * lanes] + rows_of(lower_ref, part) for part in range(2)],
                axis=1,
            )
            field = mm(total.astype(BF16), recv_ref[...])
            mask = jnp.concatenate(
                [kept[pl.ds(start, parents_y, stride=2), :] for start in starts], axis=0
            )
            for part in range(2):
                value = (field[:, part * lanes : (part + 1) * lanes] + rows_of(near_ref, part)) * mask
                for p, start in enumerate(starts):
                    out_ref[pl.ds(2 * start + part, parents_y, stride=4), :] = value[
                        p * parents_y : (p + 1) * parents_y
                    ]


def swap(first, last, axis):
    count = lax.axis_size(axis)
    odd = lax.axis_index(axis) % 2 == 1
    low = [(i, i ^ 1) for i in range(count)]
    high = [(i, (i ^ 1) if i in (0, count - 1) else ((i + 1) ^ 1) - 1) for i in range(count)]
    high = [(i, j) for i, j in high if i not in (0, count - 1)]
    inner = lax.ppermute(jnp.where(odd, first, last), axis, low)
    outer = lax.ppermute(jnp.where(odd, last, first), axis, high)
    return jnp.where(odd, inner, outer), jnp.where(odd, outer, inner)


def body(
    currents, box_count, aggregate, near_blocks, low_translator, child_to_parent, coarse_list,
    coarse_kind, coarse_count, up_translator, parent_to_child, receive_map,
):
    tile_x, tile_y = box_count.shape
    boxes = tile_x * tile_y
    lanes = currents.shape[-1]
    parents_x, parents_y, slots = coarse_list.shape
    parents = parents_x * parents_y
    kinds, _, half = up_translator.shape
    wide = 2 * half
    chunks = lax.axis_size("gy")

    live, coarse = pl.pallas_call(
        functools.partial(parents_kernel, tile_x, tile_y),
        name="parents",
        out_shape=[
            jax.ShapeDtypeStruct((boxes, 2 * lanes), BF16),
            jax.ShapeDtypeStruct((4 * parents, wide // 4), BF16),
        ],
        in_specs=[pl.BlockSpec(memory_space=pltpu.HBM)] * 4,
        out_specs=vmem(2),
        scratch_shapes=[
            pltpu.VMEM((2 * boxes, lanes), BF16),
            pltpu.VMEM((tile_x, tile_y), jnp.int32),
            pltpu.VMEM((2 * lanes, 2 * lanes), BF16),
            pltpu.VMEM((8 * lanes, wide), BF16),
            pltpu.VMEM((2 * boxes, lanes), F32),
            pltpu.VMEM((2, boxes, lanes), F32),
            pltpu.VMEM((4 * parents, wide // 4), F32),
            pltpu.SemaphoreType.DMA((4,)),
        ],
        compiler_params=params(24),
        cost_estimate=cost(200 * MIB, 3 * MIB),
    )(
        hbm(currents.reshape(2 * boxes, lanes)),
        hbm(box_count),
        hbm(aggregate),
        hbm(child_to_parent.reshape(8 * lanes, wide)),
    )

    sources = [coarse] + [
        lax.ppermute(coarse, "gy", [(i, i ^ d) for i in range(chunks)]) for d in range(1, chunks)
    ]
    top, bottom = swap(live[: 2 * tile_y], live[boxes - 2 * tile_y :], "gx")
    tall = jnp.concatenate([top, live, bottom], axis=0).reshape(tile_x + 4, tile_y, 2 * lanes)

    def edge(cells):
        cells = cells.reshape(2 * (tile_x + 4), 2 * lanes)
        return jnp.pad(cells, ((0, -cells.shape[0] % 16), (0, 0)))

    left, right = swap(edge(tall[:, :2]), edge(tall[:, tile_y - 2 :]), "gy")

    near_rows = near_blocks.reshape(3, 6 * lanes, 2 * lanes)
    low_rows = low_translator.reshape(-1, lanes)
    padded = (tile_x + 4) * (tile_y + 2 * LEFT)
    pair = [jax.ShapeDtypeStruct((2, boxes, lanes), F32)] * 2
    lower, near = pl.pallas_call(
        functools.partial(local_kernel, tile_x, tile_y),
        name="local",
        out_shape=pair,
        in_specs=vmem(6),
        out_specs=vmem(2),
        scratch_shapes=[
            pltpu.VMEM((2, padded, lanes), F32),
            pltpu.VMEM((padded, 2 * lanes), BF16),
            pltpu.VMEM((3, padded, lanes), F32),
            pltpu.VMEM(((tile_x + 2) * tile_y, 6 * lanes), BF16),
            pltpu.VMEM((3 * len(OFFSETS), lanes), F32),
        ],
        compiler_params=params(24),
        cost_estimate=cost(2000 * MIB, 5 * MIB),
    )(live, top, bottom, aggregate, near_rows, low_rows)

    lower, near = pl.pallas_call(
        functools.partial(columns_kernel, tile_x, tile_y),
        name="columns",
        out_shape=pair,
        in_specs=vmem(7),
        out_specs=vmem(2),
        scratch_shapes=[pltpu.VMEM((2, left.shape[0], lanes), F32)] * 2,
        compiler_params=params(16),
        cost_estimate=cost(100 * MIB, 5 * MIB),
    )(left, right, aggregate, near_rows, low_rows, lower, near)

    me = lax.axis_index("gy")
    across = parents_y * chunks
    row, column = coarse_list // across, coarse_list % across
    place = (column // parents_y) ^ me
    source_rows = 8 * (place * parents + row * parents_y + column % parents_y)
    used = lax.broadcasted_iota(jnp.int32, coarse_list.shape, 2) < coarse_count[:, :, None]
    table_rows = 8 * jnp.where(used, coarse_kind, kinds)
    table = up_translator.reshape(kinds, 2, 2, half // 2).transpose(0, 2, 1, 3).reshape(4 * kinds, half // 2)

    out = pl.pallas_call(
        functools.partial(lists_kernel, chunks, tile_x, tile_y),
        name="lists",
        out_shape=jax.ShapeDtypeStruct((2 * boxes, lanes), F32),
        in_specs=vmem(chunks) + [pl.BlockSpec(memory_space=pltpu.SMEM)] * 2 + vmem(6),
        out_specs=pl.BlockSpec(memory_space=pltpu.VMEM),
        scratch_shapes=[
            pltpu.VMEM((chunks * parents // 2, 2, 8, lanes), F32),
            pltpu.VMEM((8 * kinds + 8, lanes), F32),
            pltpu.VMEM((8 * parents, lanes), F32),
            pltpu.VMEM((boxes, lanes), F32),
        ],
        compiler_params=params(24 if chunks <= 4 else 48),
        cost_estimate=cost(3000 * MIB, 8 * MIB),
    )(
        *sources, source_rows.reshape(-1), table_rows.reshape(-1), table,
        box_count, lower, near, parent_to_child, receive_map,
    )
    return out.reshape(tile_x, tile_y, 2, lanes)


def solution(mesh):
    tiles = P("gx", "gy")
    in_specs = (tiles, tiles, P(), P(), P(), P(), tiles, tiles, tiles, P(), P(), P())
    return jax.shard_map(body, mesh=mesh, in_specs=in_specs, out_specs=tiles, check_vma=False)
```

time: 49.4 us -> 31.6 us (0.64)
  the two profiles are of different devices: /device:TPU:0 before, /device:TPU:19 now
where the time goes in v2:
time: 31.6 us; the launch traced here: 31.4 us
  Pallas kernels  16.2 us (51%)
  starting transfers between devices  12.1 us (38%)
  waiting for transfers between devices  1.48 us (5%)
  local copies, waits for them, and re-layouts  0.87 us (3%)
  other arithmetic  0.45 us (1%)
    pallas_call x1, Pallas kernels, body(): pl.pallas_call(functools.partial(lists_kernel, chunks, tile_x, tile_y), n...  9.15 us
    ppermute x2, starting transfers between devices, swap(): outer = lax.ppermute(jnp.where(odd, last, first), axis, high)  7.17 us
    pallas_call x1, Pallas kernels, body(): pl.pallas_call(functools.partial(local_kernel, tile_x, tile_y), name='loc...  4.15 us
    ppermute x3, starting transfers between devices, body(): lax.ppermute(coarse, 'gy', [(i, i ^ d) for i in range(chunks)])  2.71 us
    pallas_call x1, Pallas kernels, body(): pl.pallas_call(functools.partial(parents_kernel, tile_x, tile_y), name='p...  2.28 us
    ppermute x2, starting transfers between devices, swap(): inner = lax.ppermute(jnp.where(odd, first, last), axis, low)  2.18 us
    ppermute x2, waiting for transfers between devices, swap(): outer = lax.ppermute(jnp.where(odd, last, first), axis, high)  1.46 us
    pallas_call x1, Pallas kernels, body(): pl.pallas_call(functools.partial(columns_kernel, tile_x, tile_y), name='c...  0.65 us
  transfers between devices with their start and end apart: 7, of which 1 were waited for; matrix products, arithmetic and copies ran while one was open for 2% of the time, Pallas kernels for 15%

profile of v2, /device:TPU:19, one launch (start us, length us, event | category | flops | bytes accessed | tf_op | source)
XLA Modules:
  0.0 31.4 jit_solution(5128345751445188090)
XLA Ops:
  0.0 0.0 copy-start.7
  0.0 0.0 copy-start.9
  0.0 0.0 copy-start.8
  0.0 2.3 %parents.1 = (bf16[1024,256]{1,0:T(8,128)(2,1)S(1)}, bf16[1024,128]{1,0:T(8,128)(2,1)S(1)}) custom-call(bf16[2048,128]{1,0:T(8,128)(2,1)} %bitcast.18, s32[32,32]{1,0:T(8,128)} %refs_7_.1, bf16[256,256]{1,0:T(8,128)(2,1)} %agg_ref.3, bf16[1024,512]{1,0:T(8,128)(2,1)} %bitcast.16), custom_call_target="tpu_custom_call" | custom-call | flops 419430400 | bytes 3145728 | tf_op jit(solution)/shard_map/parents/pallas_call | solution.py:304
  2.3 0.3 %collective-permute-start = (bf16[1024,128]{1,0:T(8,128)(2,1)S(1)}, bf16[1024,128]{1,0:T(8,128)(2,1)S(1)}, u32[]{:S(2)}, u32[]{:S(2)}) collective-permute-start(bf16[1024,128]{1,0:T(8,128)(2,1)S(1)} %get-tuple-element.11.refs_0_), channel_id=1, source_target_pairs={{0,1},{1,0},{2,3},{3,2},{4,5},{5,4},{6,7},{7,6},{8,9},{9,8},{10,11... | collective-permute-start | bytes 786440 | tf_op jit(solution)/shard_map/ppermute | solution.py:333
  2.6 1.2 %collective-permute-start.1 = (bf16[1024,128]{1,0:T(8,128)(2,1)S(1)}, bf16[1024,128]{1,0:T(8,128)(2,1)S(1)}, u32[]{:S(2)}, u32[]{:S(2)}) collective-permute-start(bf16[1024,128]{1,0:T(8,128)(2,1)S(1)} %get-tuple-element.11.refs_0_), channel_id=1, source_target_pairs={{0,2},{1,3},{2,0},{3,1},{4,6},{5,7},{6,4},{7,5},{8,10},{9,11},{10,... | collective-permute-start | bytes 786440 | tf_op jit(solution)/shard_map/ppermute | solution.py:333
  3.9 1.2 %collective-permute-start.2 = (bf16[1024,128]{1,0:T(8,128)(2,1)S(1)}, bf16[1024,128]{1,0:T(8,128)(2,1)S(1)}, u32[]{:S(2)}, u32[]{:S(2)}) collective-permute-start(bf16[1024,128]{1,0:T(8,128)(2,1)S(1)} %get-tuple-element.11.refs_0_), channel_id=1, source_target_pairs={{0,3},{1,2},{2,1},{3,0},{4,7},{5,6},{6,5},{7,4},{8,11},{9,10},{10,... | collective-permute-start | bytes 786440 | tf_op jit(solution)/shard_map/ppermute | solution.py:333
  5.0 1.6 %collective-permute-start.3 = (bf16[64,256]{1,0:T(8,128)(2,1)S(1)}, bf16[64,256]{1,0:T(8,128)(2,1)S(1)}, u32[]{:S(2)}, u32[]{:S(2)}) collective-permute-start(bf16[64,256]{1,0:T(8,128)(2,1)S(1)} %get-tuple-element.19), channel_id=1, source_target_pairs={{0,4},{4,0},{8,12},{12,8},{16,20},{20,16},{24,28},{28,24},{1,5},{5... | collective-permute-start | bytes 98312 | tf_op jit(solution)/shard_map/ppermute | solution.py:286
  6.6 3.1 %collective-permute-start.4 = (bf16[64,256]{1,0:T(8,128)(2,1)S(1)}, bf16[64,256]{1,0:T(8,128)(2,1)S(1)}, u32[]{:S(2)}, u32[]{:S(2)}) collective-permute-start(bf16[64,256]{1,0:T(8,128)(2,1)S(1)} %get-tuple-element.20), channel_id=1, source_target_pairs={{4,8},{8,4},{12,16},{16,12},{20,24},{24,20},{5,9},{9,5},{13,17},{1... | collective-permute-start | bytes 98312 | tf_op jit(solution)/shard_map/ppermute | solution.py:287
  9.7 0.0 copy-done.7
  9.7 0.0 copy-done.9
  9.7 0.1 select_multiply_fusion
  9.8 0.0 copy-done.8
  9.9 0.0 copy-start
  9.9 0.0 copy-start.1
  9.9 0.0 copy-start.2
  9.9 0.3 fusion.4
  10.2 0.1 reshape.39.refs_4_
  10.3 0.1 reshape.40.refs_5_
  10.4 0.0 collective-permute-done.3
  10.4 1.5 %collective-permute-done.4 = bf16[64,256]{1,0:T(8,128)(2,1)S(1)} collective-permute-done((bf16[64,256]{1,0:T(8,128)(2,1)S(1)}, bf16[64,256]{1,0:T(8,128)(2,1)S(1)}, u32[]{:S(2)}, u32[]{:S(2)}) %collective-permute-start.4) | collective-permute-done | bytes 32800 | tf_op jit(solution)/shard_map/ppermute | solution.py:287
  11.9 0.1 fusion.12
  12.1 0.6 %collective-permute-start.5 = (bf16[80,256]{1,0:T(8,128)(2,1)S(1)}, bf16[80,256]{1,0:T(8,128)(2,1)S(1)}, u32[]{:S(2)}, u32[]{:S(2)}) collective-permute-start(bf16[80,256]{1,0:T(8,128)(2,1)S(1)} %get-tuple-element.24), channel_id=1, source_target_pairs={{0,1},{1,0},{2,3},{3,2},{4,5},{5,4},{6,7},{7,6},{8,9},{9,8},{10,11... | collective-permute-start | bytes 122888 | tf_op jit(solution)/shard_map/ppermute | solution.py:286
  12.6 4.1 %collective-permute-start.6 = (bf16[80,256]{1,0:T(8,128)(2,1)S(1)}, bf16[80,256]{1,0:T(8,128)(2,1)S(1)}, u32[]{:S(2)}, u32[]{:S(2)}) collective-permute-start(bf16[80,256]{1,0:T(8,128)(2,1)S(1)} %get-tuple-element.23), channel_id=1, source_target_pairs={{1,2},{2,1},{5,6},{6,5},{9,10},{10,9},{13,14},{14,13},{17,18},{18,... | collective-permute-start | bytes 122888 | tf_op jit(solution)/shard_map/ppermute | solution.py:287
  16.7 0.0 copy-done
  16.7 0.0 copy-done.1
  16.7 0.0 copy-done.2
  16.8 4.2 %local.1 = (f32[2,1024,128]{2,1,0:T(8,128)S(1)}, f32[2,1024,128]{2,1,0:T(8,128)S(1)}) custom-call(bf16[1024,256]{1,0:T(8,128)(2,1)S(1)} %get-tuple-element.12.live_ref, bf16[64,256]{1,0:T(8,128)(2,1)S(1)} %get-tuple-element.25.top_ref, bf16[64,256]{1,0:T(8,128)(2,1)S(1)} %get-tuple-element.26.bottom_ref, bf16[256,256]{1,0:T(8,128)(2,1)S(1)} %copy-done.1, ...), custom_call_target="tpu_custom_call" | custom-call | flops 4194304000 | bytes 5242880 | tf_op jit(solution)/shard_map/local/pallas_call | solution.py:348
  20.9 0.0 collective-permute-done.5
  20.9 0.0 collective-permute-done.6
  21.0 0.0 copy-start.3
  21.0 0.0 copy-start.4
  21.0 0.0 copy-start.5
  21.0 0.0 copy-start.6
  21.0 0.6 %columns.1 = (f32[2,1024,128]{2,1,0:T(8,128)S(1)}, f32[2,1024,128]{2,1,0:T(8,128)S(1)}) custom-call(bf16[80,256]{1,0:T(8,128)(2,1)S(1)} %get-tuple-element.22.left_ref, bf16[80,256]{1,0:T(8,128)(2,1)S(1)} %get-tuple-element.21.right_ref, bf16[256,256]{1,0:T(8,128)(2,1)S(1)} %copy-done.1, bf16[3,768,256]{2,1,0:T(8,128)(2,1)S(1)} %bitcast.12, ...), custom_call_target="tpu_custom_call" | custom-call | flops 209715200 | bytes 5242880 | tf_op jit(solution)/shard_map/columns/pallas_call | solution.py:365
  21.7 0.0 collective-permute-done.refs_1_
  21.7 0.0 collective-permute-done.1.refs_2_
  21.7 0.0 collective-permute-done.2.refs_3_
  21.7 0.0 copy-done.3
  21.7 0.5 %copy-done.4 = bf16[4,512,256]{2,1,0:T(8,128)(2,1)S(1)} copy-done((bf16[4,512,256]{2,1,0:T(8,128)(2,1)S(1)}, bf16[4,512,256]{2,1,0:T(8,128)(2,1)}, u32[]{:S(2)}) %copy-start.4) | copy-done | bytes 1048600
  22.2 0.0 copy-done.5
  22.2 0.0 copy-done.6
  22.2 9.2 %lists.1 = f32[2048,128]{1,0:T(8,128)} custom-call(bf16[1024,128]{1,0:T(8,128)(2,1)S(1)} %get-tuple-element.11.refs_0_, bf16[1024,128]{1,0:T(8,128)(2,1)S(1)} %collective-permute-done.refs_1_, bf16[1024,128]{1,0:T(8,128)(2,1)S(1)} %collective-permute-done.1.refs_2_, bf16[1024,128]{1,0:T(8,128)(2,1)S(1)} %collective-permute-done.2.refs_3_, ...), custom_call_target="tpu_custom_call" | custom-call | flops 6291456000 | bytes 8388608 | tf_op jit(solution)/shard_map/lists/pallas_call | solution.py:385
  (7 shorter events, 0.1 us)
Async XLA Ops:
  0.0 9.7 %copy-start.7 = (s32[16,16,16]{2,1,0:T(8,128)S(1)}, s32[16,16,16]{2,1,0:T(8,128)}, u32[]{:S(2)}) copy-start(s32[16,16,16]{2,1,0:T(8,128)} %param.19) | copy-start | bytes 49156
  0.0 9.7 %copy-start.9 = (s32[16,16]{1,0:T(8,128)S(1)}, s32[16,16]{1,0:T(8,128)}, u32[]{:S(2)}) copy-start(s32[16,16]{1,0:T(8,128)} %param.20) | copy-start | bytes 3076
  0.0 9.8 %copy-start.8 = (s32[16,16,16]{2,1,0:T(8,128)S(1)}, s32[16,16,16]{2,1,0:T(8,128)}, u32[]{:S(2)}) copy-start(s32[16,16,16]{2,1,0:T(8,128)} %param.18) | copy-start | bytes 49156
  2.3 19.4 %collective-permute-start = (bf16[1024,128]{1,0:T(8,128)(2,1)S(1)}, bf16[1024,128]{1,0:T(8,128)(2,1)S(1)}, u32[]{:S(2)}, u32[]{:S(2)}) collective-permute-start(bf16[1024,128]{1,0:T(8,128)(2,1)S(1)} %get-tuple-element.11.refs_0_), channel_id=1, source_target_pairs={{0,1},{1,0},{2,3},{3,2},{4,5},{5,4},{6,7},{7,6},{8,9},{9,8},{10,11... | collective-permute-start | bytes 786440 | tf_op jit(solution)/shard_map/ppermute | solution.py:333
  2.6 19.1 %collective-permute-start.1 = (bf16[1024,128]{1,0:T(8,128)(2,1)S(1)}, bf16[1024,128]{1,0:T(8,128)(2,1)S(1)}, u32[]{:S(2)}, u32[]{:S(2)}) collective-permute-start(bf16[1024,128]{1,0:T(8,128)(2,1)S(1)} %get-tuple-element.11.refs_0_), channel_id=1, source_target_pairs={{0,2},{1,3},{2,0},{3,1},{4,6},{5,7},{6,4},{7,5},{8,10},{9,11},{10,... | collective-permute-start | bytes 786440 | tf_op jit(solution)/shard_map/ppermute | solution.py:333
  3.9 17.8 %collective-permute-start.2 = (bf16[1024,128]{1,0:T(8,128)(2,1)S(1)}, bf16[1024,128]{1,0:T(8,128)(2,1)S(1)}, u32[]{:S(2)}, u32[]{:S(2)}) collective-permute-start(bf16[1024,128]{1,0:T(8,128)(2,1)S(1)} %get-tuple-element.11.refs_0_), channel_id=1, source_target_pairs={{0,3},{1,2},{2,1},{3,0},{4,7},{5,6},{6,5},{7,4},{8,11},{9,10},{10,... | collective-permute-start | bytes 786440 | tf_op jit(solution)/shard_map/ppermute | solution.py:333
  5.0 5.4 %collective-permute-start.3 = (bf16[64,256]{1,0:T(8,128)(2,1)S(1)}, bf16[64,256]{1,0:T(8,128)(2,1)S(1)}, u32[]{:S(2)}, u32[]{:S(2)}) collective-permute-start(bf16[64,256]{1,0:T(8,128)(2,1)S(1)} %get-tuple-element.19), channel_id=1, source_target_pairs={{0,4},{4,0},{8,12},{12,8},{16,20},{20,16},{24,28},{28,24},{1,5},{5... | collective-permute-start | bytes 98312 | tf_op jit(solution)/shard_map/ppermute | solution.py:286
  6.6 5.2 %collective-permute-start.4 = (bf16[64,256]{1,0:T(8,128)(2,1)S(1)}, bf16[64,256]{1,0:T(8,128)(2,1)S(1)}, u32[]{:S(2)}, u32[]{:S(2)}) collective-permute-start(bf16[64,256]{1,0:T(8,128)(2,1)S(1)} %get-tuple-element.20), channel_id=1, source_target_pairs={{4,8},{8,4},{12,16},{16,12},{20,24},{24,20},{5,9},{9,5},{13,17},{1... | collective-permute-start | bytes 98312 | tf_op jit(solution)/shard_map/ppermute | solution.py:287
  9.9 6.9 %copy-start = (bf16[9,256,256]{2,1,0:T(8,128)(2,1)S(1)}, bf16[9,256,256]{2,1,0:T(8,128)(2,1)}, u32[]{:S(2)}) copy-start(bf16[9,256,256]{2,1,0:T(8,128)(2,1)} %param.15) | copy-start | bytes 3538948
  9.9 6.9 %copy-start.1 = (bf16[256,256]{1,0:T(8,128)(2,1)S(1)}, bf16[256,256]{1,0:T(8,128)(2,1)}, u32[]{:S(2)}) copy-start(bf16[256,256]{1,0:T(8,128)(2,1)} %agg_ref.3) | copy-start | bytes 393220
  9.9 6.9 %copy-start.2 = (f32[16,2,128]{2,1,0:T(2,128)S(1)}, f32[16,2,128]{2,1,0:T(2,128)}, u32[]{:S(2)}) copy-start(f32[16,2,128]{2,1,0:T(2,128)} %param.16) | copy-start | bytes 49156
  12.1 8.9 %collective-permute-start.5 = (bf16[80,256]{1,0:T(8,128)(2,1)S(1)}, bf16[80,256]{1,0:T(8,128)(2,1)S(1)}, u32[]{:S(2)}, u32[]{:S(2)}) collective-permute-start(bf16[80,256]{1,0:T(8,128)(2,1)S(1)} %get-tuple-element.24), channel_id=1, source_target_pairs={{0,1},{1,0},{2,3},{3,2},{4,5},{5,4},{6,7},{7,6},{8,9},{9,8},{10,11... | collective-permute-start | bytes 122888 | tf_op jit(solution)/shard_map/ppermute | solution.py:286
  12.6 8.3 %collective-permute-start.6 = (bf16[80,256]{1,0:T(8,128)(2,1)S(1)}, bf16[80,256]{1,0:T(8,128)(2,1)S(1)}, u32[]{:S(2)}, u32[]{:S(2)}) collective-permute-start(bf16[80,256]{1,0:T(8,128)(2,1)S(1)} %get-tuple-element.23), channel_id=1, source_target_pairs={{1,2},{2,1},{5,6},{6,5},{9,10},{10,9},{13,14},{14,13},{17,18},{18,... | collective-permute-start | bytes 122888 | tf_op jit(solution)/shard_map/ppermute | solution.py:287
  21.0 0.7 %copy-start.3 = (s32[32,32]{1,0:T(8,128)S(1)}, s32[32,32]{1,0:T(8,128)}, u32[]{:S(2)}) copy-start(s32[32,32]{1,0:T(8,128)} %refs_7_.1) | copy-start | bytes 12292
  21.0 1.2 %copy-start.4 = (bf16[4,512,256]{2,1,0:T(8,128)(2,1)S(1)}, bf16[4,512,256]{2,1,0:T(8,128)(2,1)}, u32[]{:S(2)}) copy-start(bf16[4,512,256]{2,1,0:T(8,128)(2,1)} %refs_10_.1) | copy-start | bytes 3145732
  21.0 1.2 %copy-start.5 = (f32[64,2,256]{2,1,0:T(2,128)S(1)}, f32[64,2,256]{2,1,0:T(2,128)}, u32[]{:S(2)}) copy-start(f32[64,2,256]{2,1,0:T(2,128)} %param.21) | copy-start | bytes 393220
  21.0 1.2 %copy-start.6 = (bf16[256,256]{1,0:T(8,128)(2,1)S(1)}, bf16[256,256]{1,0:T(8,128)(2,1)}, u32[]{:S(2)}) copy-start(bf16[256,256]{1,0:T(8,128)(2,1)} %refs_11_.1) | copy-start | bytes 393220

commit v3 on v2

v3 whole, which is shorter than its diff:
```python
import functools

import jax
import jax.numpy as jnp
from jax import lax
from jax.experimental import pallas as pl
from jax.experimental.pallas import tpu as pltpu
from jax.sharding import PartitionSpec as P

F32 = jnp.float32
BF16 = jnp.bfloat16
MIB = 1 << 20


def vmem(count):
    return [pl.BlockSpec(memory_space=pltpu.VMEM)] * count


def hbm(array):
    return pltpu.with_memory_space_constraint(array, pltpu.HBM)


def params(mib):
    return pltpu.CompilerParams(vmem_limit_bytes=mib * MIB)


def cost(macs, moved):
    return pl.CostEstimate(flops=2 * macs, bytes_accessed=moved, transcendentals=0)


def mm(left, right):
    return jnp.dot(left, right, preferred_element_type=F32)


def count_rows(counts_ref, tile_x, tile_y, lanes):
    eye = lax.broadcasted_iota(jnp.int32, (tile_y, tile_y), 0) == lax.broadcasted_iota(
        jnp.int32, (tile_y, tile_y), 1
    )
    counts = counts_ref[...].astype(F32)
    diag = [
        jnp.where(eye, jnp.broadcast_to(counts[i : i + 1], (tile_y, tile_y)), 0.0) for i in range(tile_x)
    ]
    return mm(jnp.concatenate(diag, axis=0).astype(BF16), jnp.ones((tile_y, lanes), BF16))


def live_kernel(tile_x, tile_y, cur_hbm, counts_hbm, live_ref, kept_ref, low_ref, high_ref, cur_ref, counts_ref,
                wide, sems):
    loads = [
        pltpu.make_async_copy(counts_hbm, counts_ref, sems.at[0]),
        pltpu.make_async_copy(cur_hbm, cur_ref, sems.at[1]),
    ]
    for load in loads:
        load.start()
    lanes = cur_ref.shape[1]
    boxes = tile_x * tile_y
    loads[0].wait()
    limits = count_rows(counts_ref, tile_x, tile_y, lanes)
    keep = lax.broadcasted_iota(jnp.int32, (boxes, lanes), 1).astype(F32) < limits
    kept_ref[...] = jnp.where(keep, 1.0, 0.0)
    odd = lax.axis_index("gy") % 2 == 1
    loads[1].wait()
    wide[...] = cur_ref[...].astype(F32)
    for part in range(2):
        cols = slice(part * lanes, (part + 1) * lanes)
        live_ref[:, cols] = jnp.where(keep, wide[pl.ds(part, boxes, stride=2), :], 0.0).astype(BF16)

        def edge(column):
            rows = wide[pl.ds(2 * column + part, tile_x, stride=2 * tile_y), :]
            return rows * kept_ref[pl.ds(column, tile_x, stride=tile_y), :]

        first = jnp.concatenate([edge(0), edge(1)], axis=0).astype(BF16)
        last = jnp.concatenate([edge(tile_y - 2), edge(tile_y - 1)], axis=0).astype(BF16)
        low_ref[:, cols] = jnp.where(odd, first, last)
        high_ref[:, cols] = jnp.where(odd, last, first)


def parents_kernel(tile_x, tile_y, live_ref, agg_ref, up_ref, coarse_ref, pats, rows4):
    lanes = pats.shape[2]
    pattern = mm(live_ref[...], agg_ref[...])
    pats[0] = pattern[:, :lanes]
    pats[1] = pattern[:, lanes:]
    children = []
    for side_x in range(2):
        for side_y in range(2):
            for part in range(2):
                rows = [
                    pats[part, pl.ds((2 * p + side_x) * tile_y + side_y, tile_y // 2, stride=2), :]
                    for p in range(tile_x // 2)
                ]
                children.append(jnp.concatenate(rows, axis=0).astype(BF16))
    coarse = mm(jnp.concatenate(children, axis=1), up_ref[...])
    for place, column in enumerate((0, 2, 1, 3)):
        rows4[pl.ds(place, coarse.shape[0], stride=4), :] = coarse[:, column * 128 : (column + 1) * 128]
    coarse_ref[...] = rows4[...].astype(BF16)


def rims_kernel(tile_x, tile_y, live_ref, inner_ref, outer_ref, low_ref, high_ref, first, last):
    odd_y = lax.axis_index("gy") % 2 == 1
    odd_x = lax.axis_index("gx") % 2 == 1
    inner, outer = inner_ref[...].astype(F32), outer_ref[...].astype(F32)
    boxes = tile_x * tile_y
    sides = (jnp.where(odd_y, inner, outer), jnp.where(odd_y, outer, inner))
    for rim, start in ((first, 0), (last, tile_x - 2)):
        rim[0 : 2 * tile_y, :] = live_ref[start * tile_y : (start + 2) * tile_y, :].astype(F32)
        place = 2 * tile_y
        for side in sides:
            for column in range(2):
                at = column * tile_x + start
                rim[place : place + 2, :] = side[at : at + 2]
                place += 2
        rim[place:, :] = jnp.zeros((rim.shape[0] - place, rim.shape[1]), F32)
    low_ref[...] = jnp.where(odd_x, first[...], last[...]).astype(BF16)
    high_ref[...] = jnp.where(odd_x, last[...], first[...]).astype(BF16)


LEFT = 8
OFFSETS = [(dx, dy) for dx in range(-2, 3) for dy in range(-2, 3) if max(abs(dx), abs(dy)) == 2]


def local_kernel(
    tile_x, tile_y, live_ref, agg_ref, near_ref, low_ref, lower_ref, field_ref, cells, pats, shifted, tables, sums,
):
    lanes = lower_ref.shape[2]
    width = tile_y + 2 * LEFT
    none = jnp.zeros((LEFT, lanes), F32)
    pattern = mm(live_ref[...], agg_ref[...]).astype(BF16).astype(F32)
    values = [pattern[:, :lanes], pattern[:, lanes:], pattern[:, :lanes] + pattern[:, lanes:]]
    for i in range(tile_x):
        base = i * width
        rows = slice(i * tile_y, (i + 1) * tile_y)
        for k in range(3):
            pats[k, base : base + LEFT, :] = none
            pats[k, base + LEFT : base + LEFT + tile_y, :] = values[k][rows]
            pats[k, base + LEFT + tile_y : base + width, :] = none
    ends = jnp.zeros((tile_y, 6 * lanes), BF16)
    shifted[0:tile_y, :] = ends
    shifted[(tile_x + 1) * tile_y : (tile_x + 2) * tile_y, :] = ends
    shifted[tile_y : (tile_x + 1) * tile_y, 2 * lanes : 4 * lanes] = live_ref[...]
    for part in range(2):
        cols = slice(part * lanes, (part + 1) * lanes)
        for i in range(tile_x):
            base = i * width
            cells[part, base : base + LEFT, :] = none
            cells[part, base + LEFT : base + LEFT + tile_y, :] = live_ref[
                i * tile_y : (i + 1) * tile_y, cols
            ].astype(F32)
            cells[part, base + LEFT + tile_y : base + width, :] = none
            for shift in (-1, 1):
                place = (2 * (shift + 1) + part) * lanes
                shifted[(i + 1) * tile_y : (i + 2) * tile_y, place : place + lanes] = cells[
                    part, base + LEFT + shift : base + LEFT + shift + tile_y, :
                ].astype(BF16)
    for k in range(len(OFFSETS)):
        t_real, t_imag = low_ref[2 * k : 2 * k + 1, :], low_ref[2 * k + 1 : 2 * k + 2, :]
        for n, value in enumerate((t_imag - t_real, t_imag + t_real, t_real)):
            tables[3 * k + n] = jnp.broadcast_to(value, (8, lanes))

    passes = [
        [(dx, dy) for dx, dy in OFFSETS if dy == -2],
        [(dx, dy) for dx, dy in OFFSETS if dy == 2],
        [(dx, dy) for dx, dy in OFFSETS if abs(dy) < 2],
    ]
    blocks = tile_y // 8
    size = tile_x * tile_y // blocks

    def block(b, carry):
        total = None
        for shift in range(3):
            start = pl.multiple_of(b * size + shift * tile_y, tile_y)
            term = mm(shifted[pl.ds(start, size), :], near_ref[shift])
            total = term if total is None else total + term
        start = pl.multiple_of(b * size, size)
        field_ref[0, pl.ds(start, size), :] = total[:, :lanes]
        field_ref[1, pl.ds(start, size), :] = total[:, lanes:]
        shift_y = pl.multiple_of(b * 8, 8)
        for number, offsets in enumerate(passes):
            running = {}
            for row in range(tile_x):
                for dy in sorted({dy for _, dy in offsets}):
                    rows = pl.ds(shift_y + (row * width + LEFT + dy), 8)
                    source = [pats[k, rows, :] for k in range(3)]
                    for dx in range(-2, 3):
                        i = row - dx
                        if (dx, dy) not in offsets or not 0 <= i < tile_x:
                            continue
                        k = OFFSETS.index((dx, dy))
                        if i not in running:
                            running[i] = [None] * 3 if number == 0 else [sums[n, i] for n in range(3)]
                        running[i] = [
                            tables[3 * k + n] * source[n]
                            if running[i][n] is None
                            else running[i][n] + tables[3 * k + n] * source[n]
                            for n in range(3)
                        ]
                for i in sorted(running):
                    if i + 2 <= row or row == tile_x - 1:
                        value = running.pop(i)
                        if number < 2:
                            for n in range(3):
                                sums[n, i] = value[n]
                        else:
                            place = pl.ds(pl.multiple_of(shift_y + i * tile_y, 8), 8)
                            lower_ref[0, place, :] = value[2] - value[1]
                            lower_ref[1, place, :] = value[2] + value[0]
        return carry

    lax.fori_loop(0, blocks, block, 0)


def halos_kernel(
    tile_x, tile_y, inner_y, outer_y, inner_x, outer_x, agg_ref, near_ref, low_ref, lower_in, field_in,
    lower_ref, field_ref, columns, rims,
):
    lanes = lower_ref.shape[2]
    width = tile_y + 2 * LEFT
    odd_y = lax.axis_index("gy") % 2 == 1
    odd_x = lax.axis_index("gx") % 2 == 1
    sides = [jnp.where(odd_y, inner_y[...], outer_y[...]), jnp.where(odd_y, outer_y[...], inner_y[...])]
    ends = [jnp.where(odd_x, inner_x[...], outer_x[...]), jnp.where(odd_x, outer_x[...], inner_x[...])]
    lower_ref[...] = lower_in[...]
    field_ref[...] = field_in[...]
    halo = jnp.concatenate(sides + ends, axis=0)
    pattern = mm(halo, agg_ref[...]).astype(BF16).astype(F32)
    halo = halo.astype(F32)
    values = [halo[:, :lanes], halo[:, lanes:], pattern[:, :lanes], pattern[:, lanes:]]
    two = jnp.zeros((8, lanes), F32)
    rim_size = inner_x.shape[0]
    for n, value in enumerate(values):
        for side in range(2):
            for c in range(2):
                at = (2 * side + c) * tile_x
                columns[n, 2 * side + c, 0:8, :] = two
                columns[n, 2 * side + c, 8 : 8 + tile_x, :] = value[at : at + tile_x]
                columns[n, 2 * side + c, 8 + tile_x : 16 + tile_x, :] = two
        for end in range(2):
            at = 4 * tile_x + end * rim_size
            corner = at + 2 * tile_y
            for row in range(2):
                base = (2 * end + row) * width + LEFT
                rims[n, base : base + tile_y, :] = value[at + row * tile_y : at + (row + 1) * tile_y]
                for side in range(2):
                    for c in range(2):
                        place = base + (tile_y + c if side else c - 2)
                        line = corner + 4 * side + 2 * c + row
                        rims[n, place : place + 1, :] = value[line : line + 1]

    def translate(terms):
        first = second = 0.0
        for dx, dy, real, imag in terms:
            k = OFFSETS.index((dx, dy))
            t_real, t_imag = low_ref[2 * k : 2 * k + 1, :], low_ref[2 * k + 1 : 2 * k + 2, :]
            first = first + (t_real * real - t_imag * imag)
            second = second + (t_real * imag + t_imag * real)
        return first, second

    def column(n, side, c, dx):
        return columns[n, 2 * side + c, 8 + dx : 8 + dx + tile_x, :]

    def rim(n, end, row, dy):
        base = (2 * end + row) * width + LEFT + dy
        return rims[n, base : base + tile_y, :]

    for side in range(2):
        for box in ((tile_y - 1, tile_y - 2) if side else (0, 1)):
            terms = []
            for c in range(2):
                dy = (tile_y + c if side else c - 2) - box
                for dx in range(-2, 3):
                    if (dx, dy) in OFFSETS:
                        terms.append((dx, dy, column(2, side, c, dx), column(3, side, c, dx)))
            rows = pl.ds(box, tile_x, stride=tile_y)
            for part, value in enumerate(translate(terms)):
                lower_ref[part, rows, :] = lower_ref[part, rows, :] + value
        source = jnp.concatenate(
            [column(part, side, 1 - side, dx) for dx in range(-1, 2) for part in range(2)], axis=1
        ).astype(BF16)
        weights = [near_ref[dx, (4 * side) * lanes : (4 * side + 2) * lanes, :] for dx in range(3)]
        value = mm(source, jnp.concatenate(weights, axis=0))
        rows = pl.ds(tile_y - 1 if side else 0, tile_x, stride=tile_y)
        for part in range(2):
            field_ref[part, rows, :] = field_ref[part, rows, :] + value[:, part * lanes : (part + 1) * lanes]
    for end in range(2):
        for box in ((tile_x - 1, tile_x - 2) if end else (0, 1)):
            terms = []
            for row in range(2):
                dx = (tile_x + row if end else row - 2) - box
                for dy in range(-2, 3):
                    if (dx, dy) in OFFSETS:
                        terms.append((dx, dy, rim(2, end, row, dy), rim(3, end, row, dy)))
            rows = slice(box * tile_y, (box + 1) * tile_y)
            for part, value in enumerate(translate(terms)):
                lower_ref[part, rows, :] = lower_ref[part, rows, :] + value
        source = jnp.concatenate(
            [rim(part, end, 1 - end, dy) for dy in range(-1, 2) for part in range(2)], axis=1
        ).astype(BF16)
        value = mm(source, near_ref[2 * end])
        box = tile_x - 1 if end else 0
        rows = slice(box * tile_y, (box + 1) * tile_y)
        for part in range(2):
            field_ref[part, rows, :] = field_ref[part, rows, :] + value[:, part * lanes : (part + 1) * lanes]


def order_kernel(chunks, kinds, parents_x, parents_y, list_ref, kind_ref, count_ref, source_ref, table_ref,
                 number_ref, back_ref):
    parents = parents_x * parents_y
    slots = list_ref.shape[1]
    down = lax.broadcasted_iota(jnp.int32, (parents, parents), 0)
    along = lax.broadcasted_iota(jnp.int32, (parents, parents), 1)
    column = count_rows(count_ref, parents_x, parents_y, parents)
    row = jnp.sum(jnp.where(down == along, column, 0.0), axis=0, keepdims=True)
    before = (column > row) | ((column == row) & (down < along))
    rank = jnp.sum(jnp.where(before, 1.0, 0.0), axis=0, keepdims=True)
    move = jnp.where(down.astype(F32) == rank, 1.0, 0.0).astype(BF16)
    after = (row > column) | ((row == column) & (along < down))
    rank = jnp.sum(jnp.where(after, 1.0, 0.0), axis=1, keepdims=True)
    back_ref[...] = jnp.where(along.astype(F32) == rank, 1.0, 0.0).astype(BF16)

    across = parents_y * chunks
    entry = list_ref[...]
    line, place = entry // across, entry % across
    source = ((place // parents_y) ^ lax.axis_index("gy")) * parents + line * parents_y + place % parents_y
    count = column[:, :slots]
    used = lax.broadcasted_iota(jnp.int32, (parents, slots), 1).astype(F32) < count
    kind = jnp.where(used, kind_ref[...], kinds).astype(F32).astype(BF16)

    def moved(value):
        return mm(move, value).astype(jnp.int32)

    high = moved((source // 256).astype(F32).astype(BF16))
    source_ref[...] = high * 256 + moved((source % 256).astype(F32).astype(BF16))
    table_ref[...] = moved(kind)
    number_ref[...] = moved(count.astype(BF16))


GROUP = 8


def lists_kernel(chunks, tile_x, tile_y, *refs):
    sources = refs[:chunks]
    (source_at, table_at, number_at, table_ref, kept_ref, lower_ref, near_ref, back_ref, recv_ref, down_hbm, out_hbm,
     cells, table8, sums, down_ref, out_ref, sems) = refs[chunks:]
    parents_x, parents_y = tile_x // 2, tile_y // 2
    parents = parents_x * parents_y
    slots = source_at.shape[0] // parents
    kinds = table_ref.shape[0] // 4
    lanes = lower_ref.shape[2]
    load = pltpu.make_async_copy(down_hbm, down_ref, sems.at[0])
    load.start()
    rows8 = table8.reshape(8 * kinds + 8, lanes)
    for place, row in enumerate((0, 0, 2, 2, 1, 1, 3, 3)):
        rows8[pl.ds(place, kinds, stride=8), :] = table_ref[pl.ds(row, kinds, stride=4), :]
    table8[kinds] = jnp.zeros((8, lanes), F32)
    pairs = cells.reshape(chunks * parents // 2, 2, 8, lanes)
    for c in range(chunks):
        rows = sources[c][...].astype(F32).reshape(parents // 2, 8, lanes)
        for half in range(2):
            own = rows[:, 4 * half : 4 * half + 4, :]
            pairs[c * (parents // 2) : (c + 1) * (parents // 2), half] = jnp.concatenate([own, own], axis=1)

    def step(n, carry):
        first = n * (GROUP * slots)
        number = number_at[n * GROUP]
        for length in range(2, slots + 1, 2):

            @pl.when((number == length) | (number == length - 1))
            def _():
                for k in range(GROUP):
                    total = [None, None]
                    for s in range(length):
                        at = first + (k * slots + s)
                        term = cells[source_at[at]] * table8[table_at[at]]
                        total[s % 2] = term if total[s % 2] is None else total[s % 2] + term
                    sums[n * GROUP + k] = total[0] + total[1]

        @pl.when(number == 0)
        def _():
            for k in range(GROUP):
                sums[n * GROUP + k] = jnp.zeros((8, lanes), F32)

        return carry

    lax.fori_loop(0, parents // GROUP, step, 0)
    lines = sums.reshape(8 * parents, lanes)

    def row(place):
        return lines[pl.ds(place, parents, stride=8), :]

    ordered = jnp.concatenate(
        [row(0) - row(5), row(2) - row(7), row(1) + row(4), row(3) + row(6)], axis=1
    ).astype(BF16)
    incoming = mm(back_ref[...], ordered).astype(BF16)
    load.wait()
    stores = []
    count = parents_x // 2
    for half in range(2):
        part_in = incoming[half * count * parents_y : (half + 1) * count * parents_y]
        for side_x in range(2):
            for side_y in range(2):
                down = mm(part_in, down_ref[2 * side_x + side_y])
                starts = [
                    (2 * p + side_x) * tile_y + side_y for p in range(half * count, (half + 1) * count)
                ]

                def rows_of(ref):
                    return jnp.concatenate(
                        [ref[pl.ds(start, parents_y, stride=2), :] for start in starts], axis=0
                    )

                total = jnp.concatenate(
                    [
                        down[:, part * lanes : (part + 1) * lanes] + rows_of(lower_ref.at[part])
                        for part in range(2)
                    ],
                    axis=1,
                )
                field = mm(total.astype(BF16), recv_ref[...])
                mask = rows_of(kept_ref)
                for part in range(2):
                    value = field[:, part * lanes : (part + 1) * lanes] + rows_of(near_ref.at[part])
                    value = value * mask
                    for p, start in enumerate(starts):
                        out_ref[pl.ds(2 * start + part, parents_y, stride=4), :] = value[
                            p * parents_y : (p + 1) * parents_y
                        ]
        size = out_ref.shape[0] // 2
        rows = pl.ds(half * size, size)
        stores.append(pltpu.make_async_copy(out_ref.at[rows], out_hbm.at[rows], sems.at[1 + half]))
        stores[-1].start()
    for store in stores:
        store.wait()


def swap(low, high, axis):
    count = lax.axis_size(axis)
    lows = [(i, i ^ 1) for i in range(count)]
    highs = [(i, ((i + 1) ^ 1) - 1) for i in range(1, count - 1)]
    return lax.ppermute(low, axis, lows), lax.ppermute(high, axis, highs)


def body(
    currents, box_count, aggregate, near_blocks, low_translator, child_to_parent, coarse_list,
    coarse_kind, coarse_count, up_translator, parent_to_child, receive_map,
):
    tile_x, tile_y = box_count.shape
    boxes = tile_x * tile_y
    lanes = currents.shape[-1]
    parents_x, parents_y, slots = coarse_list.shape
    parents = parents_x * parents_y
    kinds, _, half = up_translator.shape
    wide = 2 * half
    chunks = lax.axis_size("gy")
    in_hbm = pl.BlockSpec(memory_space=pltpu.HBM)

    edge = jax.ShapeDtypeStruct((2 * tile_x, 2 * lanes), BF16)
    live, kept, low, high = pl.pallas_call(
        functools.partial(live_kernel, tile_x, tile_y),
        name="live",
        out_shape=[
            jax.ShapeDtypeStruct((boxes, 2 * lanes), BF16),
            jax.ShapeDtypeStruct((boxes, lanes), F32),
            edge,
            edge,
        ],
        in_specs=[in_hbm] * 2,
        out_specs=vmem(4),
        scratch_shapes=[
            pltpu.VMEM((2 * boxes, lanes), BF16),
            pltpu.VMEM((tile_x, tile_y), jnp.int32),
            pltpu.VMEM((2 * boxes, lanes), F32),
            pltpu.SemaphoreType.DMA((2,)),
        ],
        compiler_params=params(16),
        cost_estimate=cost(100 * MIB, 2 * MIB),
    )(hbm(currents.reshape(2 * boxes, lanes)), hbm(box_count))
    inner_y, outer_y = swap(low, high, "gy")

    coarse = pl.pallas_call(
        functools.partial(parents_kernel, tile_x, tile_y),
        name="parents",
        out_shape=jax.ShapeDtypeStruct((4 * parents, wide // 4), BF16),
        in_specs=vmem(3),
        out_specs=pl.BlockSpec(memory_space=pltpu.VMEM),
        scratch_shapes=[pltpu.VMEM((2, boxes, lanes), F32), pltpu.VMEM((4 * parents, wide // 4), F32)],
        compiler_params=params(16),
        cost_estimate=cost(200 * MIB, 3 * MIB),
    )(live, aggregate, child_to_parent.reshape(8 * lanes, wide))
    sources = [coarse] + [
        lax.ppermute(coarse, "gy", [(i, i ^ d) for i in range(chunks)]) for d in range(1, chunks)
    ]

    rim = 2 * tile_y + 8
    rim += -rim % 16
    low, high = pl.pallas_call(
        functools.partial(rims_kernel, tile_x, tile_y),
        name="rims",
        out_shape=[jax.ShapeDtypeStruct((rim, 2 * lanes), BF16)] * 2,
        in_specs=vmem(3),
        out_specs=vmem(2),
        scratch_shapes=[pltpu.VMEM((rim, 2 * lanes), F32)] * 2,
        compiler_params=params(16),
        cost_estimate=cost(MIB, MIB),
    )(live, inner_y, outer_y)
    inner_x, outer_x = swap(low, high, "gx")

    near_rows = near_blocks.reshape(3, 6 * lanes, 2 * lanes)
    low_rows = low_translator.reshape(-1, lanes)
    width = tile_y + 2 * LEFT
    pair = [jax.ShapeDtypeStruct((2, boxes, lanes), F32)] * 2
    lower, near = pl.pallas_call(
        functools.partial(local_kernel, tile_x, tile_y),
        name="local",
        out_shape=pair,
        in_specs=vmem(4),
        out_specs=vmem(2),
        scratch_shapes=[
            pltpu.VMEM((2, tile_x * width, lanes), F32),
            pltpu.VMEM((3, tile_x * width, lanes), F32),
            pltpu.VMEM(((tile_x + 2) * tile_y, 6 * lanes), BF16),
            pltpu.VMEM((3 * len(OFFSETS), 8, lanes), F32),
            pltpu.VMEM((3, tile_x, 8, lanes), F32),
        ],
        compiler_params=params(24),
        cost_estimate=cost(2000 * MIB, 5 * MIB),
    )(live, aggregate, near_rows, low_rows)

    entries = jax.ShapeDtypeStruct((parents, slots), jnp.int32)
    source_at, table_at, number_at, back = pl.pallas_call(
        functools.partial(order_kernel, chunks, kinds, parents_x, parents_y),
        name="order",
        out_shape=[entries, entries, entries, jax.ShapeDtypeStruct((parents, parents), BF16)],
        in_specs=vmem(3),
        out_specs=vmem(4),
        compiler_params=params(16),
        cost_estimate=cost(300 * MIB, MIB),
    )(coarse_list.reshape(parents, slots), coarse_kind.reshape(parents, slots), coarse_count)

    lower, near = pl.pallas_call(
        functools.partial(halos_kernel, tile_x, tile_y),
        name="halos",
        out_shape=pair,
        in_specs=vmem(9),
        out_specs=vmem(2),
        scratch_shapes=[
            pltpu.VMEM((4, 4, tile_x + 16, lanes), F32),
            pltpu.VMEM((4, 4 * width, lanes), F32),
        ],
        compiler_params=params(16),
        cost_estimate=cost(100 * MIB, 5 * MIB),
    )(inner_y, outer_y, inner_x, outer_x, aggregate, near_rows, low_rows, lower, near)

    table = up_translator.reshape(kinds, 2, 2, half // 2).transpose(0, 2, 1, 3).reshape(4 * kinds, half // 2)
    out = pl.pallas_call(
        functools.partial(lists_kernel, chunks, tile_x, tile_y),
        name="lists",
        out_shape=jax.ShapeDtypeStruct((2 * boxes, lanes), F32),
        in_specs=vmem(chunks) + [pl.BlockSpec(memory_space=pltpu.SMEM)] * 3 + vmem(6) + [in_hbm],
        out_specs=in_hbm,
        scratch_shapes=[
            pltpu.VMEM((chunks * parents, 8, lanes), F32),
            pltpu.VMEM((kinds + 1, 8, lanes), F32),
            pltpu.VMEM((parents, 8, lanes), F32),
            pltpu.VMEM((4, wide, 2 * lanes), BF16),
            pltpu.VMEM((2 * boxes, lanes), F32),
            pltpu.SemaphoreType.DMA((3,)),
        ],
        compiler_params=params(24 if chunks <= 4 else 48),
        cost_estimate=cost(3000 * MIB, 8 * MIB),
    )(
        *sources, source_at.reshape(-1), table_at.reshape(-1), number_at[:, 0], table,
        kept, lower, near, back, receive_map, hbm(parent_to_child),
    )
    return out.reshape(tile_x, tile_y, 2, lanes)


def solution(mesh):
    tiles = P("gx", "gy")
    in_specs = (tiles, tiles, P(), P(), P(), P(), tiles, tiles, tiles, P(), P(), P())
    return jax.shard_map(body, mesh=mesh, in_specs=in_specs, out_specs=tiles, check_vma=False)
```

time: 31.6 us -> 44.1 us (1.40)
  local copies, waits for them, and re-layouts: 0.87 us -> 7.9 us
  Pallas kernels: 16.2 us -> 19.6 us
  waiting for transfers between devices: 1.48 us -> 4.42 us
  starting transfers between devices: 12.1 us -> 11.5 us
  other arithmetic: 0.45 us -> 0 us
    unnamed x20 -> x40, local copies, waits for them, and re-layouts: 0.58 us -> 4.01 us
    pallas_call x1 -> x4, Pallas kernels: 0.65 us -> 3.84 us  [the longest x1 1.53 us: body(): pl.pallas_call(functools.partial(live_kernel, tile_x, tile_y), name='live...]
    reshape x4 -> x2, local copies, waits for them, and re-layouts: 0.23 us -> 3.2 us  [the longest x1 1.6 us: body(): table_at.reshape(-1)]
    ppermute x4, waiting for transfers between devices: 1.47 us -> 4.41 us  [swap(): return (lax.ppermute(low, axis, lows), lax.ppermute(high, axis, highs))]
    pallas_call x1, Pallas kernels: 9.15 us -> 11.2 us  [body(): pl.pallas_call(functools.partial(lists_kernel, chunks, tile_x, tile_y), n...]
    pallas_call x1, Pallas kernels: 4.15 us -> 3.18 us  [body(): pl.pallas_call(functools.partial(local_kernel, tile_x, tile_y), name='loc...]
    pallas_call x1, Pallas kernels: 2.28 us -> 1.42 us  [body(): pl.pallas_call(functools.partial(parents_kernel, tile_x, tile_y), name='p...]
    slice x1, local copies, waits for them, and re-layouts: 0.06 us -> 0.69 us  [body(): number_at[:, 0]]
  transfers between devices with their start and end apart: 7 -> 7, of which waited for: 1 -> 2; matrix products, arithmetic and copies ran while one was open for 2% -> 9% of each run, Pallas kernels for 15% -> 13%
where the time goes in v3:
time: 44.1 us; the launch traced here: 43.7 us
  Pallas kernels  19.6 us (44%)
  starting transfers between devices  11.5 us (26%)
  local copies, waits for them, and re-layouts  7.9 us (18%)
  waiting for transfers between devices  4.42 us (10%)
    pallas_call x1, Pallas kernels, body(): pl.pallas_call(functools.partial(lists_kernel, chunks, tile_x, tile_y), n...  11.2 us
    ppermute x4, starting transfers between devices, swap(): return (lax.ppermute(low, axis, lows), lax.ppermute(high, axis, highs))  8.86 us
    ppermute x4, waiting for transfers between devices, swap(): return (lax.ppermute(low, axis, lows), lax.ppermute(high, axis, highs))  4.41 us
    unnamed x40, local copies, waits for them, and re-layouts  4.01 us
    pallas_call x1, Pallas kernels, body(): pl.pallas_call(functools.partial(local_kernel, tile_x, tile_y), name='loc...  3.18 us
    ppermute x3, starting transfers between devices, body(): lax.ppermute(coarse, 'gy', [(i, i ^ d) for i in range(chunks)])  2.65 us
    reshape x1, local copies, waits for them, and re-layouts, body(): table_at.reshape(-1)  1.6 us
    reshape x1, local copies, waits for them, and re-layouts, body(): source_at.reshape(-1)  1.6 us
  transfers between devices with their start and end apart: 7, of which 2 were waited for; matrix products, arithmetic and copies ran while one was open for 9% of the time, Pallas kernels for 13%

profile of v3, /device:TPU:19, one launch (start us, length us, event | category | flops | bytes accessed | tf_op | source)
XLA Modules:
  0.0 43.7 jit_solution(3012714234736954447)
XLA Ops:
  0.0 0.0 copy-start.3
  0.0 0.0 copy-start.6
  0.0 1.5 %live.1 = (bf16[1024,256]{1,0:T(8,128)(2,1)S(1)}, f32[1024,128]{1,0:T(8,128)S(1)}, bf16[64,256]{1,0:T(8,128)(2,1)S(1)}, bf16[64,256]{1,0:T(8,128)(2,1)S(1)}) custom-call(bf16[2048,128]{1,0:T(8,128)(2,1)} %bitcast.20, s32[32,32]{1,0:T(8,128)} %counts_hbm.1), custom_call_target="tpu_custom_call" | custom-call | flops 209715200 | bytes 2097152 | tf_op jit(solution)/shard_map/live/pallas_call | solution.py:455
  1.5 0.0 copy-start.16
  1.6 0.8 %copy-done.16 = f32[1024,128]{1,0:T(8,128)} copy-done((f32[1024,128]{1,0:T(8,128)}, f32[1024,128]{1,0:T(8,128)S(1)}, u32[]{:S(2)}) %copy-start.16) | copy-done | bytes 524312
  2.3 0.0 copy-start
  2.3 0.0 copy-start.1
  2.3 1.3 %copy-done.1 = bf16[4,256,512]{2,1,0:T(8,128)(2,1)S(1)} copy-done((bf16[4,256,512]{2,1,0:T(8,128)(2,1)S(1)}, bf16[4,256,512]{2,1,0:T(8,128)(2,1)}, u32[]{:S(2)}) %copy-start.1) | copy-done | bytes 1048600
  3.7 0.0 copy-start.2
  3.7 0.9 %copy-done.2 = bf16[256,256]{1,0:T(8,128)(2,1)S(1)} copy-done((bf16[256,256]{1,0:T(8,128)(2,1)S(1)}, bf16[256,256]{1,0:T(8,128)(2,1)}, u32[]{:S(2)}) %copy-start.2) | copy-done | bytes 131096
  4.6 1.4 %parents.1.refs_0_ = bf16[1024,128]{1,0:T(8,128)(2,1)} custom-call(bf16[1024,256]{1,0:T(8,128)(2,1)S(1)} %get-tuple-element.19.live_ref, bf16[256,256]{1,0:T(8,128)(2,1)S(1)} %copy-done.2, bf16[1024,512]{1,0:T(8,128)(2,1)S(1)} %bitcast.14), custom_call_target="tpu_custom_call" | custom-call | flops 419430400 | bytes 3145728 | tf_op jit(solution)/shard_map/parents/pallas_call | solution.py:477
  6.0 0.3 collective-permute-start
  6.2 1.2 %collective-permute-start.1 = (bf16[1024,128]{1,0:T(8,128)(2,1)}, bf16[1024,128]{1,0:T(8,128)(2,1)}, u32[]{:S(2)}, u32[]{:S(2)}) collective-permute-start(bf16[1024,128]{1,0:T(8,128)(2,1)} %parents.1.refs_0_), channel_id=1, source_target_pairs={{0,2},{1,3},{2,0},{3,1},{4,6},{5,7},{6,4},{7,5},{8,10},{9,11},{10,... | collective-permute-start | bytes 786440 | tf_op jit(solution)/shard_map/ppermute | solution.py:488
  7.5 1.1 %collective-permute-start.2 = (bf16[1024,128]{1,0:T(8,128)(2,1)}, bf16[1024,128]{1,0:T(8,128)(2,1)}, u32[]{:S(2)}, u32[]{:S(2)}) collective-permute-start(bf16[1024,128]{1,0:T(8,128)(2,1)} %parents.1.refs_0_), channel_id=1, source_target_pairs={{0,3},{1,2},{2,1},{3,0},{4,7},{5,6},{6,5},{7,4},{8,11},{9,10},{10,... | collective-permute-start | bytes 786440 | tf_op jit(solution)/shard_map/ppermute | solution.py:488
  8.6 0.3 collective-permute-start.3
  8.9 4.1 %collective-permute-start.4 = (bf16[64,256]{1,0:T(8,128)(2,1)S(1)}, bf16[64,256]{1,0:T(8,128)(2,1)S(1)}, u32[]{:S(2)}, u32[]{:S(2)}) collective-permute-start(bf16[64,256]{1,0:T(8,128)(2,1)S(1)} %get-tuple-element.25), channel_id=1, source_target_pairs={{1,2},{2,1},{5,6},{6,5},{9,10},{10,9},{13,14},{14,13},{17,18},{18,... | collective-permute-start | bytes 98312 | tf_op jit(solution)/shard_map/ppermute | solution.py:437
  13.0 0.0 copy-done.3
  13.0 0.0 copy-done.6
  13.0 0.0 copy-done
  13.0 0.0 copy-start.11
  13.0 0.0 copy-start.12
  13.0 0.0 copy-start.15
  13.0 3.2 %local.1 = (f32[2,1024,128]{2,1,0:T(8,128)S(1)}, f32[2,1024,128]{2,1,0:T(8,128)S(1)}) custom-call(bf16[1024,256]{1,0:T(8,128)(2,1)S(1)} %get-tuple-element.19.live_ref, bf16[256,256]{1,0:T(8,128)(2,1)S(1)} %copy-done.3, bf16[3,768,256]{2,1,0:T(8,128)(2,1)S(1)} %bitcast.12, f32[32,128]{1,0:T(8,128)S(1)} %bitcast.15), custom_call_target="tpu_custom_call" | custom-call | flops 4194304000 | bytes 5242880 | tf_op jit(solution)/shard_map/local/pallas_call | solution.py:509
  16.2 0.0 copy-done.11
  16.2 0.0 copy-done.12
  16.2 0.0 copy-done.15
  16.3 0.8 %order.1 = (s32[256,16]{1,0:T(8,128)S(1)}, s32[256,16]{1,0:T(8,128)S(1)}, s32[256,16]{1,0:T(8,128)S(1)}, bf16[256,256]{1,0:T(8,128)(2,1)S(1)}) custom-call(s32[256,16]{1,0:T(8,128)S(1)} %bitcast.17, s32[256,16]{1,0:T(8,128)S(1)} %bitcast.18, s32[16,16]{1,0:T(8,128)S(1)} %copy-done.15), custom_call_target="tpu_custom_call" | custom-call | flops 629145600 | bytes 1048576 | tf_op jit(solution)/shard_map/order/pallas_call | solution.py:527
  17.0 0.0 copy-start.4
  17.0 0.0 copy-start.5
  17.0 0.0 copy-start.18
  17.0 2.8 %collective-permute-done.3.inner_ref.inner_y = bf16[64,256]{1,0:T(8,128)(2,1)S(1)} collective-permute-done((bf16[64,256]{1,0:T(8,128)(2,1)S(1)}, bf16[64,256]{1,0:T(8,128)(2,1)S(1)}, u32[]{:S(2)}, u32[]{:S(2)}) %collective-permute-start.3) | collective-permute-done | bytes 32800 | tf_op jit(solution)/shard_map/ppermute | solution.py:437
  19.8 1.6 %collective-permute-done.4.outer_ref.outer_y = bf16[64,256]{1,0:T(8,128)(2,1)S(1)} collective-permute-done((bf16[64,256]{1,0:T(8,128)(2,1)S(1)}, bf16[64,256]{1,0:T(8,128)(2,1)S(1)}, u32[]{:S(2)}, u32[]{:S(2)}) %collective-permute-start.4) | collective-permute-done | bytes 32800 | tf_op jit(solution)/shard_map/ppermute | solution.py:437
  21.5 0.7 %rims.1 = (bf16[80,256]{1,0:T(8,128)(2,1)}, bf16[80,256]{1,0:T(8,128)(2,1)}) custom-call(bf16[1024,256]{1,0:T(8,128)(2,1)S(1)} %get-tuple-element.19.live_ref, bf16[64,256]{1,0:T(8,128)(2,1)S(1)} %collective-permute-done.3.inner_ref.inner_y, bf16[64,256]{1,0:T(8,128)(2,1)S(1)} %collective-permute-done.4.outer_ref.outer_y), custom_call_target="tpu_custom_call" | custom-call | flops 2097152 | bytes 1048576 | tf_op jit(solution)/shard_map/rims/pallas_call | solution.py:493
  22.1 0.0 copy-done.4
  22.1 0.0 copy-done.5
  22.1 1.4 %collective-permute-start.5 = (bf16[80,256]{1,0:T(8,128)(2,1)}, bf16[80,256]{1,0:T(8,128)(2,1)S(1)}, u32[]{:S(2)}, u32[]{:S(2)}) collective-permute-start(bf16[80,256]{1,0:T(8,128)(2,1)} %get-tuple-element.26), channel_id=1, source_target_pairs={{0,4},{4,0},{8,12},{12,8},{16,20},{20,16},{24,28},{28,24},{1,5},{5... | collective-permute-start | bytes 122888 | tf_op jit(solution)/shard_map/ppermute | solution.py:437
  23.6 3.1 %collective-permute-start.6 = (bf16[80,256]{1,0:T(8,128)(2,1)}, bf16[80,256]{1,0:T(8,128)(2,1)S(1)}, u32[]{:S(2)}, u32[]{:S(2)}) collective-permute-start(bf16[80,256]{1,0:T(8,128)(2,1)} %get-tuple-element.27), channel_id=1, source_target_pairs={{4,8},{8,4},{12,16},{16,12},{20,24},{24,20},{5,9},{9,5},{13,17},{1... | collective-permute-start | bytes 122888 | tf_op jit(solution)/shard_map/ppermute | solution.py:437
  26.7 0.7 %slice_reduce_fusion.refs_6_ = s32[256]{0:T(256)} fusion(s32[256,16]{1,0:T(8,128)S(1)} %get-tuple-element.22), kind=kLoop, calls=%fused_computation | loop fusion | bytes 2048 | tf_op jit(solution)/shard_map/slice | solution.py:569
  27.4 0.0 copy-done.18
  27.4 1.6 %reshape.37.refs_4_ = s32[4096]{0:T(1024)} reshape(s32[256,16]{1,0:T(8,128)} %copy-done.5) | data formatting | bytes 32768 | tf_op jit(solution)/shard_map/reshape | solution.py:569
  29.0 1.6 %reshape.38.refs_5_ = s32[4096]{0:T(1024)} reshape(s32[256,16]{1,0:T(8,128)} %copy-done.4) | data formatting | bytes 32768 | tf_op jit(solution)/shard_map/reshape | solution.py:569
  30.6 0.0 collective-permute-done.5.inner_x
  30.6 0.0 collective-permute-done.6.outer_x
  30.6 0.0 copy-start.7
  30.6 0.7 %copy-done.7 = f32[16,2,128]{2,1,0:T(2,128)S(1)} copy-done((f32[16,2,128]{2,1,0:T(2,128)S(1)}, f32[16,2,128]{2,1,0:T(2,128)}, u32[]{:S(2)}) %copy-start.7) | copy-done | bytes 16408
  31.3 0.0 copy-start.8
  31.3 0.0 copy-start.9
  31.3 0.0 copy-start.10
  31.3 0.0 copy-start.13
  31.3 0.0 copy-start.14
  31.3 0.0 copy-start.17
  31.3 0.0 copy-start.19
  31.3 0.9 %halos.1 = (f32[2,1024,128]{2,1,0:T(8,128)S(1)}, f32[2,1024,128]{2,1,0:T(8,128)S(1)}) custom-call(bf16[64,256]{1,0:T(8,128)(2,1)S(1)} %collective-permute-done.3.inner_ref.inner_y, bf16[64,256]{1,0:T(8,128)(2,1)S(1)} %collective-permute-done.4.outer_ref.outer_y, bf16[80,256]{1,0:T(8,128)(2,1)S(1)} %collective-permute-done.5.inner_x, ...), custom_call_target="tpu_custom_call" | custom-call | flops 209715200 | bytes 5242880 | tf_op jit(solution)/shard_map/halos/pallas_call | solution.py:537
  32.2 0.0 collective-permute-done.refs_1_
  32.2 0.0 collective-permute-done.1.refs_2_
  32.2 0.0 collective-permute-done.2.refs_3_
  32.3 0.0 copy-done.8
  32.3 0.0 copy-done.9
  32.3 0.0 copy-done.10
  32.3 0.0 copy-done.13
  32.3 0.0 copy-done.14
  32.3 0.2 copy-done.17
  32.5 0.0 copy-done.19
  32.5 11.2 %lists.1 = f32[2048,128]{1,0:T(8,128)} custom-call(bf16[1024,128]{1,0:T(8,128)(2,1)} %parents.1.refs_0_, bf16[1024,128]{1,0:T(8,128)(2,1)} %collective-permute-done.refs_1_, bf16[1024,128]{1,0:T(8,128)(2,1)} %collective-permute-done.1.refs_2_, bf16[1024,128]{1,0:T(8,128)(2,1)} %collective-permute-done.2.refs_3_, s32[4096]{0:T(1024)S(1)} %copy-done.8, ...), custom_call_target="tpu_custom_call" | custom-call | flops 6291456000 | bytes 8388608 | tf_op jit(solution)/shard_map/lists/pallas_call | solution.py:552
Async XLA Ops:
  0.0 13.0 %copy-start.3 = (bf16[256,256]{1,0:T(8,128)(2,1)S(1)}, bf16[256,256]{1,0:T(8,128)(2,1)}, u32[]{:S(2)}) copy-start(bf16[256,256]{1,0:T(8,128)(2,1)} %agg_ref.5) | copy-start | bytes 393220
  0.0 13.0 %copy-start.6 = (f32[16,2,128]{2,1,0:T(2,128)S(1)}, f32[16,2,128]{2,1,0:T(2,128)}, u32[]{:S(2)}) copy-start(f32[16,2,128]{2,1,0:T(2,128)} %param.16) | copy-start | bytes 49156
  1.5 0.8 %copy-start.16 = (f32[1024,128]{1,0:T(8,128)}, f32[1024,128]{1,0:T(8,128)S(1)}, u32[]{:S(2)}) copy-start(f32[1024,128]{1,0:T(8,128)S(1)} %get-tuple-element.23.refs_8_) | copy-start | bytes 1572868
  2.3 10.7 %copy-start = (bf16[9,256,256]{2,1,0:T(8,128)(2,1)S(1)}, bf16[9,256,256]{2,1,0:T(8,128)(2,1)}, u32[]{:S(2)}) copy-start(bf16[9,256,256]{2,1,0:T(8,128)(2,1)} %param.15) | copy-start | bytes 3538948
  2.3 1.3 %copy-start.1 = (bf16[4,256,512]{2,1,0:T(8,128)(2,1)S(1)}, bf16[4,256,512]{2,1,0:T(8,128)(2,1)}, u32[]{:S(2)}) copy-start(bf16[4,256,512]{2,1,0:T(8,128)(2,1)} %param.17) | copy-start | bytes 3145732
  3.7 0.9 %copy-start.2 = (bf16[256,256]{1,0:T(8,128)(2,1)S(1)}, bf16[256,256]{1,0:T(8,128)(2,1)}, u32[]{:S(2)}) copy-start(bf16[256,256]{1,0:T(8,128)(2,1)} %agg_ref.5) | copy-start | bytes 393220
  6.0 26.2 %collective-permute-start = (bf16[1024,128]{1,0:T(8,128)(2,1)}, bf16[1024,128]{1,0:T(8,128)(2,1)}, u32[]{:S(2)}, u32[]{:S(2)}) collective-permute-start(bf16[1024,128]{1,0:T(8,128)(2,1)} %parents.1.refs_0_), channel_id=1, source_target_pairs={{0,1},{1,0},{2,3},{3,2},{4,5},{5,4},{6,7},{7,6},{8,9},{9,8},{10,11... | collective-permute-start | bytes 786440 | tf_op jit(solution)/shard_map/ppermute | solution.py:488
  6.2 26.0 %collective-permute-start.1 = (bf16[1024,128]{1,0:T(8,128)(2,1)}, bf16[1024,128]{1,0:T(8,128)(2,1)}, u32[]{:S(2)}, u32[]{:S(2)}) collective-permute-start(bf16[1024,128]{1,0:T(8,128)(2,1)} %parents.1.refs_0_), channel_id=1, source_target_pairs={{0,2},{1,3},{2,0},{3,1},{4,6},{5,7},{6,4},{7,5},{8,10},{9,11},{10,... | collective-permute-start | bytes 786440 | tf_op jit(solution)/shard_map/ppermute | solution.py:488
  7.5 24.8 %collective-permute-start.2 = (bf16[1024,128]{1,0:T(8,128)(2,1)}, bf16[1024,128]{1,0:T(8,128)(2,1)}, u32[]{:S(2)}, u32[]{:S(2)}) collective-permute-start(bf16[1024,128]{1,0:T(8,128)(2,1)} %parents.1.refs_0_), channel_id=1, source_target_pairs={{0,3},{1,2},{2,1},{3,0},{4,7},{5,6},{6,5},{7,4},{8,11},{9,10},{10,... | collective-permute-start | bytes 786440 | tf_op jit(solution)/shard_map/ppermute | solution.py:488
  8.6 11.2 %collective-permute-start.3 = (bf16[64,256]{1,0:T(8,128)(2,1)S(1)}, bf16[64,256]{1,0:T(8,128)(2,1)S(1)}, u32[]{:S(2)}, u32[]{:S(2)}) collective-permute-start(bf16[64,256]{1,0:T(8,128)(2,1)S(1)} %get-tuple-element.24), channel_id=1, source_target_pairs={{0,1},{1,0},{2,3},{3,2},{4,5},{5,4},{6,7},{7,6},{8,9},{9,8},{10,11... | collective-permute-start | bytes 98312 | tf_op jit(solution)/shard_map/ppermute | solution.py:437
  8.9 12.6 %collective-permute-start.4 = (bf16[64,256]{1,0:T(8,128)(2,1)S(1)}, bf16[64,256]{1,0:T(8,128)(2,1)S(1)}, u32[]{:S(2)}, u32[]{:S(2)}) collective-permute-start(bf16[64,256]{1,0:T(8,128)(2,1)S(1)} %get-tuple-element.25), channel_id=1, source_target_pairs={{1,2},{2,1},{5,6},{6,5},{9,10},{10,9},{13,14},{14,13},{17,18},{18,... | collective-permute-start | bytes 98312 | tf_op jit(solution)/shard_map/ppermute | solution.py:437
  13.0 3.2 %copy-start.11 = (s32[16,16,16]{2,1,0:T(8,128)S(1)}, s32[16,16,16]{2,1,0:T(8,128)}, u32[]{:S(2)}) copy-start(s32[16,16,16]{2,1,0:T(8,128)} %param.18) | copy-start | bytes 49156
  13.0 3.2 %copy-start.12 = (s32[16,16,16]{2,1,0:T(8,128)S(1)}, s32[16,16,16]{2,1,0:T(8,128)}, u32[]{:S(2)}) copy-start(s32[16,16,16]{2,1,0:T(8,128)} %param.19) | copy-start | bytes 49156
  13.0 3.2 %copy-start.15 = (s32[16,16]{1,0:T(8,128)S(1)}, s32[16,16]{1,0:T(8,128)}, u32[]{:S(2)}) copy-start(s32[16,16]{1,0:T(8,128)} %count_ref.1) | copy-start | bytes 3076
  17.0 5.1 %copy-start.4 = (s32[256,16]{1,0:T(8,128)}, s32[256,16]{1,0:T(8,128)S(1)}, u32[]{:S(2)}) copy-start(s32[256,16]{1,0:T(8,128)S(1)} %get-tuple-element.21) | copy-start | bytes 49156
  17.0 5.1 %copy-start.5 = (s32[256,16]{1,0:T(8,128)}, s32[256,16]{1,0:T(8,128)S(1)}, u32[]{:S(2)}) copy-start(s32[256,16]{1,0:T(8,128)S(1)} %get-tuple-element.20) | copy-start | bytes 49156
  17.0 10.3 %copy-start.18 = (bf16[256,256]{1,0:T(8,128)(2,1)}, bf16[256,256]{1,0:T(8,128)(2,1)S(1)}, u32[]{:S(2)}) copy-start(bf16[256,256]{1,0:T(8,128)(2,1)S(1)} %get-tuple-element.32.refs_11_) | copy-start | bytes 393220
  22.1 8.4 %collective-permute-start.5 = (bf16[80,256]{1,0:T(8,128)(2,1)}, bf16[80,256]{1,0:T(8,128)(2,1)S(1)}, u32[]{:S(2)}, u32[]{:S(2)}) collective-permute-start(bf16[80,256]{1,0:T(8,128)(2,1)} %get-tuple-element.26), channel_id=1, source_target_pairs={{0,4},{4,0},{8,12},{12,8},{16,20},{20,16},{24,28},{28,24},{1,5},{5... | collective-permute-start | bytes 122888 | tf_op jit(solution)/shard_map/ppermute | solution.py:437
  23.6 7.0 %collective-permute-start.6 = (bf16[80,256]{1,0:T(8,128)(2,1)}, bf16[80,256]{1,0:T(8,128)(2,1)S(1)}, u32[]{:S(2)}, u32[]{:S(2)}) collective-permute-start(bf16[80,256]{1,0:T(8,128)(2,1)} %get-tuple-element.27), channel_id=1, source_target_pairs={{4,8},{8,4},{12,16},{16,12},{20,24},{24,20},{5,9},{9,5},{13,17},{1... | collective-permute-start | bytes 122888 | tf_op jit(solution)/shard_map/ppermute | solution.py:437
  30.6 0.7 %copy-start.7 = (f32[16,2,128]{2,1,0:T(2,128)S(1)}, f32[16,2,128]{2,1,0:T(2,128)}, u32[]{:S(2)}) copy-start(f32[16,2,128]{2,1,0:T(2,128)} %param.16) | copy-start | bytes 49156
  31.3 1.0 %copy-start.8 = (s32[4096]{0:T(1024)S(1)}, s32[4096]{0:T(1024)}, u32[]{:S(2)}) copy-start(s32[4096]{0:T(1024)} %reshape.37.refs_4_) | copy-start | bytes 49156
  31.3 1.0 %copy-start.9 = (s32[4096]{0:T(1024)S(1)}, s32[4096]{0:T(1024)}, u32[]{:S(2)}) copy-start(s32[4096]{0:T(1024)} %reshape.38.refs_5_) | copy-start | bytes 49156
  31.3 1.0 %copy-start.10 = (s32[256]{0:T(256)S(1)}, s32[256]{0:T(256)}, u32[]{:S(2)}) copy-start(s32[256]{0:T(256)} %slice_reduce_fusion.refs_6_) | copy-start | bytes 3076
  31.3 1.0 %copy-start.13 = (f32[64,2,256]{2,1,0:T(2,128)S(1)}, f32[64,2,256]{2,1,0:T(2,128)}, u32[]{:S(2)}) copy-start(f32[64,2,256]{2,1,0:T(2,128)} %param.21) | copy-start | bytes 393220
  31.3 1.0 %copy-start.14 = (bf16[256,256]{1,0:T(8,128)(2,1)S(1)}, bf16[256,256]{1,0:T(8,128)(2,1)}, u32[]{:S(2)}) copy-start(bf16[256,256]{1,0:T(8,128)(2,1)} %refs_12_.1) | copy-start | bytes 393220
  31.3 1.2 %copy-start.17 = (f32[1024,128]{1,0:T(8,128)S(1)}, f32[1024,128]{1,0:T(8,128)}, u32[]{:S(2)}) copy-start(f32[1024,128]{1,0:T(8,128)} %copy-done.16) | copy-start | bytes 1572868
  31.3 1.2 %copy-start.19 = (bf16[256,256]{1,0:T(8,128)(2,1)S(1)}, bf16[256,256]{1,0:T(8,128)(2,1)}, u32[]{:S(2)}) copy-start(bf16[256,256]{1,0:T(8,128)(2,1)} %copy-done.18) | copy-start | bytes 393220

commit v4 on v3

--- a/solution.py
+++ b/solution.py
@@ -43,11 +43,23 @@
     return mm(jnp.concatenate(diag, axis=0).astype(BF16), jnp.ones((tile_y, lanes), BF16))
 
 
-def live_kernel(tile_x, tile_y, cur_hbm, counts_hbm, live_ref, kept_ref, low_ref, high_ref, cur_ref, counts_ref,
-                wide, sems):
+def halo_pair(inner_ref, outer_ref, axis):
+    at = lax.axis_index(axis)
+    odd = at % 2 == 1
+    inner, outer = inner_ref[...].astype(F32), outer_ref[...].astype(F32)
+    before, after = jnp.where(odd, inner, outer), jnp.where(odd, outer, inner)
+    return jnp.where(at > 0, before, 0.0), jnp.where(at < lax.axis_size(axis) - 1, after, 0.0)
+
+
+def live_kernel(tile_x, tile_y, cur_hbm, counts_hbm, list_hbm, kind_hbm, number_hbm,
+                live_ref, kept_ref, low_ref, high_ref, list_ref, kind_ref, number_ref,
+                cur_ref, counts_ref, wide, sems):
+    pairs = [
+        (counts_hbm, counts_ref), (cur_hbm, cur_ref), (list_hbm, list_ref), (kind_hbm, kind_ref),
+        (number_hbm, number_ref),
+    ]
     loads = [
-        pltpu.make_async_copy(counts_hbm, counts_ref, sems.at[0]),
-        pltpu.make_async_copy(cur_hbm, cur_ref, sems.at[1]),
+        pltpu.make_async_copy(source, target, sems.at[k]) for k, (source, target) in enumerate(pairs)
     ]
     for load in loads:
         load.start()
@@ -72,10 +84,19 @@
         last = jnp.concatenate([edge(tile_y - 2), edge(tile_y - 1)], axis=0).astype(BF16)
         low_ref[:, cols] = jnp.where(odd, first, last)
         high_ref[:, cols] = jnp.where(odd, last, first)
-
-
-def parents_kernel(tile_x, tile_y, live_ref, agg_ref, up_ref, coarse_ref, pats, rows4):
+    for load in loads[2:]:
+        load.wait()
+
+
+LEFT = 8
+
+
+def parents_kernel(
+    tile_x, tile_y, live_ref, agg_ref, up_ref, inner_ref, outer_ref, coarse_ref, pats_ref, low_ref, high_ref,
+    pats, rows4, first, last,
+):
     lanes = pats.shape[2]
+    width = tile_y + 2 * LEFT
     pattern = mm(live_ref[...], agg_ref[...])
     pats[0] = pattern[:, :lanes]
     pats[1] = pattern[:, lanes:]
@@ -93,13 +114,18 @@
         rows4[pl.ds(place, coarse.shape[0], stride=4), :] = coarse[:, column * 128 : (column + 1) * 128]
     coarse_ref[...] = rows4[...].astype(BF16)
 
-
-def rims_kernel(tile_x, tile_y, live_ref, inner_ref, outer_ref, low_ref, high_ref, first, last):
-    odd_y = lax.axis_index("gy") % 2 == 1
-    odd_x = lax.axis_index("gx") % 2 == 1
-    inner, outer = inner_ref[...].astype(F32), outer_ref[...].astype(F32)
-    boxes = tile_x * tile_y
-    sides = (jnp.where(odd_y, inner, outer), jnp.where(odd_y, outer, inner))
+    pattern = pattern.astype(BF16).astype(F32)
+    values = [pattern[:, :lanes], pattern[:, lanes:], pattern[:, :lanes] + pattern[:, lanes:]]
+    none = jnp.zeros((LEFT, lanes), F32)
+    for i in range(tile_x):
+        base = i * width
+        for k in range(3):
+            pats_ref[k, base : base + LEFT, :] = none
+            pats_ref[k, base + LEFT : base + LEFT + tile_y, :] = values[k][i * tile_y : (i + 1) * tile_y]
+            pats_ref[k, base + LEFT + tile_y : base + width, :] = none
+
+    odd = lax.axis_index("gx") % 2 == 1
+    sides = halo_pair(inner_ref, outer_ref, "gy")
     for rim, start in ((first, 0), (last, tile_x - 2)):
         rim[0 : 2 * tile_y, :] = live_ref[start * tile_y : (start + 2) * tile_y, :].astype(F32)
         place = 2 * tile_y
@@ -109,29 +135,19 @@
                 rim[place : place + 2, :] = side[at : at + 2]
                 place += 2
         rim[place:, :] = jnp.zeros((rim.shape[0] - place, rim.shape[1]), F32)
-    low_ref[...] = jnp.where(odd_x, first[...], last[...]).astype(BF16)
-    high_ref[...] = jnp.where(odd_x, last[...], first[...]).astype(BF16)
-
-
-LEFT = 8
+    low_ref[...] = jnp.where(odd, first[...], last[...]).astype(BF16)
+    high_ref[...] = jnp.where(odd, last[...], first[...]).astype(BF16)
+
+
 OFFSETS = [(dx, dy) for dx in range(-2, 3) for dy in range(-2, 3) if max(abs(dx), abs(dy)) == 2]
 
 
 def local_kernel(
-    tile_x, tile_y, live_ref, agg_ref, near_ref, low_ref, lower_ref, field_ref, cells, pats, shifted, tables, sums,
+    tile_x, tile_y, live_ref, pats, near_ref, low_ref, lower_ref, field_ref, cells, shifted, tables, sums,
 ):
     lanes = lower_ref.shape[2]
     width = tile_y + 2 * LEFT
     none = jnp.zeros((LEFT, lanes), F32)
-    pattern = mm(live_ref[...], agg_ref[...]).astype(BF16).astype(F32)
-    values = [pattern[:, :lanes], pattern[:, lanes:], pattern[:, :lanes] + pattern[:, lanes:]]
-    for i in range(tile_x):
-        base = i * width
-        rows = slice(i * tile_y, (i + 1) * tile_y)
-        for k in range(3):
-            pats[k, base : base + LEFT, :] = none
-            pats[k, base + LEFT : base + LEFT + tile_y, :] = values[k][rows]
-            pats[k, base + LEFT + tile_y : base + width, :] = none
     ends = jnp.zeros((tile_y, 6 * lanes), BF16)
     shifted[0:tile_y, :] = ends
     shifted[(tile_x + 1) * tile_y : (tile_x + 2) * tile_y, :] = ends
@@ -213,15 +229,11 @@
 ):
     lanes = lower_ref.shape[2]
     width = tile_y + 2 * LEFT
-    odd_y = lax.axis_index("gy") % 2 == 1
-    odd_x = lax.axis_index("gx") % 2 == 1
-    sides = [jnp.where(odd_y, inner_y[...], outer_y[...]), jnp.where(odd_y, outer_y[...], inner_y[...])]
-    ends = [jnp.where(odd_x, inner_x[...], outer_x[...]), jnp.where(odd_x, outer_x[...], inner_x[...])]
+    halo = halo_pair(inner_y, outer_y, "gy") + halo_pair(inner_x, outer_x, "gx")
     lower_ref[...] = lower_in[...]
     field_ref[...] = field_in[...]
-    halo = jnp.concatenate(sides + ends, axis=0)
-    pattern = mm(halo, agg_ref[...]).astype(BF16).astype(F32)
-    halo = halo.astype(F32)
+    halo = jnp.concatenate(halo, axis=0)
+    pattern = mm(halo.astype(BF16), agg_ref[...]).astype(BF16).astype(F32)
     values = [halo[:, :lanes], halo[:, lanes:], pattern[:, :lanes], pattern[:, lanes:]]
     two = jnp.zeros((8, lanes), F32)
     rim_size = inner_x.shape[0]
@@ -300,52 +312,71 @@
             field_ref[part, rows, :] = field_ref[part, rows, :] + value[:, part * lanes : (part + 1) * lanes]
 
 
-def order_kernel(chunks, kinds, parents_x, parents_y, list_ref, kind_ref, count_ref, source_ref, table_ref,
-                 number_ref, back_ref):
+GROUP = 8
+
+
+def order_kernel(chunks, kinds, parents_x, parents_y, list_ref, kind_ref, count_ref, agg_hbm, up_hbm,
+                 at_ref, back_ref, agg_ref, up_ref, sems):
+    loads = [
+        pltpu.make_async_copy(agg_hbm, agg_ref, sems.at[0]),
+        pltpu.make_async_copy(up_hbm, up_ref, sems.at[1]),
+    ]
+    for load in loads:
+        load.start()
     parents = parents_x * parents_y
     slots = list_ref.shape[1]
+    groups = parents // GROUP
+    lanes = at_ref.shape[1]
     down = lax.broadcasted_iota(jnp.int32, (parents, parents), 0)
     along = lax.broadcasted_iota(jnp.int32, (parents, parents), 1)
     column = count_rows(count_ref, parents_x, parents_y, parents)
     row = jnp.sum(jnp.where(down == along, column, 0.0), axis=0, keepdims=True)
     before = (column > row) | ((column == row) & (down < along))
     rank = jnp.sum(jnp.where(before, 1.0, 0.0), axis=0, keepdims=True)
-    move = jnp.where(down.astype(F32) == rank, 1.0, 0.0).astype(BF16)
     after = (row > column) | ((row == column) & (along < down))
-    rank = jnp.sum(jnp.where(after, 1.0, 0.0), axis=1, keepdims=True)
-    back_ref[...] = jnp.where(along.astype(F32) == rank, 1.0, 0.0).astype(BF16)
+    rank_down = jnp.sum(jnp.where(after, 1.0, 0.0), axis=1, keepdims=True)
+    back_ref[...] = jnp.where(along.astype(F32) == rank_down, 1.0, 0.0).astype(BF16)
 
     across = parents_y * chunks
     entry = list_ref[...]
     line, place = entry // across, entry % across
     source = ((place // parents_y) ^ lax.axis_index("gy")) * parents + line * parents_y + place % parents_y
-    count = column[:, :slots]
-    used = lax.broadcasted_iota(jnp.int32, (parents, slots), 1).astype(F32) < count
-    kind = jnp.where(used, kind_ref[...], kinds).astype(F32).astype(BF16)
-
-    def moved(value):
-        return mm(move, value).astype(jnp.int32)
-
-    high = moved((source // 256).astype(F32).astype(BF16))
-    source_ref[...] = high * 256 + moved((source % 256).astype(F32).astype(BF16))
-    table_ref[...] = moved(kind)
-    number_ref[...] = moved(count.astype(BF16))
-
-
-GROUP = 8
-
-
-def lists_kernel(chunks, tile_x, tile_y, *refs):
+    used = lax.broadcasted_iota(jnp.int32, (parents, slots), 1).astype(F32) < column[:, :slots]
+    kind = jnp.where(used, kind_ref[...], kinds)
+    values = [(source // 256).astype(F32), (source % 256).astype(F32), kind.astype(F32)]
+    values = [value.astype(BF16) for value in values]
+    totals = [jnp.zeros((groups, lanes), F32)] * 3
+    first = GROUP * lax.broadcasted_iota(jnp.int32, (groups, parents), 0)
+    slot = lax.broadcasted_iota(jnp.int32, (slots, lanes), 0)
+    lane = lax.broadcasted_iota(jnp.int32, (slots, lanes), 1)
+    for k in range(GROUP):
+        move = jnp.where((first + k).astype(F32) == rank, 1.0, 0.0).astype(BF16)
+        spread = jnp.where(lane == slot + k * slots, 1.0, 0.0).astype(BF16)
+        totals = [
+            total + mm(mm(move, value).astype(BF16), spread) for total, value in zip(totals, values)
+        ]
+    high, low, kind = [total.astype(jnp.int32) for total in totals]
+    at_ref[0:groups, :] = high * 256 + low
+    at_ref[groups : 2 * groups, :] = kind
+    least = (slots - 1 - 2 * lax.broadcasted_iota(jnp.int32, (parents, lanes), 1)).astype(F32)
+    reach = jnp.sum(jnp.where(column[:, :lanes] >= least, 1.0, 0.0), axis=0, keepdims=True).astype(jnp.int32)
+    at_ref[2 * groups :, :] = jnp.broadcast_to((reach + (GROUP - 1)) // GROUP, (8, lanes))
+    for load in loads:
+        load.wait()
+
+
+def lists_kernel(chunks, parents, slots, *refs):
     sources = refs[:chunks]
-    (source_at, table_at, number_at, table_ref, kept_ref, lower_ref, near_ref, back_ref, recv_ref, down_hbm, out_hbm,
-     cells, table8, sums, down_ref, out_ref, sems) = refs[chunks:]
-    parents_x, parents_y = tile_x // 2, tile_y // 2
-    parents = parents_x * parents_y
-    slots = source_at.shape[0] // parents
+    at_any, table_ref, back_ref, down_hbm, incoming_ref, down_ref, cells, table8, sums, at, sems = refs[chunks:]
     kinds = table_ref.shape[0] // 4
-    lanes = lower_ref.shape[2]
-    load = pltpu.make_async_copy(down_hbm, down_ref, sems.at[0])
-    load.start()
+    lanes = table_ref.shape[1]
+    groups = parents // GROUP
+    loads = [
+        pltpu.make_async_copy(at_any, at, sems.at[0]),
+        pltpu.make_async_copy(down_hbm, down_ref, sems.at[1]),
+    ]
+    for load in loads:
+        load.start()
     rows8 = table8.reshape(8 * kinds + 8, lanes)
     for place, row in enumerate((0, 0, 2, 2, 1, 1, 3, 3)):
         rows8[pl.ds(place, kinds, stride=8), :] = table_ref[pl.ds(row, kinds, stride=4), :]
@@ -356,30 +387,23 @@
         for half in range(2):
             own = rows[:, 4 * half : 4 * half + 4, :]
             pairs[c * (parents // 2) : (c + 1) * (parents // 2), half] = jnp.concatenate([own, own], axis=1)
-
-    def step(n, carry):
-        first = n * (GROUP * slots)
-        number = number_at[n * GROUP]
-        for length in range(2, slots + 1, 2):
-
-            @pl.when((number == length) | (number == length - 1))
-            def _():
-                for k in range(GROUP):
-                    total = [None, None]
-                    for s in range(length):
-                        at = first + (k * slots + s)
-                        term = cells[source_at[at]] * table8[table_at[at]]
-                        total[s % 2] = term if total[s % 2] is None else total[s % 2] + term
-                    sums[n * GROUP + k] = total[0] + total[1]
-
-        @pl.when(number == 0)
-        def _():
-            for k in range(GROUP):
-                sums[n * GROUP + k] = jnp.zeros((8, lanes), F32)
-
+    loads[0].wait()
+
+    def step(length, n, carry):
+        for k in range(GROUP):
+            total = [None, None]
+            for s in range(length):
+                term = cells[at[n, k * slots + s]] * table8[at[groups + n, k * slots + s]]
+                total[s % 2] = term if total[s % 2] is None else total[s % 2] + term
+            sums[n * GROUP + k] = total[0] + total[1] if length else jnp.zeros((8, lanes), F32)
         return carry
 
-    lax.fori_loop(0, parents // GROUP, step, 0)
+    start = 0
+    for j, length in enumerate(range(slots, 0, -2)):
+        end = at[2 * groups, j]
+        lax.fori_loop(start, end, functools.partial(step, length), 0)
+        start = end
+    lax.fori_loop(start, groups, functools.partial(step, 0), 0)
     lines = sums.reshape(8 * parents, lanes)
 
     def row(place):
@@ -388,43 +412,45 @@
     ordered = jnp.concatenate(
         [row(0) - row(5), row(2) - row(7), row(1) + row(4), row(3) + row(6)], axis=1
     ).astype(BF16)
-    incoming = mm(back_ref[...], ordered).astype(BF16)
-    load.wait()
+    incoming_ref[...] = mm(back_ref[...], ordered).astype(BF16)
+    loads[1].wait()
+
+
+def finish_kernel(tile_x, tile_y, incoming_ref, down_ref, kept_ref, lower_ref, near_ref, recv_ref, out_hbm,
+                  total_ref, out_ref, sems):
+    parents_x, parents_y = tile_x // 2, tile_y // 2
+    parents = parents_x * parents_y
+    lanes = lower_ref.shape[2]
+    starts = [
+        [(2 * p + child // 2) * tile_y + child % 2 for p in range(parents_x)] for child in range(4)
+    ]
+
+    def rows_of(ref, lines):
+        return jnp.concatenate([ref[pl.ds(line, parents_y, stride=2), :] for line in lines], axis=0)
+
+    for child in range(4):
+        down = mm(incoming_ref[...], down_ref[child])
+        for part in range(2):
+            value = down[:, part * lanes : (part + 1) * lanes] + rows_of(lower_ref.at[part], starts[child])
+            total_ref[child, :, part * lanes : (part + 1) * lanes] = value.astype(BF16)
     stores = []
-    count = parents_x // 2
     for half in range(2):
-        part_in = incoming[half * count * parents_y : (half + 1) * count * parents_y]
-        for side_x in range(2):
-            for side_y in range(2):
-                down = mm(part_in, down_ref[2 * side_x + side_y])
-                starts = [
-                    (2 * p + side_x) * tile_y + side_y for p in range(half * count, (half + 1) * count)
-                ]
-
-                def rows_of(ref):
-                    return jnp.concatenate(
-                        [ref[pl.ds(start, parents_y, stride=2), :] for start in starts], axis=0
-                    )
-
-                total = jnp.concatenate(
-                    [
-                        down[:, part * lanes : (part + 1) * lanes] + rows_of(lower_ref.at[part])
-                        for part in range(2)
-                    ],
-                    axis=1,
-                )
-                field = mm(total.astype(BF16), recv_ref[...])
-                mask = rows_of(kept_ref)
-                for part in range(2):
-                    value = field[:, part * lanes : (part + 1) * lanes] + rows_of(near_ref.at[part])
-                    value = value * mask
-                    for p, start in enumerate(starts):
-                        out_ref[pl.ds(2 * start + part, parents_y, stride=4), :] = value[
-                            p * parents_y : (p + 1) * parents_y
-                        ]
+        count = parents_x // 2
+        rows = slice(half * parents // 2, (half + 1) * parents // 2)
+        for child in range(4):
+            field = mm(total_ref[child, rows, :], recv_ref[...])
+            lines = starts[child][half * count : (half + 1) * count]
+            mask = rows_of(kept_ref, lines)
+            for part in range(2):
+                value = field[:, part * lanes : (part + 1) * lanes] + rows_of(near_ref.at[part], lines)
+                value = value * mask
+                for p, line in enumerate(lines):
+                    out_ref[pl.ds(2 * line + part, parents_y, stride=4), :] = value[
+                        p * parents_y : (p + 1) * parents_y
+                    ]
         size = out_ref.shape[0] // 2
         rows = pl.ds(half * size, size)
-        stores.append(pltpu.make_async_copy(out_ref.at[rows], out_hbm.at[rows], sems.at[1 + half]))
+        stores.append(pltpu.make_async_copy(out_ref.at[rows], out_hbm.at[rows], sems.at[half]))
         stores[-1].start()
     for store in stores:
         store.wait()
@@ -433,7 +459,7 @@
 def swap(low, high, axis):
     count = lax.axis_size(axis)
     lows = [(i, i ^ 1) for i in range(count)]
-    highs = [(i, ((i + 1) ^ 1) - 1) for i in range(1, count - 1)]
+    highs = [(i, (((i + 1) % count ^ 1) - 1) % count) for i in range(count)]
     return lax.ppermute(low, axis, lows), lax.ppermute(high, axis, highs)
 
 
@@ -452,7 +478,8 @@
     in_hbm = pl.BlockSpec(memory_space=pltpu.HBM)
 
     edge = jax.ShapeDtypeStruct((2 * tile_x, 2 * lanes), BF16)
-    live, kept, low, high = pl.pallas_call(
+    entries = jax.ShapeDtypeStruct((parents, slots), jnp.int32)
+    live, kept, low, high, lists, list_kinds, numbers = pl.pallas_call(
         functools.partial(live_kernel, tile_x, tile_y),
         name="live",
         out_shape=[
@@ -460,51 +487,76 @@
             jax.ShapeDtypeStruct((boxes, lanes), F32),
             edge,
             edge,
-        ],
-        in_specs=[in_hbm] * 2,
-        out_specs=vmem(4),
+            entries,
+            entries,
+            jax.ShapeDtypeStruct((parents_x, parents_y), jnp.int32),
+        ],
+        in_specs=[in_hbm] * 5,
+        out_specs=vmem(7),
         scratch_shapes=[
             pltpu.VMEM((2 * boxes, lanes), BF16),
             pltpu.VMEM((tile_x, tile_y), jnp.int32),
             pltpu.VMEM((2 * boxes, lanes), F32),
-            pltpu.SemaphoreType.DMA((2,)),
+            pltpu.SemaphoreType.DMA((5,)),
         ],
         compiler_params=params(16),
         cost_estimate=cost(100 * MIB, 2 * MIB),
-    )(hbm(currents.reshape(2 * boxes, lanes)), hbm(box_count))
+    )(
+        hbm(currents.reshape(2 * boxes, lanes)), hbm(box_count), hbm(coarse_list.reshape(parents, slots)),
+        hbm(coarse_kind.reshape(parents, slots)), hbm(coarse_count),
+    )
     inner_y, outer_y = swap(low, high, "gy")
 
-    coarse = pl.pallas_call(
+    groups = parents // GROUP
+    at, back, agg_near, up_near = pl.pallas_call(
+        functools.partial(order_kernel, chunks, kinds, parents_x, parents_y),
+        name="order",
+        out_shape=[
+            jax.ShapeDtypeStruct((2 * groups + 8, GROUP * slots), jnp.int32),
+            jax.ShapeDtypeStruct((parents, parents), BF16),
+            jax.ShapeDtypeStruct((2 * lanes, 2 * lanes), BF16),
+            jax.ShapeDtypeStruct((8 * lanes, wide), BF16),
+        ],
+        in_specs=vmem(3) + [in_hbm] * 2,
+        out_specs=vmem(4),
+        scratch_shapes=[pltpu.SemaphoreType.DMA((2,))],
+        compiler_params=params(16),
+        cost_estimate=cost(300 * MIB, 3 * MIB),
+    )(
+        lists, list_kinds, numbers,
+        hbm(aggregate), hbm(child_to_parent.reshape(8 * lanes, wide)),
+    )
+
+    width = tile_y + 2 * LEFT
+    rim = 2 * tile_y + 8
+    rim += -rim % 16
+    coarse, pats, low, high = pl.pallas_call(
         functools.partial(parents_kernel, tile_x, tile_y),
         name="parents",
-        out_shape=jax.ShapeDtypeStruct((4 * parents, wide // 4), BF16),
-        in_specs=vmem(3),
-        out_specs=pl.BlockSpec(memory_space=pltpu.VMEM),
-        scratch_shapes=[pltpu.VMEM((2, boxes, lanes), F32), pltpu.VMEM((4 * parents, wide // 4), F32)],
+        out_shape=[
+            jax.ShapeDtypeStruct((4 * parents, wide // 4), BF16),
+            jax.ShapeDtypeStruct((3, tile_x * width, lanes), F32),
+            jax.ShapeDtypeStruct((rim, 2 * lanes), BF16),
+            jax.ShapeDtypeStruct((rim, 2 * lanes), BF16),
+        ],
+        in_specs=vmem(5),
+        out_specs=vmem(4),
+        scratch_shapes=[
+            pltpu.VMEM((2, boxes, lanes), F32),
+            pltpu.VMEM((4 * parents, wide // 4), F32),
+            pltpu.VMEM((rim, 2 * lanes), F32),
+            pltpu.VMEM((rim, 2 * lanes), F32),
+        ],
         compiler_params=params(16),
         cost_estimate=cost(200 * MIB, 3 * MIB),
-    )(live, aggregate, child_to_parent.reshape(8 * lanes, wide))
+    )(live, agg_near, up_near, inner_y, outer_y)
     sources = [coarse] + [
         lax.ppermute(coarse, "gy", [(i, i ^ d) for i in range(chunks)]) for d in range(1, chunks)
     ]
-
-    rim = 2 * tile_y + 8
-    rim += -rim % 16
-    low, high = pl.pallas_call(
-        functools.partial(rims_kernel, tile_x, tile_y),
-        name="rims",
-        out_shape=[jax.ShapeDtypeStruct((rim, 2 * lanes), BF16)] * 2,
-        in_specs=vmem(3),
-        out_specs=vmem(2),
-        scratch_shapes=[pltpu.VMEM((rim, 2 * lanes), F32)] * 2,
-        compiler_params=params(16),
-        cost_estimate=cost(MIB, MIB),
-    )(live, inner_y, outer_y)
     inner_x, outer_x = swap(low, high, "gx")
 
     near_rows = near_blocks.reshape(3, 6 * lanes, 2 * lanes)
     low_rows = low_translator.reshape(-1, lanes)
-    width = tile_y + 2 * LEFT
     pair = [jax.ShapeDtypeStruct((2, boxes, lanes), F32)] * 2
     lower, near = pl.pallas_call(
         functools.partial(local_kernel, tile_x, tile_y),
@@ -514,25 +566,13 @@
         out_specs=vmem(2),
         scratch_shapes=[
             pltpu.VMEM((2, tile_x * width, lanes), F32),
-            pltpu.VMEM((3, tile_x * width, lanes), F32),
             pltpu.VMEM(((tile_x + 2) * tile_y, 6 * lanes), BF16),
             pltpu.VMEM((3 * len(OFFSETS), 8, lanes), F32),
             pltpu.VMEM((3, tile_x, 8, lanes), F32),
         ],
-        compiler_params=params(24),
+        compiler_params=params(16),
         cost_estimate=cost(2000 * MIB, 5 * MIB),
-    )(live, aggregate, near_rows, low_rows)
-
-    entries = jax.ShapeDtypeStruct((parents, slots), jnp.int32)
-    source_at, table_at, number_at, back = pl.pallas_call(
-        functools.partial(order_kernel, chunks, kinds, parents_x, parents_y),
-        name="order",
-        out_shape=[entries, entries, entries, jax.ShapeDtypeStruct((parents, parents), BF16)],
-        in_specs=vmem(3),
-        out_specs=vmem(4),
-        compiler_params=params(16),
-        cost_estimate=cost(300 * MIB, MIB),
-    )(coarse_list.reshape(parents, slots), coarse_kind.reshape(parents, slots), coarse_count)
+    )(live, pats, near_rows, low_rows)
 
     lower, near = pl.pallas_call(
         functools.partial(halos_kernel, tile_x, tile_y),
@@ -546,29 +586,42 @@
         ],
         compiler_params=params(16),
         cost_estimate=cost(100 * MIB, 5 * MIB),
-    )(inner_y, outer_y, inner_x, outer_x, aggregate, near_rows, low_rows, lower, near)
+    )(inner_y, outer_y, inner_x, outer_x, agg_near, near_rows, low_rows, lower, near)
 
     table = up_translator.reshape(kinds, 2, 2, half // 2).transpose(0, 2, 1, 3).reshape(4 * kinds, half // 2)
+    incoming, down = pl.pallas_call(
+        functools.partial(lists_kernel, chunks, parents, slots),
+        name="lists",
+        out_shape=[
+            jax.ShapeDtypeStruct((parents, wide), BF16),
+            jax.ShapeDtypeStruct((4, wide, 2 * lanes), BF16),
+        ],
+        in_specs=vmem(chunks) + [pl.BlockSpec(memory_space=pl.ANY)] + vmem(2) + [in_hbm],
+        out_specs=vmem(2),
+        scratch_shapes=[
+            pltpu.VMEM((chunks * parents, 8, wide // 4), F32),
+            pltpu.VMEM((kinds + 1, 8, wide // 4), F32),
+            pltpu.VMEM((parents, 8, wide // 4), F32),
+            pltpu.SMEM(at.shape, jnp.int32),
+            pltpu.SemaphoreType.DMA((2,)),
+        ],
+        compiler_params=params(16 if chunks <= 4 else 40),
+        cost_estimate=cost(2000 * MIB, 8 * MIB),
+    )(*sources, at, table, back, hbm(parent_to_child))
     out = pl.pallas_call(
-        functools.partial(lists_kernel, chunks, tile_x, tile_y),
-        name="lists",
+        functools.partial(finish_kernel, tile_x, tile_y),
+        name="finish",
         out_shape=jax.ShapeDtypeStruct((2 * boxes, lanes), F32),
-        in_specs=vmem(chunks) + [pl.BlockSpec(memory_space=pltpu.SMEM)] * 3 + vmem(6) + [in_hbm],
+        in_specs=vmem(6),
         out_specs=in_hbm,
         scratch_shapes=[
-            pltpu.VMEM((chunks * parents, 8, lanes), F32),
-            pltpu.VMEM((kinds + 1, 8, lanes), F32),
-            pltpu.VMEM((parents, 8, lanes), F32),
-            pltpu.VMEM((4, wide, 2 * lanes), BF16),
+            pltpu.VMEM((4, parents, 2 * lanes), BF16),
             pltpu.VMEM((2 * boxes, lanes), F32),
-            pltpu.SemaphoreType.DMA((3,)),
-        ],
-        compiler_params=params(24 if chunks <= 4 else 48),
-        cost_estimate=cost(3000 * MIB, 8 * MIB),
-    )(
-        *sources, source_at.reshape(-1), table_at.reshape(-1), number_at[:, 0], table,
-        kept, lower, near, back, receive_map, hbm(parent_to_child),
-    )
+            pltpu.SemaphoreType.DMA((2,)),
+        ],
+        compiler_params=params(16),
+        cost_estimate=cost(300 * MIB, 4 * MIB),
+    )(incoming, down, kept, lower, near, receive_map)
     return out.reshape(tile_x, tile_y, 2, lanes)
 
 

time: 44.1 us -> 32.1 us (0.73)
  the two profiles are of different devices: /device:TPU:19 before, /device:TPU:0 now
where the time goes in v4:
time: 32.1 us; the launch traced here: 32 us
  Pallas kernels  16.8 us (52%)
  starting transfers between devices  11.8 us (37%)
  waiting for transfers between devices  3.37 us (10%)
    ppermute x4, starting transfers between devices, swap(): return (lax.ppermute(low, axis, lows), lax.ppermute(high, axis, highs))  8.22 us
    pallas_call x1, Pallas kernels, body(): pl.pallas_call(functools.partial(lists_kernel, chunks, parents, slots), n...  6.7 us
    ppermute x3, starting transfers between devices, body(): lax.ppermute(coarse, 'gy', [(i, i ^ d) for i in range(chunks)])  3.55 us
    pallas_call x1, Pallas kernels, body(): pl.pallas_call(functools.partial(local_kernel, tile_x, tile_y), name='loc...  2.82 us
    ppermute x3, waiting for transfers between devices, body(): lax.ppermute(coarse, 'gy', [(i, i ^ d) for i in range(chunks)])  2.5 us
    pallas_call x1, Pallas kernels, body(): pl.pallas_call(functools.partial(order_kernel, chunks, kinds, parents_x,...  2.44 us
    pallas_call x1, Pallas kernels, body(): pl.pallas_call(functools.partial(live_kernel, tile_x, tile_y), name='live...  1.62 us
    pallas_call x1, Pallas kernels, body(): pl.pallas_call(functools.partial(finish_kernel, tile_x, tile_y), name='fi...  1.54 us
  transfers between devices with their start and end apart: 7, of which 2 were waited for; matrix products, arithmetic and copies ran while one was open for 0% of the time, Pallas kernels for 19%

profile of v4, /device:TPU:0, one launch (start us, length us, event | category | flops | bytes accessed | tf_op | source)
XLA Modules:
  0.0 32.0 jit_solution(9754134325831911696)
XLA Ops:
  0.0 0.0 copy-start
  0.0 0.0 copy-start.2
  0.0 1.6 %live.1 = (bf16[1024,256]{1,0:T(8,128)(2,1)S(1)}, f32[1024,128]{1,0:T(8,128)S(1)}, bf16[64,256]{1,0:T(8,128)(2,1)S(1)}, bf16[64,256]{1,0:T(8,128)(2,1)S(1)}, s32...) custom-call(bf16[2048,128]{1,0:T(8,128)(2,1)} %bitcast.17, s32[32,32]{1,0:T(8,128)} %counts_hbm.1, ...), custom_call_target="tpu_custom_call" | custom-call | flops 209715200 | bytes 2097152 | tf_op jit(solution)/shard_map/live/pallas_call | solution.py:482
  1.6 3.0 %collective-permute-start = (bf16[64,256]{1,0:T(8,128)(2,1)S(1)}, bf16[64,256]{1,0:T(8,128)(2,1)S(1)}, u32[]{:S(2)}, u32[]{:S(2)}) collective-permute-start(bf16[64,256]{1,0:T(8,128)(2,1)S(1)} %get-tuple-element.32), channel_id=1, source_target_pairs={{0,1},{1,0},{2,3},{3,2},{4,5},{5,4},{6,7},{7,6},{8,9},{9,8},{10,11... | collective-permute-start | bytes 98312 | tf_op jit(solution)/shard_map/ppermute | solution.py:463
  4.6 1.5 %collective-permute-start.1 = (bf16[64,256]{1,0:T(8,128)(2,1)S(1)}, bf16[64,256]{1,0:T(8,128)(2,1)S(1)}, u32[]{:S(2)}, u32[]{:S(2)}) collective-permute-start(bf16[64,256]{1,0:T(8,128)(2,1)S(1)} %get-tuple-element.33), channel_id=1, source_target_pairs={{0,3},{1,2},{2,1},{3,0},{4,7},{5,6},{6,5},{7,4},{8,11},{9,10},{10,... | collective-permute-start | bytes 98312 | tf_op jit(solution)/shard_map/ppermute | solution.py:463
  6.1 2.4 %order.1 = (s32[72,128]{1,0:T(8,128)S(1)}, bf16[256,256]{1,0:T(8,128)(2,1)S(1)}, bf16[256,256]{1,0:T(8,128)(2,1)S(1)}, bf16[1024,512]{1,0:T(8,128)(2,1)S(1)}) custom-call(s32[256,16]{1,0:T(8,128)S(1)} %get-tuple-element.27.list_ref, s32[256,16]{1,0:T(8,128)S(1)} %get-tuple-element.28.kind_ref, s32[16,16]{1,0:T(8,128)S(1)} %get-tuple-element.29.count_ref, ...), custom_call_target="tpu_custom_call" | custom-call | flops 629145600 | bytes 3145728 | tf_op jit(solution)/shard_map/order/pallas_call | solution.py:511
  8.6 0.0 collective-permute-done.inner_ref.inner_y
  8.6 0.9 %collective-permute-done.1.outer_ref.outer_y = bf16[64,256]{1,0:T(8,128)(2,1)S(1)} collective-permute-done((bf16[64,256]{1,0:T(8,128)(2,1)S(1)}, bf16[64,256]{1,0:T(8,128)(2,1)S(1)}, u32[]{:S(2)}, u32[]{:S(2)}) %collective-permute-start.1) | collective-permute-done | bytes 32800 | tf_op jit(solution)/shard_map/ppermute | solution.py:463
  9.4 0.8 %parents.1 = (bf16[1024,128]{1,0:T(8,128)(2,1)S(1)}, f32[3,1536,128]{2,1,0:T(8,128)S(1)}, bf16[80,256]{1,0:T(8,128)(2,1)S(1)}, bf16[80,256]{1,0:T(8,128)(2,1)S(1)}) custom-call(bf16[1024,256]{1,0:T(8,128)(2,1)S(1)} %get-tuple-element.26.live_ref, bf16[256,256]{1,0:T(8,128)(2,1)S(1)} %get-tuple-element.30.agg_ref, ...), custom_call_target="tpu_custom_call" | custom-call | flops 419430400 | bytes 3145728 | tf_op jit(solution)/shard_map/parents/pallas_call | solution.py:533
  10.2 0.7 %collective-permute-start.2 = (bf16[1024,128]{1,0:T(8,128)(2,1)S(1)}, bf16[1024,128]{1,0:T(8,128)(2,1)S(1)}, u32[]{:S(2)}, u32[]{:S(2)}) collective-permute-start(bf16[1024,128]{1,0:T(8,128)(2,1)S(1)} %get-tuple-element.34.refs_0_), channel_id=1, source_target_pairs={{0,1},{1,0},{2,3},{3,2},{4,5},{5,4},{6,7},{7,6},{8,9},{9,8},{10,11... | collective-permute-start | bytes 786440 | tf_op jit(solution)/shard_map/ppermute | solution.py:554
  10.9 1.4 %collective-permute-start.3 = (bf16[1024,128]{1,0:T(8,128)(2,1)S(1)}, bf16[1024,128]{1,0:T(8,128)(2,1)S(1)}, u32[]{:S(2)}, u32[]{:S(2)}) collective-permute-start(bf16[1024,128]{1,0:T(8,128)(2,1)S(1)} %get-tuple-element.34.refs_0_), channel_id=1, source_target_pairs={{0,2},{1,3},{2,0},{3,1},{4,6},{5,7},{6,4},{7,5},{8,10},{9,11},{10,... | collective-permute-start | bytes 786440 | tf_op jit(solution)/shard_map/ppermute | solution.py:554
  12.3 1.4 %collective-permute-start.4 = (bf16[1024,128]{1,0:T(8,128)(2,1)S(1)}, bf16[1024,128]{1,0:T(8,128)(2,1)S(1)}, u32[]{:S(2)}, u32[]{:S(2)}) collective-permute-start(bf16[1024,128]{1,0:T(8,128)(2,1)S(1)} %get-tuple-element.34.refs_0_), channel_id=1, source_target_pairs={{0,3},{1,2},{2,1},{3,0},{4,7},{5,6},{6,5},{7,4},{8,11},{9,10},{10,... | collective-permute-start | bytes 786440 | tf_op jit(solution)/shard_map/ppermute | solution.py:554
  13.8 0.0 collective-permute-start.5
  13.8 3.7 %collective-permute-start.6 = (bf16[80,256]{1,0:T(8,128)(2,1)S(1)}, bf16[80,256]{1,0:T(8,128)(2,1)S(1)}, u32[]{:S(2)}, u32[]{:S(2)}) collective-permute-start(bf16[80,256]{1,0:T(8,128)(2,1)S(1)} %get-tuple-element.41), channel_id=1, source_target_pairs={{0,28},{4,8},{8,4},{12,16},{16,12},{20,24},{24,20},{28,0},{1,29},{... | collective-permute-start | bytes 122888 | tf_op jit(solution)/shard_map/ppermute | solution.py:463
  17.5 0.0 copy-done
  17.5 0.0 copy-done.2
  17.5 2.8 %local.1 = (f32[2,1024,128]{2,1,0:T(8,128)S(1)}, f32[2,1024,128]{2,1,0:T(8,128)S(1)}) custom-call(bf16[1024,256]{1,0:T(8,128)(2,1)S(1)} %get-tuple-element.26.live_ref, f32[3,1536,128]{2,1,0:T(8,128)S(1)} %get-tuple-element.42.pats, bf16[3,768,256]{2,1,0:T(8,128)(2,1)S(1)} %bitcast.12, f32[32,128]{1,0:T(8,128)S(1)} %bitcast.14), custom_call_target="tpu_custom_call" | custom-call | flops 4194304000 | bytes 5242880 | tf_op jit(solution)/shard_map/local/pallas_call | solution.py:561
  20.3 0.0 copy-start.3
  20.3 0.0 collective-permute-done.5.inner_x
  20.4 0.0 collective-permute-done.6.outer_x
  20.4 0.9 %halos.1 = (f32[2,1024,128]{2,1,0:T(8,128)S(1)}, f32[2,1024,128]{2,1,0:T(8,128)S(1)}) custom-call(bf16[64,256]{1,0:T(8,128)(2,1)S(1)} %collective-permute-done.inner_ref.inner_y, bf16[64,256]{1,0:T(8,128)(2,1)S(1)} %collective-permute-done.1.outer_ref.outer_y, bf16[80,256]{1,0:T(8,128)(2,1)S(1)} %collective-permute-done.5.inner_x, ...), custom_call_target="tpu_custom_call" | custom-call | flops 209715200 | bytes 5242880 | tf_op jit(solution)/shard_map/halos/pallas_call | solution.py:577
  21.3 0.0 collective-permute-done.2.refs_1_
  21.3 2.5 %collective-permute-done.3.refs_2_ = bf16[1024,128]{1,0:T(8,128)(2,1)S(1)} collective-permute-done((bf16[1024,128]{1,0:T(8,128)(2,1)S(1)}, bf16[1024,128]{1,0:T(8,128)(2,1)S(1)}, u32[]{:S(2)}, u32[]{:S(2)}) %collective-permute-start.3) | collective-permute-done | bytes 262176 | tf_op jit(solution)/shard_map/ppermute | solution.py:554
  23.8 0.0 collective-permute-done.4.refs_3_
  23.8 0.0 copy-done.3
  23.8 0.0 copy-start.1
  23.8 6.7 %lists.1 = (bf16[256,512]{1,0:T(8,128)(2,1)S(1)}, bf16[4,512,256]{2,1,0:T(8,128)(2,1)S(1)}) custom-call(bf16[1024,128]{1,0:T(8,128)(2,1)S(1)} %get-tuple-element.34.refs_0_, bf16[1024,128]{1,0:T(8,128)(2,1)S(1)} %collective-permute-done.2.refs_1_, bf16[1024,128]{1,0:T(8,128)(2,1)S(1)} %collective-permute-done.3.refs_2_, ...), custom_call_target="tpu_custom_call" | custom-call | flops 4194304000 | bytes 8388608 | tf_op jit(solution)/shard_map/lists/pallas_call | solution.py:592
  30.5 0.0 copy-done.1
  30.5 1.5 %finish.1 = f32[2048,128]{1,0:T(8,128)} custom-call(bf16[256,512]{1,0:T(8,128)(2,1)S(1)} %get-tuple-element.37.incoming_ref, bf16[4,512,256]{2,1,0:T(8,128)(2,1)S(1)} %get-tuple-element.38.down_ref, f32[1024,128]{1,0:T(8,128)S(1)} %get-tuple-element.39.kept_ref, f32[2,1024,128]{2,1,0:T(8,128)S(1)} %get-tuple-element.45.lower_ref, ...), custom_call_target="tpu_custom_call" | custom-call | flops 629145600 | bytes 4194304 | tf_op jit(solution)/shard_map/finish/pallas_call | solution.py:611
Async XLA Ops:
  0.0 17.5 %copy-start = (bf16[9,256,256]{2,1,0:T(8,128)(2,1)S(1)}, bf16[9,256,256]{2,1,0:T(8,128)(2,1)}, u32[]{:S(2)}) copy-start(bf16[9,256,256]{2,1,0:T(8,128)(2,1)} %param.15) | copy-start | bytes 3538948
  0.0 17.5 %copy-start.2 = (f32[16,2,128]{2,1,0:T(2,128)S(1)}, f32[16,2,128]{2,1,0:T(2,128)}, u32[]{:S(2)}) copy-start(f32[16,2,128]{2,1,0:T(2,128)} %param.16) | copy-start | bytes 49156
  1.6 6.9 %collective-permute-start = (bf16[64,256]{1,0:T(8,128)(2,1)S(1)}, bf16[64,256]{1,0:T(8,128)(2,1)S(1)}, u32[]{:S(2)}, u32[]{:S(2)}) collective-permute-start(bf16[64,256]{1,0:T(8,128)(2,1)S(1)} %get-tuple-element.32), channel_id=1, source_target_pairs={{0,1},{1,0},{2,3},{3,2},{4,5},{5,4},{6,7},{7,6},{8,9},{9,8},{10,11... | collective-permute-start | bytes 98312 | tf_op jit(solution)/shard_map/ppermute | solution.py:463
  4.6 4.8 %collective-permute-start.1 = (bf16[64,256]{1,0:T(8,128)(2,1)S(1)}, bf16[64,256]{1,0:T(8,128)(2,1)S(1)}, u32[]{:S(2)}, u32[]{:S(2)}) collective-permute-start(bf16[64,256]{1,0:T(8,128)(2,1)S(1)} %get-tuple-element.33), channel_id=1, source_target_pairs={{0,3},{1,2},{2,1},{3,0},{4,7},{5,6},{6,5},{7,4},{8,11},{9,10},{10,... | collective-permute-start | bytes 98312 | tf_op jit(solution)/shard_map/ppermute | solution.py:463
  10.2 11.0 %collective-permute-start.2 = (bf16[1024,128]{1,0:T(8,128)(2,1)S(1)}, bf16[1024,128]{1,0:T(8,128)(2,1)S(1)}, u32[]{:S(2)}, u32[]{:S(2)}) collective-permute-start(bf16[1024,128]{1,0:T(8,128)(2,1)S(1)} %get-tuple-element.34.refs_0_), channel_id=1, source_target_pairs={{0,1},{1,0},{2,3},{3,2},{4,5},{5,4},{6,7},{7,6},{8,9},{9,8},{10,11... | collective-permute-start | bytes 786440 | tf_op jit(solution)/shard_map/ppermute | solution.py:554
  10.9 12.8 %collective-permute-start.3 = (bf16[1024,128]{1,0:T(8,128)(2,1)S(1)}, bf16[1024,128]{1,0:T(8,128)(2,1)S(1)}, u32[]{:S(2)}, u32[]{:S(2)}) collective-permute-start(bf16[1024,128]{1,0:T(8,128)(2,1)S(1)} %get-tuple-element.34.refs_0_), channel_id=1, source_target_pairs={{0,2},{1,3},{2,0},{3,1},{4,6},{5,7},{6,4},{7,5},{8,10},{9,11},{10,... | collective-permute-start | bytes 786440 | tf_op jit(solution)/shard_map/ppermute | solution.py:554
  12.3 11.4 %collective-permute-start.4 = (bf16[1024,128]{1,0:T(8,128)(2,1)S(1)}, bf16[1024,128]{1,0:T(8,128)(2,1)S(1)}, u32[]{:S(2)}, u32[]{:S(2)}) collective-permute-start(bf16[1024,128]{1,0:T(8,128)(2,1)S(1)} %get-tuple-element.34.refs_0_), channel_id=1, source_target_pairs={{0,3},{1,2},{2,1},{3,0},{4,7},{5,6},{6,5},{7,4},{8,11},{9,10},{10,... | collective-permute-start | bytes 786440 | tf_op jit(solution)/shard_map/ppermute | solution.py:554
  13.8 6.6 %collective-permute-start.5 = (bf16[80,256]{1,0:T(8,128)(2,1)S(1)}, bf16[80,256]{1,0:T(8,128)(2,1)S(1)}, u32[]{:S(2)}, u32[]{:S(2)}) collective-permute-start(bf16[80,256]{1,0:T(8,128)(2,1)S(1)} %get-tuple-element.40), channel_id=1, source_target_pairs={{0,4},{4,0},{8,12},{12,8},{16,20},{20,16},{24,28},{28,24},{1,5},{5... | collective-permute-start | bytes 122888 | tf_op jit(solution)/shard_map/ppermute | solution.py:463
  13.8 6.6 %collective-permute-start.6 = (bf16[80,256]{1,0:T(8,128)(2,1)S(1)}, bf16[80,256]{1,0:T(8,128)(2,1)S(1)}, u32[]{:S(2)}, u32[]{:S(2)}) collective-permute-start(bf16[80,256]{1,0:T(8,128)(2,1)S(1)} %get-tuple-element.41), channel_id=1, source_target_pairs={{0,28},{4,8},{8,4},{12,16},{16,12},{20,24},{24,20},{28,0},{1,29},{... | collective-permute-start | bytes 122888 | tf_op jit(solution)/shard_map/ppermute | solution.py:463
  20.3 3.4 %copy-start.3 = (f32[64,2,256]{2,1,0:T(2,128)S(1)}, f32[64,2,256]{2,1,0:T(2,128)}, u32[]{:S(2)}) copy-start(f32[64,2,256]{2,1,0:T(2,128)} %param.21) | copy-start | bytes 393220
  23.8 6.7 %copy-start.1 = (bf16[256,256]{1,0:T(8,128)(2,1)S(1)}, bf16[256,256]{1,0:T(8,128)(2,1)}, u32[]{:S(2)}) copy-start(bf16[256,256]{1,0:T(8,128)(2,1)} %recv_ref.1) | copy-start | bytes 393220

commit v5 on v4

--- a/solution.py
+++ b/solution.py
@@ -51,13 +51,12 @@
     return jnp.where(at > 0, before, 0.0), jnp.where(at < lax.axis_size(axis) - 1, after, 0.0)
 
 
-def live_kernel(tile_x, tile_y, cur_hbm, counts_hbm, list_hbm, kind_hbm, number_hbm,
-                live_ref, kept_ref, low_ref, high_ref, list_ref, kind_ref, number_ref,
-                cur_ref, counts_ref, wide, sems):
-    pairs = [
-        (counts_hbm, counts_ref), (cur_hbm, cur_ref), (list_hbm, list_ref), (kind_hbm, kind_ref),
-        (number_hbm, number_ref),
-    ]
+LEFT = 8
+
+
+def live_kernel(tile_x, tile_y, cur_hbm, counts_hbm, agg_hbm, up_hbm,
+                live_ref, kept_ref, low_ref, high_ref, agg_ref, up_ref, cur_ref, counts_ref, wide, sems):
+    pairs = [(counts_hbm, counts_ref), (cur_hbm, cur_ref), (agg_hbm, agg_ref), (up_hbm, up_ref)]
     loads = [
         pltpu.make_async_copy(source, target, sems.at[k]) for k, (source, target) in enumerate(pairs)
     ]
@@ -88,13 +87,23 @@
         load.wait()
 
 
-LEFT = 8
-
-
-def parents_kernel(
-    tile_x, tile_y, live_ref, agg_ref, up_ref, inner_ref, outer_ref, coarse_ref, pats_ref, low_ref, high_ref,
-    pats, rows4, first, last,
-):
+def rims_kernel(tile_x, tile_y, live_ref, inner_ref, outer_ref, low_ref, high_ref, first, last):
+    odd = lax.axis_index("gx") % 2 == 1
+    sides = halo_pair(inner_ref, outer_ref, "gy")
+    for rim, start in ((first, 0), (last, tile_x - 2)):
+        rim[0 : 2 * tile_y, :] = live_ref[start * tile_y : (start + 2) * tile_y, :].astype(F32)
+        place = 2 * tile_y
+        for side in sides:
+            for column in range(2):
+                at = column * tile_x + start
+                rim[place : place + 2, :] = side[at : at + 2]
+                place += 2
+        rim[place:, :] = jnp.zeros((rim.shape[0] - place, rim.shape[1]), F32)
+    low_ref[...] = jnp.where(odd, first[...], last[...]).astype(BF16)
+    high_ref[...] = jnp.where(odd, last[...], first[...]).astype(BF16)
+
+
+def parents_kernel(tile_x, tile_y, live_ref, agg_ref, up_ref, coarse_ref, pats_ref, pats, rows4):
     lanes = pats.shape[2]
     width = tile_y + 2 * LEFT
     pattern = mm(live_ref[...], agg_ref[...])
@@ -113,7 +122,6 @@
     for place, column in enumerate((0, 2, 1, 3)):
         rows4[pl.ds(place, coarse.shape[0], stride=4), :] = coarse[:, column * 128 : (column + 1) * 128]
     coarse_ref[...] = rows4[...].astype(BF16)
-
     pattern = pattern.astype(BF16).astype(F32)
     values = [pattern[:, :lanes], pattern[:, lanes:], pattern[:, :lanes] + pattern[:, lanes:]]
     none = jnp.zeros((LEFT, lanes), F32)
@@ -123,20 +131,6 @@
             pats_ref[k, base : base + LEFT, :] = none
             pats_ref[k, base + LEFT : base + LEFT + tile_y, :] = values[k][i * tile_y : (i + 1) * tile_y]
             pats_ref[k, base + LEFT + tile_y : base + width, :] = none
-
-    odd = lax.axis_index("gx") % 2 == 1
-    sides = halo_pair(inner_ref, outer_ref, "gy")
-    for rim, start in ((first, 0), (last, tile_x - 2)):
-        rim[0 : 2 * tile_y, :] = live_ref[start * tile_y : (start + 2) * tile_y, :].astype(F32)
-        place = 2 * tile_y
-        for side in sides:
-            for column in range(2):
-                at = column * tile_x + start
-                rim[place : place + 2, :] = side[at : at + 2]
-                place += 2
-        rim[place:, :] = jnp.zeros((rim.shape[0] - place, rim.shape[1]), F32)
-    low_ref[...] = jnp.where(odd, first[...], last[...]).astype(BF16)
-    high_ref[...] = jnp.where(odd, last[...], first[...]).astype(BF16)
 
 
 OFFSETS = [(dx, dy) for dx in range(-2, 3) for dy in range(-2, 3) if max(abs(dx), abs(dy)) == 2]
@@ -315,104 +309,68 @@
 GROUP = 8
 
 
-def order_kernel(chunks, kinds, parents_x, parents_y, list_ref, kind_ref, count_ref, agg_hbm, up_hbm,
-                 at_ref, back_ref, agg_ref, up_ref, sems):
-    loads = [
-        pltpu.make_async_copy(agg_hbm, agg_ref, sems.at[0]),
-        pltpu.make_async_copy(up_hbm, up_ref, sems.at[1]),
-    ]
-    for load in loads:
-        load.start()
-    parents = parents_x * parents_y
-    slots = list_ref.shape[1]
-    groups = parents // GROUP
-    lanes = at_ref.shape[1]
-    down = lax.broadcasted_iota(jnp.int32, (parents, parents), 0)
-    along = lax.broadcasted_iota(jnp.int32, (parents, parents), 1)
-    column = count_rows(count_ref, parents_x, parents_y, parents)
-    row = jnp.sum(jnp.where(down == along, column, 0.0), axis=0, keepdims=True)
-    before = (column > row) | ((column == row) & (down < along))
-    rank = jnp.sum(jnp.where(before, 1.0, 0.0), axis=0, keepdims=True)
-    after = (row > column) | ((row == column) & (along < down))
-    rank_down = jnp.sum(jnp.where(after, 1.0, 0.0), axis=1, keepdims=True)
-    back_ref[...] = jnp.where(along.astype(F32) == rank_down, 1.0, 0.0).astype(BF16)
-
+def expand_kernel(chunks, *refs):
+    sources = refs[:chunks]
+    table_ref, cells, table8 = refs[chunks:]
+    kinds = table_ref.shape[0] // 4
+    lanes = table_ref.shape[1]
+    rows8 = table8.reshape(8 * kinds + 8, lanes)
+    for place, row in enumerate((0, 0, 2, 2, 1, 1, 3, 3)):
+        rows8[pl.ds(place, kinds, stride=8), :] = table_ref[pl.ds(row, kinds, stride=4), :]
+    table8[kinds] = jnp.zeros((8, lanes), F32)
+    count = cells.shape[0] // chunks // 2
+    pairs = cells.reshape(chunks * count, 2, 8, lanes)
+    upper = lax.broadcasted_iota(jnp.int32, (count, 8, lanes), 1) < 4
+    for c in range(chunks):
+        rows = sources[c][...].astype(F32).reshape(count, 8, lanes)
+        turned = pltpu.roll(rows, 4, axis=1)
+        pairs[c * count : (c + 1) * count, 0] = jnp.where(upper, rows, turned)
+        pairs[c * count : (c + 1) * count, 1] = jnp.where(upper, turned, rows)
+
+
+def lists_kernel(chunks, parents_y, slots, cells, table8, list_ref, kind_ref, number_ref, down_hbm,
+                 incoming_ref, down_ref, sums, places, at, sems):
+    groups, lanes = list_ref.shape
+    parents = groups * GROUP
+    kinds = table8.shape[0] - 1
     across = parents_y * chunks
     entry = list_ref[...]
     line, place = entry // across, entry % across
-    source = ((place // parents_y) ^ lax.axis_index("gy")) * parents + line * parents_y + place % parents_y
-    used = lax.broadcasted_iota(jnp.int32, (parents, slots), 1).astype(F32) < column[:, :slots]
-    kind = jnp.where(used, kind_ref[...], kinds)
-    values = [(source // 256).astype(F32), (source % 256).astype(F32), kind.astype(F32)]
-    values = [value.astype(BF16) for value in values]
-    totals = [jnp.zeros((groups, lanes), F32)] * 3
-    first = GROUP * lax.broadcasted_iota(jnp.int32, (groups, parents), 0)
-    slot = lax.broadcasted_iota(jnp.int32, (slots, lanes), 0)
-    lane = lax.broadcasted_iota(jnp.int32, (slots, lanes), 1)
-    for k in range(GROUP):
-        move = jnp.where((first + k).astype(F32) == rank, 1.0, 0.0).astype(BF16)
-        spread = jnp.where(lane == slot + k * slots, 1.0, 0.0).astype(BF16)
-        totals = [
-            total + mm(mm(move, value).astype(BF16), spread) for total, value in zip(totals, values)
-        ]
-    high, low, kind = [total.astype(jnp.int32) for total in totals]
-    at_ref[0:groups, :] = high * 256 + low
-    at_ref[groups : 2 * groups, :] = kind
-    least = (slots - 1 - 2 * lax.broadcasted_iota(jnp.int32, (parents, lanes), 1)).astype(F32)
-    reach = jnp.sum(jnp.where(column[:, :lanes] >= least, 1.0, 0.0), axis=0, keepdims=True).astype(jnp.int32)
-    at_ref[2 * groups :, :] = jnp.broadcast_to((reach + (GROUP - 1)) // GROUP, (8, lanes))
-    for load in loads:
-        load.wait()
-
-
-def lists_kernel(chunks, parents, slots, *refs):
-    sources = refs[:chunks]
-    at_any, table_ref, back_ref, down_hbm, incoming_ref, down_ref, cells, table8, sums, at, sems = refs[chunks:]
-    kinds = table_ref.shape[0] // 4
-    lanes = table_ref.shape[1]
-    groups = parents // GROUP
+    places[0:groups, :] = (
+        ((place // parents_y) ^ lax.axis_index("gy")) * parents + line * parents_y + place % parents_y
+    )
+    spread = lax.broadcasted_iota(jnp.int32, (GROUP, lanes), 0) == (
+        lax.broadcasted_iota(jnp.int32, (GROUP, lanes), 1) // slots
+    )
+    numbers = mm(number_ref[...].astype(F32).astype(BF16), jnp.where(spread, 1.0, 0.0).astype(BF16))
+    slot = lax.broadcasted_iota(jnp.int32, (groups, lanes), 1) % slots
+    places[groups:, :] = jnp.where(slot < numbers.astype(jnp.int32), kind_ref[...], kinds)
     loads = [
-        pltpu.make_async_copy(at_any, at, sems.at[0]),
+        pltpu.make_async_copy(places, at, sems.at[0]),
         pltpu.make_async_copy(down_hbm, down_ref, sems.at[1]),
     ]
     for load in loads:
         load.start()
-    rows8 = table8.reshape(8 * kinds + 8, lanes)
-    for place, row in enumerate((0, 0, 2, 2, 1, 1, 3, 3)):
-        rows8[pl.ds(place, kinds, stride=8), :] = table_ref[pl.ds(row, kinds, stride=4), :]
-    table8[kinds] = jnp.zeros((8, lanes), F32)
-    pairs = cells.reshape(chunks * parents // 2, 2, 8, lanes)
-    for c in range(chunks):
-        rows = sources[c][...].astype(F32).reshape(parents // 2, 8, lanes)
-        for half in range(2):
-            own = rows[:, 4 * half : 4 * half + 4, :]
-            pairs[c * (parents // 2) : (c + 1) * (parents // 2), half] = jnp.concatenate([own, own], axis=1)
     loads[0].wait()
 
-    def step(length, n, carry):
+    def step(n, carry):
         for k in range(GROUP):
             total = [None, None]
-            for s in range(length):
+            for s in range(slots):
                 term = cells[at[n, k * slots + s]] * table8[at[groups + n, k * slots + s]]
                 total[s % 2] = term if total[s % 2] is None else total[s % 2] + term
-            sums[n * GROUP + k] = total[0] + total[1] if length else jnp.zeros((8, lanes), F32)
+            sums[n * GROUP + k] = total[0] + total[1]
         return carry
 
-    start = 0
-    for j, length in enumerate(range(slots, 0, -2)):
-        end = at[2 * groups, j]
-        lax.fori_loop(start, end, functools.partial(step, length), 0)
-        start = end
-    lax.fori_loop(start, groups, functools.partial(step, 0), 0)
-    lines = sums.reshape(8 * parents, lanes)
+    lax.fori_loop(0, groups, step, 0)
+    lines = sums.reshape(8 * parents, sums.shape[2])
 
     def row(place):
         return lines[pl.ds(place, parents, stride=8), :]
 
-    ordered = jnp.concatenate(
+    incoming_ref[...] = jnp.concatenate(
         [row(0) - row(5), row(2) - row(7), row(1) + row(4), row(3) + row(6)], axis=1
     ).astype(BF16)
-    incoming_ref[...] = mm(back_ref[...], ordered).astype(BF16)
     loads[1].wait()
 
 
@@ -459,7 +417,7 @@
 def swap(low, high, axis):
     count = lax.axis_size(axis)
     lows = [(i, i ^ 1) for i in range(count)]
-    highs = [(i, (((i + 1) % count ^ 1) - 1) % count) for i in range(count)]
+    highs = [(i, i if i in (0, count - 1) else ((i + 1) ^ 1) - 1) for i in range(count)]
     return lax.ppermute(low, axis, lows), lax.ppermute(high, axis, highs)
 
 
@@ -478,8 +436,9 @@
     in_hbm = pl.BlockSpec(memory_space=pltpu.HBM)
 
     edge = jax.ShapeDtypeStruct((2 * tile_x, 2 * lanes), BF16)
-    entries = jax.ShapeDtypeStruct((parents, slots), jnp.int32)
-    live, kept, low, high, lists, list_kinds, numbers = pl.pallas_call(
+    edge = jax.ShapeDtypeStruct((2 * tile_x, 2 * lanes), BF16)
+    width = tile_y + 2 * LEFT
+    live, kept, low, high, agg_near, up_near = pl.pallas_call(
         functools.partial(live_kernel, tile_x, tile_y),
         name="live",
         out_shape=[
@@ -487,72 +446,56 @@
             jax.ShapeDtypeStruct((boxes, lanes), F32),
             edge,
             edge,
-            entries,
-            entries,
-            jax.ShapeDtypeStruct((parents_x, parents_y), jnp.int32),
-        ],
-        in_specs=[in_hbm] * 5,
-        out_specs=vmem(7),
+            jax.ShapeDtypeStruct((2 * lanes, 2 * lanes), BF16),
+            jax.ShapeDtypeStruct((8 * lanes, wide), BF16),
+        ],
+        in_specs=[in_hbm] * 4,
+        out_specs=vmem(6),
         scratch_shapes=[
             pltpu.VMEM((2 * boxes, lanes), BF16),
             pltpu.VMEM((tile_x, tile_y), jnp.int32),
             pltpu.VMEM((2 * boxes, lanes), F32),
-            pltpu.SemaphoreType.DMA((5,)),
+            pltpu.SemaphoreType.DMA((4,)),
         ],
         compiler_params=params(16),
-        cost_estimate=cost(100 * MIB, 2 * MIB),
+        cost_estimate=cost(100 * MIB, 3 * MIB),
     )(
-        hbm(currents.reshape(2 * boxes, lanes)), hbm(box_count), hbm(coarse_list.reshape(parents, slots)),
-        hbm(coarse_kind.reshape(parents, slots)), hbm(coarse_count),
+        hbm(currents.reshape(2 * boxes, lanes)), hbm(box_count), hbm(aggregate),
+        hbm(child_to_parent.reshape(8 * lanes, wide)),
     )
-    inner_y, outer_y = swap(low, high, "gy")
-
-    groups = parents // GROUP
-    at, back, agg_near, up_near = pl.pallas_call(
-        functools.partial(order_kernel, chunks, kinds, parents_x, parents_y),
-        name="order",
-        out_shape=[
-            jax.ShapeDtypeStruct((2 * groups + 8, GROUP * slots), jnp.int32),
-            jax.ShapeDtypeStruct((parents, parents), BF16),
-            jax.ShapeDtypeStruct((2 * lanes, 2 * lanes), BF16),
-            jax.ShapeDtypeStruct((8 * lanes, wide), BF16),
-        ],
-        in_specs=vmem(3) + [in_hbm] * 2,
-        out_specs=vmem(4),
-        scratch_shapes=[pltpu.SemaphoreType.DMA((2,))],
-        compiler_params=params(16),
-        cost_estimate=cost(300 * MIB, 3 * MIB),
-    )(
-        lists, list_kinds, numbers,
-        hbm(aggregate), hbm(child_to_parent.reshape(8 * lanes, wide)),
-    )
-
-    width = tile_y + 2 * LEFT
-    rim = 2 * tile_y + 8
-    rim += -rim % 16
-    coarse, pats, low, high = pl.pallas_call(
+    coarse, pats = pl.pallas_call(
         functools.partial(parents_kernel, tile_x, tile_y),
         name="parents",
         out_shape=[
             jax.ShapeDtypeStruct((4 * parents, wide // 4), BF16),
             jax.ShapeDtypeStruct((3, tile_x * width, lanes), F32),
-            jax.ShapeDtypeStruct((rim, 2 * lanes), BF16),
-            jax.ShapeDtypeStruct((rim, 2 * lanes), BF16),
-        ],
-        in_specs=vmem(5),
-        out_specs=vmem(4),
+        ],
+        in_specs=vmem(3),
+        out_specs=vmem(2),
         scratch_shapes=[
             pltpu.VMEM((2, boxes, lanes), F32),
             pltpu.VMEM((4 * parents, wide // 4), F32),
-            pltpu.VMEM((rim, 2 * lanes), F32),
-            pltpu.VMEM((rim, 2 * lanes), F32),
         ],
         compiler_params=params(16),
         cost_estimate=cost(200 * MIB, 3 * MIB),
-    )(live, agg_near, up_near, inner_y, outer_y)
+    )(live, agg_near, up_near)
+    inner_y, outer_y = swap(low, high, "gy")
     sources = [coarse] + [
         lax.ppermute(coarse, "gy", [(i, i ^ d) for i in range(chunks)]) for d in range(1, chunks)
     ]
+
+    rim = 2 * tile_y + 8
+    rim += -rim % 16
+    low, high = pl.pallas_call(
+        functools.partial(rims_kernel, tile_x, tile_y),
+        name="rims",
+        out_shape=[jax.ShapeDtypeStruct((rim, 2 * lanes), BF16)] * 2,
+        in_specs=vmem(3),
+        out_specs=vmem(2),
+        scratch_shapes=[pltpu.VMEM((rim, 2 * lanes), F32)] * 2,
+        compiler_params=params(16),
+        cost_estimate=cost(1 * MIB, MIB),
+    )(live, inner_y, outer_y)
     inner_x, outer_x = swap(low, high, "gx")
 
     near_rows = near_blocks.reshape(3, 6 * lanes, 2 * lanes)
@@ -589,25 +532,40 @@
     )(inner_y, outer_y, inner_x, outer_x, agg_near, near_rows, low_rows, lower, near)
 
     table = up_translator.reshape(kinds, 2, 2, half // 2).transpose(0, 2, 1, 3).reshape(4 * kinds, half // 2)
+    cells, table8 = pl.pallas_call(
+        functools.partial(expand_kernel, chunks),
+        name="expand",
+        out_shape=[
+            jax.ShapeDtypeStruct((chunks * parents, 8, wide // 4), F32),
+            jax.ShapeDtypeStruct((kinds + 1, 8, wide // 4), F32),
+        ],
+        in_specs=vmem(chunks + 1),
+        out_specs=vmem(2),
+        compiler_params=params(16 if chunks <= 4 else 32),
+        cost_estimate=cost(MIB, 6 * MIB),
+    )(*sources, table)
+    groups = parents // GROUP
     incoming, down = pl.pallas_call(
-        functools.partial(lists_kernel, chunks, parents, slots),
+        functools.partial(lists_kernel, chunks, parents_y, slots),
         name="lists",
         out_shape=[
             jax.ShapeDtypeStruct((parents, wide), BF16),
             jax.ShapeDtypeStruct((4, wide, 2 * lanes), BF16),
         ],
-        in_specs=vmem(chunks) + [pl.BlockSpec(memory_space=pl.ANY)] + vmem(2) + [in_hbm],
+        in_specs=vmem(5) + [in_hbm],
         out_specs=vmem(2),
         scratch_shapes=[
-            pltpu.VMEM((chunks * parents, 8, wide // 4), F32),
-            pltpu.VMEM((kinds + 1, 8, wide // 4), F32),
             pltpu.VMEM((parents, 8, wide // 4), F32),
-            pltpu.SMEM(at.shape, jnp.int32),
+            pltpu.VMEM((2 * groups, GROUP * slots), jnp.int32),
+            pltpu.SMEM((2 * groups, GROUP * slots), jnp.int32),
             pltpu.SemaphoreType.DMA((2,)),
         ],
-        compiler_params=params(16 if chunks <= 4 else 40),
+        compiler_params=params(16 if chunks <= 4 else 32),
         cost_estimate=cost(2000 * MIB, 8 * MIB),
-    )(*sources, at, table, back, hbm(parent_to_child))
+    )(
+        cells, table8, coarse_list.reshape(groups, GROUP * slots), coarse_kind.reshape(groups, GROUP * slots),
+        coarse_count.reshape(groups, GROUP), hbm(parent_to_child),
+    )
     out = pl.pallas_call(
         functools.partial(finish_kernel, tile_x, tile_y),
         name="finish",

time: 32.1 us -> 40.1 us (1.25)
  the two profiles are of different devices: /device:TPU:0 before, /device:TPU:1 now
where the time goes in v5:
time: 40.1 us; the launch traced here: 39.8 us
  Pallas kernels  21.8 us (54%)
  starting transfers between devices  12.5 us (31%)
  local copies, waits for them, and re-layouts  5.35 us (13%)
    pallas_call x1, Pallas kernels, body(): pl.pallas_call(functools.partial(lists_kernel, chunks, parents_y, slots),...  11.1 us
    ppermute x4, starting transfers between devices, swap(): return (lax.ppermute(low, axis, lows), lax.ppermute(high, axis, highs))  7.63 us
    ppermute x3, starting transfers between devices, body(): lax.ppermute(coarse, 'gy', [(i, i ^ d) for i in range(chunks)])  4.85 us
    pallas_call x1, Pallas kernels, body(): pl.pallas_call(functools.partial(local_kernel, tile_x, tile_y), name='loc...  2.83 us
    pallas_call x1, Pallas kernels, body(): pl.pallas_call(functools.partial(expand_kernel, chunks), name='expand', o...  1.63 us
    pallas_call x1, Pallas kernels, body(): pl.pallas_call(functools.partial(live_kernel, tile_x, tile_y), name='live...  1.61 us
    reshape x1, local copies, waits for them, and re-layouts, body(): coarse_list.reshape(groups, GROUP * slots)  1.6 us
    reshape x1, local copies, waits for them, and re-layouts, body(): coarse_kind.reshape(groups, GROUP * slots)  1.6 us
  transfers between devices with their start and end apart: 7, of which 0 were waited for; matrix products, arithmetic and copies ran while one was open for 11% of the time, Pallas kernels for 15%

profile of v5, /device:TPU:1, one launch (start us, length us, event | category | flops | bytes accessed | tf_op | source)
XLA Modules:
  0.0 39.8 jit_solution(14868090241376327868)
XLA Ops:
  0.0 0.0 copy-start.5
  0.0 0.0 copy-start
  0.0 1.6 %live.1 = (bf16[1024,256]{1,0:T(8,128)(2,1)S(1)}, f32[1024,128]{1,0:T(8,128)S(1)}, bf16[64,256]{1,0:T(8,128)(2,1)S(1)}, bf16[64,256]{1,0:T(8,128)(2,1)S(1)}, bf1...) custom-call(bf16[2048,128]{1,0:T(8,128)(2,1)} %bitcast.16, s32[32,32]{1,0:T(8,128)} %counts_hbm.1, ...), custom_call_target="tpu_custom_call" | custom-call | flops 209715200 | bytes 3145728 | tf_op jit(solution)/shard_map/live/pallas_call | solution.py:441
  1.6 0.0 copy-start.1
  1.6 2.1 %collective-permute-start.3 = (bf16[64,256]{1,0:T(8,128)(2,1)S(1)}, bf16[64,256]{1,0:T(8,128)(2,1)S(1)}, u32[]{:S(2)}, u32[]{:S(2)}) collective-permute-start(bf16[64,256]{1,0:T(8,128)(2,1)S(1)} %get-tuple-element.32), channel_id=1, source_target_pairs={{0,1},{1,0},{2,3},{3,2},{4,5},{5,4},{6,7},{7,6},{8,9},{9,8},{10,11... | collective-permute-start | bytes 98312 | tf_op jit(solution)/shard_map/ppermute | solution.py:421
  3.7 0.7 %collective-permute-start.4 = (bf16[64,256]{1,0:T(8,128)(2,1)S(1)}, bf16[64,256]{1,0:T(8,128)(2,1)S(1)}, u32[]{:S(2)}, u32[]{:S(2)}) collective-permute-start(bf16[64,256]{1,0:T(8,128)(2,1)S(1)} %get-tuple-element.33), channel_id=1, source_target_pairs={{0,0},{1,2},{2,1},{3,3},{4,4},{5,6},{6,5},{7,7},{8,8},{9,10},{10,9... | collective-permute-start | bytes 98312 | tf_op jit(solution)/shard_map/ppermute | solution.py:421
  4.4 1.5 %parents.1 = (bf16[1024,128]{1,0:T(8,128)(2,1)}, f32[3,1536,128]{2,1,0:T(8,128)S(1)}) custom-call(bf16[1024,256]{1,0:T(8,128)(2,1)S(1)} %get-tuple-element.23.live_ref, bf16[256,256]{1,0:T(8,128)(2,1)S(1)} %get-tuple-element.24.agg_ref, bf16[1024,512]{1,0:T(8,128)(2,1)S(1)} %get-tuple-element.25.up_ref), custom_call_target="tpu_custom_call" | custom-call | flops 419430400 | bytes 3145728 | tf_op jit(solution)/shard_map/parents/pallas_call | solution.py:466
  5.9 1.2 %collective-permute-start.2 = (bf16[1024,128]{1,0:T(8,128)(2,1)}, bf16[1024,128]{1,0:T(8,128)(2,1)}, u32[]{:S(2)}, u32[]{:S(2)}) collective-permute-start(bf16[1024,128]{1,0:T(8,128)(2,1)} %get-tuple-element.26.refs_0_), channel_id=1, source_target_pairs={{0,3},{1,2},{2,1},{3,0},{4,7},{5,6},{6,5},{7,4},{8,11},{9,10},{10,... | collective-permute-start | bytes 786440 | tf_op jit(solution)/shard_map/ppermute | solution.py:484
  7.1 3.6 %collective-permute-start.1 = (bf16[1024,128]{1,0:T(8,128)(2,1)}, bf16[1024,128]{1,0:T(8,128)(2,1)}, u32[]{:S(2)}, u32[]{:S(2)}) collective-permute-start(bf16[1024,128]{1,0:T(8,128)(2,1)} %get-tuple-element.26.refs_0_), channel_id=1, source_target_pairs={{0,2},{1,3},{2,0},{3,1},{4,6},{5,7},{6,4},{7,5},{8,10},{9,11},{10,... | collective-permute-start | bytes 786440 | tf_op jit(solution)/shard_map/ppermute | solution.py:484
  10.7 0.0 collective-permute-start
  10.7 0.0 collective-permute-done.3.inner_ref.inner_y
  10.7 0.0 collective-permute-done.4.outer_ref.outer_y
  10.7 0.7 %rims.1 = (bf16[80,256]{1,0:T(8,128)(2,1)}, bf16[80,256]{1,0:T(8,128)(2,1)}) custom-call(bf16[1024,256]{1,0:T(8,128)(2,1)S(1)} %get-tuple-element.23.live_ref, bf16[64,256]{1,0:T(8,128)(2,1)S(1)} %collective-permute-done.3.inner_ref.inner_y, bf16[64,256]{1,0:T(8,128)(2,1)S(1)} %collective-permute-done.4.outer_ref.outer_y), custom_call_target="tpu_custom_call" | custom-call | flops 2097152 | bytes 1048576 | tf_op jit(solution)/shard_map/rims/pallas_call | solution.py:489
  11.4 1.8 %collective-permute-start.5 = (bf16[80,256]{1,0:T(8,128)(2,1)}, bf16[80,256]{1,0:T(8,128)(2,1)S(1)}, u32[]{:S(2)}, u32[]{:S(2)}) collective-permute-start(bf16[80,256]{1,0:T(8,128)(2,1)} %get-tuple-element.34), channel_id=1, source_target_pairs={{0,4},{4,0},{8,12},{12,8},{16,20},{20,16},{24,28},{28,24},{1,5},{5... | collective-permute-start | bytes 122888 | tf_op jit(solution)/shard_map/ppermute | solution.py:421
  13.2 3.1 %collective-permute-start.6 = (bf16[80,256]{1,0:T(8,128)(2,1)}, bf16[80,256]{1,0:T(8,128)(2,1)S(1)}, u32[]{:S(2)}, u32[]{:S(2)}) collective-permute-start(bf16[80,256]{1,0:T(8,128)(2,1)} %get-tuple-element.35), channel_id=1, source_target_pairs={{0,0},{4,8},{8,4},{12,16},{16,12},{20,24},{24,20},{28,28},{1,1},{5... | collective-permute-start | bytes 122888 | tf_op jit(solution)/shard_map/ppermute | solution.py:421
  16.3 0.0 copy-done.1
  16.3 0.0 copy-done.5
  16.3 0.0 copy-done
  16.3 2.8 %local.1 = (f32[2,1024,128]{2,1,0:T(8,128)S(1)}, f32[2,1024,128]{2,1,0:T(8,128)S(1)}) custom-call(bf16[1024,256]{1,0:T(8,128)(2,1)S(1)} %get-tuple-element.23.live_ref, f32[3,1536,128]{2,1,0:T(8,128)S(1)} %get-tuple-element.36.pats, bf16[3,768,256]{2,1,0:T(8,128)(2,1)S(1)} %bitcast.10, f32[32,128]{1,0:T(8,128)S(1)} %bitcast.13), custom_call_target="tpu_custom_call" | custom-call | flops 4194304000 | bytes 5242880 | tf_op jit(solution)/shard_map/local/pallas_call | solution.py:504
  19.1 1.6 %reshape.34.list_ref = s32[32,128]{1,0:T(8,128)} reshape(s32[16,16,16]{2,1,0:T(8,128)} %param.18) | data formatting | bytes 32768 | tf_op jit(solution)/shard_map/reshape | solution.py:566
  20.7 1.6 %reshape.35.kind_ref = s32[32,128]{1,0:T(8,128)} reshape(s32[16,16,16]{2,1,0:T(8,128)} %param.19) | data formatting | bytes 32768 | tf_op jit(solution)/shard_map/reshape | solution.py:566
  22.3 1.4 %reshape.36.number_ref = s32[32,8]{1,0:T(8,128)} reshape(s32[16,16]{1,0:T(8,128)} %param.20) | data formatting | bytes 2048 | tf_op jit(solution)/shard_map/reshape | solution.py:567
  23.7 0.0 copy-start.3
  23.7 0.0 collective-permute-done.5.inner_x
  23.7 0.0 collective-permute-done.6.outer_x
  23.7 0.0 copy-start.6
  23.7 0.7 %copy-done.6 = f32[16,2,128]{2,1,0:T(2,128)S(1)} copy-done((f32[16,2,128]{2,1,0:T(2,128)S(1)}, f32[16,2,128]{2,1,0:T(2,128)}, u32[]{:S(2)}) %copy-start.6) | copy-done | bytes 16408
  24.5 0.0 copy-start.7
  24.5 0.0 copy-start.8
  24.5 0.0 copy-start.9
  24.5 0.9 %halos.1 = (f32[2,1024,128]{2,1,0:T(8,128)S(1)}, f32[2,1024,128]{2,1,0:T(8,128)S(1)}) custom-call(bf16[64,256]{1,0:T(8,128)(2,1)S(1)} %collective-permute-done.3.inner_ref.inner_y, bf16[64,256]{1,0:T(8,128)(2,1)S(1)} %collective-permute-done.4.outer_ref.outer_y, bf16[80,256]{1,0:T(8,128)(2,1)S(1)} %collective-permute-done.5.inner_x, ...), custom_call_target="tpu_custom_call" | custom-call | flops 209715200 | bytes 5242880 | tf_op jit(solution)/shard_map/halos/pallas_call | solution.py:520
  25.4 0.0 collective-permute-done.2.refs_3_
  25.4 0.0 collective-permute-done.1.refs_2_
  25.4 0.0 collective-permute-done.refs_1_
  25.4 0.0 copy-done.3
  25.4 1.6 %expand.1 = (f32[1024,8,128]{2,1,0:T(8,128)S(1)}, f32[65,8,128]{2,1,0:T(8,128)S(1)}) custom-call(bf16[1024,128]{1,0:T(8,128)(2,1)} %get-tuple-element.26.refs_0_, bf16[1024,128]{1,0:T(8,128)(2,1)} %collective-permute-done.refs_1_, bf16[1024,128]{1,0:T(8,128)(2,1)} %collective-permute-done.1.refs_2_, bf16[1024,128]{1,0:T(8,128)(2,1)} %collective-permute-done.2.refs_3_, ...), custom_call_target="tpu_custom_call" | custom-call | flops 2097152 | bytes 6291456 | tf_op jit(solution)/shard_map/expand/pallas_call | solution.py:535
  27.1 0.0 copy-done.7
  27.1 0.0 copy-done.8
  27.1 0.0 copy-done.9
  27.1 0.0 copy-start.2
  27.1 0.0 copy-start.4
  27.1 11.1 %lists.1 = (bf16[256,512]{1,0:T(8,128)(2,1)S(1)}, bf16[4,512,256]{2,1,0:T(8,128)(2,1)S(1)}) custom-call(f32[1024,8,128]{2,1,0:T(8,128)S(1)} %get-tuple-element.27.cells, f32[65,8,128]{2,1,0:T(8,128)S(1)} %get-tuple-element.28.table8, s32[32,128]{1,0:T(8,128)S(1)} %copy-done.7, s32[32,128]{1,0:T(8,128)S(1)} %copy-done.8, s32[32,8]{1,0:T(8,128)S(1)} %copy-done.9, ...), custom_call_target="tpu_custom_call" | custom-call | flops 4194304000 | bytes 8388608 | tf_op jit(solution)/shard_map/lists/pallas_call | solution.py:548
  38.2 0.0 copy-done.2
  38.2 0.0 copy-done.4
  38.2 1.6 %finish.1 = f32[2048,128]{1,0:T(8,128)} custom-call(bf16[256,512]{1,0:T(8,128)(2,1)S(1)} %get-tuple-element.29.incoming_ref, bf16[4,512,256]{2,1,0:T(8,128)(2,1)S(1)} %get-tuple-element.30.down_ref, f32[1024,128]{1,0:T(8,128)S(1)} %copy-done.2, f32[2,1024,128]{2,1,0:T(8,128)S(1)} %get-tuple-element.39.lower_ref, ...), custom_call_target="tpu_custom_call" | custom-call | flops 629145600 | bytes 4194304 | tf_op jit(solution)/shard_map/finish/pallas_call | solution.py:569
Async XLA Ops:
  0.0 16.3 %copy-start.5 = (f32[16,2,128]{2,1,0:T(2,128)S(1)}, f32[16,2,128]{2,1,0:T(2,128)}, u32[]{:S(2)}) copy-start(f32[16,2,128]{2,1,0:T(2,128)} %param.16) | copy-start | bytes 49156
  0.0 16.3 %copy-start = (bf16[9,256,256]{2,1,0:T(8,128)(2,1)S(1)}, bf16[9,256,256]{2,1,0:T(8,128)(2,1)}, u32[]{:S(2)}) copy-start(bf16[9,256,256]{2,1,0:T(8,128)(2,1)} %param.15) | copy-start | bytes 3538948
  1.6 14.7 %copy-start.1 = (f32[1024,128]{1,0:T(8,128)}, f32[1024,128]{1,0:T(8,128)S(1)}, u32[]{:S(2)}) copy-start(f32[1024,128]{1,0:T(8,128)S(1)} %get-tuple-element.31.kept_ref) | copy-start | bytes 1572868
  1.6 9.1 %collective-permute-start.3 = (bf16[64,256]{1,0:T(8,128)(2,1)S(1)}, bf16[64,256]{1,0:T(8,128)(2,1)S(1)}, u32[]{:S(2)}, u32[]{:S(2)}) collective-permute-start(bf16[64,256]{1,0:T(8,128)(2,1)S(1)} %get-tuple-element.32), channel_id=1, source_target_pairs={{0,1},{1,0},{2,3},{3,2},{4,5},{5,4},{6,7},{7,6},{8,9},{9,8},{10,11... | collective-permute-start | bytes 98312 | tf_op jit(solution)/shard_map/ppermute | solution.py:421
  3.7 7.0 %collective-permute-start.4 = (bf16[64,256]{1,0:T(8,128)(2,1)S(1)}, bf16[64,256]{1,0:T(8,128)(2,1)S(1)}, u32[]{:S(2)}, u32[]{:S(2)}) collective-permute-start(bf16[64,256]{1,0:T(8,128)(2,1)S(1)} %get-tuple-element.33), channel_id=1, source_target_pairs={{0,0},{1,2},{2,1},{3,3},{4,4},{5,6},{6,5},{7,7},{8,8},{9,10},{10,9... | collective-permute-start | bytes 98312 | tf_op jit(solution)/shard_map/ppermute | solution.py:421
  5.9 19.5 %collective-permute-start.2 = (bf16[1024,128]{1,0:T(8,128)(2,1)}, bf16[1024,128]{1,0:T(8,128)(2,1)}, u32[]{:S(2)}, u32[]{:S(2)}) collective-permute-start(bf16[1024,128]{1,0:T(8,128)(2,1)} %get-tuple-element.26.refs_0_), channel_id=1, source_target_pairs={{0,3},{1,2},{2,1},{3,0},{4,7},{5,6},{6,5},{7,4},{8,11},{9,10},{10,... | collective-permute-start | bytes 786440 | tf_op jit(solution)/shard_map/ppermute | solution.py:484
  7.1 18.3 %collective-permute-start.1 = (bf16[1024,128]{1,0:T(8,128)(2,1)}, bf16[1024,128]{1,0:T(8,128)(2,1)}, u32[]{:S(2)}, u32[]{:S(2)}) collective-permute-start(bf16[1024,128]{1,0:T(8,128)(2,1)} %get-tuple-element.26.refs_0_), channel_id=1, source_target_pairs={{0,2},{1,3},{2,0},{3,1},{4,6},{5,7},{6,4},{7,5},{8,10},{9,11},{10,... | collective-permute-start | bytes 786440 | tf_op jit(solution)/shard_map/ppermute | solution.py:484
  10.7 14.7 %collective-permute-start = (bf16[1024,128]{1,0:T(8,128)(2,1)}, bf16[1024,128]{1,0:T(8,128)(2,1)}, u32[]{:S(2)}, u32[]{:S(2)}) collective-permute-start(bf16[1024,128]{1,0:T(8,128)(2,1)} %get-tuple-element.26.refs_0_), channel_id=1, source_target_pairs={{0,1},{1,0},{2,3},{3,2},{4,5},{5,4},{6,7},{7,6},{8,9},{9,8},{10,11... | collective-permute-start | bytes 786440 | tf_op jit(solution)/shard_map/ppermute | solution.py:484
  11.4 12.3 %collective-permute-start.5 = (bf16[80,256]{1,0:T(8,128)(2,1)}, bf16[80,256]{1,0:T(8,128)(2,1)S(1)}, u32[]{:S(2)}, u32[]{:S(2)}) collective-permute-start(bf16[80,256]{1,0:T(8,128)(2,1)} %get-tuple-element.34), channel_id=1, source_target_pairs={{0,4},{4,0},{8,12},{12,8},{16,20},{20,16},{24,28},{28,24},{1,5},{5... | collective-permute-start | bytes 122888 | tf_op jit(solution)/shard_map/ppermute | solution.py:421
  13.2 10.5 %collective-permute-start.6 = (bf16[80,256]{1,0:T(8,128)(2,1)}, bf16[80,256]{1,0:T(8,128)(2,1)S(1)}, u32[]{:S(2)}, u32[]{:S(2)}) collective-permute-start(bf16[80,256]{1,0:T(8,128)(2,1)} %get-tuple-element.35), channel_id=1, source_target_pairs={{0,0},{4,8},{8,4},{12,16},{16,12},{20,24},{24,20},{28,28},{1,1},{5... | collective-permute-start | bytes 122888 | tf_op jit(solution)/shard_map/ppermute | solution.py:421
  23.7 1.7 %copy-start.3 = (f32[64,2,256]{2,1,0:T(2,128)S(1)}, f32[64,2,256]{2,1,0:T(2,128)}, u32[]{:S(2)}) copy-start(f32[64,2,256]{2,1,0:T(2,128)} %param.21) | copy-start | bytes 393220
  23.7 0.8 %copy-start.6 = (f32[16,2,128]{2,1,0:T(2,128)S(1)}, f32[16,2,128]{2,1,0:T(2,128)}, u32[]{:S(2)}) copy-start(f32[16,2,128]{2,1,0:T(2,128)} %param.16) | copy-start | bytes 49156
  24.5 2.6 %copy-start.7 = (s32[32,128]{1,0:T(8,128)S(1)}, s32[32,128]{1,0:T(8,128)}, u32[]{:S(2)}) copy-start(s32[32,128]{1,0:T(8,128)} %reshape.34.list_ref) | copy-start | bytes 49156
  24.5 2.6 %copy-start.8 = (s32[32,128]{1,0:T(8,128)S(1)}, s32[32,128]{1,0:T(8,128)}, u32[]{:S(2)}) copy-start(s32[32,128]{1,0:T(8,128)} %reshape.35.kind_ref) | copy-start | bytes 49156
  24.5 2.6 %copy-start.9 = (s32[32,8]{1,0:T(8,128)S(1)}, s32[32,8]{1,0:T(8,128)}, u32[]{:S(2)}) copy-start(s32[32,8]{1,0:T(8,128)} %reshape.36.number_ref) | copy-start | bytes 3076
  27.1 11.1 %copy-start.2 = (f32[1024,128]{1,0:T(8,128)S(1)}, f32[1024,128]{1,0:T(8,128)}, u32[]{:S(2)}) copy-start(f32[1024,128]{1,0:T(8,128)} %copy-done.1) | copy-start | bytes 1572868
  27.1 11.1 %copy-start.4 = (bf16[256,256]{1,0:T(8,128)(2,1)S(1)}, bf16[256,256]{1,0:T(8,128)(2,1)}, u32[]{:S(2)}) copy-start(bf16[256,256]{1,0:T(8,128)(2,1)} %recv_ref.1) | copy-start | bytes 393220

commit v6 on v5

--- a/solution.py
+++ b/solution.py
@@ -309,16 +309,69 @@
 GROUP = 8
 
 
-def expand_kernel(chunks, *refs):
+def order_kernel(chunks, kinds, parents_x, parents_y, list_ref, kind_ref, count_ref, at_ref, back_ref):
+    parents = parents_x * parents_y
+    slots = list_ref.shape[1]
+    groups = parents // GROUP
+    lanes = at_ref.shape[1]
+    down = lax.broadcasted_iota(jnp.int32, (parents, parents), 0)
+    along = lax.broadcasted_iota(jnp.int32, (parents, parents), 1)
+    column = count_rows(count_ref, parents_x, parents_y, parents)
+    row = jnp.sum(jnp.where(down == along, column, 0.0), axis=0, keepdims=True)
+    before = (column > row) | ((column == row) & (down < along))
+    rank = jnp.sum(jnp.where(before, 1.0, 0.0), axis=0, keepdims=True)
+    after = (row > column) | ((row == column) & (along < down))
+    rank_down = jnp.sum(jnp.where(after, 1.0, 0.0), axis=1, keepdims=True)
+    back_ref[...] = jnp.where(along.astype(F32) == rank_down, 1.0, 0.0).astype(BF16)
+
+    across = parents_y * chunks
+    entry = list_ref[...]
+    line, place = entry // across, entry % across
+    source = ((place // parents_y) ^ lax.axis_index("gy")) * parents + line * parents_y + place % parents_y
+    used = lax.broadcasted_iota(jnp.int32, (parents, slots), 1).astype(F32) < column[:, :slots]
+    kind = jnp.where(used, kind_ref[...], kinds)
+    slot = lax.broadcasted_iota(jnp.int32, (slots, lanes), 0)
+    lane = lax.broadcasted_iota(jnp.int32, (slots, lanes), 1)
+    values = [
+        mm(value.astype(F32).astype(BF16), jnp.where(lane == slot + n * slots, 1.0, 0.0).astype(BF16))
+        for n, value in enumerate((source // 256, source % 256, kind))
+    ]
+    values = (values[0] + values[1] + values[2]).astype(BF16)
+    wanted = GROUP * (down % groups) + down // groups
+    moved = mm(jnp.where(wanted.astype(F32) == rank, 1.0, 0.0).astype(BF16), values).astype(BF16)
+    moved = jnp.concatenate([moved[k * groups : (k + 1) * groups] for k in range(GROUP)], axis=1)
+    totals = []
+    from_lane = lax.broadcasted_iota(jnp.int32, (GROUP * lanes, lanes), 0)
+    to_lane = lax.broadcasted_iota(jnp.int32, (GROUP * lanes, lanes), 1)
+    for n in range(3):
+        spread = from_lane == (to_lane // slots) * lanes + n * slots + to_lane % slots
+        totals.append(mm(moved, jnp.where(spread, 1.0, 0.0).astype(BF16)).astype(jnp.int32))
+    at_ref[0:groups, :] = (totals[0] * 256 + totals[1]) * 8
+    at_ref[groups : 2 * groups, :] = totals[2] * 8
+    least = (slots - 1 - 2 * lax.broadcasted_iota(jnp.int32, (parents, lanes), 1)).astype(F32)
+    reach = jnp.sum(jnp.where(column[:, :lanes] >= least, 1.0, 0.0), axis=0, keepdims=True).astype(jnp.int32)
+    at_ref[2 * groups :, :] = jnp.broadcast_to((reach + (GROUP - 1)) // GROUP, (8, lanes))
+
+
+def lists_kernel(chunks, tile_x, tile_y, slots, *refs):
     sources = refs[:chunks]
-    table_ref, cells, table8 = refs[chunks:]
+    (at_any, table_ref, back_ref, kept_ref, lower_ref, near_ref, recv_ref, down_hbm, out_hbm,
+     cells, table8, sums, at, down_ref, total_ref, out_ref, sems) = refs[chunks:]
+    parents_x, parents_y = tile_x // 2, tile_y // 2
+    parents = parents_x * parents_y
     kinds = table_ref.shape[0] // 4
     lanes = table_ref.shape[1]
-    rows8 = table8.reshape(8 * kinds + 8, lanes)
+    groups = parents // GROUP
+    loads = [
+        pltpu.make_async_copy(at_any, at, sems.at[0]),
+        pltpu.make_async_copy(down_hbm, down_ref, sems.at[1]),
+    ]
+    for load in loads:
+        load.start()
     for place, row in enumerate((0, 0, 2, 2, 1, 1, 3, 3)):
-        rows8[pl.ds(place, kinds, stride=8), :] = table_ref[pl.ds(row, kinds, stride=4), :]
-    table8[kinds] = jnp.zeros((8, lanes), F32)
-    count = cells.shape[0] // chunks // 2
+        table8[pl.ds(place, kinds, stride=8), :] = table_ref[pl.ds(row, kinds, stride=4), :]
+    table8[8 * kinds : 8 * kinds + 8, :] = jnp.zeros((8, lanes), F32)
+    count = parents // 2
     pairs = cells.reshape(chunks * count, 2, 8, lanes)
     upper = lax.broadcasted_iota(jnp.int32, (count, 8, lanes), 1) < 4
     for c in range(chunks):
@@ -326,59 +379,37 @@
         turned = pltpu.roll(rows, 4, axis=1)
         pairs[c * count : (c + 1) * count, 0] = jnp.where(upper, rows, turned)
         pairs[c * count : (c + 1) * count, 1] = jnp.where(upper, turned, rows)
-
-
-def lists_kernel(chunks, parents_y, slots, cells, table8, list_ref, kind_ref, number_ref, down_hbm,
-                 incoming_ref, down_ref, sums, places, at, sems):
-    groups, lanes = list_ref.shape
-    parents = groups * GROUP
-    kinds = table8.shape[0] - 1
-    across = parents_y * chunks
-    entry = list_ref[...]
-    line, place = entry // across, entry % across
-    places[0:groups, :] = (
-        ((place // parents_y) ^ lax.axis_index("gy")) * parents + line * parents_y + place % parents_y
-    )
-    spread = lax.broadcasted_iota(jnp.int32, (GROUP, lanes), 0) == (
-        lax.broadcasted_iota(jnp.int32, (GROUP, lanes), 1) // slots
-    )
-    numbers = mm(number_ref[...].astype(F32).astype(BF16), jnp.where(spread, 1.0, 0.0).astype(BF16))
-    slot = lax.broadcasted_iota(jnp.int32, (groups, lanes), 1) % slots
-    places[groups:, :] = jnp.where(slot < numbers.astype(jnp.int32), kind_ref[...], kinds)
-    loads = [
-        pltpu.make_async_copy(places, at, sems.at[0]),
-        pltpu.make_async_copy(down_hbm, down_ref, sems.at[1]),
-    ]
-    for load in loads:
-        load.start()
     loads[0].wait()
 
-    def step(n, carry):
+    def step(length, n, carry):
+        first = n * (GROUP * slots)
+        second = first + groups * GROUP * slots
         for k in range(GROUP):
             total = [None, None]
-            for s in range(slots):
-                term = cells[at[n, k * slots + s]] * table8[at[groups + n, k * slots + s]]
+            for s in range(length):
+                source = pl.multiple_of(at[first + (k * slots + s)], 8)
+                kind = pl.multiple_of(at[second + (k * slots + s)], 8)
+                term = cells[pl.ds(source, 8), :] * table8[pl.ds(kind, 8), :]
                 total[s % 2] = term if total[s % 2] is None else total[s % 2] + term
-            sums[n * GROUP + k] = total[0] + total[1]
+            total = total[0] + total[1] if length else jnp.zeros((8, lanes), F32)
+            sums[pl.ds(pl.multiple_of((n * GROUP + k) * 8, 8), 8), :] = total
         return carry
 
-    lax.fori_loop(0, groups, step, 0)
-    lines = sums.reshape(8 * parents, sums.shape[2])
+    start = 0
+    for j, length in enumerate(range(slots, 0, -2)):
+        end = at[2 * groups * GROUP * slots + j]
+        lax.fori_loop(start, end, functools.partial(step, length), 0)
+        start = end
+    lax.fori_loop(start, groups, functools.partial(step, 0), 0)
 
     def row(place):
-        return lines[pl.ds(place, parents, stride=8), :]
-
-    incoming_ref[...] = jnp.concatenate(
+        return sums[pl.ds(place, parents, stride=8), :]
+
+    ordered = jnp.concatenate(
         [row(0) - row(5), row(2) - row(7), row(1) + row(4), row(3) + row(6)], axis=1
     ).astype(BF16)
+    incoming = mm(back_ref[...], ordered).astype(BF16)
     loads[1].wait()
-
-
-def finish_kernel(tile_x, tile_y, incoming_ref, down_ref, kept_ref, lower_ref, near_ref, recv_ref, out_hbm,
-                  total_ref, out_ref, sems):
-    parents_x, parents_y = tile_x // 2, tile_y // 2
-    parents = parents_x * parents_y
-    lanes = lower_ref.shape[2]
     starts = [
         [(2 * p + child // 2) * tile_y + child % 2 for p in range(parents_x)] for child in range(4)
     ]
@@ -387,7 +418,7 @@
         return jnp.concatenate([ref[pl.ds(line, parents_y, stride=2), :] for line in lines], axis=0)
 
     for child in range(4):
-        down = mm(incoming_ref[...], down_ref[child])
+        down = mm(incoming, down_ref[child])
         for part in range(2):
             value = down[:, part * lanes : (part + 1) * lanes] + rows_of(lower_ref.at[part], starts[child])
             total_ref[child, :, part * lanes : (part + 1) * lanes] = value.astype(BF16)
@@ -408,7 +439,7 @@
                     ]
         size = out_ref.shape[0] // 2
         rows = pl.ds(half * size, size)
-        stores.append(pltpu.make_async_copy(out_ref.at[rows], out_hbm.at[rows], sems.at[half]))
+        stores.append(pltpu.make_async_copy(out_ref.at[rows], out_hbm.at[rows], sems.at[2 + half]))
         stores[-1].start()
     for store in stores:
         store.wait()
@@ -417,7 +448,7 @@
 def swap(low, high, axis):
     count = lax.axis_size(axis)
     lows = [(i, i ^ 1) for i in range(count)]
-    highs = [(i, i if i in (0, count - 1) else ((i + 1) ^ 1) - 1) for i in range(count)]
+    highs = [(i, (((i + 1) % count ^ 1) - 1) % count) for i in range(count)]
     return lax.ppermute(low, axis, lows), lax.ppermute(high, axis, highs)
 
 
@@ -457,7 +488,7 @@
             pltpu.VMEM((2 * boxes, lanes), F32),
             pltpu.SemaphoreType.DMA((4,)),
         ],
-        compiler_params=params(16),
+        compiler_params=params(10),
         cost_estimate=cost(100 * MIB, 3 * MIB),
     )(
         hbm(currents.reshape(2 * boxes, lanes)), hbm(box_count), hbm(aggregate),
@@ -476,7 +507,7 @@
             pltpu.VMEM((2, boxes, lanes), F32),
             pltpu.VMEM((4 * parents, wide // 4), F32),
         ],
-        compiler_params=params(16),
+        compiler_params=params(10),
         cost_estimate=cost(200 * MIB, 3 * MIB),
     )(live, agg_near, up_near)
     inner_y, outer_y = swap(low, high, "gy")
@@ -493,10 +524,11 @@
         in_specs=vmem(3),
         out_specs=vmem(2),
         scratch_shapes=[pltpu.VMEM((rim, 2 * lanes), F32)] * 2,
-        compiler_params=params(16),
+        compiler_params=params(10),
         cost_estimate=cost(1 * MIB, MIB),
     )(live, inner_y, outer_y)
     inner_x, outer_x = swap(low, high, "gx")
+    live, coarse_count, _ = lax.optimization_barrier((live, coarse_count, low))
 
     near_rows = near_blocks.reshape(3, 6 * lanes, 2 * lanes)
     low_rows = low_translator.reshape(-1, lanes)
@@ -513,7 +545,7 @@
             pltpu.VMEM((3 * len(OFFSETS), 8, lanes), F32),
             pltpu.VMEM((3, tile_x, 8, lanes), F32),
         ],
-        compiler_params=params(16),
+        compiler_params=params(10),
         cost_estimate=cost(2000 * MIB, 5 * MIB),
     )(live, pats, near_rows, low_rows)
 
@@ -527,59 +559,44 @@
             pltpu.VMEM((4, 4, tile_x + 16, lanes), F32),
             pltpu.VMEM((4, 4 * width, lanes), F32),
         ],
-        compiler_params=params(16),
+        compiler_params=params(10),
         cost_estimate=cost(100 * MIB, 5 * MIB),
     )(inner_y, outer_y, inner_x, outer_x, agg_near, near_rows, low_rows, lower, near)
 
     table = up_translator.reshape(kinds, 2, 2, half // 2).transpose(0, 2, 1, 3).reshape(4 * kinds, half // 2)
-    cells, table8 = pl.pallas_call(
-        functools.partial(expand_kernel, chunks),
-        name="expand",
+    groups = parents // GROUP
+    at, back = pl.pallas_call(
+        functools.partial(order_kernel, chunks, kinds, parents_x, parents_y),
+        name="order",
         out_shape=[
-            jax.ShapeDtypeStruct((chunks * parents, 8, wide // 4), F32),
-            jax.ShapeDtypeStruct((kinds + 1, 8, wide // 4), F32),
-        ],
-        in_specs=vmem(chunks + 1),
+            jax.ShapeDtypeStruct((2 * groups + 8, GROUP * slots), jnp.int32),
+            jax.ShapeDtypeStruct((parents, parents), BF16),
+        ],
+        in_specs=vmem(3),
         out_specs=vmem(2),
-        compiler_params=params(16 if chunks <= 4 else 32),
-        cost_estimate=cost(MIB, 6 * MIB),
-    )(*sources, table)
-    groups = parents // GROUP
-    incoming, down = pl.pallas_call(
-        functools.partial(lists_kernel, chunks, parents_y, slots),
+        compiler_params=params(8),
+        cost_estimate=cost(300 * MIB, MIB),
+    )(coarse_list.reshape(parents, slots), coarse_kind.reshape(parents, slots), coarse_count)
+    at = at.reshape(-1)
+    out = pl.pallas_call(
+        functools.partial(lists_kernel, chunks, tile_x, tile_y, slots),
         name="lists",
-        out_shape=[
-            jax.ShapeDtypeStruct((parents, wide), BF16),
-            jax.ShapeDtypeStruct((4, wide, 2 * lanes), BF16),
-        ],
-        in_specs=vmem(5) + [in_hbm],
-        out_specs=vmem(2),
-        scratch_shapes=[
-            pltpu.VMEM((parents, 8, wide // 4), F32),
-            pltpu.VMEM((2 * groups, GROUP * slots), jnp.int32),
-            pltpu.SMEM((2 * groups, GROUP * slots), jnp.int32),
-            pltpu.SemaphoreType.DMA((2,)),
-        ],
-        compiler_params=params(16 if chunks <= 4 else 32),
-        cost_estimate=cost(2000 * MIB, 8 * MIB),
-    )(
-        cells, table8, coarse_list.reshape(groups, GROUP * slots), coarse_kind.reshape(groups, GROUP * slots),
-        coarse_count.reshape(groups, GROUP), hbm(parent_to_child),
-    )
-    out = pl.pallas_call(
-        functools.partial(finish_kernel, tile_x, tile_y),
-        name="finish",
         out_shape=jax.ShapeDtypeStruct((2 * boxes, lanes), F32),
-        in_specs=vmem(6),
+        in_specs=vmem(chunks) + [pl.BlockSpec(memory_space=pl.ANY)] + vmem(6) + [in_hbm],
         out_specs=in_hbm,
         scratch_shapes=[
+            pltpu.VMEM((chunks * parents * 8, wide // 4), F32),
+            pltpu.VMEM((8 * kinds + 8, wide // 4), F32),
+            pltpu.VMEM((8 * parents, wide // 4), F32),
+            pltpu.SMEM(at.shape, jnp.int32),
+            pltpu.VMEM((4, wide, 2 * lanes), BF16),
             pltpu.VMEM((4, parents, 2 * lanes), BF16),
             pltpu.VMEM((2 * boxes, lanes), F32),
-            pltpu.SemaphoreType.DMA((2,)),
-        ],
-        compiler_params=params(16),
-        cost_estimate=cost(300 * MIB, 4 * MIB),
-    )(incoming, down, kept, lower, near, receive_map)
+            pltpu.SemaphoreType.DMA((4,)),
+        ],
+        compiler_params=params(16 if chunks <= 4 else 40),
+        cost_estimate=cost(2000 * MIB, 8 * MIB),
+    )(*sources, at, table, back, kept, lower, near, receive_map, hbm(parent_to_child))
     return out.reshape(tile_x, tile_y, 2, lanes)
 
 

time: 40.1 us -> 28.3 us (0.71)
  the two profiles are of different devices: /device:TPU:1 before, /device:TPU:0 now
where the time goes in v6:
time: 28.3 us; the launch traced here: 28.2 us
  Pallas kernels  14 us (49%)
  starting transfers between devices  11.8 us (42%)
  waiting for transfers between devices  2.19 us (8%)
    ppermute x4, starting transfers between devices, swap(): return (lax.ppermute(low, axis, lows), lax.ppermute(high, axis, highs))  8.26 us
    pallas_call x1, Pallas kernels, body(): pl.pallas_call(functools.partial(lists_kernel, chunks, tile_x, tile_y, sl...  6.9 us
    ppermute x3, starting transfers between devices, body(): lax.ppermute(coarse, 'gy', [(i, i ^ d) for i in range(chunks)])  3.55 us
    pallas_call x1, Pallas kernels, body(): pl.pallas_call(functools.partial(local_kernel, tile_x, tile_y), name='loc...  2.83 us
    ppermute x3, waiting for transfers between devices, body(): lax.ppermute(coarse, 'gy', [(i, i ^ d) for i in range(chunks)])  2.17 us
    pallas_call x1, Pallas kernels, body(): pl.pallas_call(functools.partial(live_kernel, tile_x, tile_y), name='live...  1.61 us
    pallas_call x1, Pallas kernels, body(): pl.pallas_call(functools.partial(order_kernel, chunks, kinds, parents_x,...  0.97 us
    pallas_call x1, Pallas kernels, body(): pl.pallas_call(functools.partial(halos_kernel, tile_x, tile_y), name='hal...  0.9 us
  transfers between devices with their start and end apart: 7, of which 1 were waited for; matrix products, arithmetic and copies ran while one was open for 0% of the time, Pallas kernels for 19%

profile of v6, /device:TPU:0, one launch (start us, length us, event | category | flops | bytes accessed | tf_op | source)
XLA Modules:
  0.0 28.2 jit_solution(13816077424243099727)
XLA Ops:
  0.0 0.0 copy-start
  0.0 0.0 copy-start.1
  0.0 1.6 %live.1 = (bf16[1024,256]{1,0:T(8,128)(2,1)S(1)}, f32[1024,128]{1,0:T(8,128)S(1)}, bf16[64,256]{1,0:T(8,128)(2,1)S(1)}, bf16[64,256]{1,0:T(8,128)(2,1)S(1)}, bf1...) custom-call(bf16[2048,128]{1,0:T(8,128)(2,1)} %bitcast.22, s32[32,32]{1,0:T(8,128)} %counts_hbm.1, ...), custom_call_target="tpu_custom_call" | custom-call | flops 209715200 | bytes 3145728 | tf_op jit(solution)/shard_map/live/pallas_call | solution.py:472
  1.6 3.0 %collective-permute-start.3 = (bf16[64,256]{1,0:T(8,128)(2,1)S(1)}, bf16[64,256]{1,0:T(8,128)(2,1)S(1)}, u32[]{:S(2)}, u32[]{:S(2)}) collective-permute-start(bf16[64,256]{1,0:T(8,128)(2,1)S(1)} %get-tuple-element.27), channel_id=1, source_target_pairs={{0,1},{1,0},{2,3},{3,2},{4,5},{5,4},{6,7},{7,6},{8,9},{9,8},{10,11... | collective-permute-start | bytes 98312 | tf_op jit(solution)/shard_map/ppermute | solution.py:452
  4.6 1.5 %collective-permute-start.4 = (bf16[64,256]{1,0:T(8,128)(2,1)S(1)}, bf16[64,256]{1,0:T(8,128)(2,1)S(1)}, u32[]{:S(2)}, u32[]{:S(2)}) collective-permute-start(bf16[64,256]{1,0:T(8,128)(2,1)S(1)} %get-tuple-element.28), channel_id=1, source_target_pairs={{0,3},{1,2},{2,1},{3,0},{4,7},{5,6},{6,5},{7,4},{8,11},{9,10},{10,... | collective-permute-start | bytes 98312 | tf_op jit(solution)/shard_map/ppermute | solution.py:452
  6.1 0.8 %parents.1 = (bf16[1024,128]{1,0:T(8,128)(2,1)S(1)}, f32[3,1536,128]{2,1,0:T(8,128)S(1)}) custom-call(bf16[1024,256]{1,0:T(8,128)(2,1)S(1)} %get-tuple-element.35.live_ref, bf16[256,256]{1,0:T(8,128)(2,1)S(1)} %get-tuple-element.24.agg_ref, bf16[1024,512]{1,0:T(8,128)(2,1)S(1)} %get-tuple-element.25.up_ref), custom_call_target="tpu_custom_call" | custom-call | flops 419430400 | bytes 3145728 | tf_op jit(solution)/shard_map/parents/pallas_call | solution.py:497
  6.9 1.6 %collective-permute-start = (bf16[1024,128]{1,0:T(8,128)(2,1)S(1)}, bf16[1024,128]{1,0:T(8,128)(2,1)S(1)}, u32[]{:S(2)}, u32[]{:S(2)}) collective-permute-start(bf16[1024,128]{1,0:T(8,128)(2,1)S(1)} %get-tuple-element.26.refs_0_), channel_id=1, source_target_pairs={{0,1},{1,0},{2,3},{3,2},{4,5},{5,4},{6,7},{7,6},{8,9},{9,8},{10,11... | collective-permute-start | bytes 786440 | tf_op jit(solution)/shard_map/ppermute | solution.py:515
  8.5 0.5 %collective-permute-start.1 = (bf16[1024,128]{1,0:T(8,128)(2,1)S(1)}, bf16[1024,128]{1,0:T(8,128)(2,1)S(1)}, u32[]{:S(2)}, u32[]{:S(2)}) collective-permute-start(bf16[1024,128]{1,0:T(8,128)(2,1)S(1)} %get-tuple-element.26.refs_0_), channel_id=1, source_target_pairs={{0,2},{1,3},{2,0},{3,1},{4,6},{5,7},{6,4},{7,5},{8,10},{9,11},{10,... | collective-permute-start | bytes 786440 | tf_op jit(solution)/shard_map/ppermute | solution.py:515
  9.0 1.5 %collective-permute-start.2 = (bf16[1024,128]{1,0:T(8,128)(2,1)S(1)}, bf16[1024,128]{1,0:T(8,128)(2,1)S(1)}, u32[]{:S(2)}, u32[]{:S(2)}) collective-permute-start(bf16[1024,128]{1,0:T(8,128)(2,1)S(1)} %get-tuple-element.26.refs_0_), channel_id=1, source_target_pairs={{0,3},{1,2},{2,1},{3,0},{4,7},{5,6},{6,5},{7,4},{8,11},{9,10},{10,... | collective-permute-start | bytes 786440 | tf_op jit(solution)/shard_map/ppermute | solution.py:515
  10.4 0.0 collective-permute-done.3.inner_ref.inner_y
  10.4 0.0 collective-permute-done.4.outer_ref.outer_y
  10.5 0.1 collective-permute-start.5
  10.6 3.7 %collective-permute-start.6 = (bf16[80,256]{1,0:T(8,128)(2,1)S(1)}, bf16[80,256]{1,0:T(8,128)(2,1)S(1)}, u32[]{:S(2)}, u32[]{:S(2)}) collective-permute-start(bf16[80,256]{1,0:T(8,128)(2,1)S(1)} %get-tuple-element.34), channel_id=1, source_target_pairs={{0,28},{4,8},{8,4},{12,16},{16,12},{20,24},{24,20},{28,0},{1,29},{... | collective-permute-start | bytes 122888 | tf_op jit(solution)/shard_map/ppermute | solution.py:452
  14.3 0.0 copy-done
  14.3 0.0 copy-done.1
  14.3 0.0 copy-start.2
  14.3 0.0 copy-start.3
  14.3 0.0 copy-start.6
  14.3 2.8 %local.1 = (f32[2,1024,128]{2,1,0:T(8,128)S(1)}, f32[2,1024,128]{2,1,0:T(8,128)S(1)}) custom-call(bf16[1024,256]{1,0:T(8,128)(2,1)S(1)} %get-tuple-element.35.live_ref, f32[3,1536,128]{2,1,0:T(8,128)S(1)} %get-tuple-element.36.pats, bf16[3,768,256]{2,1,0:T(8,128)(2,1)S(1)} %bitcast.13, f32[32,128]{1,0:T(8,128)S(1)} %bitcast.15), custom_call_target="tpu_custom_call" | custom-call | flops 4194304000 | bytes 5242880 | tf_op jit(solution)/shard_map/local/pallas_call | solution.py:536
  17.1 0.0 copy-done.2
  17.1 0.0 copy-done.3
  17.1 0.0 copy-done.6
  17.2 1.0 %order.1 = (s32[72,128]{1,0:T(8,128)S(1)}, bf16[256,256]{1,0:T(8,128)(2,1)S(1)}) custom-call(s32[256,16]{1,0:T(8,128)S(1)} %bitcast.17, s32[256,16]{1,0:T(8,128)S(1)} %bitcast.18, s32[16,16]{1,0:T(8,128)S(1)} %copy-done.6), custom_call_target="tpu_custom_call" | custom-call | flops 629145600 | bytes 1048576 | tf_op jit(solution)/shard_map/order/pallas_call | solution.py:568
  18.1 0.0 copy-start.4
  18.1 0.0 copy-start.5
  18.2 0.0 collective-permute-done.5.inner_x
  18.2 0.0 collective-permute-done.6.outer_x
  18.2 0.9 %halos.1 = (f32[2,1024,128]{2,1,0:T(8,128)S(1)}, f32[2,1024,128]{2,1,0:T(8,128)S(1)}) custom-call(bf16[64,256]{1,0:T(8,128)(2,1)S(1)} %collective-permute-done.3.inner_ref.inner_y, bf16[64,256]{1,0:T(8,128)(2,1)S(1)} %collective-permute-done.4.outer_ref.outer_y, bf16[80,256]{1,0:T(8,128)(2,1)S(1)} %collective-permute-done.5.inner_x, ...), custom_call_target="tpu_custom_call" | custom-call | flops 209715200 | bytes 5242880 | tf_op jit(solution)/shard_map/halos/pallas_call | solution.py:552
  19.1 0.0 collective-permute-done.refs_1_
  19.1 2.2 %collective-permute-done.1.refs_2_ = bf16[1024,128]{1,0:T(8,128)(2,1)S(1)} collective-permute-done((bf16[1024,128]{1,0:T(8,128)(2,1)S(1)}, bf16[1024,128]{1,0:T(8,128)(2,1)S(1)}, u32[]{:S(2)}, u32[]{:S(2)}) %collective-permute-start.1) | collective-permute-done | bytes 262176 | tf_op jit(solution)/shard_map/ppermute | solution.py:515
  21.3 0.0 collective-permute-done.2.refs_3_
  21.3 0.0 copy-done.4
  21.3 0.0 copy-done.5
  21.3 6.9 %lists.1 = f32[2048,128]{1,0:T(8,128)} custom-call(bf16[1024,128]{1,0:T(8,128)(2,1)S(1)} %get-tuple-element.26.refs_0_, bf16[1024,128]{1,0:T(8,128)(2,1)S(1)} %collective-permute-done.refs_1_, bf16[1024,128]{1,0:T(8,128)(2,1)S(1)} %collective-permute-done.1.refs_2_, bf16[1024,128]{1,0:T(8,128)(2,1)S(1)} %collective-permute-done.2.refs_3_, ...), custom_call_target="tpu_custom_call" | custom-call | flops 4194304000 | bytes 8388608 | tf_op jit(solution)/shard_map/lists/pallas_call | solution.py:581
  (1 shorter events, 0.0 us)
Async XLA Ops:
  0.0 14.3 %copy-start = (bf16[9,256,256]{2,1,0:T(8,128)(2,1)S(1)}, bf16[9,256,256]{2,1,0:T(8,128)(2,1)}, u32[]{:S(2)}) copy-start(bf16[9,256,256]{2,1,0:T(8,128)(2,1)} %param.15) | copy-start | bytes 3538948
  0.0 14.3 %copy-start.1 = (f32[16,2,128]{2,1,0:T(2,128)S(1)}, f32[16,2,128]{2,1,0:T(2,128)}, u32[]{:S(2)}) copy-start(f32[16,2,128]{2,1,0:T(2,128)} %param.16) | copy-start | bytes 49156
  1.6 8.8 %collective-permute-start.3 = (bf16[64,256]{1,0:T(8,128)(2,1)S(1)}, bf16[64,256]{1,0:T(8,128)(2,1)S(1)}, u32[]{:S(2)}, u32[]{:S(2)}) collective-permute-start(bf16[64,256]{1,0:T(8,128)(2,1)S(1)} %get-tuple-element.27), channel_id=1, source_target_pairs={{0,1},{1,0},{2,3},{3,2},{4,5},{5,4},{6,7},{7,6},{8,9},{9,8},{10,11... | collective-permute-start | bytes 98312 | tf_op jit(solution)/shard_map/ppermute | solution.py:452
  4.6 5.8 %collective-permute-start.4 = (bf16[64,256]{1,0:T(8,128)(2,1)S(1)}, bf16[64,256]{1,0:T(8,128)(2,1)S(1)}, u32[]{:S(2)}, u32[]{:S(2)}) collective-permute-start(bf16[64,256]{1,0:T(8,128)(2,1)S(1)} %get-tuple-element.28), channel_id=1, source_target_pairs={{0,3},{1,2},{2,1},{3,0},{4,7},{5,6},{6,5},{7,4},{8,11},{9,10},{10,... | collective-permute-start | bytes 98312 | tf_op jit(solution)/shard_map/ppermute | solution.py:452
  6.9 12.2 %collective-permute-start = (bf16[1024,128]{1,0:T(8,128)(2,1)S(1)}, bf16[1024,128]{1,0:T(8,128)(2,1)S(1)}, u32[]{:S(2)}, u32[]{:S(2)}) collective-permute-start(bf16[1024,128]{1,0:T(8,128)(2,1)S(1)} %get-tuple-element.26.refs_0_), channel_id=1, source_target_pairs={{0,1},{1,0},{2,3},{3,2},{4,5},{5,4},{6,7},{7,6},{8,9},{9,8},{10,11... | collective-permute-start | bytes 786440 | tf_op jit(solution)/shard_map/ppermute | solution.py:515
  8.5 12.8 %collective-permute-start.1 = (bf16[1024,128]{1,0:T(8,128)(2,1)S(1)}, bf16[1024,128]{1,0:T(8,128)(2,1)S(1)}, u32[]{:S(2)}, u32[]{:S(2)}) collective-permute-start(bf16[1024,128]{1,0:T(8,128)(2,1)S(1)} %get-tuple-element.26.refs_0_), channel_id=1, source_target_pairs={{0,2},{1,3},{2,0},{3,1},{4,6},{5,7},{6,4},{7,5},{8,10},{9,11},{10,... | collective-permute-start | bytes 786440 | tf_op jit(solution)/shard_map/ppermute | solution.py:515
  9.0 12.3 %collective-permute-start.2 = (bf16[1024,128]{1,0:T(8,128)(2,1)S(1)}, bf16[1024,128]{1,0:T(8,128)(2,1)S(1)}, u32[]{:S(2)}, u32[]{:S(2)}) collective-permute-start(bf16[1024,128]{1,0:T(8,128)(2,1)S(1)} %get-tuple-element.26.refs_0_), channel_id=1, source_target_pairs={{0,3},{1,2},{2,1},{3,0},{4,7},{5,6},{6,5},{7,4},{8,11},{9,10},{10,... | collective-permute-start | bytes 786440 | tf_op jit(solution)/shard_map/ppermute | solution.py:515
  10.5 7.7 %collective-permute-start.5 = (bf16[80,256]{1,0:T(8,128)(2,1)S(1)}, bf16[80,256]{1,0:T(8,128)(2,1)S(1)}, u32[]{:S(2)}, u32[]{:S(2)}) collective-permute-start(bf16[80,256]{1,0:T(8,128)(2,1)S(1)} %get-tuple-element.29), channel_id=1, source_target_pairs={{0,4},{4,0},{8,12},{12,8},{16,20},{20,16},{24,28},{28,24},{1,5},{5... | collective-permute-start | bytes 122888 | tf_op jit(solution)/shard_map/ppermute | solution.py:452
  10.6 7.6 %collective-permute-start.6 = (bf16[80,256]{1,0:T(8,128)(2,1)S(1)}, bf16[80,256]{1,0:T(8,128)(2,1)S(1)}, u32[]{:S(2)}, u32[]{:S(2)}) collective-permute-start(bf16[80,256]{1,0:T(8,128)(2,1)S(1)} %get-tuple-element.34), channel_id=1, source_target_pairs={{0,28},{4,8},{8,4},{12,16},{16,12},{20,24},{24,20},{28,0},{1,29},{... | collective-permute-start | bytes 122888 | tf_op jit(solution)/shard_map/ppermute | solution.py:452
  14.3 2.9 %copy-start.2 = (s32[16,16,16]{2,1,0:T(8,128)S(1)}, s32[16,16,16]{2,1,0:T(8,128)}, u32[]{:S(2)}) copy-start(s32[16,16,16]{2,1,0:T(8,128)} %param.18) | copy-start | bytes 49156
  14.3 2.9 %copy-start.3 = (s32[16,16,16]{2,1,0:T(8,128)S(1)}, s32[16,16,16]{2,1,0:T(8,128)}, u32[]{:S(2)}) copy-start(s32[16,16,16]{2,1,0:T(8,128)} %param.19) | copy-start | bytes 49156
  14.3 2.9 %copy-start.6 = (s32[16,16]{1,0:T(8,128)S(1)}, s32[16,16]{1,0:T(8,128)}, u32[]{:S(2)}) copy-start(s32[16,16]{1,0:T(8,128)} %count_ref) | copy-start | bytes 3076
  18.1 3.1 %copy-start.4 = (f32[64,2,256]{2,1,0:T(2,128)S(1)}, f32[64,2,256]{2,1,0:T(2,128)}, u32[]{:S(2)}) copy-start(f32[64,2,256]{2,1,0:T(2,128)} %param.21) | copy-start | bytes 393220
  18.1 3.1 %copy-start.5 = (bf16[256,256]{1,0:T(8,128)(2,1)S(1)}, bf16[256,256]{1,0:T(8,128)(2,1)}, u32[]{:S(2)}) copy-start(bf16[256,256]{1,0:T(8,128)(2,1)} %refs_10_.1) | copy-start | bytes 393220

commit v7 on v6

--- a/solution.py
+++ b/solution.py
@@ -119,8 +119,8 @@
                 ]
                 children.append(jnp.concatenate(rows, axis=0).astype(BF16))
     coarse = mm(jnp.concatenate(children, axis=1), up_ref[...])
-    for place, column in enumerate((0, 2, 1, 3)):
-        rows4[pl.ds(place, coarse.shape[0], stride=4), :] = coarse[:, column * 128 : (column + 1) * 128]
+    for place in range(4):
+        rows4[pl.ds(place, coarse.shape[0], stride=4), :] = coarse[:, place * 128 : (place + 1) * 128]
     coarse_ref[...] = rows4[...].astype(BF16)
     pattern = pattern.astype(BF16).astype(F32)
     values = [pattern[:, :lanes], pattern[:, lanes:], pattern[:, :lanes] + pattern[:, lanes:]]
@@ -218,14 +218,34 @@
 
 
 def halos_kernel(
-    tile_x, tile_y, inner_y, outer_y, inner_x, outer_x, agg_ref, near_ref, low_ref, lower_in, field_in,
-    lower_ref, field_ref, columns, rims,
+    tile_x, tile_y, inner_y, outer_y, inner_x, outer_x, agg_ref, near_ref, low_ref, lower_in, field_in, kept_in,
+    lower_ref, field_ref, kept_ref, columns, rims, line_ref,
 ):
-    lanes = lower_ref.shape[2]
+    lanes = lower_in.shape[2]
     width = tile_y + 2 * LEFT
     halo = halo_pair(inner_y, outer_y, "gy") + halo_pair(inner_x, outer_x, "gx")
-    lower_ref[...] = lower_in[...]
-    field_ref[...] = field_in[...]
+    half_x, half_y = tile_x // 2, tile_y // 2
+    for child in range(4):
+        for p in range(half_x):
+            rows = slice(p * half_y, (p + 1) * half_y)
+            boxes = pl.ds((2 * p + child // 2) * tile_y + child % 2, half_y, stride=2)
+            for part in range(2):
+                lower_ref[part, child, rows, :] = lower_in[part, boxes, :]
+                field_ref[part, child, rows, :] = field_in[part, boxes, :]
+            kept_ref[child, rows, :] = kept_in[boxes, :]
+
+    def add_column(ref, part, box, value):
+        line_ref[...] = value
+        for side_x in range(2):
+            child, rows = 2 * side_x + box % 2, pl.ds(box // 2, half_x, stride=half_y)
+            ref[part, child, rows, :] = ref[part, child, rows, :] + line_ref[pl.ds(side_x, half_x, stride=2), :]
+
+    def add_row(ref, part, box, value):
+        line_ref[...] = value
+        for side_y in range(2):
+            child, rows = 2 * (box % 2) + side_y, slice(box // 2 * half_y, (box // 2 + 1) * half_y)
+            ref[part, child, rows, :] = ref[part, child, rows, :] + line_ref[pl.ds(side_y, half_y, stride=2), :]
+
     halo = jnp.concatenate(halo, axis=0)
     pattern = mm(halo.astype(BF16), agg_ref[...]).astype(BF16).astype(F32)
     values = [halo[:, :lanes], halo[:, lanes:], pattern[:, :lanes], pattern[:, lanes:]]
@@ -274,17 +294,15 @@
                 for dx in range(-2, 3):
                     if (dx, dy) in OFFSETS:
                         terms.append((dx, dy, column(2, side, c, dx), column(3, side, c, dx)))
-            rows = pl.ds(box, tile_x, stride=tile_y)
             for part, value in enumerate(translate(terms)):
-                lower_ref[part, rows, :] = lower_ref[part, rows, :] + value
+                add_column(lower_ref, part, box, value)
         source = jnp.concatenate(
             [column(part, side, 1 - side, dx) for dx in range(-1, 2) for part in range(2)], axis=1
         ).astype(BF16)
         weights = [near_ref[dx, (4 * side) * lanes : (4 * side + 2) * lanes, :] for dx in range(3)]
         value = mm(source, jnp.concatenate(weights, axis=0))
-        rows = pl.ds(tile_y - 1 if side else 0, tile_x, stride=tile_y)
         for part in range(2):
-            field_ref[part, rows, :] = field_ref[part, rows, :] + value[:, part * lanes : (part + 1) * lanes]
+            add_column(field_ref, part, tile_y - 1 if side else 0, value[:, part * lanes : (part + 1) * lanes])
     for end in range(2):
         for box in ((tile_x - 1, tile_x - 2) if end else (0, 1)):
             terms = []
@@ -293,23 +311,27 @@
                 for dy in range(-2, 3):
                     if (dx, dy) in OFFSETS:
                         terms.append((dx, dy, rim(2, end, row, dy), rim(3, end, row, dy)))
-            rows = slice(box * tile_y, (box + 1) * tile_y)
             for part, value in enumerate(translate(terms)):
-                lower_ref[part, rows, :] = lower_ref[part, rows, :] + value
+                add_row(lower_ref, part, box, value)
         source = jnp.concatenate(
             [rim(part, end, 1 - end, dy) for dy in range(-1, 2) for part in range(2)], axis=1
         ).astype(BF16)
         value = mm(source, near_ref[2 * end])
-        box = tile_x - 1 if end else 0
-        rows = slice(box * tile_y, (box + 1) * tile_y)
         for part in range(2):
-            field_ref[part, rows, :] = field_ref[part, rows, :] + value[:, part * lanes : (part + 1) * lanes]
+            add_row(field_ref, part, tile_x - 1 if end else 0, value[:, part * lanes : (part + 1) * lanes])
 
 
 GROUP = 8
 
 
-def order_kernel(chunks, kinds, parents_x, parents_y, list_ref, kind_ref, count_ref, at_ref, back_ref):
+def order_kernel(
+    chunks, kinds, parents_x, parents_y, list_ref, kind_ref, count_ref, table_ref, at_ref, back_ref, table8
+):
+    width = table_ref.shape[1]
+    for place, row in enumerate((0, 2, 0, 2, 1, 3, 1, 3)):
+        value = table_ref[pl.ds(row, kinds, stride=4), :]
+        table8[pl.ds(place, kinds, stride=8), :] = -value if place in (4, 5) else value
+    table8[8 * kinds : 8 * kinds + 8, :] = jnp.zeros((8, width), F32)
     parents = parents_x * parents_y
     slots = list_ref.shape[1]
     groups = parents // GROUP
@@ -355,12 +377,11 @@
 
 def lists_kernel(chunks, tile_x, tile_y, slots, *refs):
     sources = refs[:chunks]
-    (at_any, table_ref, back_ref, kept_ref, lower_ref, near_ref, recv_ref, down_hbm, out_hbm,
-     cells, table8, sums, at, down_ref, total_ref, out_ref, sems) = refs[chunks:]
+    (at_any, table8, back_ref, kept_ref, lower_ref, near_ref, recv_ref, down_hbm, out_hbm,
+     cells, wide, sums, at, down_ref, total_ref, out_ref, sems) = refs[chunks:]
     parents_x, parents_y = tile_x // 2, tile_y // 2
     parents = parents_x * parents_y
-    kinds = table_ref.shape[0] // 4
-    lanes = table_ref.shape[1]
+    lanes = table8.shape[1]
     groups = parents // GROUP
     loads = [
         pltpu.make_async_copy(at_any, at, sems.at[0]),
@@ -368,22 +389,27 @@
     ]
     for load in loads:
         load.start()
-    for place, row in enumerate((0, 0, 2, 2, 1, 1, 3, 3)):
-        table8[pl.ds(place, kinds, stride=8), :] = table_ref[pl.ds(row, kinds, stride=4), :]
-    table8[8 * kinds : 8 * kinds + 8, :] = jnp.zeros((8, lanes), F32)
     count = parents // 2
     pairs = cells.reshape(chunks * count, 2, 8, lanes)
-    upper = lax.broadcasted_iota(jnp.int32, (count, 8, lanes), 1) < 4
+    place = lax.broadcasted_iota(jnp.int32, (count, 8, lanes), 1)
+    wide[0:8, :] = jnp.zeros((8, lanes), F32)
+    wide[8 + 8 * count :, :] = jnp.zeros((8, lanes), F32)
     for c in range(chunks):
-        rows = sources[c][...].astype(F32).reshape(count, 8, lanes)
-        turned = pltpu.roll(rows, 4, axis=1)
-        pairs[c * count : (c + 1) * count, 0] = jnp.where(upper, rows, turned)
-        pairs[c * count : (c + 1) * count, 1] = jnp.where(upper, turned, rows)
+        wide[8 : 8 + 8 * count, :] = sources[c][...].astype(F32)
+
+        def shifted(by):
+            return wide[8 + by : 8 + by + 8 * count, :].reshape(count, 8, lanes)
+
+        here = slice(c * count, (c + 1) * count)
+        pairs[here, 0] = jnp.where(place < 4, shifted(0), jnp.where(place < 6, shifted(-2), shifted(-6)))
+        pairs[here, 1] = jnp.where(place < 4, shifted(4), jnp.where(place < 6, shifted(2), shifted(-2)))
     loads[0].wait()
+    upper = lax.broadcasted_iota(jnp.int32, (8, lanes), 0) < 4
 
     def step(length, n, carry):
         first = n * (GROUP * slots)
         second = first + groups * GROUP * slots
+        before = None
         for k in range(GROUP):
             total = [None, None]
             for s in range(length):
@@ -392,7 +418,11 @@
                 term = cells[pl.ds(source, 8), :] * table8[pl.ds(kind, 8), :]
                 total[s % 2] = term if total[s % 2] is None else total[s % 2] + term
             total = total[0] + total[1] if length else jnp.zeros((8, lanes), F32)
-            sums[pl.ds(pl.multiple_of((n * GROUP + k) * 8, 8), 8), :] = total
+            total = total + pltpu.roll(total, 4, axis=0)
+            if k % 2:
+                tile = pl.multiple_of(n * (GROUP * 4) + (k // 2) * 8, 8)
+                sums[pl.ds(tile, 8), :] = jnp.where(upper, before, total)
+            before = total
         return carry
 
     start = 0
@@ -402,38 +432,25 @@
         start = end
     lax.fori_loop(start, groups, functools.partial(step, 0), 0)
 
-    def row(place):
-        return sums[pl.ds(place, parents, stride=8), :]
-
-    ordered = jnp.concatenate(
-        [row(0) - row(5), row(2) - row(7), row(1) + row(4), row(3) + row(6)], axis=1
-    ).astype(BF16)
-    incoming = mm(back_ref[...], ordered).astype(BF16)
+    ordered = [sums[pl.ds(place, parents, stride=4), :].astype(BF16) for place in range(4)]
+    incoming = mm(back_ref[...], jnp.concatenate(ordered, axis=1)).astype(BF16)
     loads[1].wait()
-    starts = [
-        [(2 * p + child // 2) * tile_y + child % 2 for p in range(parents_x)] for child in range(4)
-    ]
-
-    def rows_of(ref, lines):
-        return jnp.concatenate([ref[pl.ds(line, parents_y, stride=2), :] for line in lines], axis=0)
-
     for child in range(4):
         down = mm(incoming, down_ref[child])
         for part in range(2):
-            value = down[:, part * lanes : (part + 1) * lanes] + rows_of(lower_ref.at[part], starts[child])
+            value = down[:, part * lanes : (part + 1) * lanes] + lower_ref[part, child]
             total_ref[child, :, part * lanes : (part + 1) * lanes] = value.astype(BF16)
     stores = []
     for half in range(2):
-        count = parents_x // 2
-        rows = slice(half * parents // 2, (half + 1) * parents // 2)
+        first, size = half * parents // 2, parents // 2
+        rows = slice(first, first + size)
         for child in range(4):
             field = mm(total_ref[child, rows, :], recv_ref[...])
-            lines = starts[child][half * count : (half + 1) * count]
-            mask = rows_of(kept_ref, lines)
+            mask = kept_ref[child, rows, :]
             for part in range(2):
-                value = field[:, part * lanes : (part + 1) * lanes] + rows_of(near_ref.at[part], lines)
-                value = value * mask
-                for p, line in enumerate(lines):
+                value = (field[:, part * lanes : (part + 1) * lanes] + near_ref[part, child, rows, :]) * mask
+                for p in range(parents_x // 2):
+                    line = (2 * (half * parents_x // 2 + p) + child // 2) * tile_y + child % 2
                     out_ref[pl.ds(2 * line + part, parents_y, stride=4), :] = value[
                         p * parents_y : (p + 1) * parents_y
                     ]
@@ -511,9 +528,11 @@
         cost_estimate=cost(200 * MIB, 3 * MIB),
     )(live, agg_near, up_near)
     inner_y, outer_y = swap(low, high, "gy")
-    sources = [coarse] + [
-        lax.ppermute(coarse, "gy", [(i, i ^ d) for i in range(chunks)]) for d in range(1, chunks)
-    ]
+    arrived = {
+        d: lax.ppermute(coarse, "gy", [(i, i ^ d) for i in range(chunks)])
+        for d in [chunks - 1] + list(range(1, chunks - 1))
+    }
+    sources = [coarse] + [arrived[d] for d in range(1, chunks)]
 
     rim = 2 * tile_y + 8
     rim += -rim % 16
@@ -549,34 +568,37 @@
         cost_estimate=cost(2000 * MIB, 5 * MIB),
     )(live, pats, near_rows, low_rows)
 
-    lower, near = pl.pallas_call(
+    pair = [jax.ShapeDtypeStruct((2, 4, parents, lanes), F32)] * 2
+    lower, near, kept = pl.pallas_call(
         functools.partial(halos_kernel, tile_x, tile_y),
         name="halos",
-        out_shape=pair,
-        in_specs=vmem(9),
-        out_specs=vmem(2),
+        out_shape=pair + [jax.ShapeDtypeStruct((4, parents, lanes), F32)],
+        in_specs=vmem(10),
+        out_specs=vmem(3),
         scratch_shapes=[
             pltpu.VMEM((4, 4, tile_x + 16, lanes), F32),
             pltpu.VMEM((4, 4 * width, lanes), F32),
+            pltpu.VMEM((tile_x, lanes), F32),
         ],
         compiler_params=params(10),
         cost_estimate=cost(100 * MIB, 5 * MIB),
-    )(inner_y, outer_y, inner_x, outer_x, agg_near, near_rows, low_rows, lower, near)
+    )(inner_y, outer_y, inner_x, outer_x, agg_near, near_rows, low_rows, lower, near, kept)
 
     table = up_translator.reshape(kinds, 2, 2, half // 2).transpose(0, 2, 1, 3).reshape(4 * kinds, half // 2)
     groups = parents // GROUP
-    at, back = pl.pallas_call(
+    at, back, table8 = pl.pallas_call(
         functools.partial(order_kernel, chunks, kinds, parents_x, parents_y),
         name="order",
         out_shape=[
             jax.ShapeDtypeStruct((2 * groups + 8, GROUP * slots), jnp.int32),
             jax.ShapeDtypeStruct((parents, parents), BF16),
-        ],
-        in_specs=vmem(3),
-        out_specs=vmem(2),
+            jax.ShapeDtypeStruct((8 * kinds + 8, half // 2), F32),
+        ],
+        in_specs=vmem(4),
+        out_specs=vmem(3),
         compiler_params=params(8),
         cost_estimate=cost(300 * MIB, MIB),
-    )(coarse_list.reshape(parents, slots), coarse_kind.reshape(parents, slots), coarse_count)
+    )(coarse_list.reshape(parents, slots), coarse_kind.reshape(parents, slots), coarse_count, table)
     at = at.reshape(-1)
     out = pl.pallas_call(
         functools.partial(lists_kernel, chunks, tile_x, tile_y, slots),
@@ -586,8 +608,8 @@
         out_specs=in_hbm,
         scratch_shapes=[
             pltpu.VMEM((chunks * parents * 8, wide // 4), F32),
-            pltpu.VMEM((8 * kinds + 8, wide // 4), F32),
-            pltpu.VMEM((8 * parents, wide // 4), F32),
+            pltpu.VMEM((4 * parents + 16, wide // 4), F32),
+            pltpu.VMEM((4 * parents, wide // 4), F32),
             pltpu.SMEM(at.shape, jnp.int32),
             pltpu.VMEM((4, wide, 2 * lanes), BF16),
             pltpu.VMEM((4, parents, 2 * lanes), BF16),
@@ -596,7 +618,7 @@
         ],
         compiler_params=params(16 if chunks <= 4 else 40),
         cost_estimate=cost(2000 * MIB, 8 * MIB),
-    )(*sources, at, table, back, kept, lower, near, receive_map, hbm(parent_to_child))
+    )(*sources, at, table8, back, kept, lower, near, receive_map, hbm(parent_to_child))
     return out.reshape(tile_x, tile_y, 2, lanes)
 
 

time: 28.3 us -> 29.4 us (1.039)
  Pallas kernels: 14 us -> 14.8 us
    pallas_call x1, Pallas kernels: 6.9 us -> 7.74 us  [body(): pl.pallas_call(functools.partial(lists_kernel, chunks, tile_x, tile_y, sl...]
where the time goes in v7:
time: 29.4 us; the launch traced here: 29 us
  Pallas kernels  14.8 us (50%)
  starting transfers between devices  11.8 us (40%)
  waiting for transfers between devices  2.2 us (7%)
    ppermute x4, starting transfers between devices, swap(): return (lax.ppermute(low, axis, lows), lax.ppermute(high, axis, highs))  8.28 us
    pallas_call x1, Pallas kernels, body(): pl.pallas_call(functools.partial(lists_kernel, chunks, tile_x, tile_y, sl...  7.74 us
    ppermute x3, starting transfers between devices, body(): lax.ppermute(coarse, 'gy', [(i, i ^ d) for i in range(chunks)])  3.55 us
    pallas_call x1, Pallas kernels, body(): pl.pallas_call(functools.partial(local_kernel, tile_x, tile_y), name='loc...  2.83 us
    ppermute x3, waiting for transfers between devices, body(): lax.ppermute(coarse, 'gy', [(i, i ^ d) for i in range(chunks)])  2.19 us
    pallas_call x1, Pallas kernels, body(): pl.pallas_call(functools.partial(live_kernel, tile_x, tile_y), name='live...  1.61 us
    pallas_call x1, Pallas kernels, body(): pl.pallas_call(functools.partial(order_kernel, chunks, kinds, parents_x,...  1.02 us
    pallas_call x1, Pallas kernels, body(): pl.pallas_call(functools.partial(halos_kernel, tile_x, tile_y), name='hal...  0.83 us
  transfers between devices with their start and end apart: 7, of which 1 were waited for; matrix products, arithmetic and copies ran while one was open for 0% of the time, Pallas kernels for 19%

profile of v7, /device:TPU:0, one launch (start us, length us, event | category | flops | bytes accessed | tf_op | source)
XLA Modules:
  0.0 29.0 jit_solution(7918892696650084399)
XLA Ops:
  0.0 0.0 copy-start
  0.0 0.0 copy-start.1
  0.0 1.6 %live.1 = (bf16[1024,256]{1,0:T(8,128)(2,1)S(1)}, f32[1024,128]{1,0:T(8,128)S(1)}, bf16[64,256]{1,0:T(8,128)(2,1)S(1)}, bf16[64,256]{1,0:T(8,128)(2,1)S(1)}, bf1...) custom-call(bf16[2048,128]{1,0:T(8,128)(2,1)} %bitcast.22, s32[32,32]{1,0:T(8,128)} %counts_hbm.1, ...), custom_call_target="tpu_custom_call" | custom-call | flops 209715200 | bytes 3145728 | tf_op jit(solution)/shard_map/live/pallas_call | solution.py:489
  1.6 3.0 %collective-permute-start.3 = (bf16[64,256]{1,0:T(8,128)(2,1)S(1)}, bf16[64,256]{1,0:T(8,128)(2,1)S(1)}, u32[]{:S(2)}, u32[]{:S(2)}) collective-permute-start(bf16[64,256]{1,0:T(8,128)(2,1)S(1)} %get-tuple-element.29), channel_id=1, source_target_pairs={{0,1},{1,0},{2,3},{3,2},{4,5},{5,4},{6,7},{7,6},{8,9},{9,8},{10,11... | collective-permute-start | bytes 98312 | tf_op jit(solution)/shard_map/ppermute | solution.py:469
  4.6 1.5 %collective-permute-start.4 = (bf16[64,256]{1,0:T(8,128)(2,1)S(1)}, bf16[64,256]{1,0:T(8,128)(2,1)S(1)}, u32[]{:S(2)}, u32[]{:S(2)}) collective-permute-start(bf16[64,256]{1,0:T(8,128)(2,1)S(1)} %get-tuple-element.30), channel_id=1, source_target_pairs={{0,3},{1,2},{2,1},{3,0},{4,7},{5,6},{6,5},{7,4},{8,11},{9,10},{10,... | collective-permute-start | bytes 98312 | tf_op jit(solution)/shard_map/ppermute | solution.py:469
  6.1 0.8 %parents.1 = (bf16[1024,128]{1,0:T(8,128)(2,1)S(1)}, f32[3,1536,128]{2,1,0:T(8,128)S(1)}) custom-call(bf16[1024,256]{1,0:T(8,128)(2,1)S(1)} %get-tuple-element.37.live_ref, bf16[256,256]{1,0:T(8,128)(2,1)S(1)} %get-tuple-element.26.agg_ref, bf16[1024,512]{1,0:T(8,128)(2,1)S(1)} %get-tuple-element.27.up_ref), custom_call_target="tpu_custom_call" | custom-call | flops 419430400 | bytes 3145728 | tf_op jit(solution)/shard_map/parents/pallas_call | solution.py:514
  6.9 1.6 %collective-permute-start = (bf16[1024,128]{1,0:T(8,128)(2,1)S(1)}, bf16[1024,128]{1,0:T(8,128)(2,1)S(1)}, u32[]{:S(2)}, u32[]{:S(2)}) collective-permute-start(bf16[1024,128]{1,0:T(8,128)(2,1)S(1)} %get-tuple-element.28.refs_0_), channel_id=1, source_target_pairs={{0,1},{1,0},{2,3},{3,2},{4,5},{5,4},{6,7},{7,6},{8,9},{9,8},{10,11... | collective-permute-start | bytes 786440 | tf_op jit(solution)/shard_map/ppermute | solution.py:532
  8.4 0.5 %collective-permute-start.1 = (bf16[1024,128]{1,0:T(8,128)(2,1)S(1)}, bf16[1024,128]{1,0:T(8,128)(2,1)S(1)}, u32[]{:S(2)}, u32[]{:S(2)}) collective-permute-start(bf16[1024,128]{1,0:T(8,128)(2,1)S(1)} %get-tuple-element.28.refs_0_), channel_id=1, source_target_pairs={{0,2},{1,3},{2,0},{3,1},{4,6},{5,7},{6,4},{7,5},{8,10},{9,11},{10,... | collective-permute-start | bytes 786440 | tf_op jit(solution)/shard_map/ppermute | solution.py:532
  9.0 1.5 %collective-permute-start.2 = (bf16[1024,128]{1,0:T(8,128)(2,1)S(1)}, bf16[1024,128]{1,0:T(8,128)(2,1)S(1)}, u32[]{:S(2)}, u32[]{:S(2)}) collective-permute-start(bf16[1024,128]{1,0:T(8,128)(2,1)S(1)} %get-tuple-element.28.refs_0_), channel_id=1, source_target_pairs={{0,3},{1,2},{2,1},{3,0},{4,7},{5,6},{6,5},{7,4},{8,11},{9,10},{10,... | collective-permute-start | bytes 786440 | tf_op jit(solution)/shard_map/ppermute | solution.py:532
  10.4 0.0 collective-permute-done.3.inner_ref.inner_y
  10.4 0.0 collective-permute-done.4.outer_ref.outer_y
  10.5 0.1 collective-permute-start.5
  10.6 3.7 %collective-permute-start.6 = (bf16[80,256]{1,0:T(8,128)(2,1)S(1)}, bf16[80,256]{1,0:T(8,128)(2,1)S(1)}, u32[]{:S(2)}, u32[]{:S(2)}) collective-permute-start(bf16[80,256]{1,0:T(8,128)(2,1)S(1)} %get-tuple-element.36), channel_id=1, source_target_pairs={{0,28},{4,8},{8,4},{12,16},{16,12},{20,24},{24,20},{28,0},{1,29},{... | collective-permute-start | bytes 122888 | tf_op jit(solution)/shard_map/ppermute | solution.py:469
  14.3 0.0 copy-done
  14.3 0.0 copy-done.1
  14.3 0.0 copy-start.2
  14.3 0.0 copy-start.3
  14.3 0.0 copy-start.4
  14.3 0.0 copy-start.6
  14.3 2.8 %local.1 = (f32[2,1024,128]{2,1,0:T(8,128)S(1)}, f32[2,1024,128]{2,1,0:T(8,128)S(1)}) custom-call(bf16[1024,256]{1,0:T(8,128)(2,1)S(1)} %get-tuple-element.37.live_ref, f32[3,1536,128]{2,1,0:T(8,128)S(1)} %get-tuple-element.38.pats, bf16[3,768,256]{2,1,0:T(8,128)(2,1)S(1)} %bitcast.13, f32[32,128]{1,0:T(8,128)S(1)} %bitcast.15), custom_call_target="tpu_custom_call" | custom-call | flops 4194304000 | bytes 5242880 | tf_op jit(solution)/shard_map/local/pallas_call | solution.py:555
  17.2 0.0 copy-done.2
  17.2 0.0 copy-done.3
  17.2 0.0 copy-done.4
  17.2 0.0 copy-done.6
  17.2 1.0 %order.1 = (s32[72,128]{1,0:T(8,128)S(1)}, bf16[256,256]{1,0:T(8,128)(2,1)S(1)}, f32[520,128]{1,0:T(8,128)S(1)}) custom-call(s32[256,16]{1,0:T(8,128)S(1)} %bitcast.17, s32[256,16]{1,0:T(8,128)S(1)} %bitcast.18, s32[16,16]{1,0:T(8,128)S(1)} %copy-done.6, f32[256,128]{1,0:T(8,128)S(1)} %bitcast.19), custom_call_target="tpu_custom_call" | custom-call | flops 629145600 | bytes 1048576 | tf_op jit(solution)/shard_map/order/pallas_call | solution.py:589
  18.2 0.0 copy-start.5
  18.2 0.0 collective-permute-done.5.inner_x
  18.2 0.0 collective-permute-done.6.outer_x
  18.2 0.8 %halos.1 = (f32[2,4,256,128]{3,2,1,0:T(8,128)S(1)}, f32[2,4,256,128]{3,2,1,0:T(8,128)S(1)}, f32[4,256,128]{2,1,0:T(8,128)S(1)}) custom-call(bf16[64,256]{1,0:T(8,128)(2,1)S(1)} %collective-permute-done.3.inner_ref.inner_y, bf16[64,256]{1,0:T(8,128)(2,1)S(1)} %collective-permute-done.4.outer_ref.outer_y, bf16[80,256]{1,0:T(8,128)(2,1)S(1)} %collective-permute-done.5.inner_x, ...), custom_call_target="tpu_custom_call" | custom-call | flops 209715200 | bytes 5242880 | tf_op jit(solution)/shard_map/halos/pallas_call | solution.py:572
  19.1 0.0 collective-permute-done.refs_1_
  19.1 2.2 %collective-permute-done.1.refs_2_ = bf16[1024,128]{1,0:T(8,128)(2,1)S(1)} collective-permute-done((bf16[1024,128]{1,0:T(8,128)(2,1)S(1)}, bf16[1024,128]{1,0:T(8,128)(2,1)S(1)}, u32[]{:S(2)}, u32[]{:S(2)}) %collective-permute-start.1) | collective-permute-done | bytes 262176 | tf_op jit(solution)/shard_map/ppermute | solution.py:532
  21.3 0.0 collective-permute-done.2.refs_3_
  21.3 0.0 copy-done.5
  21.3 7.7 %lists.1 = f32[2048,128]{1,0:T(8,128)} custom-call(bf16[1024,128]{1,0:T(8,128)(2,1)S(1)} %get-tuple-element.28.refs_0_, bf16[1024,128]{1,0:T(8,128)(2,1)S(1)} %collective-permute-done.refs_1_, bf16[1024,128]{1,0:T(8,128)(2,1)S(1)} %collective-permute-done.1.refs_2_, bf16[1024,128]{1,0:T(8,128)(2,1)S(1)} %collective-permute-done.2.refs_3_, ...), custom_call_target="tpu_custom_call" | custom-call | flops 4194304000 | bytes 8388608 | tf_op jit(solution)/shard_map/lists/pallas_call | solution.py:603
  (1 shorter events, 0.0 us)
Async XLA Ops:
  0.0 14.3 %copy-start = (bf16[9,256,256]{2,1,0:T(8,128)(2,1)S(1)}, bf16[9,256,256]{2,1,0:T(8,128)(2,1)}, u32[]{:S(2)}) copy-start(bf16[9,256,256]{2,1,0:T(8,128)(2,1)} %param.15) | copy-start | bytes 3538948
  0.0 14.3 %copy-start.1 = (f32[16,2,128]{2,1,0:T(2,128)S(1)}, f32[16,2,128]{2,1,0:T(2,128)}, u32[]{:S(2)}) copy-start(f32[16,2,128]{2,1,0:T(2,128)} %param.16) | copy-start | bytes 49156
  1.6 8.8 %collective-permute-start.3 = (bf16[64,256]{1,0:T(8,128)(2,1)S(1)}, bf16[64,256]{1,0:T(8,128)(2,1)S(1)}, u32[]{:S(2)}, u32[]{:S(2)}) collective-permute-start(bf16[64,256]{1,0:T(8,128)(2,1)S(1)} %get-tuple-element.29), channel_id=1, source_target_pairs={{0,1},{1,0},{2,3},{3,2},{4,5},{5,4},{6,7},{7,6},{8,9},{9,8},{10,11... | collective-permute-start | bytes 98312 | tf_op jit(solution)/shard_map/ppermute | solution.py:469
  4.6 5.8 %collective-permute-start.4 = (bf16[64,256]{1,0:T(8,128)(2,1)S(1)}, bf16[64,256]{1,0:T(8,128)(2,1)S(1)}, u32[]{:S(2)}, u32[]{:S(2)}) collective-permute-start(bf16[64,256]{1,0:T(8,128)(2,1)S(1)} %get-tuple-element.30), channel_id=1, source_target_pairs={{0,3},{1,2},{2,1},{3,0},{4,7},{5,6},{6,5},{7,4},{8,11},{9,10},{10,... | collective-permute-start | bytes 98312 | tf_op jit(solution)/shard_map/ppermute | solution.py:469
  6.9 12.2 %collective-permute-start = (bf16[1024,128]{1,0:T(8,128)(2,1)S(1)}, bf16[1024,128]{1,0:T(8,128)(2,1)S(1)}, u32[]{:S(2)}, u32[]{:S(2)}) collective-permute-start(bf16[1024,128]{1,0:T(8,128)(2,1)S(1)} %get-tuple-element.28.refs_0_), channel_id=1, source_target_pairs={{0,1},{1,0},{2,3},{3,2},{4,5},{5,4},{6,7},{7,6},{8,9},{9,8},{10,11... | collective-permute-start | bytes 786440 | tf_op jit(solution)/shard_map/ppermute | solution.py:532
  8.4 12.8 %collective-permute-start.1 = (bf16[1024,128]{1,0:T(8,128)(2,1)S(1)}, bf16[1024,128]{1,0:T(8,128)(2,1)S(1)}, u32[]{:S(2)}, u32[]{:S(2)}) collective-permute-start(bf16[1024,128]{1,0:T(8,128)(2,1)S(1)} %get-tuple-element.28.refs_0_), channel_id=1, source_target_pairs={{0,2},{1,3},{2,0},{3,1},{4,6},{5,7},{6,4},{7,5},{8,10},{9,11},{10,... | collective-permute-start | bytes 786440 | tf_op jit(solution)/shard_map/ppermute | solution.py:532
  9.0 12.3 %collective-permute-start.2 = (bf16[1024,128]{1,0:T(8,128)(2,1)S(1)}, bf16[1024,128]{1,0:T(8,128)(2,1)S(1)}, u32[]{:S(2)}, u32[]{:S(2)}) collective-permute-start(bf16[1024,128]{1,0:T(8,128)(2,1)S(1)} %get-tuple-element.28.refs_0_), channel_id=1, source_target_pairs={{0,3},{1,2},{2,1},{3,0},{4,7},{5,6},{6,5},{7,4},{8,11},{9,10},{10,... | collective-permute-start | bytes 786440 | tf_op jit(solution)/shard_map/ppermute | solution.py:532
  10.5 7.7 %collective-permute-start.5 = (bf16[80,256]{1,0:T(8,128)(2,1)S(1)}, bf16[80,256]{1,0:T(8,128)(2,1)S(1)}, u32[]{:S(2)}, u32[]{:S(2)}) collective-permute-start(bf16[80,256]{1,0:T(8,128)(2,1)S(1)} %get-tuple-element.31), channel_id=1, source_target_pairs={{0,4},{4,0},{8,12},{12,8},{16,20},{20,16},{24,28},{28,24},{1,5},{5... | collective-permute-start | bytes 122888 | tf_op jit(solution)/shard_map/ppermute | solution.py:469
  10.6 7.7 %collective-permute-start.6 = (bf16[80,256]{1,0:T(8,128)(2,1)S(1)}, bf16[80,256]{1,0:T(8,128)(2,1)S(1)}, u32[]{:S(2)}, u32[]{:S(2)}) collective-permute-start(bf16[80,256]{1,0:T(8,128)(2,1)S(1)} %get-tuple-element.36), channel_id=1, source_target_pairs={{0,28},{4,8},{8,4},{12,16},{16,12},{20,24},{24,20},{28,0},{1,29},{... | collective-permute-start | bytes 122888 | tf_op jit(solution)/shard_map/ppermute | solution.py:469
  14.3 2.9 %copy-start.2 = (s32[16,16,16]{2,1,0:T(8,128)S(1)}, s32[16,16,16]{2,1,0:T(8,128)}, u32[]{:S(2)}) copy-start(s32[16,16,16]{2,1,0:T(8,128)} %param.18) | copy-start | bytes 49156
  14.3 2.9 %copy-start.3 = (s32[16,16,16]{2,1,0:T(8,128)S(1)}, s32[16,16,16]{2,1,0:T(8,128)}, u32[]{:S(2)}) copy-start(s32[16,16,16]{2,1,0:T(8,128)} %param.19) | copy-start | bytes 49156
  14.3 2.9 %copy-start.4 = (f32[64,2,256]{2,1,0:T(2,128)S(1)}, f32[64,2,256]{2,1,0:T(2,128)}, u32[]{:S(2)}) copy-start(f32[64,2,256]{2,1,0:T(2,128)} %param.21) | copy-start | bytes 393220
  14.3 2.9 %copy-start.6 = (s32[16,16]{1,0:T(8,128)S(1)}, s32[16,16]{1,0:T(8,128)}, u32[]{:S(2)}) copy-start(s32[16,16]{1,0:T(8,128)} %count_ref) | copy-start | bytes 3076
  18.2 3.1 %copy-start.5 = (bf16[256,256]{1,0:T(8,128)(2,1)S(1)}, bf16[256,256]{1,0:T(8,128)(2,1)}, u32[]{:S(2)}) copy-start(bf16[256,256]{1,0:T(8,128)(2,1)} %refs_10_.1) | copy-start | bytes 393220

commit v8 on v7

--- a/solution.py
+++ b/solution.py
@@ -329,8 +329,7 @@
 ):
     width = table_ref.shape[1]
     for place, row in enumerate((0, 2, 0, 2, 1, 3, 1, 3)):
-        value = table_ref[pl.ds(row, kinds, stride=4), :]
-        table8[pl.ds(place, kinds, stride=8), :] = -value if place in (4, 5) else value
+        table8[pl.ds(place, kinds, stride=8), :] = table_ref[pl.ds(row, kinds, stride=4), :]
     table8[8 * kinds : 8 * kinds + 8, :] = jnp.zeros((8, width), F32)
     parents = parents_x * parents_y
     slots = list_ref.shape[1]
@@ -378,7 +377,7 @@
 def lists_kernel(chunks, tile_x, tile_y, slots, *refs):
     sources = refs[:chunks]
     (at_any, table8, back_ref, kept_ref, lower_ref, near_ref, recv_ref, down_hbm, out_hbm,
-     cells, wide, sums, at, down_ref, total_ref, out_ref, sems) = refs[chunks:]
+     cells, sums, at, down_ref, total_ref, out_ref, sems) = refs[chunks:]
     parents_x, parents_y = tile_x // 2, tile_y // 2
     parents = parents_x * parents_y
     lanes = table8.shape[1]
@@ -391,20 +390,15 @@
         load.start()
     count = parents // 2
     pairs = cells.reshape(chunks * count, 2, 8, lanes)
-    place = lax.broadcasted_iota(jnp.int32, (count, 8, lanes), 1)
-    wide[0:8, :] = jnp.zeros((8, lanes), F32)
-    wide[8 + 8 * count :, :] = jnp.zeros((8, lanes), F32)
-    for c in range(chunks):
-        wide[8 : 8 + 8 * count, :] = sources[c][...].astype(F32)
-
-        def shifted(by):
-            return wide[8 + by : 8 + by + 8 * count, :].reshape(count, 8, lanes)
-
-        here = slice(c * count, (c + 1) * count)
-        pairs[here, 0] = jnp.where(place < 4, shifted(0), jnp.where(place < 6, shifted(-2), shifted(-6)))
-        pairs[here, 1] = jnp.where(place < 4, shifted(4), jnp.where(place < 6, shifted(2), shifted(-2)))
+    first_half = lax.broadcasted_iota(jnp.int32, (count, 8, lanes), 1) < 4
+    for c, source in zip([0, chunks - 1] + list(range(1, chunks - 1)), sources):
+        rows = source[...].astype(F32).reshape(count, 8, lanes)
+        turned = pltpu.roll(rows, 4, axis=1)
+        pairs[c * count : (c + 1) * count, 0] = jnp.where(first_half, rows, turned)
+        pairs[c * count : (c + 1) * count, 1] = jnp.where(first_half, turned, rows)
     loads[0].wait()
-    upper = lax.broadcasted_iota(jnp.int32, (8, lanes), 0) < 4
+    line = lax.broadcasted_iota(jnp.int32, (8, lanes), 0)
+    upper, real = line < 4, line % 4 < 2
 
     def step(length, n, carry):
         first = n * (GROUP * slots)
@@ -418,10 +412,12 @@
                 term = cells[pl.ds(source, 8), :] * table8[pl.ds(kind, 8), :]
                 total[s % 2] = term if total[s % 2] is None else total[s % 2] + term
             total = total[0] + total[1] if length else jnp.zeros((8, lanes), F32)
-            total = total + pltpu.roll(total, 4, axis=0)
             if k % 2:
+                with_real = jnp.where(upper, before, pltpu.roll(total, 4, axis=0))
+                with_imag = jnp.where(upper, pltpu.roll(before, 4, axis=0), total)
+                turned = jnp.where(real, -pltpu.roll(with_imag, 6, axis=0), pltpu.roll(with_imag, 2, axis=0))
                 tile = pl.multiple_of(n * (GROUP * 4) + (k // 2) * 8, 8)
-                sums[pl.ds(tile, 8), :] = jnp.where(upper, before, total)
+                sums[pl.ds(tile, 8), :] = with_real + turned
             before = total
         return carry
 
@@ -528,11 +524,10 @@
         cost_estimate=cost(200 * MIB, 3 * MIB),
     )(live, agg_near, up_near)
     inner_y, outer_y = swap(low, high, "gy")
-    arrived = {
-        d: lax.ppermute(coarse, "gy", [(i, i ^ d) for i in range(chunks)])
+    sources = [coarse] + [
+        lax.ppermute(coarse, "gy", [(i, i ^ d) for i in range(chunks)])
         for d in [chunks - 1] + list(range(1, chunks - 1))
-    }
-    sources = [coarse] + [arrived[d] for d in range(1, chunks)]
+    ]
 
     rim = 2 * tile_y + 8
     rim += -rim % 16
@@ -608,7 +603,6 @@
         out_specs=in_hbm,
         scratch_shapes=[
             pltpu.VMEM((chunks * parents * 8, wide // 4), F32),
-            pltpu.VMEM((4 * parents + 16, wide // 4), F32),
             pltpu.VMEM((4 * parents, wide // 4), F32),
             pltpu.SMEM(at.shape, jnp.int32),
             pltpu.VMEM((4, wide, 2 * lanes), BF16),

time: 29.4 us -> 28.8 us (0.980); the launches traced: 29 us -> 28.8 us
  waiting for transfers between devices: 2.2 us -> 1.88 us
    ppermute x3, waiting for transfers between devices: 2.19 us -> 1.87 us  [body(): lax.ppermute(coarse, 'gy', [(i, i ^ d) for i in range(chunks)])]
  transfers between devices with their start and end apart: 7 -> 7, of which waited for: 1 -> 2; matrix products, arithmetic and copies ran while one was open for 0% -> 0% of each run, Pallas kernels for 19% -> 19%
where the time goes in v8:
time: 28.8 us
  Pallas kernels  14.9 us (52%)
  starting transfers between devices  11.8 us (41%)
  waiting for transfers between devices  1.88 us (7%)
    ppermute x4, starting transfers between devices, swap(): return (lax.ppermute(low, axis, lows), lax.ppermute(high, axis, highs))  8.28 us
    pallas_call x1, Pallas kernels, body(): pl.pallas_call(functools.partial(lists_kernel, chunks, tile_x, tile_y, sl...  7.82 us
    ppermute x3, starting transfers between devices, body(): lax.ppermute(coarse, 'gy', [(i, i ^ d) for i in range(chunks)])  3.55 us
    pallas_call x1, Pallas kernels, body(): pl.pallas_call(functools.partial(local_kernel, tile_x, tile_y), name='loc...  2.83 us
    ppermute x3, waiting for transfers between devices, body(): lax.ppermute(coarse, 'gy', [(i, i ^ d) for i in range(chunks)])  1.87 us
    pallas_call x1, Pallas kernels, body(): pl.pallas_call(functools.partial(live_kernel, tile_x, tile_y), name='live...  1.61 us
    pallas_call x1, Pallas kernels, body(): pl.pallas_call(functools.partial(order_kernel, chunks, kinds, parents_x,...  1.02 us
    pallas_call x1, Pallas kernels, body(): pl.pallas_call(functools.partial(halos_kernel, tile_x, tile_y), name='hal...  0.83 us
  transfers between devices with their start and end apart: 7, of which 2 were waited for; matrix products, arithmetic and copies ran while one was open for 0% of the time, Pallas kernels for 19%

profile of v8, /device:TPU:0, one launch (start us, length us, event | category | flops | bytes accessed | tf_op | source)
XLA Modules:
  0.0 28.8 jit_solution(13099316524320186792)
XLA Ops:
  0.0 0.0 copy-start
  0.0 0.0 copy-start.1
  0.0 1.6 %live.1 = (bf16[1024,256]{1,0:T(8,128)(2,1)S(1)}, f32[1024,128]{1,0:T(8,128)S(1)}, bf16[64,256]{1,0:T(8,128)(2,1)S(1)}, bf16[64,256]{1,0:T(8,128)(2,1)S(1)}, bf1...) custom-call(bf16[2048,128]{1,0:T(8,128)(2,1)} %bitcast.22, s32[32,32]{1,0:T(8,128)} %counts_hbm.1, ...), custom_call_target="tpu_custom_call" | custom-call | flops 209715200 | bytes 3145728 | tf_op jit(solution)/shard_map/live/pallas_call | solution.py:485
  1.6 3.0 %collective-permute-start.3 = (bf16[64,256]{1,0:T(8,128)(2,1)S(1)}, bf16[64,256]{1,0:T(8,128)(2,1)S(1)}, u32[]{:S(2)}, u32[]{:S(2)}) collective-permute-start(bf16[64,256]{1,0:T(8,128)(2,1)S(1)} %get-tuple-element.29), channel_id=1, source_target_pairs={{0,1},{1,0},{2,3},{3,2},{4,5},{5,4},{6,7},{7,6},{8,9},{9,8},{10,11... | collective-permute-start | bytes 98312 | tf_op jit(solution)/shard_map/ppermute | solution.py:465
  4.6 1.5 %collective-permute-start.4 = (bf16[64,256]{1,0:T(8,128)(2,1)S(1)}, bf16[64,256]{1,0:T(8,128)(2,1)S(1)}, u32[]{:S(2)}, u32[]{:S(2)}) collective-permute-start(bf16[64,256]{1,0:T(8,128)(2,1)S(1)} %get-tuple-element.30), channel_id=1, source_target_pairs={{0,3},{1,2},{2,1},{3,0},{4,7},{5,6},{6,5},{7,4},{8,11},{9,10},{10,... | collective-permute-start | bytes 98312 | tf_op jit(solution)/shard_map/ppermute | solution.py:465
  6.1 0.8 %parents.1 = (bf16[1024,128]{1,0:T(8,128)(2,1)S(1)}, f32[3,1536,128]{2,1,0:T(8,128)S(1)}) custom-call(bf16[1024,256]{1,0:T(8,128)(2,1)S(1)} %get-tuple-element.37.live_ref, bf16[256,256]{1,0:T(8,128)(2,1)S(1)} %get-tuple-element.26.agg_ref, bf16[1024,512]{1,0:T(8,128)(2,1)S(1)} %get-tuple-element.27.up_ref), custom_call_target="tpu_custom_call" | custom-call | flops 419430400 | bytes 3145728 | tf_op jit(solution)/shard_map/parents/pallas_call | solution.py:510
  6.9 1.5 %collective-permute-start = (bf16[1024,128]{1,0:T(8,128)(2,1)S(1)}, bf16[1024,128]{1,0:T(8,128)(2,1)S(1)}, u32[]{:S(2)}, u32[]{:S(2)}) collective-permute-start(bf16[1024,128]{1,0:T(8,128)(2,1)S(1)} %get-tuple-element.28.refs_0_), channel_id=1, source_target_pairs={{0,3},{1,2},{2,1},{3,0},{4,7},{5,6},{6,5},{7,4},{8,11},{9,10},{10,... | collective-permute-start | bytes 786440 | tf_op jit(solution)/shard_map/ppermute | solution.py:528
  8.4 0.1 collective-permute-start.1
  8.5 1.9 %collective-permute-start.2 = (bf16[1024,128]{1,0:T(8,128)(2,1)S(1)}, bf16[1024,128]{1,0:T(8,128)(2,1)S(1)}, u32[]{:S(2)}, u32[]{:S(2)}) collective-permute-start(bf16[1024,128]{1,0:T(8,128)(2,1)S(1)} %get-tuple-element.28.refs_0_), channel_id=1, source_target_pairs={{0,2},{1,3},{2,0},{3,1},{4,6},{5,7},{6,4},{7,5},{8,10},{9,11},{10,... | collective-permute-start | bytes 786440 | tf_op jit(solution)/shard_map/ppermute | solution.py:528
  10.4 0.0 collective-permute-done.3.inner_ref.inner_y
  10.4 0.0 collective-permute-done.4.outer_ref.outer_y
  10.5 0.1 collective-permute-start.5
  10.6 3.7 %collective-permute-start.6 = (bf16[80,256]{1,0:T(8,128)(2,1)S(1)}, bf16[80,256]{1,0:T(8,128)(2,1)S(1)}, u32[]{:S(2)}, u32[]{:S(2)}) collective-permute-start(bf16[80,256]{1,0:T(8,128)(2,1)S(1)} %get-tuple-element.36), channel_id=1, source_target_pairs={{0,28},{4,8},{8,4},{12,16},{16,12},{20,24},{24,20},{28,0},{1,29},{... | collective-permute-start | bytes 122888 | tf_op jit(solution)/shard_map/ppermute | solution.py:465
  14.3 0.0 copy-done
  14.3 0.0 copy-done.1
  14.3 0.0 copy-start.2
  14.3 0.0 copy-start.3
  14.3 0.0 copy-start.4
  14.3 0.0 copy-start.6
  14.3 2.8 %local.1 = (f32[2,1024,128]{2,1,0:T(8,128)S(1)}, f32[2,1024,128]{2,1,0:T(8,128)S(1)}) custom-call(bf16[1024,256]{1,0:T(8,128)(2,1)S(1)} %get-tuple-element.37.live_ref, f32[3,1536,128]{2,1,0:T(8,128)S(1)} %get-tuple-element.38.pats, bf16[3,768,256]{2,1,0:T(8,128)(2,1)S(1)} %bitcast.13, f32[32,128]{1,0:T(8,128)S(1)} %bitcast.15), custom_call_target="tpu_custom_call" | custom-call | flops 4194304000 | bytes 5242880 | tf_op jit(solution)/shard_map/local/pallas_call | solution.py:550
  17.2 0.0 copy-done.2
  17.2 0.0 copy-done.3
  17.2 0.0 copy-done.4
  17.2 0.0 copy-done.6
  17.2 1.0 %order.1 = (s32[72,128]{1,0:T(8,128)S(1)}, bf16[256,256]{1,0:T(8,128)(2,1)S(1)}, f32[520,128]{1,0:T(8,128)S(1)}) custom-call(s32[256,16]{1,0:T(8,128)S(1)} %bitcast.17, s32[256,16]{1,0:T(8,128)S(1)} %bitcast.18, s32[16,16]{1,0:T(8,128)S(1)} %copy-done.6, f32[256,128]{1,0:T(8,128)S(1)} %bitcast.19), custom_call_target="tpu_custom_call" | custom-call | flops 629145600 | bytes 1048576 | tf_op jit(solution)/shard_map/order/pallas_call | solution.py:584
  18.2 0.0 copy-start.5
  18.2 0.0 collective-permute-done.5.inner_x
  18.2 0.0 collective-permute-done.6.outer_x
  18.2 0.8 %halos.1 = (f32[2,4,256,128]{3,2,1,0:T(8,128)S(1)}, f32[2,4,256,128]{3,2,1,0:T(8,128)S(1)}, f32[4,256,128]{2,1,0:T(8,128)S(1)}) custom-call(bf16[64,256]{1,0:T(8,128)(2,1)S(1)} %collective-permute-done.3.inner_ref.inner_y, bf16[64,256]{1,0:T(8,128)(2,1)S(1)} %collective-permute-done.4.outer_ref.outer_y, bf16[80,256]{1,0:T(8,128)(2,1)S(1)} %collective-permute-done.5.inner_x, ...), custom_call_target="tpu_custom_call" | custom-call | flops 209715200 | bytes 5242880 | tf_op jit(solution)/shard_map/halos/pallas_call | solution.py:567
  19.1 0.0 collective-permute-done.refs_1_
  19.1 1.1 %collective-permute-done.1.refs_2_ = bf16[1024,128]{1,0:T(8,128)(2,1)S(1)} collective-permute-done((bf16[1024,128]{1,0:T(8,128)(2,1)S(1)}, bf16[1024,128]{1,0:T(8,128)(2,1)S(1)}, u32[]{:S(2)}, u32[]{:S(2)}) %collective-permute-start.1) | collective-permute-done | bytes 262176 | tf_op jit(solution)/shard_map/ppermute | solution.py:528
  20.2 0.7 %collective-permute-done.2.refs_3_ = bf16[1024,128]{1,0:T(8,128)(2,1)S(1)} collective-permute-done((bf16[1024,128]{1,0:T(8,128)(2,1)S(1)}, bf16[1024,128]{1,0:T(8,128)(2,1)S(1)}, u32[]{:S(2)}, u32[]{:S(2)}) %collective-permute-start.2) | collective-permute-done | bytes 262176 | tf_op jit(solution)/shard_map/ppermute | solution.py:528
  21.0 0.0 copy-done.5
  21.0 7.8 %lists.1 = f32[2048,128]{1,0:T(8,128)} custom-call(bf16[1024,128]{1,0:T(8,128)(2,1)S(1)} %get-tuple-element.28.refs_0_, bf16[1024,128]{1,0:T(8,128)(2,1)S(1)} %collective-permute-done.refs_1_, bf16[1024,128]{1,0:T(8,128)(2,1)S(1)} %collective-permute-done.1.refs_2_, bf16[1024,128]{1,0:T(8,128)(2,1)S(1)} %collective-permute-done.2.refs_3_, ...), custom_call_target="tpu_custom_call" | custom-call | flops 4194304000 | bytes 8388608 | tf_op jit(solution)/shard_map/lists/pallas_call | solution.py:598
  (1 shorter events, 0.0 us)
Async XLA Ops:
  0.0 14.3 %copy-start = (bf16[9,256,256]{2,1,0:T(8,128)(2,1)S(1)}, bf16[9,256,256]{2,1,0:T(8,128)(2,1)}, u32[]{:S(2)}) copy-start(bf16[9,256,256]{2,1,0:T(8,128)(2,1)} %param.15) | copy-start | bytes 3538948
  0.0 14.3 %copy-start.1 = (f32[16,2,128]{2,1,0:T(2,128)S(1)}, f32[16,2,128]{2,1,0:T(2,128)}, u32[]{:S(2)}) copy-start(f32[16,2,128]{2,1,0:T(2,128)} %param.16) | copy-start | bytes 49156
  1.6 8.8 %collective-permute-start.3 = (bf16[64,256]{1,0:T(8,128)(2,1)S(1)}, bf16[64,256]{1,0:T(8,128)(2,1)S(1)}, u32[]{:S(2)}, u32[]{:S(2)}) collective-permute-start(bf16[64,256]{1,0:T(8,128)(2,1)S(1)} %get-tuple-element.29), channel_id=1, source_target_pairs={{0,1},{1,0},{2,3},{3,2},{4,5},{5,4},{6,7},{7,6},{8,9},{9,8},{10,11... | collective-permute-start | bytes 98312 | tf_op jit(solution)/shard_map/ppermute | solution.py:465
  4.6 5.8 %collective-permute-start.4 = (bf16[64,256]{1,0:T(8,128)(2,1)S(1)}, bf16[64,256]{1,0:T(8,128)(2,1)S(1)}, u32[]{:S(2)}, u32[]{:S(2)}) collective-permute-start(bf16[64,256]{1,0:T(8,128)(2,1)S(1)} %get-tuple-element.30), channel_id=1, source_target_pairs={{0,3},{1,2},{2,1},{3,0},{4,7},{5,6},{6,5},{7,4},{8,11},{9,10},{10,... | collective-permute-start | bytes 98312 | tf_op jit(solution)/shard_map/ppermute | solution.py:465
  6.9 12.2 %collective-permute-start = (bf16[1024,128]{1,0:T(8,128)(2,1)S(1)}, bf16[1024,128]{1,0:T(8,128)(2,1)S(1)}, u32[]{:S(2)}, u32[]{:S(2)}) collective-permute-start(bf16[1024,128]{1,0:T(8,128)(2,1)S(1)} %get-tuple-element.28.refs_0_), channel_id=1, source_target_pairs={{0,3},{1,2},{2,1},{3,0},{4,7},{5,6},{6,5},{7,4},{8,11},{9,10},{10,... | collective-permute-start | bytes 786440 | tf_op jit(solution)/shard_map/ppermute | solution.py:528
  8.4 11.8 %collective-permute-start.1 = (bf16[1024,128]{1,0:T(8,128)(2,1)S(1)}, bf16[1024,128]{1,0:T(8,128)(2,1)S(1)}, u32[]{:S(2)}, u32[]{:S(2)}) collective-permute-start(bf16[1024,128]{1,0:T(8,128)(2,1)S(1)} %get-tuple-element.28.refs_0_), channel_id=1, source_target_pairs={{0,1},{1,0},{2,3},{3,2},{4,5},{5,4},{6,7},{7,6},{8,9},{9,8},{10,11... | collective-permute-start | bytes 786440 | tf_op jit(solution)/shard_map/ppermute | solution.py:528
  8.5 12.4 %collective-permute-start.2 = (bf16[1024,128]{1,0:T(8,128)(2,1)S(1)}, bf16[1024,128]{1,0:T(8,128)(2,1)S(1)}, u32[]{:S(2)}, u32[]{:S(2)}) collective-permute-start(bf16[1024,128]{1,0:T(8,128)(2,1)S(1)} %get-tuple-element.28.refs_0_), channel_id=1, source_target_pairs={{0,2},{1,3},{2,0},{3,1},{4,6},{5,7},{6,4},{7,5},{8,10},{9,11},{10,... | collective-permute-start | bytes 786440 | tf_op jit(solution)/shard_map/ppermute | solution.py:528
  10.5 7.7 %collective-permute-start.5 = (bf16[80,256]{1,0:T(8,128)(2,1)S(1)}, bf16[80,256]{1,0:T(8,128)(2,1)S(1)}, u32[]{:S(2)}, u32[]{:S(2)}) collective-permute-start(bf16[80,256]{1,0:T(8,128)(2,1)S(1)} %get-tuple-element.31), channel_id=1, source_target_pairs={{0,4},{4,0},{8,12},{12,8},{16,20},{20,16},{24,28},{28,24},{1,5},{5... | collective-permute-start | bytes 122888 | tf_op jit(solution)/shard_map/ppermute | solution.py:465
  10.6 7.7 %collective-permute-start.6 = (bf16[80,256]{1,0:T(8,128)(2,1)S(1)}, bf16[80,256]{1,0:T(8,128)(2,1)S(1)}, u32[]{:S(2)}, u32[]{:S(2)}) collective-permute-start(bf16[80,256]{1,0:T(8,128)(2,1)S(1)} %get-tuple-element.36), channel_id=1, source_target_pairs={{0,28},{4,8},{8,4},{12,16},{16,12},{20,24},{24,20},{28,0},{1,29},{... | collective-permute-start | bytes 122888 | tf_op jit(solution)/shard_map/ppermute | solution.py:465
  14.3 2.9 %copy-start.2 = (s32[16,16,16]{2,1,0:T(8,128)S(1)}, s32[16,16,16]{2,1,0:T(8,128)}, u32[]{:S(2)}) copy-start(s32[16,16,16]{2,1,0:T(8,128)} %param.18) | copy-start | bytes 49156
  14.3 2.9 %copy-start.3 = (s32[16,16,16]{2,1,0:T(8,128)S(1)}, s32[16,16,16]{2,1,0:T(8,128)}, u32[]{:S(2)}) copy-start(s32[16,16,16]{2,1,0:T(8,128)} %param.19) | copy-start | bytes 49156
  14.3 2.9 %copy-start.4 = (f32[64,2,256]{2,1,0:T(2,128)S(1)}, f32[64,2,256]{2,1,0:T(2,128)}, u32[]{:S(2)}) copy-start(f32[64,2,256]{2,1,0:T(2,128)} %param.21) | copy-start | bytes 393220
  14.3 2.9 %copy-start.6 = (s32[16,16]{1,0:T(8,128)S(1)}, s32[16,16]{1,0:T(8,128)}, u32[]{:S(2)}) copy-start(s32[16,16]{1,0:T(8,128)} %count_ref) | copy-start | bytes 3076
  18.2 2.7 %copy-start.5 = (bf16[256,256]{1,0:T(8,128)(2,1)S(1)}, bf16[256,256]{1,0:T(8,128)(2,1)}, u32[]{:S(2)}) copy-start(bf16[256,256]{1,0:T(8,128)(2,1)} %refs_10_.1) | copy-start | bytes 393220

commit v9 on v8

--- a/solution.py
+++ b/solution.py
@@ -321,7 +321,8 @@
             add_row(field_ref, part, tile_x - 1 if end else 0, value[:, part * lanes : (part + 1) * lanes])
 
 
-GROUP = 8
+ROW = 8
+GROUP = 16
 
 
 def order_kernel(
@@ -333,7 +334,7 @@
     table8[8 * kinds : 8 * kinds + 8, :] = jnp.zeros((8, width), F32)
     parents = parents_x * parents_y
     slots = list_ref.shape[1]
-    groups = parents // GROUP
+    groups = parents // ROW
     lanes = at_ref.shape[1]
     down = lax.broadcasted_iota(jnp.int32, (parents, parents), 0)
     along = lax.broadcasted_iota(jnp.int32, (parents, parents), 1)
@@ -358,12 +359,12 @@
         for n, value in enumerate((source // 256, source % 256, kind))
     ]
     values = (values[0] + values[1] + values[2]).astype(BF16)
-    wanted = GROUP * (down % groups) + down // groups
+    wanted = ROW * (down % groups) + down // groups
     moved = mm(jnp.where(wanted.astype(F32) == rank, 1.0, 0.0).astype(BF16), values).astype(BF16)
-    moved = jnp.concatenate([moved[k * groups : (k + 1) * groups] for k in range(GROUP)], axis=1)
+    moved = jnp.concatenate([moved[k * groups : (k + 1) * groups] for k in range(ROW)], axis=1)
     totals = []
-    from_lane = lax.broadcasted_iota(jnp.int32, (GROUP * lanes, lanes), 0)
-    to_lane = lax.broadcasted_iota(jnp.int32, (GROUP * lanes, lanes), 1)
+    from_lane = lax.broadcasted_iota(jnp.int32, (ROW * lanes, lanes), 0)
+    to_lane = lax.broadcasted_iota(jnp.int32, (ROW * lanes, lanes), 1)
     for n in range(3):
         spread = from_lane == (to_lane // slots) * lanes + n * slots + to_lane % slots
         totals.append(mm(moved, jnp.where(spread, 1.0, 0.0).astype(BF16)).astype(jnp.int32))
@@ -377,7 +378,7 @@
 def lists_kernel(chunks, tile_x, tile_y, slots, *refs):
     sources = refs[:chunks]
     (at_any, table8, back_ref, kept_ref, lower_ref, near_ref, recv_ref, down_hbm, out_hbm,
-     cells, sums, at, down_ref, total_ref, out_ref, sems) = refs[chunks:]
+     cells, sums, lines, at, down_ref, total_ref, out_ref, sems) = refs[chunks:]
     parents_x, parents_y = tile_x // 2, tile_y // 2
     parents = parents_x * parents_y
     lanes = table8.shape[1]
@@ -397,13 +398,10 @@
         pairs[c * count : (c + 1) * count, 0] = jnp.where(first_half, rows, turned)
         pairs[c * count : (c + 1) * count, 1] = jnp.where(first_half, turned, rows)
     loads[0].wait()
-    line = lax.broadcasted_iota(jnp.int32, (8, lanes), 0)
-    upper, real = line < 4, line % 4 < 2
 
     def step(length, n, carry):
         first = n * (GROUP * slots)
-        second = first + groups * GROUP * slots
-        before = None
+        second = first + parents * slots
         for k in range(GROUP):
             total = [None, None]
             for s in range(length):
@@ -412,23 +410,24 @@
                 term = cells[pl.ds(source, 8), :] * table8[pl.ds(kind, 8), :]
                 total[s % 2] = term if total[s % 2] is None else total[s % 2] + term
             total = total[0] + total[1] if length else jnp.zeros((8, lanes), F32)
-            if k % 2:
-                with_real = jnp.where(upper, before, pltpu.roll(total, 4, axis=0))
-                with_imag = jnp.where(upper, pltpu.roll(before, 4, axis=0), total)
-                turned = jnp.where(real, -pltpu.roll(with_imag, 6, axis=0), pltpu.roll(with_imag, 2, axis=0))
-                tile = pl.multiple_of(n * (GROUP * 4) + (k // 2) * 8, 8)
-                sums[pl.ds(tile, 8), :] = with_real + turned
-            before = total
+            sums[pl.ds(pl.multiple_of((n * GROUP + k) * 8, 8), 8), :] = total
         return carry
 
     start = 0
     for j, length in enumerate(range(slots, 0, -2)):
-        end = at[2 * groups * GROUP * slots + j]
+        end = at[2 * parents * slots + j]
         lax.fori_loop(start, end, functools.partial(step, length), 0)
         start = end
     lax.fori_loop(start, groups, functools.partial(step, 0), 0)
 
-    ordered = [sums[pl.ds(place, parents, stride=4), :].astype(BF16) for place in range(4)]
+    raw = sums[...].reshape(count, 2, 8, lanes)
+    one, other = raw[:, 0], raw[:, 1]
+    with_real = jnp.where(first_half, one, pltpu.roll(other, 4, axis=1))
+    with_imag = jnp.where(first_half, pltpu.roll(one, 4, axis=1), other)
+    real = lax.broadcasted_iota(jnp.int32, (count, 8, lanes), 1) % 4 < 2
+    turned = jnp.where(real, -pltpu.roll(with_imag, 6, axis=1), pltpu.roll(with_imag, 2, axis=1))
+    lines[...] = (with_real + turned).reshape(4 * parents, lanes)
+    ordered = [lines[pl.ds(place, parents, stride=4), :].astype(BF16) for place in range(4)]
     incoming = mm(back_ref[...], jnp.concatenate(ordered, axis=1)).astype(BF16)
     loads[1].wait()
     for child in range(4):
@@ -458,7 +457,19 @@
         store.wait()
 
 
-def swap(low, high, axis):
+def swap(low, high, axis, other):
+    count, breadth = lax.axis_size(axis), lax.axis_size(other)
+    lows = [(i, i ^ 1) for i in range(count)]
+    highs = []
+    for i in range(count):
+        for j in range(breadth):
+            end = i in (0, count - 1)
+            target = (i, j ^ 1) if end else (((i + 1) ^ 1) - 1, j)
+            highs.append((i * breadth + j, target[0] * breadth + target[1]))
+    return lax.ppermute(low, axis, lows), lax.ppermute(high, (axis, other), highs)
+
+
+def swap_rows(low, high, axis):
     count = lax.axis_size(axis)
     lows = [(i, i ^ 1) for i in range(count)]
     highs = [(i, (((i + 1) % count ^ 1) - 1) % count) for i in range(count)]
@@ -523,7 +534,7 @@
         compiler_params=params(10),
         cost_estimate=cost(200 * MIB, 3 * MIB),
     )(live, agg_near, up_near)
-    inner_y, outer_y = swap(low, high, "gy")
+    inner_y, outer_y = swap_rows(low, high, "gy")
     sources = [coarse] + [
         lax.ppermute(coarse, "gy", [(i, i ^ d) for i in range(chunks)])
         for d in [chunks - 1] + list(range(1, chunks - 1))
@@ -541,7 +552,7 @@
         compiler_params=params(10),
         cost_estimate=cost(1 * MIB, MIB),
     )(live, inner_y, outer_y)
-    inner_x, outer_x = swap(low, high, "gx")
+    inner_x, outer_x = swap(low, high, "gx", "gy")
     live, coarse_count, _ = lax.optimization_barrier((live, coarse_count, low))
 
     near_rows = near_blocks.reshape(3, 6 * lanes, 2 * lanes)
@@ -580,12 +591,11 @@
     )(inner_y, outer_y, inner_x, outer_x, agg_near, near_rows, low_rows, lower, near, kept)
 
     table = up_translator.reshape(kinds, 2, 2, half // 2).transpose(0, 2, 1, 3).reshape(4 * kinds, half // 2)
-    groups = parents // GROUP
     at, back, table8 = pl.pallas_call(
         functools.partial(order_kernel, chunks, kinds, parents_x, parents_y),
         name="order",
         out_shape=[
-            jax.ShapeDtypeStruct((2 * groups + 8, GROUP * slots), jnp.int32),
+            jax.ShapeDtypeStruct((2 * parents // ROW + 8, ROW * slots), jnp.int32),
             jax.ShapeDtypeStruct((parents, parents), BF16),
             jax.ShapeDtypeStruct((8 * kinds + 8, half // 2), F32),
         ],
@@ -603,6 +613,7 @@
         out_specs=in_hbm,
         scratch_shapes=[
             pltpu.VMEM((chunks * parents * 8, wide // 4), F32),
+            pltpu.VMEM((8 * parents, wide // 4), F32),
             pltpu.VMEM((4 * parents, wide // 4), F32),
             pltpu.SMEM(at.shape, jnp.int32),
             pltpu.VMEM((4, wide, 2 * lanes), BF16),

time: 28.8 us -> 28.8 us (level)
  waiting for transfers between devices: 1.88 us -> 4.61 us
  starting transfers between devices: 11.8 us -> 9.68 us
  Pallas kernels: 14.9 us -> 14.2 us
    ppermute x4, waiting for transfers between devices: 0.01 us -> 4.6 us  [the longest x1 4.59 us: swap(): lax.ppermute(high, (axis, other), highs)]
    ppermute x4, starting transfers between devices: 8.28 us -> 6.13 us  [the longest x2 4.49 us: swap_rows(): return (lax.ppermute(low, axis, lows), lax.ppermute(high, axis, highs))]
    ppermute x3, waiting for transfers between devices: 1.87 us -> 0.01 us  [body(): lax.ppermute(coarse, 'gy', [(i, i ^ d) for i in range(chunks)])]
    pallas_call x1, Pallas kernels: 7.82 us -> 7.08 us  [body(): pl.pallas_call(functools.partial(lists_kernel, chunks, tile_x, tile_y, sl...]
  transfers between devices with their start and end apart: 7 -> 7, of which waited for: 2 -> 1; matrix products, arithmetic and copies ran while one was open for 0% -> 0% of each run, Pallas kernels for 19% -> 19%
where the time goes in v9:
time: 28.8 us; the launch traced here: 28.6 us
  Pallas kernels  14.2 us (49%)
  starting transfers between devices  9.68 us (34%)
  waiting for transfers between devices  4.61 us (16%)
    pallas_call x1, Pallas kernels, body(): pl.pallas_call(functools.partial(lists_kernel, chunks, tile_x, tile_y, sl...  7.08 us
    ppermute x1, waiting for transfers between devices, swap(): lax.ppermute(high, (axis, other), highs)  4.59 us
    ppermute x2, starting transfers between devices, swap_rows(): return (lax.ppermute(low, axis, lows), lax.ppermute(high, axis, highs))  4.49 us
    ppermute x3, starting transfers between devices, body(): lax.ppermute(coarse, 'gy', [(i, i ^ d) for i in range(chunks)])  3.55 us
    pallas_call x1, Pallas kernels, body(): pl.pallas_call(functools.partial(local_kernel, tile_x, tile_y), name='loc...  2.82 us
    pallas_call x1, Pallas kernels, body(): pl.pallas_call(functools.partial(live_kernel, tile_x, tile_y), name='live...  1.61 us
    ppermute x1, starting transfers between devices, swap(): lax.ppermute(high, (axis, other), highs)  1.56 us
    pallas_call x1, Pallas kernels, body(): pl.pallas_call(functools.partial(order_kernel, chunks, kinds, parents_x,...  1.02 us
  transfers between devices with their start and end apart: 7, of which 1 were waited for; matrix products, arithmetic and copies ran while one was open for 0% of the time, Pallas kernels for 19%

profile of v9, /device:TPU:0, one launch (start us, length us, event | category | flops | bytes accessed | tf_op | source)
XLA Modules:
  0.0 28.6 jit_solution(11782615819653883278)
XLA Ops:
  0.0 0.0 copy-start
  0.0 0.0 copy-start.1
  0.0 1.6 %live.1 = (bf16[1024,256]{1,0:T(8,128)(2,1)S(1)}, f32[1024,128]{1,0:T(8,128)S(1)}, bf16[64,256]{1,0:T(8,128)(2,1)S(1)}, bf16[64,256]{1,0:T(8,128)(2,1)S(1)}, bf1...) custom-call(bf16[2048,128]{1,0:T(8,128)(2,1)} %bitcast.22, s32[32,32]{1,0:T(8,128)} %counts_hbm.1, ...), custom_call_target="tpu_custom_call" | custom-call | flops 209715200 | bytes 3145728 | tf_op jit(solution)/shard_map/live/pallas_call | solution.py:496
  1.6 3.0 %collective-permute-start.3 = (bf16[64,256]{1,0:T(8,128)(2,1)S(1)}, bf16[64,256]{1,0:T(8,128)(2,1)S(1)}, u32[]{:S(2)}, u32[]{:S(2)}) collective-permute-start(bf16[64,256]{1,0:T(8,128)(2,1)S(1)} %get-tuple-element.29), channel_id=1, source_target_pairs={{0,1},{1,0},{2,3},{3,2},{4,5},{5,4},{6,7},{7,6},{8,9},{9,8},{10,11... | collective-permute-start | bytes 98312 | tf_op jit(solution)/shard_map/ppermute | solution.py:476
  4.6 1.5 %collective-permute-start.4 = (bf16[64,256]{1,0:T(8,128)(2,1)S(1)}, bf16[64,256]{1,0:T(8,128)(2,1)S(1)}, u32[]{:S(2)}, u32[]{:S(2)}) collective-permute-start(bf16[64,256]{1,0:T(8,128)(2,1)S(1)} %get-tuple-element.30), channel_id=1, source_target_pairs={{0,3},{1,2},{2,1},{3,0},{4,7},{5,6},{6,5},{7,4},{8,11},{9,10},{10,... | collective-permute-start | bytes 98312 | tf_op jit(solution)/shard_map/ppermute | solution.py:476
  6.1 0.8 %parents.1 = (bf16[1024,128]{1,0:T(8,128)(2,1)S(1)}, f32[3,1536,128]{2,1,0:T(8,128)S(1)}) custom-call(bf16[1024,256]{1,0:T(8,128)(2,1)S(1)} %get-tuple-element.37.live_ref, bf16[256,256]{1,0:T(8,128)(2,1)S(1)} %get-tuple-element.26.agg_ref, bf16[1024,512]{1,0:T(8,128)(2,1)S(1)} %get-tuple-element.27.up_ref), custom_call_target="tpu_custom_call" | custom-call | flops 419430400 | bytes 3145728 | tf_op jit(solution)/shard_map/parents/pallas_call | solution.py:521
  6.9 1.5 %collective-permute-start = (bf16[1024,128]{1,0:T(8,128)(2,1)S(1)}, bf16[1024,128]{1,0:T(8,128)(2,1)S(1)}, u32[]{:S(2)}, u32[]{:S(2)}) collective-permute-start(bf16[1024,128]{1,0:T(8,128)(2,1)S(1)} %get-tuple-element.28.refs_0_), channel_id=1, source_target_pairs={{0,3},{1,2},{2,1},{3,0},{4,7},{5,6},{6,5},{7,4},{8,11},{9,10},{10,... | collective-permute-start | bytes 786440 | tf_op jit(solution)/shard_map/ppermute | solution.py:539
  8.4 0.1 collective-permute-start.1
  8.5 1.9 %collective-permute-start.2 = (bf16[1024,128]{1,0:T(8,128)(2,1)S(1)}, bf16[1024,128]{1,0:T(8,128)(2,1)S(1)}, u32[]{:S(2)}, u32[]{:S(2)}) collective-permute-start(bf16[1024,128]{1,0:T(8,128)(2,1)S(1)} %get-tuple-element.28.refs_0_), channel_id=1, source_target_pairs={{0,2},{1,3},{2,0},{3,1},{4,6},{5,7},{6,4},{7,5},{8,10},{9,11},{10,... | collective-permute-start | bytes 786440 | tf_op jit(solution)/shard_map/ppermute | solution.py:539
  10.4 0.0 collective-permute-done.3.inner_ref.inner_y
  10.4 0.0 collective-permute-done.4.outer_ref.outer_y
  10.5 0.1 collective-permute-start.5
  10.6 1.6 %collective-permute-start.6 = (bf16[80,256]{1,0:T(8,128)(2,1)S(1)}, bf16[80,256]{1,0:T(8,128)(2,1)S(1)}, u32[]{:S(2)}, u32[]{:S(2)}) collective-permute-start(bf16[80,256]{1,0:T(8,128)(2,1)S(1)} %get-tuple-element.36), channel_id=1, source_target_pairs={{0,1},{1,0},{2,3},{3,2},{4,8},{5,9},{6,10},{7,11},{8,4},{9,5},{10,... | collective-permute-start | bytes 122888 | tf_op jit(solution)/shard_map/ppermute | solution.py:469
  12.1 0.0 copy-done
  12.1 0.0 copy-done.1
  12.1 0.0 copy-start.2
  12.1 0.0 copy-start.3
  12.1 0.0 copy-start.4
  12.2 0.0 copy-start.6
  12.2 2.8 %local.1 = (f32[2,1024,128]{2,1,0:T(8,128)S(1)}, f32[2,1024,128]{2,1,0:T(8,128)S(1)}) custom-call(bf16[1024,256]{1,0:T(8,128)(2,1)S(1)} %get-tuple-element.37.live_ref, f32[3,1536,128]{2,1,0:T(8,128)S(1)} %get-tuple-element.38.pats, bf16[3,768,256]{2,1,0:T(8,128)(2,1)S(1)} %bitcast.13, f32[32,128]{1,0:T(8,128)S(1)} %bitcast.15), custom_call_target="tpu_custom_call" | custom-call | flops 4194304000 | bytes 5242880 | tf_op jit(solution)/shard_map/local/pallas_call | solution.py:561
  15.0 0.0 copy-done.2
  15.0 0.0 copy-done.3
  15.0 0.0 copy-done.4
  15.0 0.0 copy-done.6
  15.0 1.0 %order.1 = (s32[72,128]{1,0:T(8,128)S(1)}, bf16[256,256]{1,0:T(8,128)(2,1)S(1)}, f32[520,128]{1,0:T(8,128)S(1)}) custom-call(s32[256,16]{1,0:T(8,128)S(1)} %bitcast.17, s32[256,16]{1,0:T(8,128)S(1)} %bitcast.18, s32[16,16]{1,0:T(8,128)S(1)} %copy-done.6, f32[256,128]{1,0:T(8,128)S(1)} %bitcast.19), custom_call_target="tpu_custom_call" | custom-call | flops 629145600 | bytes 1048576 | tf_op jit(solution)/shard_map/order/pallas_call | solution.py:594
  16.1 0.0 copy-start.5
  16.1 0.0 collective-permute-done.5.inner_x
  16.1 4.6 %collective-permute-done.6.outer_x = bf16[80,256]{1,0:T(8,128)(2,1)S(1)} collective-permute-done((bf16[80,256]{1,0:T(8,128)(2,1)S(1)}, bf16[80,256]{1,0:T(8,128)(2,1)S(1)}, u32[]{:S(2)}, u32[]{:S(2)}) %collective-permute-start.6) | collective-permute-done | bytes 40992 | tf_op jit(solution)/shard_map/ppermute | solution.py:469
  20.7 0.8 %halos.1 = (f32[2,4,256,128]{3,2,1,0:T(8,128)S(1)}, f32[2,4,256,128]{3,2,1,0:T(8,128)S(1)}, f32[4,256,128]{2,1,0:T(8,128)S(1)}) custom-call(bf16[64,256]{1,0:T(8,128)(2,1)S(1)} %collective-permute-done.3.inner_ref.inner_y, bf16[64,256]{1,0:T(8,128)(2,1)S(1)} %collective-permute-done.4.outer_ref.outer_y, bf16[80,256]{1,0:T(8,128)(2,1)S(1)} %collective-permute-done.5.inner_x, ...), custom_call_target="tpu_custom_call" | custom-call | flops 209715200 | bytes 5242880 | tf_op jit(solution)/shard_map/halos/pallas_call | solution.py:578
  21.5 0.0 collective-permute-done.refs_1_
  21.5 0.0 collective-permute-done.1.refs_2_
  21.5 0.0 collective-permute-done.2.refs_3_
  21.5 0.0 copy-done.5
  21.5 7.1 %lists.1 = f32[2048,128]{1,0:T(8,128)} custom-call(bf16[1024,128]{1,0:T(8,128)(2,1)S(1)} %get-tuple-element.28.refs_0_, bf16[1024,128]{1,0:T(8,128)(2,1)S(1)} %collective-permute-done.refs_1_, bf16[1024,128]{1,0:T(8,128)(2,1)S(1)} %collective-permute-done.1.refs_2_, bf16[1024,128]{1,0:T(8,128)(2,1)S(1)} %collective-permute-done.2.refs_3_, ...), custom_call_target="tpu_custom_call" | custom-call | flops 4194304000 | bytes 8388608 | tf_op jit(solution)/shard_map/lists/pallas_call | solution.py:608
  (1 shorter events, 0.0 us)
Async XLA Ops:
  0.0 12.1 %copy-start = (bf16[9,256,256]{2,1,0:T(8,128)(2,1)S(1)}, bf16[9,256,256]{2,1,0:T(8,128)(2,1)}, u32[]{:S(2)}) copy-start(bf16[9,256,256]{2,1,0:T(8,128)(2,1)} %param.15) | copy-start | bytes 3538948
  0.0 12.1 %copy-start.1 = (f32[16,2,128]{2,1,0:T(2,128)S(1)}, f32[16,2,128]{2,1,0:T(2,128)}, u32[]{:S(2)}) copy-start(f32[16,2,128]{2,1,0:T(2,128)} %param.16) | copy-start | bytes 49156
  1.6 8.8 %collective-permute-start.3 = (bf16[64,256]{1,0:T(8,128)(2,1)S(1)}, bf16[64,256]{1,0:T(8,128)(2,1)S(1)}, u32[]{:S(2)}, u32[]{:S(2)}) collective-permute-start(bf16[64,256]{1,0:T(8,128)(2,1)S(1)} %get-tuple-element.29), channel_id=1, source_target_pairs={{0,1},{1,0},{2,3},{3,2},{4,5},{5,4},{6,7},{7,6},{8,9},{9,8},{10,11... | collective-permute-start | bytes 98312 | tf_op jit(solution)/shard_map/ppermute | solution.py:476
  4.6 5.8 %collective-permute-start.4 = (bf16[64,256]{1,0:T(8,128)(2,1)S(1)}, bf16[64,256]{1,0:T(8,128)(2,1)S(1)}, u32[]{:S(2)}, u32[]{:S(2)}) collective-permute-start(bf16[64,256]{1,0:T(8,128)(2,1)S(1)} %get-tuple-element.30), channel_id=1, source_target_pairs={{0,3},{1,2},{2,1},{3,0},{4,7},{5,6},{6,5},{7,4},{8,11},{9,10},{10,... | collective-permute-start | bytes 98312 | tf_op jit(solution)/shard_map/ppermute | solution.py:476
  6.9 14.6 %collective-permute-start = (bf16[1024,128]{1,0:T(8,128)(2,1)S(1)}, bf16[1024,128]{1,0:T(8,128)(2,1)S(1)}, u32[]{:S(2)}, u32[]{:S(2)}) collective-permute-start(bf16[1024,128]{1,0:T(8,128)(2,1)S(1)} %get-tuple-element.28.refs_0_), channel_id=1, source_target_pairs={{0,3},{1,2},{2,1},{3,0},{4,7},{5,6},{6,5},{7,4},{8,11},{9,10},{10,... | collective-permute-start | bytes 786440 | tf_op jit(solution)/shard_map/ppermute | solution.py:539
  8.4 13.1 %collective-permute-start.1 = (bf16[1024,128]{1,0:T(8,128)(2,1)S(1)}, bf16[1024,128]{1,0:T(8,128)(2,1)S(1)}, u32[]{:S(2)}, u32[]{:S(2)}) collective-permute-start(bf16[1024,128]{1,0:T(8,128)(2,1)S(1)} %get-tuple-element.28.refs_0_), channel_id=1, source_target_pairs={{0,1},{1,0},{2,3},{3,2},{4,5},{5,4},{6,7},{7,6},{8,9},{9,8},{10,11... | collective-permute-start | bytes 786440 | tf_op jit(solution)/shard_map/ppermute | solution.py:539
  8.5 13.0 %collective-permute-start.2 = (bf16[1024,128]{1,0:T(8,128)(2,1)S(1)}, bf16[1024,128]{1,0:T(8,128)(2,1)S(1)}, u32[]{:S(2)}, u32[]{:S(2)}) collective-permute-start(bf16[1024,128]{1,0:T(8,128)(2,1)S(1)} %get-tuple-element.28.refs_0_), channel_id=1, source_target_pairs={{0,2},{1,3},{2,0},{3,1},{4,6},{5,7},{6,4},{7,5},{8,10},{9,11},{10,... | collective-permute-start | bytes 786440 | tf_op jit(solution)/shard_map/ppermute | solution.py:539
  10.5 5.6 %collective-permute-start.5 = (bf16[80,256]{1,0:T(8,128)(2,1)S(1)}, bf16[80,256]{1,0:T(8,128)(2,1)S(1)}, u32[]{:S(2)}, u32[]{:S(2)}) collective-permute-start(bf16[80,256]{1,0:T(8,128)(2,1)S(1)} %get-tuple-element.31), channel_id=1, source_target_pairs={{0,4},{4,0},{8,12},{12,8},{16,20},{20,16},{24,28},{28,24},{1,5},{5... | collective-permute-start | bytes 122888 | tf_op jit(solution)/shard_map/ppermute | solution.py:469
  10.6 10.1 %collective-permute-start.6 = (bf16[80,256]{1,0:T(8,128)(2,1)S(1)}, bf16[80,256]{1,0:T(8,128)(2,1)S(1)}, u32[]{:S(2)}, u32[]{:S(2)}) collective-permute-start(bf16[80,256]{1,0:T(8,128)(2,1)S(1)} %get-tuple-element.36), channel_id=1, source_target_pairs={{0,1},{1,0},{2,3},{3,2},{4,8},{5,9},{6,10},{7,11},{8,4},{9,5},{10,... | collective-permute-start | bytes 122888 | tf_op jit(solution)/shard_map/ppermute | solution.py:469
  12.1 2.9 %copy-start.2 = (s32[16,16,16]{2,1,0:T(8,128)S(1)}, s32[16,16,16]{2,1,0:T(8,128)}, u32[]{:S(2)}) copy-start(s32[16,16,16]{2,1,0:T(8,128)} %param.18) | copy-start | bytes 49156
  12.1 2.9 %copy-start.3 = (s32[16,16,16]{2,1,0:T(8,128)S(1)}, s32[16,16,16]{2,1,0:T(8,128)}, u32[]{:S(2)}) copy-start(s32[16,16,16]{2,1,0:T(8,128)} %param.19) | copy-start | bytes 49156
  12.1 2.9 %copy-start.4 = (f32[64,2,256]{2,1,0:T(2,128)S(1)}, f32[64,2,256]{2,1,0:T(2,128)}, u32[]{:S(2)}) copy-start(f32[64,2,256]{2,1,0:T(2,128)} %param.21) | copy-start | bytes 393220
  12.2 2.9 %copy-start.6 = (s32[16,16]{1,0:T(8,128)S(1)}, s32[16,16]{1,0:T(8,128)}, u32[]{:S(2)}) copy-start(s32[16,16]{1,0:T(8,128)} %count_ref) | copy-start | bytes 3076
  16.1 5.5 %copy-start.5 = (bf16[256,256]{1,0:T(8,128)(2,1)S(1)}, bf16[256,256]{1,0:T(8,128)(2,1)}, u32[]{:S(2)}) copy-start(bf16[256,256]{1,0:T(8,128)(2,1)} %refs_10_.1) | copy-start | bytes 393220

commit v10 on v9

--- a/solution.py
+++ b/solution.py
@@ -326,7 +326,7 @@
 
 
 def order_kernel(
-    chunks, kinds, parents_x, parents_y, list_ref, kind_ref, count_ref, table_ref, at_ref, back_ref, table8
+    chunks, kinds, parents_x, parents_y, list_ref, kind_ref, count_ref, table_ref, early_ref, late_ref, table8, words
 ):
     width = table_ref.shape[1]
     for place, row in enumerate((0, 2, 0, 2, 1, 3, 1, 3)):
@@ -335,73 +335,81 @@
     parents = parents_x * parents_y
     slots = list_ref.shape[1]
     groups = parents // ROW
-    lanes = at_ref.shape[1]
-    down = lax.broadcasted_iota(jnp.int32, (parents, parents), 0)
-    along = lax.broadcasted_iota(jnp.int32, (parents, parents), 1)
-    column = count_rows(count_ref, parents_x, parents_y, parents)
-    row = jnp.sum(jnp.where(down == along, column, 0.0), axis=0, keepdims=True)
-    before = (column > row) | ((column == row) & (down < along))
-    rank = jnp.sum(jnp.where(before, 1.0, 0.0), axis=0, keepdims=True)
-    after = (row > column) | ((row == column) & (along < down))
-    rank_down = jnp.sum(jnp.where(after, 1.0, 0.0), axis=1, keepdims=True)
-    back_ref[...] = jnp.where(along.astype(F32) == rank_down, 1.0, 0.0).astype(BF16)
-
+    lanes = early_ref.shape[1]
     across = parents_y * chunks
     entry = list_ref[...]
     line, place = entry // across, entry % across
-    source = ((place // parents_y) ^ lax.axis_index("gy")) * parents + line * parents_y + place % parents_y
-    used = lax.broadcasted_iota(jnp.int32, (parents, slots), 1).astype(F32) < column[:, :slots]
-    kind = jnp.where(used, kind_ref[...], kinds)
-    slot = lax.broadcasted_iota(jnp.int32, (slots, lanes), 0)
-    lane = lax.broadcasted_iota(jnp.int32, (slots, lanes), 1)
-    values = [
-        mm(value.astype(F32).astype(BF16), jnp.where(lane == slot + n * slots, 1.0, 0.0).astype(BF16))
-        for n, value in enumerate((source // 256, source % 256, kind))
-    ]
-    values = (values[0] + values[1] + values[2]).astype(BF16)
-    wanted = ROW * (down % groups) + down // groups
-    moved = mm(jnp.where(wanted.astype(F32) == rank, 1.0, 0.0).astype(BF16), values).astype(BF16)
-    moved = jnp.concatenate([moved[k * groups : (k + 1) * groups] for k in range(ROW)], axis=1)
-    totals = []
+    chunk = (place // parents_y) ^ lax.axis_index("gy")
+    is_late = (chunk > 0) & (chunk < chunks - 1)
+    chunk = jnp.where(is_late, chunk - 1, jnp.where(chunk > 0, 1, 0))
+    source = chunk * parents + line * parents_y + place % parents_y
+    column = count_rows(count_ref, parents_x, parents_y, slots)
+    used = lax.broadcasted_iota(jnp.int32, (parents, slots), 1).astype(F32) < column
+    part = jnp.where(used, jnp.where(is_late, 2, 1), 0)
+    words[:, 0:slots] = (source * 128 + kind_ref[...] + part * (1 << 20)).astype(F32)
+    turned = words[...].T[0:slots].astype(jnp.int32)
+    word, turned_part = turned & ((1 << 20) - 1), turned >> 20
+
+    down = lax.broadcasted_iota(jnp.int32, (parents, parents), 0)
+    along = lax.broadcasted_iota(jnp.int32, (parents, parents), 1)
+    wanted = (ROW * (down % groups) + down // groups).astype(F32)
+    earlier = lax.broadcasted_iota(jnp.int32, (slots, slots), 1) < lax.broadcasted_iota(jnp.int32, (slots, slots), 0)
+    earlier = jnp.where(earlier, 1.0, 0.0).astype(BF16)
+    slot = lax.broadcasted_iota(jnp.int32, (slots, parents), 0)
     from_lane = lax.broadcasted_iota(jnp.int32, (ROW * lanes, lanes), 0)
     to_lane = lax.broadcasted_iota(jnp.int32, (ROW * lanes, lanes), 1)
-    for n in range(3):
-        spread = from_lane == (to_lane // slots) * lanes + n * slots + to_lane % slots
-        totals.append(mm(moved, jnp.where(spread, 1.0, 0.0).astype(BF16)).astype(jnp.int32))
-    at_ref[0:groups, :] = (totals[0] * 256 + totals[1]) * 8
-    at_ref[groups : 2 * groups, :] = totals[2] * 8
+    spreads = [
+        jnp.where(from_lane == (to_lane // slots) * lanes + n * slots + to_lane % slots, 1.0, 0.0).astype(BF16)
+        for n in range(4)
+    ]
     least = (slots - 1 - 2 * lax.broadcasted_iota(jnp.int32, (parents, lanes), 1)).astype(F32)
-    reach = jnp.sum(jnp.where(column[:, :lanes] >= least, 1.0, 0.0), axis=0, keepdims=True).astype(jnp.int32)
-    at_ref[2 * groups :, :] = jnp.broadcast_to((reach + (GROUP - 1)) // GROUP, (8, lanes))
-
-
-def lists_kernel(chunks, tile_x, tile_y, slots, *refs):
-    sources = refs[:chunks]
-    (at_any, table8, back_ref, kept_ref, lower_ref, near_ref, recv_ref, down_hbm, out_hbm,
-     cells, sums, lines, at, down_ref, total_ref, out_ref, sems) = refs[chunks:]
-    parents_x, parents_y = tile_x // 2, tile_y // 2
-    parents = parents_x * parents_y
-    lanes = table8.shape[1]
-    groups = parents // GROUP
-    loads = [
-        pltpu.make_async_copy(at_any, at, sems.at[0]),
-        pltpu.make_async_copy(down_hbm, down_ref, sems.at[1]),
-    ]
-    for load in loads:
-        load.start()
-    count = parents // 2
-    pairs = cells.reshape(chunks * count, 2, 8, lanes)
-    first_half = lax.broadcasted_iota(jnp.int32, (count, 8, lanes), 1) < 4
-    for c, source in zip([0, chunks - 1] + list(range(1, chunks - 1)), sources):
+    for number, at_ref in ((1, early_ref), (2, late_ref)):
+        hit = jnp.where(turned_part == number, 1.0, 0.0)
+        mine = jnp.where(part == number, 1.0, 0.0).astype(BF16)
+        column = mm(mine, jnp.ones((slots, parents), BF16))
+        row = jnp.sum(hit, axis=0, keepdims=True)
+        before = (column > row) | ((column == row) & (down < along))
+        rank = jnp.sum(jnp.where(before, 1.0, 0.0), axis=0, keepdims=True)
+        place = mm(earlier, hit.astype(BF16)).astype(jnp.int32)
+        place = jnp.where(turned_part == number, place, -1)
+        dense = jnp.zeros((slots, parents), jnp.int32)
+        for n in range(slots):
+            dense = dense + jnp.where(place[n : n + 1] == slot, word[n : n + 1], 0)
+        kind = jnp.where(slot.astype(F32) < row, dense & 127, kinds)
+        source = dense >> 7
+        rest = jnp.zeros((lanes - 4 * slots, parents), F32)
+        values = [source >> 8, source & 255, kind, along[0:slots]]
+        values = jnp.concatenate([value.astype(F32) for value in values] + [rest], axis=0).astype(BF16)
+        move = jnp.where(wanted == rank, 1.0, 0.0).astype(BF16)
+        moved = lax.dot_general(move, values, (((1,), (1,)), ((), ())), preferred_element_type=F32).astype(BF16)
+        moved = jnp.concatenate([moved[k * groups : (k + 1) * groups] for k in range(ROW)], axis=1)
+        high, low, kind, parent = [mm(moved, spread).astype(jnp.int32) for spread in spreads]
+        at_ref[0:groups, :] = (high * 256 + low) * 8
+        at_ref[groups : 2 * groups, :] = kind * 8
+        at_ref[2 * groups : 3 * groups, :] = parent * 8
+        reach = jnp.sum(jnp.where(column[:, :lanes] >= least, 1.0, 0.0), axis=0, keepdims=True).astype(jnp.int32)
+        at_ref[3 * groups :, :] = jnp.broadcast_to((reach + (GROUP - 1)) // GROUP, (8, lanes))
+
+
+def expand(sources, cells):
+    lanes = cells.shape[1]
+    count = sources[0].shape[0] // 8
+    pairs = cells.reshape(len(sources) * count, 2, 8, lanes)
+    upper = lax.broadcasted_iota(jnp.int32, (count, 8, lanes), 1) < 4
+    for c, source in enumerate(sources):
         rows = source[...].astype(F32).reshape(count, 8, lanes)
         turned = pltpu.roll(rows, 4, axis=1)
-        pairs[c * count : (c + 1) * count, 0] = jnp.where(first_half, rows, turned)
-        pairs[c * count : (c + 1) * count, 1] = jnp.where(first_half, turned, rows)
-    loads[0].wait()
+        pairs[c * count : (c + 1) * count, 0] = jnp.where(upper, rows, turned)
+        pairs[c * count : (c + 1) * count, 1] = jnp.where(upper, turned, rows)
+
+
+def add_lists(parents, slots, at, cells, table8, sums):
+    lanes = cells.shape[1]
+    groups = parents // GROUP
 
     def step(length, n, carry):
         first = n * (GROUP * slots)
-        second = first + parents * slots
+        second, third = first + parents * slots, first + 2 * parents * slots
         for k in range(GROUP):
             total = [None, None]
             for s in range(length):
@@ -410,25 +418,52 @@
                 term = cells[pl.ds(source, 8), :] * table8[pl.ds(kind, 8), :]
                 total[s % 2] = term if total[s % 2] is None else total[s % 2] + term
             total = total[0] + total[1] if length else jnp.zeros((8, lanes), F32)
-            sums[pl.ds(pl.multiple_of((n * GROUP + k) * 8, 8), 8), :] = total
+            sums[pl.ds(pl.multiple_of(at[third + k * slots], 8), 8), :] = total
         return carry
 
     start = 0
     for j, length in enumerate(range(slots, 0, -2)):
-        end = at[2 * parents * slots + j]
+        end = at[3 * parents * slots + j]
         lax.fori_loop(start, end, functools.partial(step, length), 0)
         start = end
     lax.fori_loop(start, groups, functools.partial(step, 0), 0)
 
-    raw = sums[...].reshape(count, 2, 8, lanes)
+
+def early_kernel(count, parents, slots, *refs):
+    sources = refs[:count]
+    at_any, table8, sums, cells, at, sem = refs[count:]
+    load = pltpu.make_async_copy(at_any, at, sem)
+    load.start()
+    expand(sources, cells)
+    load.wait()
+    add_lists(parents, slots, at, cells, table8, sums)
+
+
+def late_kernel(count, tile_x, tile_y, slots, *refs):
+    sources = refs[:count]
+    (at_any, table8, early_ref, kept_ref, lower_ref, near_ref, recv_ref, down_hbm, out_hbm,
+     cells, sums, lines, at, down_ref, total_ref, out_ref, sems) = refs[count:]
+    parents_x, parents_y = tile_x // 2, tile_y // 2
+    parents = parents_x * parents_y
+    lanes = table8.shape[1]
+    loads = [
+        pltpu.make_async_copy(at_any, at, sems.at[0]),
+        pltpu.make_async_copy(down_hbm, down_ref, sems.at[1]),
+    ]
+    for load in loads:
+        load.start()
+    expand(sources, cells)
+    loads[0].wait()
+    add_lists(parents, slots, at, cells, table8, sums)
+    raw = (sums[...] + early_ref[...]).reshape(parents // 2, 2, 8, lanes)
     one, other = raw[:, 0], raw[:, 1]
-    with_real = jnp.where(first_half, one, pltpu.roll(other, 4, axis=1))
-    with_imag = jnp.where(first_half, pltpu.roll(one, 4, axis=1), other)
-    real = lax.broadcasted_iota(jnp.int32, (count, 8, lanes), 1) % 4 < 2
-    turned = jnp.where(real, -pltpu.roll(with_imag, 6, axis=1), pltpu.roll(with_imag, 2, axis=1))
+    line = lax.broadcasted_iota(jnp.int32, one.shape, 1)
+    with_real = jnp.where(line < 4, one, pltpu.roll(other, 4, axis=1))
+    with_imag = jnp.where(line < 4, pltpu.roll(one, 4, axis=1), other)
+    turned = jnp.where(line % 4 < 2, -pltpu.roll(with_imag, 6, axis=1), pltpu.roll(with_imag, 2, axis=1))
     lines[...] = (with_real + turned).reshape(4 * parents, lanes)
     ordered = [lines[pl.ds(place, parents, stride=4), :].astype(BF16) for place in range(4)]
-    incoming = mm(back_ref[...], jnp.concatenate(ordered, axis=1)).astype(BF16)
+    incoming = jnp.concatenate(ordered, axis=1)
     loads[1].wait()
     for child in range(4):
         down = mm(incoming, down_ref[child])
@@ -457,19 +492,7 @@
         store.wait()
 
 
-def swap(low, high, axis, other):
-    count, breadth = lax.axis_size(axis), lax.axis_size(other)
-    lows = [(i, i ^ 1) for i in range(count)]
-    highs = []
-    for i in range(count):
-        for j in range(breadth):
-            end = i in (0, count - 1)
-            target = (i, j ^ 1) if end else (((i + 1) ^ 1) - 1, j)
-            highs.append((i * breadth + j, target[0] * breadth + target[1]))
-    return lax.ppermute(low, axis, lows), lax.ppermute(high, (axis, other), highs)
-
-
-def swap_rows(low, high, axis):
+def swap(low, high, axis):
     count = lax.axis_size(axis)
     lows = [(i, i ^ 1) for i in range(count)]
     highs = [(i, (((i + 1) % count ^ 1) - 1) % count) for i in range(count)]
@@ -534,7 +557,7 @@
         compiler_params=params(10),
         cost_estimate=cost(200 * MIB, 3 * MIB),
     )(live, agg_near, up_near)
-    inner_y, outer_y = swap_rows(low, high, "gy")
+    inner_y, outer_y = swap(low, high, "gy")
     sources = [coarse] + [
         lax.ppermute(coarse, "gy", [(i, i ^ d) for i in range(chunks)])
         for d in [chunks - 1] + list(range(1, chunks - 1))
@@ -552,7 +575,7 @@
         compiler_params=params(10),
         cost_estimate=cost(1 * MIB, MIB),
     )(live, inner_y, outer_y)
-    inner_x, outer_x = swap(low, high, "gx", "gy")
+    inner_x, outer_x = swap(low, high, "gx")
     live, coarse_count, _ = lax.optimization_barrier((live, coarse_count, low))
 
     near_rows = near_blocks.reshape(3, 6 * lanes, 2 * lanes)
@@ -591,31 +614,45 @@
     )(inner_y, outer_y, inner_x, outer_x, agg_near, near_rows, low_rows, lower, near, kept)
 
     table = up_translator.reshape(kinds, 2, 2, half // 2).transpose(0, 2, 1, 3).reshape(4 * kinds, half // 2)
-    at, back, table8 = pl.pallas_call(
+    places = jax.ShapeDtypeStruct((3 * parents // ROW + 8, ROW * slots), jnp.int32)
+    early_at, late_at, table8 = pl.pallas_call(
         functools.partial(order_kernel, chunks, kinds, parents_x, parents_y),
         name="order",
-        out_shape=[
-            jax.ShapeDtypeStruct((2 * parents // ROW + 8, ROW * slots), jnp.int32),
-            jax.ShapeDtypeStruct((parents, parents), BF16),
-            jax.ShapeDtypeStruct((8 * kinds + 8, half // 2), F32),
-        ],
+        out_shape=[places, places, jax.ShapeDtypeStruct((8 * kinds + 8, half // 2), F32)],
         in_specs=vmem(4),
         out_specs=vmem(3),
-        compiler_params=params(8),
+        scratch_shapes=[pltpu.VMEM((parents, 128), F32)],
+        compiler_params=params(10),
         cost_estimate=cost(300 * MIB, MIB),
     )(coarse_list.reshape(parents, slots), coarse_kind.reshape(parents, slots), coarse_count, table)
-    at = at.reshape(-1)
+    early_at, late_at = early_at.reshape(-1), late_at.reshape(-1)
+    anywhere = pl.BlockSpec(memory_space=pl.ANY)
+    early, late = sources[:2], sources[2:]
+    early_sums = pl.pallas_call(
+        functools.partial(early_kernel, len(early), parents, slots),
+        name="early",
+        out_shape=jax.ShapeDtypeStruct((8 * parents, wide // 4), F32),
+        in_specs=vmem(len(early)) + [anywhere] + vmem(1),
+        out_specs=pl.BlockSpec(memory_space=pltpu.VMEM),
+        scratch_shapes=[
+            pltpu.VMEM((len(early) * parents * 8, wide // 4), F32),
+            pltpu.SMEM(early_at.shape, jnp.int32),
+            pltpu.SemaphoreType.DMA,
+        ],
+        compiler_params=params(10),
+        cost_estimate=cost(1000 * MIB, 4 * MIB),
+    )(*early, early_at, table8)
     out = pl.pallas_call(
-        functools.partial(lists_kernel, chunks, tile_x, tile_y, slots),
-        name="lists",
+        functools.partial(late_kernel, len(late), tile_x, tile_y, slots),
+        name="late",
         out_shape=jax.ShapeDtypeStruct((2 * boxes, lanes), F32),
-        in_specs=vmem(chunks) + [pl.BlockSpec(memory_space=pl.ANY)] + vmem(6) + [in_hbm],
+        in_specs=vmem(len(late)) + [anywhere] + vmem(6) + [in_hbm],
         out_specs=in_hbm,
         scratch_shapes=[
-            pltpu.VMEM((chunks * parents * 8, wide // 4), F32),
+            pltpu.VMEM((len(late) * parents * 8, wide // 4), F32),
             pltpu.VMEM((8 * parents, wide // 4), F32),
             pltpu.VMEM((4 * parents, wide // 4), F32),
-            pltpu.SMEM(at.shape, jnp.int32),
+            pltpu.SMEM(late_at.shape, jnp.int32),
             pltpu.VMEM((4, wide, 2 * lanes), BF16),
             pltpu.VMEM((4, parents, 2 * lanes), BF16),
             pltpu.VMEM((2 * boxes, lanes), F32),
@@ -623,7 +660,7 @@
         ],
         compiler_params=params(16 if chunks <= 4 else 40),
         cost_estimate=cost(2000 * MIB, 8 * MIB),
-    )(*sources, at, table8, back, kept, lower, near, receive_map, hbm(parent_to_child))
+    )(*late, late_at, table8, early_sums, kept, lower, near, receive_map, hbm(parent_to_child))
     return out.reshape(tile_x, tile_y, 2, lanes)
 
 

time: 28.8 us -> 29.6 us (1.028)
  waiting for transfers between devices: 4.61 us -> 0.02 us
  Pallas kernels: 14.2 us -> 17.6 us
  starting transfers between devices: 9.68 us -> 11.8 us
    ppermute x4, waiting for transfers between devices: 4.6 us -> 0.01 us  [swap(): return (lax.ppermute(low, axis, lows), lax.ppermute(high, axis, highs))]
    pallas_call x1 -> x2, Pallas kernels: 7.08 us -> 9.87 us  [the longest x1 5.94 us: body(): pl.pallas_call(functools.partial(late_kernel, len(late), tile_x, tile_y,...]
    ppermute x4, starting transfers between devices: 6.13 us -> 8.27 us  [swap(): return (lax.ppermute(low, axis, lows), lax.ppermute(high, axis, highs))]
    pallas_call x1, Pallas kernels: 1.02 us -> 1.65 us  [body(): pl.pallas_call(functools.partial(order_kernel, chunks, kinds, parents_x,...]
  transfers between devices with their start and end apart: 7 -> 7, of which waited for: 1 -> 0; matrix products, arithmetic and copies ran while one was open for 0% -> 0% of each run, Pallas kernels for 19% -> 34%
where the time goes in v10:
time: 29.6 us
  Pallas kernels  17.6 us (59%)
  starting transfers between devices  11.8 us (40%)
    ppermute x4, starting transfers between devices, swap(): return (lax.ppermute(low, axis, lows), lax.ppermute(high, axis, highs))  8.27 us
    pallas_call x1, Pallas kernels, body(): pl.pallas_call(functools.partial(late_kernel, len(late), tile_x, tile_y,...  5.94 us
    pallas_call x1, Pallas kernels, body(): pl.pallas_call(functools.partial(early_kernel, len(early), parents, slots...  3.93 us
    ppermute x3, starting transfers between devices, body(): lax.ppermute(coarse, 'gy', [(i, i ^ d) for i in range(chunks)])  3.55 us
    pallas_call x1, Pallas kernels, body(): pl.pallas_call(functools.partial(local_kernel, tile_x, tile_y), name='loc...  2.83 us
    pallas_call x1, Pallas kernels, body(): pl.pallas_call(functools.partial(order_kernel, chunks, kinds, parents_x,...  1.65 us
    pallas_call x1, Pallas kernels, body(): pl.pallas_call(functools.partial(live_kernel, tile_x, tile_y), name='live...  1.61 us
    pallas_call x1, Pallas kernels, body(): pl.pallas_call(functools.partial(halos_kernel, tile_x, tile_y), name='hal...  0.83 us
  transfers between devices with their start and end apart: 7, of which 0 were waited for; matrix products, arithmetic and copies ran while one was open for 0% of the time, Pallas kernels for 34%

profile of v10, /device:TPU:0, one launch (start us, length us, event | category | flops | bytes accessed | tf_op | source)
XLA Modules:
  0.0 29.6 jit_solution(9673896851589578368)
XLA Ops:
  0.0 0.0 copy-start.1
  0.0 0.0 copy-start
  0.0 1.6 %live.1 = (bf16[1024,256]{1,0:T(8,128)(2,1)S(1)}, f32[1024,128]{1,0:T(8,128)S(1)}, bf16[64,256]{1,0:T(8,128)(2,1)S(1)}, bf16[64,256]{1,0:T(8,128)(2,1)S(1)}, bf1...) custom-call(bf16[2048,128]{1,0:T(8,128)(2,1)} %bitcast.24, s32[32,32]{1,0:T(8,128)} %counts_hbm.1, ...), custom_call_target="tpu_custom_call" | custom-call | flops 209715200 | bytes 3145728 | tf_op jit(solution)/shard_map/live/pallas_call | solution.py:519
  1.6 3.0 %collective-permute-start.2 = (bf16[64,256]{1,0:T(8,128)(2,1)S(1)}, bf16[64,256]{1,0:T(8,128)(2,1)S(1)}, u32[]{:S(2)}, u32[]{:S(2)}) collective-permute-start(bf16[64,256]{1,0:T(8,128)(2,1)S(1)} %get-tuple-element.29), channel_id=1, source_target_pairs={{0,1},{1,0},{2,3},{3,2},{4,5},{5,4},{6,7},{7,6},{8,9},{9,8},{10,11... | collective-permute-start | bytes 98312 | tf_op jit(solution)/shard_map/ppermute | solution.py:499
  4.6 1.5 %collective-permute-start.3 = (bf16[64,256]{1,0:T(8,128)(2,1)S(1)}, bf16[64,256]{1,0:T(8,128)(2,1)S(1)}, u32[]{:S(2)}, u32[]{:S(2)}) collective-permute-start(bf16[64,256]{1,0:T(8,128)(2,1)S(1)} %get-tuple-element.30), channel_id=1, source_target_pairs={{0,3},{1,2},{2,1},{3,0},{4,7},{5,6},{6,5},{7,4},{8,11},{9,10},{10,... | collective-permute-start | bytes 98312 | tf_op jit(solution)/shard_map/ppermute | solution.py:499
  6.1 0.8 %parents.1 = (bf16[1024,128]{1,0:T(8,128)(2,1)S(1)}, f32[3,1536,128]{2,1,0:T(8,128)S(1)}) custom-call(bf16[1024,256]{1,0:T(8,128)(2,1)S(1)} %get-tuple-element.37.live_ref, bf16[256,256]{1,0:T(8,128)(2,1)S(1)} %get-tuple-element.26.agg_ref, bf16[1024,512]{1,0:T(8,128)(2,1)S(1)} %get-tuple-element.27.up_ref), custom_call_target="tpu_custom_call" | custom-call | flops 419430400 | bytes 3145728 | tf_op jit(solution)/shard_map/parents/pallas_call | solution.py:544
  6.9 1.5 %collective-permute-start.4 = (bf16[1024,128]{1,0:T(8,128)(2,1)S(1)}, bf16[1024,128]{1,0:T(8,128)(2,1)S(1)}, u32[]{:S(2)}, u32[]{:S(2)}) collective-permute-start(bf16[1024,128]{1,0:T(8,128)(2,1)S(1)} %get-tuple-element.28.refs_0_), channel_id=1, source_target_pairs={{0,3},{1,2},{2,1},{3,0},{4,7},{5,6},{6,5},{7,4},{8,11},{9,10},{10,... | collective-permute-start | bytes 786440 | tf_op jit(solution)/shard_map/ppermute | solution.py:562
  8.4 0.1 collective-permute-start
  8.5 1.9 %collective-permute-start.1 = (bf16[1024,128]{1,0:T(8,128)(2,1)S(1)}, bf16[1024,128]{1,0:T(8,128)(2,1)S(1)}, u32[]{:S(2)}, u32[]{:S(2)}) collective-permute-start(bf16[1024,128]{1,0:T(8,128)(2,1)S(1)} %get-tuple-element.28.refs_0_), channel_id=1, source_target_pairs={{0,2},{1,3},{2,0},{3,1},{4,6},{5,7},{6,4},{7,5},{8,10},{9,11},{10,... | collective-permute-start | bytes 786440 | tf_op jit(solution)/shard_map/ppermute | solution.py:562
  10.4 0.0 collective-permute-done.2.inner_ref.inner_y
  10.4 0.0 collective-permute-done.3.outer_ref.outer_y
  10.5 0.1 collective-permute-start.5
  10.6 3.7 %collective-permute-start.6 = (bf16[80,256]{1,0:T(8,128)(2,1)S(1)}, bf16[80,256]{1,0:T(8,128)(2,1)S(1)}, u32[]{:S(2)}, u32[]{:S(2)}) collective-permute-start(bf16[80,256]{1,0:T(8,128)(2,1)S(1)} %get-tuple-element.36), channel_id=1, source_target_pairs={{0,28},{4,8},{8,4},{12,16},{16,12},{20,24},{24,20},{28,0},{1,29},{... | collective-permute-start | bytes 122888 | tf_op jit(solution)/shard_map/ppermute | solution.py:499
  14.3 0.0 copy-done.1
  14.3 0.0 copy-done
  14.3 0.0 copy-start.2
  14.3 0.0 copy-start.3
  14.3 0.0 copy-start.4
  14.3 0.0 copy-start.6
  14.3 2.8 %local.1 = (f32[2,1024,128]{2,1,0:T(8,128)S(1)}, f32[2,1024,128]{2,1,0:T(8,128)S(1)}) custom-call(bf16[1024,256]{1,0:T(8,128)(2,1)S(1)} %get-tuple-element.37.live_ref, f32[3,1536,128]{2,1,0:T(8,128)S(1)} %get-tuple-element.38.pats, bf16[3,768,256]{2,1,0:T(8,128)(2,1)S(1)} %bitcast.14, f32[32,128]{1,0:T(8,128)S(1)} %bitcast.16), custom_call_target="tpu_custom_call" | custom-call | flops 4194304000 | bytes 5242880 | tf_op jit(solution)/shard_map/local/pallas_call | solution.py:584
  17.2 0.0 copy-done.2
  17.2 0.0 copy-done.3
  17.2 0.0 copy-done.4
  17.2 0.0 copy-done.6
  17.2 1.6 %order.1 = (s32[104,128]{1,0:T(8,128)S(1)}, s32[104,128]{1,0:T(8,128)S(1)}, f32[520,128]{1,0:T(8,128)S(1)}) custom-call(s32[256,16]{1,0:T(8,128)S(1)} %bitcast.18, s32[256,16]{1,0:T(8,128)S(1)} %bitcast.19, s32[16,16]{1,0:T(8,128)S(1)} %copy-done.6, f32[256,128]{1,0:T(8,128)S(1)} %bitcast.20), custom_call_target="tpu_custom_call" | custom-call | flops 629145600 | bytes 1048576 | tf_op jit(solution)/shard_map/order/pallas_call | solution.py:618
  18.8 0.0 collective-permute-done.5.inner_x
  18.9 0.0 collective-permute-done.6.outer_x
  18.9 0.8 %halos.1 = (f32[2,4,256,128]{3,2,1,0:T(8,128)S(1)}, f32[2,4,256,128]{3,2,1,0:T(8,128)S(1)}, f32[4,256,128]{2,1,0:T(8,128)S(1)}) custom-call(bf16[64,256]{1,0:T(8,128)(2,1)S(1)} %collective-permute-done.2.inner_ref.inner_y, bf16[64,256]{1,0:T(8,128)(2,1)S(1)} %collective-permute-done.3.outer_ref.outer_y, bf16[80,256]{1,0:T(8,128)(2,1)S(1)} %collective-permute-done.5.inner_x, ...), custom_call_target="tpu_custom_call" | custom-call | flops 209715200 | bytes 5242880 | tf_op jit(solution)/shard_map/halos/pallas_call | solution.py:601
  19.7 0.0 collective-permute-done.4.refs_1_
  19.7 0.0 copy-start.5
  19.7 3.9 %early.1.refs_4_ = f32[2048,128]{1,0:T(8,128)S(1)} custom-call(bf16[1024,128]{1,0:T(8,128)(2,1)S(1)} %get-tuple-element.28.refs_0_, bf16[1024,128]{1,0:T(8,128)(2,1)S(1)} %collective-permute-done.4.refs_1_, s32[13312]{0:T(1024)S(1)} %bitcast.22, f32[520,128]{1,0:T(8,128)S(1)} %get-tuple-element.34.refs_3_), custom_call_target="tpu_custom_call" | custom-call | flops 2097152000 | bytes 4194304 | tf_op jit(solution)/shard_map/early/pallas_call | solution.py:631
  23.7 0.0 collective-permute-done.refs_0_
  23.7 0.0 collective-permute-done.1.refs_1_
  23.7 0.0 copy-done.5
  23.7 5.9 %late.1 = f32[2048,128]{1,0:T(8,128)} custom-call(bf16[1024,128]{1,0:T(8,128)(2,1)S(1)} %collective-permute-done.refs_0_, bf16[1024,128]{1,0:T(8,128)(2,1)S(1)} %collective-permute-done.1.refs_1_, s32[13312]{0:T(1024)S(1)} %bitcast.21, f32[520,128]{1,0:T(8,128)S(1)} %get-tuple-element.34.refs_3_, f32[2048,128]{1,0:T(8,128)S(1)} %early.1.refs_4_, ...), custom_call_target="tpu_custom_call" | custom-call | flops 4194304000 | bytes 8388608 | tf_op jit(solution)/shard_map/late/pallas_call | solution.py:645
  (1 shorter events, 0.0 us)
Async XLA Ops:
  0.0 14.3 %copy-start.1 = (f32[16,2,128]{2,1,0:T(2,128)S(1)}, f32[16,2,128]{2,1,0:T(2,128)}, u32[]{:S(2)}) copy-start(f32[16,2,128]{2,1,0:T(2,128)} %param.16) | copy-start | bytes 49156
  0.0 14.3 %copy-start = (bf16[9,256,256]{2,1,0:T(8,128)(2,1)S(1)}, bf16[9,256,256]{2,1,0:T(8,128)(2,1)}, u32[]{:S(2)}) copy-start(bf16[9,256,256]{2,1,0:T(8,128)(2,1)} %param.15) | copy-start | bytes 3538948
  1.6 8.8 %collective-permute-start.2 = (bf16[64,256]{1,0:T(8,128)(2,1)S(1)}, bf16[64,256]{1,0:T(8,128)(2,1)S(1)}, u32[]{:S(2)}, u32[]{:S(2)}) collective-permute-start(bf16[64,256]{1,0:T(8,128)(2,1)S(1)} %get-tuple-element.29), channel_id=1, source_target_pairs={{0,1},{1,0},{2,3},{3,2},{4,5},{5,4},{6,7},{7,6},{8,9},{9,8},{10,11... | collective-permute-start | bytes 98312 | tf_op jit(solution)/shard_map/ppermute | solution.py:499
  4.6 5.8 %collective-permute-start.3 = (bf16[64,256]{1,0:T(8,128)(2,1)S(1)}, bf16[64,256]{1,0:T(8,128)(2,1)S(1)}, u32[]{:S(2)}, u32[]{:S(2)}) collective-permute-start(bf16[64,256]{1,0:T(8,128)(2,1)S(1)} %get-tuple-element.30), channel_id=1, source_target_pairs={{0,3},{1,2},{2,1},{3,0},{4,7},{5,6},{6,5},{7,4},{8,11},{9,10},{10,... | collective-permute-start | bytes 98312 | tf_op jit(solution)/shard_map/ppermute | solution.py:499
  6.9 12.8 %collective-permute-start.4 = (bf16[1024,128]{1,0:T(8,128)(2,1)S(1)}, bf16[1024,128]{1,0:T(8,128)(2,1)S(1)}, u32[]{:S(2)}, u32[]{:S(2)}) collective-permute-start(bf16[1024,128]{1,0:T(8,128)(2,1)S(1)} %get-tuple-element.28.refs_0_), channel_id=1, source_target_pairs={{0,3},{1,2},{2,1},{3,0},{4,7},{5,6},{6,5},{7,4},{8,11},{9,10},{10,... | collective-permute-start | bytes 786440 | tf_op jit(solution)/shard_map/ppermute | solution.py:562
  8.4 15.3 %collective-permute-start = (bf16[1024,128]{1,0:T(8,128)(2,1)S(1)}, bf16[1024,128]{1,0:T(8,128)(2,1)S(1)}, u32[]{:S(2)}, u32[]{:S(2)}) collective-permute-start(bf16[1024,128]{1,0:T(8,128)(2,1)S(1)} %get-tuple-element.28.refs_0_), channel_id=1, source_target_pairs={{0,1},{1,0},{2,3},{3,2},{4,5},{5,4},{6,7},{7,6},{8,9},{9,8},{10,11... | collective-permute-start | bytes 786440 | tf_op jit(solution)/shard_map/ppermute | solution.py:562
  8.5 15.2 %collective-permute-start.1 = (bf16[1024,128]{1,0:T(8,128)(2,1)S(1)}, bf16[1024,128]{1,0:T(8,128)(2,1)S(1)}, u32[]{:S(2)}, u32[]{:S(2)}) collective-permute-start(bf16[1024,128]{1,0:T(8,128)(2,1)S(1)} %get-tuple-element.28.refs_0_), channel_id=1, source_target_pairs={{0,2},{1,3},{2,0},{3,1},{4,6},{5,7},{6,4},{7,5},{8,10},{9,11},{10,... | collective-permute-start | bytes 786440 | tf_op jit(solution)/shard_map/ppermute | solution.py:562
  10.5 8.4 %collective-permute-start.5 = (bf16[80,256]{1,0:T(8,128)(2,1)S(1)}, bf16[80,256]{1,0:T(8,128)(2,1)S(1)}, u32[]{:S(2)}, u32[]{:S(2)}) collective-permute-start(bf16[80,256]{1,0:T(8,128)(2,1)S(1)} %get-tuple-element.31), channel_id=1, source_target_pairs={{0,4},{4,0},{8,12},{12,8},{16,20},{20,16},{24,28},{28,24},{1,5},{5... | collective-permute-start | bytes 122888 | tf_op jit(solution)/shard_map/ppermute | solution.py:499
  10.6 8.3 %collective-permute-start.6 = (bf16[80,256]{1,0:T(8,128)(2,1)S(1)}, bf16[80,256]{1,0:T(8,128)(2,1)S(1)}, u32[]{:S(2)}, u32[]{:S(2)}) collective-permute-start(bf16[80,256]{1,0:T(8,128)(2,1)S(1)} %get-tuple-element.36), channel_id=1, source_target_pairs={{0,28},{4,8},{8,4},{12,16},{16,12},{20,24},{24,20},{28,0},{1,29},{... | collective-permute-start | bytes 122888 | tf_op jit(solution)/shard_map/ppermute | solution.py:499
  14.3 2.9 %copy-start.2 = (s32[16,16,16]{2,1,0:T(8,128)S(1)}, s32[16,16,16]{2,1,0:T(8,128)}, u32[]{:S(2)}) copy-start(s32[16,16,16]{2,1,0:T(8,128)} %param.18) | copy-start | bytes 49156
  14.3 2.9 %copy-start.3 = (s32[16,16,16]{2,1,0:T(8,128)S(1)}, s32[16,16,16]{2,1,0:T(8,128)}, u32[]{:S(2)}) copy-start(s32[16,16,16]{2,1,0:T(8,128)} %param.19) | copy-start | bytes 49156
  14.3 2.9 %copy-start.4 = (f32[64,2,256]{2,1,0:T(2,128)S(1)}, f32[64,2,256]{2,1,0:T(2,128)}, u32[]{:S(2)}) copy-start(f32[64,2,256]{2,1,0:T(2,128)} %param.21) | copy-start | bytes 393220
  14.3 2.9 %copy-start.6 = (s32[16,16]{1,0:T(8,128)S(1)}, s32[16,16]{1,0:T(8,128)}, u32[]{:S(2)}) copy-start(s32[16,16]{1,0:T(8,128)} %count_ref) | copy-start | bytes 3076
  19.7 4.0 %copy-start.5 = (bf16[256,256]{1,0:T(8,128)(2,1)S(1)}, bf16[256,256]{1,0:T(8,128)(2,1)}, u32[]{:S(2)}) copy-start(bf16[256,256]{1,0:T(8,128)(2,1)} %refs_8_.1) | copy-start | bytes 393220

commit v11 on v10

--- a/solution.py
+++ b/solution.py
@@ -323,6 +323,7 @@
 
 ROW = 8
 GROUP = 16
+QUARTERS = 4
 
 
 def order_kernel(
@@ -360,7 +361,7 @@
     to_lane = lax.broadcasted_iota(jnp.int32, (ROW * lanes, lanes), 1)
     spreads = [
         jnp.where(from_lane == (to_lane // slots) * lanes + n * slots + to_lane % slots, 1.0, 0.0).astype(BF16)
-        for n in range(4)
+        for n in range(3)
     ]
     least = (slots - 1 - 2 * lax.broadcasted_iota(jnp.int32, (parents, lanes), 1)).astype(F32)
     for number, at_ref in ((1, early_ref), (2, late_ref)):
@@ -377,18 +378,28 @@
             dense = dense + jnp.where(place[n : n + 1] == slot, word[n : n + 1], 0)
         kind = jnp.where(slot.astype(F32) < row, dense & 127, kinds)
         source = dense >> 7
-        rest = jnp.zeros((lanes - 4 * slots, parents), F32)
-        values = [source >> 8, source & 255, kind, along[0:slots]]
+        rest = jnp.zeros((lanes - 3 * slots, parents), F32)
+        values = [source >> 8, source & 255, kind]
         values = jnp.concatenate([value.astype(F32) for value in values] + [rest], axis=0).astype(BF16)
         move = jnp.where(wanted == rank, 1.0, 0.0).astype(BF16)
         moved = lax.dot_general(move, values, (((1,), (1,)), ((), ())), preferred_element_type=F32).astype(BF16)
         moved = jnp.concatenate([moved[k * groups : (k + 1) * groups] for k in range(ROW)], axis=1)
-        high, low, kind, parent = [mm(moved, spread).astype(jnp.int32) for spread in spreads]
-        at_ref[0:groups, :] = (high * 256 + low) * 8
-        at_ref[groups : 2 * groups, :] = kind * 8
-        at_ref[2 * groups : 3 * groups, :] = parent * 8
+        high, low, kind = [mm(moved, spread).astype(jnp.int32) for spread in spreads]
+        source, kind = (high * 256 + low) * 8, kind * 8
+        rows = groups // QUARTERS
+        for q in range(QUARTERS):
+            at_ref[2 * q * rows : (2 * q + 1) * rows, :] = source[q * rows : (q + 1) * rows]
+            at_ref[(2 * q + 1) * rows : (2 * q + 2) * rows, :] = kind[q * rows : (q + 1) * rows]
+        ranked = jnp.where(down.astype(F32) == rank, 1.0, 0.0).astype(BF16)
+        parent = lax.dot_general(
+            along[0:8].astype(F32).astype(BF16), ranked, (((1,), (1,)), ((), ())), preferred_element_type=F32
+        ).astype(jnp.int32) * 8
         reach = jnp.sum(jnp.where(column[:, :lanes] >= least, 1.0, 0.0), axis=0, keepdims=True).astype(jnp.int32)
-        at_ref[3 * groups :, :] = jnp.broadcast_to((reach + (GROUP - 1)) // GROUP, (8, lanes))
+        last = jnp.broadcast_to((reach + (GROUP - 1)) // GROUP, (8, lanes))
+        line = lax.broadcasted_iota(jnp.int32, (8, lanes), 0)
+        for n in range(parents // lanes):
+            last = jnp.where(line == n, parent[:, n * lanes : (n + 1) * lanes], last)
+        at_ref[2 * groups :, :] = last
 
 
 def expand(sources, cells):
@@ -403,13 +414,25 @@
         pairs[c * count : (c + 1) * count, 1] = jnp.where(upper, turned, rows)
 
 
-def add_lists(parents, slots, at, cells, table8, sums):
+def load_lists(at_any, at, sems):
+    words = (at.shape[0] - 1024) // QUARTERS
+    loads = []
+    for n, (start, size) in enumerate([(QUARTERS * words, 1024)] + [(q * words, words) for q in range(QUARTERS)]):
+        rows = pl.ds(start, size)
+        loads.append(pltpu.make_async_copy(at_any.at[rows], at.at[rows], sems.at[n]))
+        loads[-1].start()
+    return loads
+
+
+def add_lists(parents, slots, at_any, at, sems, cells, table8, sums):
     lanes = cells.shape[1]
-    groups = parents // GROUP
-
-    def step(length, n, carry):
-        first = n * (GROUP * slots)
-        second, third = first + parents * slots, first + 2 * parents * slots
+    steps = parents // GROUP // QUARTERS
+    words = (at.shape[0] - 1024) // QUARTERS
+    tail = QUARTERS * words
+
+    def step(length, q, n, carry):
+        first = n * (GROUP * slots) + q * (words // 2)
+        second = first + words // 2
         for k in range(GROUP):
             total = [None, None]
             for s in range(length):
@@ -418,43 +441,47 @@
                 term = cells[pl.ds(source, 8), :] * table8[pl.ds(kind, 8), :]
                 total[s % 2] = term if total[s % 2] is None else total[s % 2] + term
             total = total[0] + total[1] if length else jnp.zeros((8, lanes), F32)
-            sums[pl.ds(pl.multiple_of(at[third + k * slots], 8), 8), :] = total
+            place = pl.multiple_of(at[tail + n * GROUP + k], 8)
+            sums[pl.ds(place, 8), :] = total
         return carry
 
-    start = 0
-    for j, length in enumerate(range(slots, 0, -2)):
-        end = at[3 * parents * slots + j]
-        lax.fori_loop(start, end, functools.partial(step, length), 0)
-        start = end
-    lax.fori_loop(start, groups, functools.partial(step, 0), 0)
+    def quarter(q, carry):
+        rows = pl.ds(pl.multiple_of(q * words, words), words)
+        pltpu.make_async_copy(at_any.at[rows], at.at[rows], sems.at[1 + q]).wait()
+        low, high = q * steps, (q + 1) * steps
+        start = low
+        for j, length in enumerate(range(slots, 0, -2)):
+            end = jnp.clip(at[tail + parents + j], low, high)
+            lax.fori_loop(start, end, functools.partial(step, length, q), 0)
+            start = end
+        lax.fori_loop(start, high, functools.partial(step, 0, q), 0)
+        return carry
+
+    lax.fori_loop(0, QUARTERS, quarter, 0)
 
 
 def early_kernel(count, parents, slots, *refs):
     sources = refs[:count]
-    at_any, table8, sums, cells, at, sem = refs[count:]
-    load = pltpu.make_async_copy(at_any, at, sem)
-    load.start()
+    at_any, table8, sums, cells, at, sems = refs[count:]
+    loads = load_lists(at_any, at, sems)
     expand(sources, cells)
-    load.wait()
-    add_lists(parents, slots, at, cells, table8, sums)
+    loads[0].wait()
+    add_lists(parents, slots, at_any, at, sems, cells, table8, sums)
 
 
 def late_kernel(count, tile_x, tile_y, slots, *refs):
     sources = refs[:count]
     (at_any, table8, early_ref, kept_ref, lower_ref, near_ref, recv_ref, down_hbm, out_hbm,
-     cells, sums, lines, at, down_ref, total_ref, out_ref, sems) = refs[count:]
+     cells, sums, lines, at, down_ref, total_ref, out_ref, list_sems, sems) = refs[count:]
     parents_x, parents_y = tile_x // 2, tile_y // 2
     parents = parents_x * parents_y
     lanes = table8.shape[1]
-    loads = [
-        pltpu.make_async_copy(at_any, at, sems.at[0]),
-        pltpu.make_async_copy(down_hbm, down_ref, sems.at[1]),
-    ]
-    for load in loads:
-        load.start()
+    loads = load_lists(at_any, at, list_sems)
+    weights = pltpu.make_async_copy(down_hbm, down_ref, sems.at[0])
+    weights.start()
     expand(sources, cells)
     loads[0].wait()
-    add_lists(parents, slots, at, cells, table8, sums)
+    add_lists(parents, slots, at_any, at, list_sems, cells, table8, sums)
     raw = (sums[...] + early_ref[...]).reshape(parents // 2, 2, 8, lanes)
     one, other = raw[:, 0], raw[:, 1]
     line = lax.broadcasted_iota(jnp.int32, one.shape, 1)
@@ -464,7 +491,7 @@
     lines[...] = (with_real + turned).reshape(4 * parents, lanes)
     ordered = [lines[pl.ds(place, parents, stride=4), :].astype(BF16) for place in range(4)]
     incoming = jnp.concatenate(ordered, axis=1)
-    loads[1].wait()
+    weights.wait()
     for child in range(4):
         down = mm(incoming, down_ref[child])
         for part in range(2):
@@ -486,16 +513,16 @@
                     ]
         size = out_ref.shape[0] // 2
         rows = pl.ds(half * size, size)
-        stores.append(pltpu.make_async_copy(out_ref.at[rows], out_hbm.at[rows], sems.at[2 + half]))
+        stores.append(pltpu.make_async_copy(out_ref.at[rows], out_hbm.at[rows], sems.at[1 + half]))
         stores[-1].start()
     for store in stores:
         store.wait()
 
 
-def swap(low, high, axis):
+def swap(low, high, axis, ends):
     count = lax.axis_size(axis)
     lows = [(i, i ^ 1) for i in range(count)]
-    highs = [(i, (((i + 1) % count ^ 1) - 1) % count) for i in range(count)]
+    highs = [(i, (((i + 1) % count ^ 1) - 1) % count) for i in range(0 if ends else 1, count if ends else count - 1)]
     return lax.ppermute(low, axis, lows), lax.ppermute(high, axis, highs)
 
 
@@ -557,7 +584,7 @@
         compiler_params=params(10),
         cost_estimate=cost(200 * MIB, 3 * MIB),
     )(live, agg_near, up_near)
-    inner_y, outer_y = swap(low, high, "gy")
+    inner_y, outer_y = swap(low, high, "gy", True)
     sources = [coarse] + [
         lax.ppermute(coarse, "gy", [(i, i ^ d) for i in range(chunks)])
         for d in [chunks - 1] + list(range(1, chunks - 1))
@@ -575,7 +602,7 @@
         compiler_params=params(10),
         cost_estimate=cost(1 * MIB, MIB),
     )(live, inner_y, outer_y)
-    inner_x, outer_x = swap(low, high, "gx")
+    inner_x, outer_x = swap(low, high, "gx", False)
     live, coarse_count, _ = lax.optimization_barrier((live, coarse_count, low))
 
     near_rows = near_blocks.reshape(3, 6 * lanes, 2 * lanes)
@@ -614,7 +641,7 @@
     )(inner_y, outer_y, inner_x, outer_x, agg_near, near_rows, low_rows, lower, near, kept)
 
     table = up_translator.reshape(kinds, 2, 2, half // 2).transpose(0, 2, 1, 3).reshape(4 * kinds, half // 2)
-    places = jax.ShapeDtypeStruct((3 * parents // ROW + 8, ROW * slots), jnp.int32)
+    places = jax.ShapeDtypeStruct((2 * parents // ROW + 8, ROW * slots), jnp.int32)
     early_at, late_at, table8 = pl.pallas_call(
         functools.partial(order_kernel, chunks, kinds, parents_x, parents_y),
         name="order",
@@ -637,7 +664,7 @@
         scratch_shapes=[
             pltpu.VMEM((len(early) * parents * 8, wide // 4), F32),
             pltpu.SMEM(early_at.shape, jnp.int32),
-            pltpu.SemaphoreType.DMA,
+            pltpu.SemaphoreType.DMA((1 + QUARTERS,)),
         ],
         compiler_params=params(10),
         cost_estimate=cost(1000 * MIB, 4 * MIB),
@@ -656,7 +683,8 @@
             pltpu.VMEM((4, wide, 2 * lanes), BF16),
             pltpu.VMEM((4, parents, 2 * lanes), BF16),
             pltpu.VMEM((2 * boxes, lanes), F32),
-            pltpu.SemaphoreType.DMA((4,)),
+            pltpu.SemaphoreType.DMA((1 + QUARTERS,)),
+            pltpu.SemaphoreType.DMA((3,)),
         ],
         compiler_params=params(16 if chunks <= 4 else 40),
         cost_estimate=cost(2000 * MIB, 8 * MIB),

time: 29.6 us -> 28.4 us (0.959)
  the two profiles are of different devices: /device:TPU:0 before, /device:TPU:1 now
where the time goes in v11:
time: 28.4 us
  Pallas kernels  16.9 us (60%)
  starting transfers between devices  11.3 us (40%)
    ppermute x4, starting transfers between devices, swap(): return (lax.ppermute(low, axis, lows), lax.ppermute(high, axis, highs))  8.56 us
    pallas_call x1, Pallas kernels, body(): pl.pallas_call(functools.partial(late_kernel, len(late), tile_x, tile_y,...  5.68 us
    pallas_call x1, Pallas kernels, body(): pl.pallas_call(functools.partial(early_kernel, len(early), parents, slots...  3.56 us
    pallas_call x1, Pallas kernels, body(): pl.pallas_call(functools.partial(local_kernel, tile_x, tile_y), name='loc...  2.83 us
    ppermute x3, starting transfers between devices, body(): lax.ppermute(coarse, 'gy', [(i, i ^ d) for i in range(chunks)])  2.71 us
    pallas_call x1, Pallas kernels, body(): pl.pallas_call(functools.partial(live_kernel, tile_x, tile_y), name='live...  1.61 us
    pallas_call x1, Pallas kernels, body(): pl.pallas_call(functools.partial(order_kernel, chunks, kinds, parents_x,...  1.56 us
    pallas_call x1, Pallas kernels, body(): pl.pallas_call(functools.partial(halos_kernel, tile_x, tile_y), name='hal...  0.83 us
  transfers between devices with their start and end apart: 7, of which 0 were waited for; matrix products, arithmetic and copies ran while one was open for 0% of the time, Pallas kernels for 34%

profile of v11, /device:TPU:1, one launch (start us, length us, event | category | flops | bytes accessed | tf_op | source)
XLA Modules:
  0.0 28.4 jit_solution(3749359308290092617)
XLA Ops:
  0.0 0.0 copy-start.1
  0.0 0.0 copy-start
  0.0 1.6 %live.1 = (bf16[1024,256]{1,0:T(8,128)(2,1)S(1)}, f32[1024,128]{1,0:T(8,128)S(1)}, bf16[64,256]{1,0:T(8,128)(2,1)S(1)}, bf16[64,256]{1,0:T(8,128)(2,1)S(1)}, bf1...) custom-call(bf16[2048,128]{1,0:T(8,128)(2,1)} %bitcast.24, s32[32,32]{1,0:T(8,128)} %counts_hbm.1, ...), custom_call_target="tpu_custom_call" | custom-call | flops 209715200 | bytes 3145728 | tf_op jit(solution)/shard_map/live/pallas_call | solution.py:546
  1.6 2.1 %collective-permute-start.2 = (bf16[64,256]{1,0:T(8,128)(2,1)S(1)}, bf16[64,256]{1,0:T(8,128)(2,1)S(1)}, u32[]{:S(2)}, u32[]{:S(2)}) collective-permute-start(bf16[64,256]{1,0:T(8,128)(2,1)S(1)} %get-tuple-element.29), channel_id=1, source_target_pairs={{0,1},{1,0},{2,3},{3,2},{4,5},{5,4},{6,7},{7,6},{8,9},{9,8},{10,11... | collective-permute-start | bytes 98312 | tf_op jit(solution)/shard_map/ppermute | solution.py:526
  3.7 1.2 %collective-permute-start.3 = (bf16[64,256]{1,0:T(8,128)(2,1)S(1)}, bf16[64,256]{1,0:T(8,128)(2,1)S(1)}, u32[]{:S(2)}, u32[]{:S(2)}) collective-permute-start(bf16[64,256]{1,0:T(8,128)(2,1)S(1)} %get-tuple-element.30), channel_id=1, source_target_pairs={{0,3},{1,2},{2,1},{3,0},{4,7},{5,6},{6,5},{7,4},{8,11},{9,10},{10,... | collective-permute-start | bytes 98312 | tf_op jit(solution)/shard_map/ppermute | solution.py:526
  4.9 0.8 %parents.1 = (bf16[1024,128]{1,0:T(8,128)(2,1)S(1)}, f32[3,1536,128]{2,1,0:T(8,128)S(1)}) custom-call(bf16[1024,256]{1,0:T(8,128)(2,1)S(1)} %get-tuple-element.37.live_ref, bf16[256,256]{1,0:T(8,128)(2,1)S(1)} %get-tuple-element.26.agg_ref, bf16[1024,512]{1,0:T(8,128)(2,1)S(1)} %get-tuple-element.27.up_ref), custom_call_target="tpu_custom_call" | custom-call | flops 419430400 | bytes 3145728 | tf_op jit(solution)/shard_map/parents/pallas_call | solution.py:571
  5.7 1.2 %collective-permute-start.4 = (bf16[1024,128]{1,0:T(8,128)(2,1)S(1)}, bf16[1024,128]{1,0:T(8,128)(2,1)S(1)}, u32[]{:S(2)}, u32[]{:S(2)}) collective-permute-start(bf16[1024,128]{1,0:T(8,128)(2,1)S(1)} %get-tuple-element.28.refs_0_), channel_id=1, source_target_pairs={{0,3},{1,2},{2,1},{3,0},{4,7},{5,6},{6,5},{7,4},{8,11},{9,10},{10,... | collective-permute-start | bytes 786440 | tf_op jit(solution)/shard_map/ppermute | solution.py:589
  6.9 0.1 collective-permute-start
  7.1 1.3 %collective-permute-start.1 = (bf16[1024,128]{1,0:T(8,128)(2,1)S(1)}, bf16[1024,128]{1,0:T(8,128)(2,1)S(1)}, u32[]{:S(2)}, u32[]{:S(2)}) collective-permute-start(bf16[1024,128]{1,0:T(8,128)(2,1)S(1)} %get-tuple-element.28.refs_0_), channel_id=1, source_target_pairs={{0,2},{1,3},{2,0},{3,1},{4,6},{5,7},{6,4},{7,5},{8,10},{9,11},{10,... | collective-permute-start | bytes 786440 | tf_op jit(solution)/shard_map/ppermute | solution.py:589
  8.4 0.0 collective-permute-done.2.inner_ref.inner_y
  8.4 0.0 collective-permute-done.3.outer_ref.outer_y
  8.5 2.1 %collective-permute-start.5 = (bf16[80,256]{1,0:T(8,128)(2,1)S(1)}, bf16[80,256]{1,0:T(8,128)(2,1)S(1)}, u32[]{:S(2)}, u32[]{:S(2)}) collective-permute-start(bf16[80,256]{1,0:T(8,128)(2,1)S(1)} %get-tuple-element.31), channel_id=1, source_target_pairs={{0,4},{4,0},{8,12},{12,8},{16,20},{20,16},{24,28},{28,24},{1,5},{5... | collective-permute-start | bytes 122888 | tf_op jit(solution)/shard_map/ppermute | solution.py:526
  10.6 3.1 %collective-permute-start.6 = (bf16[80,256]{1,0:T(8,128)(2,1)S(1)}, bf16[80,256]{1,0:T(8,128)(2,1)S(1)}, u32[]{:S(2)}, u32[]{:S(2)}) collective-permute-start(bf16[80,256]{1,0:T(8,128)(2,1)S(1)} %get-tuple-element.36), channel_id=1, source_target_pairs={{4,8},{8,4},{12,16},{16,12},{20,24},{24,20},{5,9},{9,5},{13,17},{1... | collective-permute-start | bytes 122888 | tf_op jit(solution)/shard_map/ppermute | solution.py:526
  13.7 0.0 copy-done.1
  13.7 0.0 copy-done
  13.7 0.0 copy-start.2
  13.8 0.0 copy-start.3
  13.8 0.0 copy-start.4
  13.8 0.0 copy-start.6
  13.8 2.8 %local.1 = (f32[2,1024,128]{2,1,0:T(8,128)S(1)}, f32[2,1024,128]{2,1,0:T(8,128)S(1)}) custom-call(bf16[1024,256]{1,0:T(8,128)(2,1)S(1)} %get-tuple-element.37.live_ref, f32[3,1536,128]{2,1,0:T(8,128)S(1)} %get-tuple-element.38.pats, bf16[3,768,256]{2,1,0:T(8,128)(2,1)S(1)} %bitcast.14, f32[32,128]{1,0:T(8,128)S(1)} %bitcast.16), custom_call_target="tpu_custom_call" | custom-call | flops 4194304000 | bytes 5242880 | tf_op jit(solution)/shard_map/local/pallas_call | solution.py:611
  16.6 0.0 copy-done.2
  16.6 0.0 copy-done.3
  16.6 0.0 copy-done.4
  16.7 0.0 copy-done.6
  16.7 1.6 %order.1 = (s32[72,128]{1,0:T(8,128)S(1)}, s32[72,128]{1,0:T(8,128)S(1)}, f32[520,128]{1,0:T(8,128)S(1)}) custom-call(s32[256,16]{1,0:T(8,128)S(1)} %bitcast.18, s32[256,16]{1,0:T(8,128)S(1)} %bitcast.19, s32[16,16]{1,0:T(8,128)S(1)} %copy-done.6, f32[256,128]{1,0:T(8,128)S(1)} %bitcast.20), custom_call_target="tpu_custom_call" | custom-call | flops 629145600 | bytes 1048576 | tf_op jit(solution)/shard_map/order/pallas_call | solution.py:645
  18.2 0.0 collective-permute-done.5.inner_x
  18.2 0.0 collective-permute-done.6.outer_x
  18.2 0.8 %halos.1 = (f32[2,4,256,128]{3,2,1,0:T(8,128)S(1)}, f32[2,4,256,128]{3,2,1,0:T(8,128)S(1)}, f32[4,256,128]{2,1,0:T(8,128)S(1)}) custom-call(bf16[64,256]{1,0:T(8,128)(2,1)S(1)} %collective-permute-done.2.inner_ref.inner_y, bf16[64,256]{1,0:T(8,128)(2,1)S(1)} %collective-permute-done.3.outer_ref.outer_y, bf16[80,256]{1,0:T(8,128)(2,1)S(1)} %collective-permute-done.5.inner_x, ...), custom_call_target="tpu_custom_call" | custom-call | flops 209715200 | bytes 5242880 | tf_op jit(solution)/shard_map/halos/pallas_call | solution.py:628
  19.1 0.0 collective-permute-done.4.refs_1_
  19.1 0.0 copy-start.5
  19.1 3.6 %early.1.refs_4_ = f32[2048,128]{1,0:T(8,128)S(1)} custom-call(bf16[1024,128]{1,0:T(8,128)(2,1)S(1)} %get-tuple-element.28.refs_0_, bf16[1024,128]{1,0:T(8,128)(2,1)S(1)} %collective-permute-done.4.refs_1_, s32[9216]{0:T(1024)S(1)} %bitcast.22, f32[520,128]{1,0:T(8,128)S(1)} %get-tuple-element.34.refs_3_), custom_call_target="tpu_custom_call" | custom-call | flops 2097152000 | bytes 4194304 | tf_op jit(solution)/shard_map/early/pallas_call | solution.py:658
  22.7 0.0 collective-permute-done.refs_0_
  22.7 0.0 collective-permute-done.1.refs_1_
  22.7 0.0 copy-done.5
  22.7 5.7 %late.1 = f32[2048,128]{1,0:T(8,128)} custom-call(bf16[1024,128]{1,0:T(8,128)(2,1)S(1)} %collective-permute-done.refs_0_, bf16[1024,128]{1,0:T(8,128)(2,1)S(1)} %collective-permute-done.1.refs_1_, s32[9216]{0:T(1024)S(1)} %bitcast.21, f32[520,128]{1,0:T(8,128)S(1)} %get-tuple-element.34.refs_3_, f32[2048,128]{1,0:T(8,128)S(1)} %early.1.refs_4_, ...), custom_call_target="tpu_custom_call" | custom-call | flops 4194304000 | bytes 8388608 | tf_op jit(solution)/shard_map/late/pallas_call | solution.py:672
  (1 shorter events, 0.0 us)
Async XLA Ops:
  0.0 13.7 %copy-start.1 = (f32[16,2,128]{2,1,0:T(2,128)S(1)}, f32[16,2,128]{2,1,0:T(2,128)}, u32[]{:S(2)}) copy-start(f32[16,2,128]{2,1,0:T(2,128)} %param.16) | copy-start | bytes 49156
  0.0 13.7 %copy-start = (bf16[9,256,256]{2,1,0:T(8,128)(2,1)S(1)}, bf16[9,256,256]{2,1,0:T(8,128)(2,1)}, u32[]{:S(2)}) copy-start(bf16[9,256,256]{2,1,0:T(8,128)(2,1)} %param.15) | copy-start | bytes 3538948
  1.6 6.8 %collective-permute-start.2 = (bf16[64,256]{1,0:T(8,128)(2,1)S(1)}, bf16[64,256]{1,0:T(8,128)(2,1)S(1)}, u32[]{:S(2)}, u32[]{:S(2)}) collective-permute-start(bf16[64,256]{1,0:T(8,128)(2,1)S(1)} %get-tuple-element.29), channel_id=1, source_target_pairs={{0,1},{1,0},{2,3},{3,2},{4,5},{5,4},{6,7},{7,6},{8,9},{9,8},{10,11... | collective-permute-start | bytes 98312 | tf_op jit(solution)/shard_map/ppermute | solution.py:526
  3.7 4.7 %collective-permute-start.3 = (bf16[64,256]{1,0:T(8,128)(2,1)S(1)}, bf16[64,256]{1,0:T(8,128)(2,1)S(1)}, u32[]{:S(2)}, u32[]{:S(2)}) collective-permute-start(bf16[64,256]{1,0:T(8,128)(2,1)S(1)} %get-tuple-element.30), channel_id=1, source_target_pairs={{0,3},{1,2},{2,1},{3,0},{4,7},{5,6},{6,5},{7,4},{8,11},{9,10},{10,... | collective-permute-start | bytes 98312 | tf_op jit(solution)/shard_map/ppermute | solution.py:526
  5.7 13.4 %collective-permute-start.4 = (bf16[1024,128]{1,0:T(8,128)(2,1)S(1)}, bf16[1024,128]{1,0:T(8,128)(2,1)S(1)}, u32[]{:S(2)}, u32[]{:S(2)}) collective-permute-start(bf16[1024,128]{1,0:T(8,128)(2,1)S(1)} %get-tuple-element.28.refs_0_), channel_id=1, source_target_pairs={{0,3},{1,2},{2,1},{3,0},{4,7},{5,6},{6,5},{7,4},{8,11},{9,10},{10,... | collective-permute-start | bytes 786440 | tf_op jit(solution)/shard_map/ppermute | solution.py:589
  6.9 15.7 %collective-permute-start = (bf16[1024,128]{1,0:T(8,128)(2,1)S(1)}, bf16[1024,128]{1,0:T(8,128)(2,1)S(1)}, u32[]{:S(2)}, u32[]{:S(2)}) collective-permute-start(bf16[1024,128]{1,0:T(8,128)(2,1)S(1)} %get-tuple-element.28.refs_0_), channel_id=1, source_target_pairs={{0,1},{1,0},{2,3},{3,2},{4,5},{5,4},{6,7},{7,6},{8,9},{9,8},{10,11... | collective-permute-start | bytes 786440 | tf_op jit(solution)/shard_map/ppermute | solution.py:589
  7.1 15.6 %collective-permute-start.1 = (bf16[1024,128]{1,0:T(8,128)(2,1)S(1)}, bf16[1024,128]{1,0:T(8,128)(2,1)S(1)}, u32[]{:S(2)}, u32[]{:S(2)}) collective-permute-start(bf16[1024,128]{1,0:T(8,128)(2,1)S(1)} %get-tuple-element.28.refs_0_), channel_id=1, source_target_pairs={{0,2},{1,3},{2,0},{3,1},{4,6},{5,7},{6,4},{7,5},{8,10},{9,11},{10,... | collective-permute-start | bytes 786440 | tf_op jit(solution)/shard_map/ppermute | solution.py:589
  8.5 9.8 %collective-permute-start.5 = (bf16[80,256]{1,0:T(8,128)(2,1)S(1)}, bf16[80,256]{1,0:T(8,128)(2,1)S(1)}, u32[]{:S(2)}, u32[]{:S(2)}) collective-permute-start(bf16[80,256]{1,0:T(8,128)(2,1)S(1)} %get-tuple-element.31), channel_id=1, source_target_pairs={{0,4},{4,0},{8,12},{12,8},{16,20},{20,16},{24,28},{28,24},{1,5},{5... | collective-permute-start | bytes 122888 | tf_op jit(solution)/shard_map/ppermute | solution.py:526
  10.6 7.6 %collective-permute-start.6 = (bf16[80,256]{1,0:T(8,128)(2,1)S(1)}, bf16[80,256]{1,0:T(8,128)(2,1)S(1)}, u32[]{:S(2)}, u32[]{:S(2)}) collective-permute-start(bf16[80,256]{1,0:T(8,128)(2,1)S(1)} %get-tuple-element.36), channel_id=1, source_target_pairs={{4,8},{8,4},{12,16},{16,12},{20,24},{24,20},{5,9},{9,5},{13,17},{1... | collective-permute-start | bytes 122888 | tf_op jit(solution)/shard_map/ppermute | solution.py:526
  13.7 2.9 %copy-start.2 = (s32[16,16,16]{2,1,0:T(8,128)S(1)}, s32[16,16,16]{2,1,0:T(8,128)}, u32[]{:S(2)}) copy-start(s32[16,16,16]{2,1,0:T(8,128)} %param.18) | copy-start | bytes 49156
  13.8 2.9 %copy-start.3 = (s32[16,16,16]{2,1,0:T(8,128)S(1)}, s32[16,16,16]{2,1,0:T(8,128)}, u32[]{:S(2)}) copy-start(s32[16,16,16]{2,1,0:T(8,128)} %param.19) | copy-start | bytes 49156
  13.8 2.9 %copy-start.4 = (f32[64,2,256]{2,1,0:T(2,128)S(1)}, f32[64,2,256]{2,1,0:T(2,128)}, u32[]{:S(2)}) copy-start(f32[64,2,256]{2,1,0:T(2,128)} %param.21) | copy-start | bytes 393220
  13.8 2.9 %copy-start.6 = (s32[16,16]{1,0:T(8,128)S(1)}, s32[16,16]{1,0:T(8,128)}, u32[]{:S(2)}) copy-start(s32[16,16]{1,0:T(8,128)} %count_ref) | copy-start | bytes 3076
  19.1 3.6 %copy-start.5 = (bf16[256,256]{1,0:T(8,128)(2,1)S(1)}, bf16[256,256]{1,0:T(8,128)(2,1)}, u32[]{:S(2)}) copy-start(bf16[256,256]{1,0:T(8,128)(2,1)} %refs_8_.1) | copy-start | bytes 393220

commit v12 on v10

--- a/solution.py
+++ b/solution.py
@@ -321,8 +321,8 @@
             add_row(field_ref, part, tile_x - 1 if end else 0, value[:, part * lanes : (part + 1) * lanes])
 
 
-ROW = 8
 GROUP = 16
+SEGMENT = 8
 
 
 def order_kernel(
@@ -334,7 +334,6 @@
     table8[8 * kinds : 8 * kinds + 8, :] = jnp.zeros((8, width), F32)
     parents = parents_x * parents_y
     slots = list_ref.shape[1]
-    groups = parents // ROW
     lanes = early_ref.shape[1]
     across = parents_y * chunks
     entry = list_ref[...]
@@ -352,23 +351,16 @@
 
     down = lax.broadcasted_iota(jnp.int32, (parents, parents), 0)
     along = lax.broadcasted_iota(jnp.int32, (parents, parents), 1)
-    wanted = (ROW * (down % groups) + down // groups).astype(F32)
     earlier = lax.broadcasted_iota(jnp.int32, (slots, slots), 1) < lax.broadcasted_iota(jnp.int32, (slots, slots), 0)
     earlier = jnp.where(earlier, 1.0, 0.0).astype(BF16)
     slot = lax.broadcasted_iota(jnp.int32, (slots, parents), 0)
-    from_lane = lax.broadcasted_iota(jnp.int32, (ROW * lanes, lanes), 0)
-    to_lane = lax.broadcasted_iota(jnp.int32, (ROW * lanes, lanes), 1)
-    spreads = [
-        jnp.where(from_lane == (to_lane // slots) * lanes + n * slots + to_lane % slots, 1.0, 0.0).astype(BF16)
-        for n in range(4)
-    ]
-    least = (slots - 1 - 2 * lax.broadcasted_iota(jnp.int32, (parents, lanes), 1)).astype(F32)
+    most = (2 * lax.broadcasted_iota(jnp.int32, (parents, lanes), 1)).astype(F32)
     for number, at_ref in ((1, early_ref), (2, late_ref)):
         hit = jnp.where(turned_part == number, 1.0, 0.0)
         mine = jnp.where(part == number, 1.0, 0.0).astype(BF16)
         column = mm(mine, jnp.ones((slots, parents), BF16))
         row = jnp.sum(hit, axis=0, keepdims=True)
-        before = (column > row) | ((column == row) & (down < along))
+        before = (column < row) | ((column == row) & (down < along))
         rank = jnp.sum(jnp.where(before, 1.0, 0.0), axis=0, keepdims=True)
         place = mm(earlier, hit.astype(BF16)).astype(jnp.int32)
         place = jnp.where(turned_part == number, place, -1)
@@ -377,18 +369,25 @@
             dense = dense + jnp.where(place[n : n + 1] == slot, word[n : n + 1], 0)
         kind = jnp.where(slot.astype(F32) < row, dense & 127, kinds)
         source = dense >> 7
-        rest = jnp.zeros((lanes - 4 * slots, parents), F32)
         values = [source >> 8, source & 255, kind, along[0:slots]]
-        values = jnp.concatenate([value.astype(F32) for value in values] + [rest], axis=0).astype(BF16)
-        move = jnp.where(wanted == rank, 1.0, 0.0).astype(BF16)
-        moved = lax.dot_general(move, values, (((1,), (1,)), ((), ())), preferred_element_type=F32).astype(BF16)
-        moved = jnp.concatenate([moved[k * groups : (k + 1) * groups] for k in range(ROW)], axis=1)
-        high, low, kind, parent = [mm(moved, spread).astype(jnp.int32) for spread in spreads]
-        at_ref[0:groups, :] = (high * 256 + low) * 8
-        at_ref[groups : 2 * groups, :] = kind * 8
-        at_ref[2 * groups : 3 * groups, :] = parent * 8
-        reach = jnp.sum(jnp.where(column[:, :lanes] >= least, 1.0, 0.0), axis=0, keepdims=True).astype(jnp.int32)
-        at_ref[3 * groups :, :] = jnp.broadcast_to((reach + (GROUP - 1)) // GROUP, (8, lanes))
+        values = jnp.concatenate([value.astype(F32) for value in values], axis=0).astype(BF16)
+        ranked = jnp.where(down.astype(F32) == rank, 1.0, 0.0).astype(BF16)
+        moved = lax.dot_general(values, ranked, (((1,), (1,)), ((), ())), preferred_element_type=F32)
+        high, low, kind, parent = [
+            moved[n * slots : (n + 1) * slots].astype(jnp.int32) * 8 for n in range(4)
+        ]
+        reach = jnp.sum(jnp.where(column[:, :lanes] <= most, 1.0, 0.0), axis=0, keepdims=True).astype(jnp.int32)
+        head = jnp.broadcast_to(reach // GROUP, (8, lanes))
+        line = lax.broadcasted_iota(jnp.int32, (8, lanes), 0)
+        for n in range(parents // lanes):
+            head = jnp.where(line == n, parent[0:8, n * lanes : (n + 1) * lanes], head)
+        at_ref[0:8, :] = head
+        at = 8
+        for segment in range(0, slots, SEGMENT):
+            for value in (high * 256 + low, kind):
+                for n in range(parents // lanes):
+                    at_ref[at : at + SEGMENT, :] = value[segment : segment + SEGMENT, n * lanes : (n + 1) * lanes]
+                    at += SEGMENT
 
 
 def expand(sources, cells):
@@ -403,58 +402,65 @@
         pairs[c * count : (c + 1) * count, 1] = jnp.where(upper, turned, rows)
 
 
-def add_lists(parents, slots, at, cells, table8, sums):
+def load_lists(at_any, at, sems):
+    first = 1024 + (at.shape[0] - 1024) // 2
+    loads = []
+    for n, (start, size) in enumerate([(0, first), (first, at.shape[0] - first)]):
+        rows = pl.ds(start, size)
+        loads.append(pltpu.make_async_copy(at_any.at[rows], at.at[rows], sems.at[n]))
+        loads[-1].start()
+    return loads
+
+
+def add_lists(parents, slots, loads, at, cells, table8, sums):
     lanes = cells.shape[1]
-    groups = parents // GROUP
+    words = parents * SEGMENT
+    per_half = 128 // GROUP
 
     def step(length, n, carry):
-        first = n * (GROUP * slots)
-        second, third = first + parents * slots, first + 2 * parents * slots
+        first = 1024 + (n // per_half) * (128 * SEGMENT) + (n % per_half) * GROUP
         for k in range(GROUP):
             total = [None, None]
             for s in range(length):
-                source = pl.multiple_of(at[first + (k * slots + s)], 8)
-                kind = pl.multiple_of(at[second + (k * slots + s)], 8)
+                place = first + ((s // SEGMENT) * 2 * words + (s % SEGMENT) * 128 + k)
+                source = pl.multiple_of(at[place], 8)
+                kind = pl.multiple_of(at[place + words], 8)
                 term = cells[pl.ds(source, 8), :] * table8[pl.ds(kind, 8), :]
                 total[s % 2] = term if total[s % 2] is None else total[s % 2] + term
             total = total[0] + total[1] if length else jnp.zeros((8, lanes), F32)
-            sums[pl.ds(pl.multiple_of(at[third + k * slots], 8), 8), :] = total
+            sums[pl.ds(pl.multiple_of(at[n * GROUP + k], 8), 8), :] = total
         return carry
 
+    loads[0].wait()
     start = 0
-    for j, length in enumerate(range(slots, 0, -2)):
-        end = at[3 * parents * slots + j]
+    for j, length in enumerate(range(0, slots + 1, 2)):
+        if length == SEGMENT + 2:
+            loads[1].wait()
+        end = at[parents + j]
         lax.fori_loop(start, end, functools.partial(step, length), 0)
         start = end
-    lax.fori_loop(start, groups, functools.partial(step, 0), 0)
 
 
 def early_kernel(count, parents, slots, *refs):
     sources = refs[:count]
-    at_any, table8, sums, cells, at, sem = refs[count:]
-    load = pltpu.make_async_copy(at_any, at, sem)
-    load.start()
+    at_any, table8, sums, cells, at, sems = refs[count:]
+    loads = load_lists(at_any, at, sems)
     expand(sources, cells)
-    load.wait()
-    add_lists(parents, slots, at, cells, table8, sums)
+    add_lists(parents, slots, loads, at, cells, table8, sums)
 
 
 def late_kernel(count, tile_x, tile_y, slots, *refs):
     sources = refs[:count]
     (at_any, table8, early_ref, kept_ref, lower_ref, near_ref, recv_ref, down_hbm, out_hbm,
-     cells, sums, lines, at, down_ref, total_ref, out_ref, sems) = refs[count:]
+     cells, sums, lines, at, down_ref, total_ref, out_ref, list_sems, sems) = refs[count:]
     parents_x, parents_y = tile_x // 2, tile_y // 2
     parents = parents_x * parents_y
     lanes = table8.shape[1]
-    loads = [
-        pltpu.make_async_copy(at_any, at, sems.at[0]),
-        pltpu.make_async_copy(down_hbm, down_ref, sems.at[1]),
-    ]
-    for load in loads:
-        load.start()
+    loads = load_lists(at_any, at, list_sems)
+    weights = pltpu.make_async_copy(down_hbm, down_ref, sems.at[0])
+    weights.start()
     expand(sources, cells)
-    loads[0].wait()
-    add_lists(parents, slots, at, cells, table8, sums)
+    add_lists(parents, slots, loads, at, cells, table8, sums)
     raw = (sums[...] + early_ref[...]).reshape(parents // 2, 2, 8, lanes)
     one, other = raw[:, 0], raw[:, 1]
     line = lax.broadcasted_iota(jnp.int32, one.shape, 1)
@@ -464,7 +470,7 @@
     lines[...] = (with_real + turned).reshape(4 * parents, lanes)
     ordered = [lines[pl.ds(place, parents, stride=4), :].astype(BF16) for place in range(4)]
     incoming = jnp.concatenate(ordered, axis=1)
-    loads[1].wait()
+    weights.wait()
     for child in range(4):
         down = mm(incoming, down_ref[child])
         for part in range(2):
@@ -486,17 +492,24 @@
                     ]
         size = out_ref.shape[0] // 2
         rows = pl.ds(half * size, size)
-        stores.append(pltpu.make_async_copy(out_ref.at[rows], out_hbm.at[rows], sems.at[2 + half]))
+        stores.append(pltpu.make_async_copy(out_ref.at[rows], out_hbm.at[rows], sems.at[1 + half]))
         stores[-1].start()
     for store in stores:
         store.wait()
 
 
-def swap(low, high, axis):
+def swap(low, high, axis, other=None):
     count = lax.axis_size(axis)
     lows = [(i, i ^ 1) for i in range(count)]
     highs = [(i, (((i + 1) % count ^ 1) - 1) % count) for i in range(count)]
-    return lax.ppermute(low, axis, lows), lax.ppermute(high, axis, highs)
+    if other is not None:
+        breadth = lax.axis_size(other)
+        highs = [
+            (i * breadth + j, i * breadth + (j ^ 1) if i in (0, count - 1) else target * breadth + j)
+            for i, target in highs
+            for j in range(breadth)
+        ]
+    return lax.ppermute(low, axis, lows), lax.ppermute(high, axis if other is None else (axis, other), highs)
 
 
 def body(
@@ -575,7 +588,7 @@
         compiler_params=params(10),
         cost_estimate=cost(1 * MIB, MIB),
     )(live, inner_y, outer_y)
-    inner_x, outer_x = swap(low, high, "gx")
+    inner_x, outer_x = swap(low, high, "gx", "gy")
     live, coarse_count, _ = lax.optimization_barrier((live, coarse_count, low))
 
     near_rows = near_blocks.reshape(3, 6 * lanes, 2 * lanes)
@@ -597,24 +610,8 @@
         cost_estimate=cost(2000 * MIB, 5 * MIB),
     )(live, pats, near_rows, low_rows)
 
-    pair = [jax.ShapeDtypeStruct((2, 4, parents, lanes), F32)] * 2
-    lower, near, kept = pl.pallas_call(
-        functools.partial(halos_kernel, tile_x, tile_y),
-        name="halos",
-        out_shape=pair + [jax.ShapeDtypeStruct((4, parents, lanes), F32)],
-        in_specs=vmem(10),
-        out_specs=vmem(3),
-        scratch_shapes=[
-            pltpu.VMEM((4, 4, tile_x + 16, lanes), F32),
-            pltpu.VMEM((4, 4 * width, lanes), F32),
-            pltpu.VMEM((tile_x, lanes), F32),
-        ],
-        compiler_params=params(10),
-        cost_estimate=cost(100 * MIB, 5 * MIB),
-    )(inner_y, outer_y, inner_x, outer_x, agg_near, near_rows, low_rows, lower, near, kept)
-
     table = up_translator.reshape(kinds, 2, 2, half // 2).transpose(0, 2, 1, 3).reshape(4 * kinds, half // 2)
-    places = jax.ShapeDtypeStruct((3 * parents // ROW + 8, ROW * slots), jnp.int32)
+    places = jax.ShapeDtypeStruct((8 + 2 * slots * parents // 128, 128), jnp.int32)
     early_at, late_at, table8 = pl.pallas_call(
         functools.partial(order_kernel, chunks, kinds, parents_x, parents_y),
         name="order",
@@ -637,11 +634,28 @@
         scratch_shapes=[
             pltpu.VMEM((len(early) * parents * 8, wide // 4), F32),
             pltpu.SMEM(early_at.shape, jnp.int32),
-            pltpu.SemaphoreType.DMA,
+            pltpu.SemaphoreType.DMA((2,)),
         ],
         compiler_params=params(10),
         cost_estimate=cost(1000 * MIB, 4 * MIB),
     )(*early, early_at, table8)
+    lower, near, _ = lax.optimization_barrier((lower, near, early_sums))
+    pair = [jax.ShapeDtypeStruct((2, 4, parents, lanes), F32)] * 2
+    lower, near, kept = pl.pallas_call(
+        functools.partial(halos_kernel, tile_x, tile_y),
+        name="halos",
+        out_shape=pair + [jax.ShapeDtypeStruct((4, parents, lanes), F32)],
+        in_specs=vmem(10),
+        out_specs=vmem(3),
+        scratch_shapes=[
+            pltpu.VMEM((4, 4, tile_x + 16, lanes), F32),
+            pltpu.VMEM((4, 4 * width, lanes), F32),
+            pltpu.VMEM((tile_x, lanes), F32),
+        ],
+        compiler_params=params(10),
+        cost_estimate=cost(100 * MIB, 5 * MIB),
+    )(inner_y, outer_y, inner_x, outer_x, agg_near, near_rows, low_rows, lower, near, kept)
+
     out = pl.pallas_call(
         functools.partial(late_kernel, len(late), tile_x, tile_y, slots),
         name="late",
@@ -656,7 +670,8 @@
             pltpu.VMEM((4, wide, 2 * lanes), BF16),
             pltpu.VMEM((4, parents, 2 * lanes), BF16),
             pltpu.VMEM((2 * boxes, lanes), F32),
-            pltpu.SemaphoreType.DMA((4,)),
+            pltpu.SemaphoreType.DMA((2,)),
+            pltpu.SemaphoreType.DMA((3,)),
         ],
         compiler_params=params(16 if chunks <= 4 else 40),
         cost_estimate=cost(2000 * MIB, 8 * MIB),

time: 29.6 us -> 27.1 us (0.916)
  starting transfers between devices: 11.8 us -> 9.67 us
  Pallas kernels: 17.6 us -> 15.9 us
  waiting for transfers between devices: 0.02 us -> 1.17 us
    ppermute x4, starting transfers between devices: 8.27 us -> 6.12 us  [the longest x2 3.07 us: swap(): lax.ppermute(low, axis, lows)]
    ppermute x3, waiting for transfers between devices: 0.01 us -> 1.16 us  [body(): lax.ppermute(coarse, 'gy', [(i, i ^ d) for i in range(chunks)])]
    pallas_call x1, Pallas kernels: 1.65 us -> 0.95 us  [body(): pl.pallas_call(functools.partial(order_kernel, chunks, kinds, parents_x,...]
    pallas_call x1, Pallas kernels: 5.94 us -> 5.37 us  [body(): pl.pallas_call(functools.partial(late_kernel, len(late), tile_x, tile_y,...]
    pallas_call x1, Pallas kernels: 3.93 us -> 3.52 us  [body(): pl.pallas_call(functools.partial(early_kernel, len(early), parents, slots...]
  transfers between devices with their start and end apart: 7 -> 7, of which waited for: 0 -> 1; matrix products, arithmetic and copies ran while one was open for 0% -> 0% of each run, Pallas kernels for 34% -> 33%
where the time goes in v12:
time: 27.1 us; the launch traced here: 26.9 us
  Pallas kernels  15.9 us (59%)
  starting transfers between devices  9.67 us (36%)
  waiting for transfers between devices  1.17 us (4%)
    pallas_call x1, Pallas kernels, body(): pl.pallas_call(functools.partial(late_kernel, len(late), tile_x, tile_y,...  5.37 us
    ppermute x3, starting transfers between devices, body(): lax.ppermute(coarse, 'gy', [(i, i ^ d) for i in range(chunks)])  3.55 us
    pallas_call x1, Pallas kernels, body(): pl.pallas_call(functools.partial(early_kernel, len(early), parents, slots...  3.52 us
    ppermute x2, starting transfers between devices, swap(): lax.ppermute(low, axis, lows)  3.07 us
    ppermute x2, starting transfers between devices, swap(): lax.ppermute(high, axis if other is None else (axis, other), highs)  3.04 us
    pallas_call x1, Pallas kernels, body(): pl.pallas_call(functools.partial(local_kernel, tile_x, tile_y), name='loc...  2.83 us
    pallas_call x1, Pallas kernels, body(): pl.pallas_call(functools.partial(live_kernel, tile_x, tile_y), name='live...  1.61 us
    ppermute x3, waiting for transfers between devices, body(): lax.ppermute(coarse, 'gy', [(i, i ^ d) for i in range(chunks)])  1.16 us
  transfers between devices with their start and end apart: 7, of which 1 were waited for; matrix products, arithmetic and copies ran while one was open for 0% of the time, Pallas kernels for 33%

profile of v12, /device:TPU:0, one launch (start us, length us, event | category | flops | bytes accessed | tf_op | source)
XLA Modules:
  0.0 26.9 jit_solution(3601231551936097706)
XLA Ops:
  0.0 0.0 copy-start.1
  0.0 0.0 copy-start
  0.0 1.6 %live.1 = (bf16[1024,256]{1,0:T(8,128)(2,1)S(1)}, f32[1024,128]{1,0:T(8,128)S(1)}, bf16[64,256]{1,0:T(8,128)(2,1)S(1)}, bf16[64,256]{1,0:T(8,128)(2,1)S(1)}, bf1...) custom-call(bf16[2048,128]{1,0:T(8,128)(2,1)} %bitcast.24, s32[32,32]{1,0:T(8,128)} %counts_hbm.1, ...), custom_call_target="tpu_custom_call" | custom-call | flops 209715200 | bytes 3145728 | tf_op jit(solution)/shard_map/live/pallas_call | solution.py:532
  1.6 3.0 %collective-permute-start.2 = (bf16[64,256]{1,0:T(8,128)(2,1)S(1)}, bf16[64,256]{1,0:T(8,128)(2,1)S(1)}, u32[]{:S(2)}, u32[]{:S(2)}) collective-permute-start(bf16[64,256]{1,0:T(8,128)(2,1)S(1)} %get-tuple-element.31), channel_id=1, source_target_pairs={{0,1},{1,0},{2,3},{3,2},{4,5},{5,4},{6,7},{7,6},{8,9},{9,8},{10,11... | collective-permute-start | bytes 98312 | tf_op jit(solution)/shard_map/ppermute | solution.py:512
  4.6 1.5 %collective-permute-start.3 = (bf16[64,256]{1,0:T(8,128)(2,1)S(1)}, bf16[64,256]{1,0:T(8,128)(2,1)S(1)}, u32[]{:S(2)}, u32[]{:S(2)}) collective-permute-start(bf16[64,256]{1,0:T(8,128)(2,1)S(1)} %get-tuple-element.32), channel_id=1, source_target_pairs={{0,3},{1,2},{2,1},{3,0},{4,7},{5,6},{6,5},{7,4},{8,11},{9,10},{10,... | collective-permute-start | bytes 98312 | tf_op jit(solution)/shard_map/ppermute | solution.py:512
  6.1 0.8 %parents.1 = (bf16[1024,128]{1,0:T(8,128)(2,1)S(1)}, f32[3,1536,128]{2,1,0:T(8,128)S(1)}) custom-call(bf16[1024,256]{1,0:T(8,128)(2,1)S(1)} %get-tuple-element.39.live_ref, bf16[256,256]{1,0:T(8,128)(2,1)S(1)} %get-tuple-element.28.agg_ref, bf16[1024,512]{1,0:T(8,128)(2,1)S(1)} %get-tuple-element.29.up_ref), custom_call_target="tpu_custom_call" | custom-call | flops 419430400 | bytes 3145728 | tf_op jit(solution)/shard_map/parents/pallas_call | solution.py:557
  6.9 1.5 %collective-permute-start.4 = (bf16[1024,128]{1,0:T(8,128)(2,1)S(1)}, bf16[1024,128]{1,0:T(8,128)(2,1)S(1)}, u32[]{:S(2)}, u32[]{:S(2)}) collective-permute-start(bf16[1024,128]{1,0:T(8,128)(2,1)S(1)} %get-tuple-element.30.refs_0_), channel_id=1, source_target_pairs={{0,3},{1,2},{2,1},{3,0},{4,7},{5,6},{6,5},{7,4},{8,11},{9,10},{10,... | collective-permute-start | bytes 786440 | tf_op jit(solution)/shard_map/ppermute | solution.py:575
  8.4 1.5 %collective-permute-start.1 = (bf16[1024,128]{1,0:T(8,128)(2,1)S(1)}, bf16[1024,128]{1,0:T(8,128)(2,1)S(1)}, u32[]{:S(2)}, u32[]{:S(2)}) collective-permute-start(bf16[1024,128]{1,0:T(8,128)(2,1)S(1)} %get-tuple-element.30.refs_0_), channel_id=1, source_target_pairs={{0,2},{1,3},{2,0},{3,1},{4,6},{5,7},{6,4},{7,5},{8,10},{9,11},{10,... | collective-permute-start | bytes 786440 | tf_op jit(solution)/shard_map/ppermute | solution.py:575
  9.9 0.5 %collective-permute-start = (bf16[1024,128]{1,0:T(8,128)(2,1)S(1)}, bf16[1024,128]{1,0:T(8,128)(2,1)S(1)}, u32[]{:S(2)}, u32[]{:S(2)}) collective-permute-start(bf16[1024,128]{1,0:T(8,128)(2,1)S(1)} %get-tuple-element.30.refs_0_), channel_id=1, source_target_pairs={{0,1},{1,0},{2,3},{3,2},{4,5},{5,4},{6,7},{7,6},{8,9},{9,8},{10,11... | collective-permute-start | bytes 786440 | tf_op jit(solution)/shard_map/ppermute | solution.py:575
  10.4 0.0 collective-permute-done.2.inner_ref.inner_y
  10.4 0.0 collective-permute-done.3.outer_ref.outer_y
  10.5 0.1 collective-permute-start.5
  10.6 1.6 %collective-permute-start.6 = (bf16[80,256]{1,0:T(8,128)(2,1)S(1)}, bf16[80,256]{1,0:T(8,128)(2,1)S(1)}, u32[]{:S(2)}, u32[]{:S(2)}) collective-permute-start(bf16[80,256]{1,0:T(8,128)(2,1)S(1)} %get-tuple-element.38), channel_id=1, source_target_pairs={{0,1},{1,0},{2,3},{3,2},{4,8},{5,9},{6,10},{7,11},{8,4},{9,5},{10,... | collective-permute-start | bytes 122888 | tf_op jit(solution)/shard_map/ppermute | solution.py:512
  12.1 0.0 copy-done.1
  12.1 0.0 copy-done
  12.1 0.0 copy-start.2
  12.1 0.0 copy-start.3
  12.1 0.0 copy-start.4
  12.1 0.0 copy-start.6
  12.2 2.8 %local.1 = (f32[2,1024,128]{2,1,0:T(8,128)S(1)}, f32[2,1024,128]{2,1,0:T(8,128)S(1)}) custom-call(bf16[1024,256]{1,0:T(8,128)(2,1)S(1)} %get-tuple-element.39.live_ref, f32[3,1536,128]{2,1,0:T(8,128)S(1)} %get-tuple-element.40.pats, bf16[3,768,256]{2,1,0:T(8,128)(2,1)S(1)} %bitcast.14, f32[32,128]{1,0:T(8,128)S(1)} %bitcast.16), custom_call_target="tpu_custom_call" | custom-call | flops 4194304000 | bytes 5242880 | tf_op jit(solution)/shard_map/local/pallas_call | solution.py:597
  15.0 0.0 copy-done.2
  15.0 0.0 copy-done.3
  15.0 0.0 copy-done.4
  15.0 0.0 copy-done.6
  15.0 0.9 %order.1 = (s32[72,128]{1,0:T(8,128)S(1)}, s32[72,128]{1,0:T(8,128)S(1)}, f32[520,128]{1,0:T(8,128)S(1)}) custom-call(s32[256,16]{1,0:T(8,128)S(1)} %bitcast.18, s32[256,16]{1,0:T(8,128)S(1)} %bitcast.19, s32[16,16]{1,0:T(8,128)S(1)} %copy-done.6, f32[256,128]{1,0:T(8,128)S(1)} %bitcast.20), custom_call_target="tpu_custom_call" | custom-call | flops 629145600 | bytes 1048576 | tf_op jit(solution)/shard_map/order/pallas_call | solution.py:615
  16.0 1.2 %collective-permute-done.4.refs_1_ = bf16[1024,128]{1,0:T(8,128)(2,1)S(1)} collective-permute-done((bf16[1024,128]{1,0:T(8,128)(2,1)S(1)}, bf16[1024,128]{1,0:T(8,128)(2,1)S(1)}, u32[]{:S(2)}, u32[]{:S(2)}) %collective-permute-start.4) | collective-permute-done | bytes 262176 | tf_op jit(solution)/shard_map/ppermute | solution.py:575
  17.1 3.5 %early.1.refs_4_ = f32[2048,128]{1,0:T(8,128)S(1)} custom-call(bf16[1024,128]{1,0:T(8,128)(2,1)S(1)} %get-tuple-element.30.refs_0_, bf16[1024,128]{1,0:T(8,128)(2,1)S(1)} %collective-permute-done.4.refs_1_, s32[9216]{0:T(1024)S(1)} %bitcast.22, f32[520,128]{1,0:T(8,128)S(1)} %get-tuple-element.36.refs_3_), custom_call_target="tpu_custom_call" | custom-call | flops 2097152000 | bytes 4194304 | tf_op jit(solution)/shard_map/early/pallas_call | solution.py:628
  20.7 0.0 copy-start.5
  20.7 0.0 collective-permute-done.6.outer_x
  20.7 0.0 collective-permute-done.5.inner_x
  20.7 0.8 %halos.1 = (f32[2,4,256,128]{3,2,1,0:T(8,128)S(1)}, f32[2,4,256,128]{3,2,1,0:T(8,128)S(1)}, f32[4,256,128]{2,1,0:T(8,128)S(1)}) custom-call(bf16[64,256]{1,0:T(8,128)(2,1)S(1)} %collective-permute-done.2.inner_ref.inner_y, bf16[64,256]{1,0:T(8,128)(2,1)S(1)} %collective-permute-done.3.outer_ref.outer_y, bf16[80,256]{1,0:T(8,128)(2,1)S(1)} %collective-permute-done.5.inner_x, ...), custom_call_target="tpu_custom_call" | custom-call | flops 209715200 | bytes 5242880 | tf_op jit(solution)/shard_map/halos/pallas_call | solution.py:644
  21.5 0.0 collective-permute-done.1.refs_1_
  21.5 0.0 collective-permute-done.refs_0_
  21.6 0.0 copy-done.5
  21.6 5.4 %late.1 = f32[2048,128]{1,0:T(8,128)} custom-call(bf16[1024,128]{1,0:T(8,128)(2,1)S(1)} %collective-permute-done.refs_0_, bf16[1024,128]{1,0:T(8,128)(2,1)S(1)} %collective-permute-done.1.refs_1_, s32[9216]{0:T(1024)S(1)} %bitcast.21, f32[520,128]{1,0:T(8,128)S(1)} %get-tuple-element.36.refs_3_, f32[2048,128]{1,0:T(8,128)S(1)} %early.1.refs_4_, ...), custom_call_target="tpu_custom_call" | custom-call | flops 4194304000 | bytes 8388608 | tf_op jit(solution)/shard_map/late/pallas_call | solution.py:659
  (1 shorter events, 0.0 us)
Async XLA Ops:
  0.0 12.1 %copy-start.1 = (f32[16,2,128]{2,1,0:T(2,128)S(1)}, f32[16,2,128]{2,1,0:T(2,128)}, u32[]{:S(2)}) copy-start(f32[16,2,128]{2,1,0:T(2,128)} %param.16) | copy-start | bytes 49156
  0.0 12.1 %copy-start = (bf16[9,256,256]{2,1,0:T(8,128)(2,1)S(1)}, bf16[9,256,256]{2,1,0:T(8,128)(2,1)}, u32[]{:S(2)}) copy-start(bf16[9,256,256]{2,1,0:T(8,128)(2,1)} %param.15) | copy-start | bytes 3538948
  1.6 8.8 %collective-permute-start.2 = (bf16[64,256]{1,0:T(8,128)(2,1)S(1)}, bf16[64,256]{1,0:T(8,128)(2,1)S(1)}, u32[]{:S(2)}, u32[]{:S(2)}) collective-permute-start(bf16[64,256]{1,0:T(8,128)(2,1)S(1)} %get-tuple-element.31), channel_id=1, source_target_pairs={{0,1},{1,0},{2,3},{3,2},{4,5},{5,4},{6,7},{7,6},{8,9},{9,8},{10,11... | collective-permute-start | bytes 98312 | tf_op jit(solution)/shard_map/ppermute | solution.py:512
  4.6 5.8 %collective-permute-start.3 = (bf16[64,256]{1,0:T(8,128)(2,1)S(1)}, bf16[64,256]{1,0:T(8,128)(2,1)S(1)}, u32[]{:S(2)}, u32[]{:S(2)}) collective-permute-start(bf16[64,256]{1,0:T(8,128)(2,1)S(1)} %get-tuple-element.32), channel_id=1, source_target_pairs={{0,3},{1,2},{2,1},{3,0},{4,7},{5,6},{6,5},{7,4},{8,11},{9,10},{10,... | collective-permute-start | bytes 98312 | tf_op jit(solution)/shard_map/ppermute | solution.py:512
  6.9 10.3 %collective-permute-start.4 = (bf16[1024,128]{1,0:T(8,128)(2,1)S(1)}, bf16[1024,128]{1,0:T(8,128)(2,1)S(1)}, u32[]{:S(2)}, u32[]{:S(2)}) collective-permute-start(bf16[1024,128]{1,0:T(8,128)(2,1)S(1)} %get-tuple-element.30.refs_0_), channel_id=1, source_target_pairs={{0,3},{1,2},{2,1},{3,0},{4,7},{5,6},{6,5},{7,4},{8,11},{9,10},{10,... | collective-permute-start | bytes 786440 | tf_op jit(solution)/shard_map/ppermute | solution.py:575
  8.4 13.1 %collective-permute-start.1 = (bf16[1024,128]{1,0:T(8,128)(2,1)S(1)}, bf16[1024,128]{1,0:T(8,128)(2,1)S(1)}, u32[]{:S(2)}, u32[]{:S(2)}) collective-permute-start(bf16[1024,128]{1,0:T(8,128)(2,1)S(1)} %get-tuple-element.30.refs_0_), channel_id=1, source_target_pairs={{0,2},{1,3},{2,0},{3,1},{4,6},{5,7},{6,4},{7,5},{8,10},{9,11},{10,... | collective-permute-start | bytes 786440 | tf_op jit(solution)/shard_map/ppermute | solution.py:575
  9.9 11.6 %collective-permute-start = (bf16[1024,128]{1,0:T(8,128)(2,1)S(1)}, bf16[1024,128]{1,0:T(8,128)(2,1)S(1)}, u32[]{:S(2)}, u32[]{:S(2)}) collective-permute-start(bf16[1024,128]{1,0:T(8,128)(2,1)S(1)} %get-tuple-element.30.refs_0_), channel_id=1, source_target_pairs={{0,1},{1,0},{2,3},{3,2},{4,5},{5,4},{6,7},{7,6},{8,9},{9,8},{10,11... | collective-permute-start | bytes 786440 | tf_op jit(solution)/shard_map/ppermute | solution.py:575
  10.5 10.2 %collective-permute-start.5 = (bf16[80,256]{1,0:T(8,128)(2,1)S(1)}, bf16[80,256]{1,0:T(8,128)(2,1)S(1)}, u32[]{:S(2)}, u32[]{:S(2)}) collective-permute-start(bf16[80,256]{1,0:T(8,128)(2,1)S(1)} %get-tuple-element.33), channel_id=1, source_target_pairs={{0,4},{4,0},{8,12},{12,8},{16,20},{20,16},{24,28},{28,24},{1,5},{5... | collective-permute-start | bytes 122888 | tf_op jit(solution)/shard_map/ppermute | solution.py:512
  10.6 10.1 %collective-permute-start.6 = (bf16[80,256]{1,0:T(8,128)(2,1)S(1)}, bf16[80,256]{1,0:T(8,128)(2,1)S(1)}, u32[]{:S(2)}, u32[]{:S(2)}) collective-permute-start(bf16[80,256]{1,0:T(8,128)(2,1)S(1)} %get-tuple-element.38), channel_id=1, source_target_pairs={{0,1},{1,0},{2,3},{3,2},{4,8},{5,9},{6,10},{7,11},{8,4},{9,5},{10,... | collective-permute-start | bytes 122888 | tf_op jit(solution)/shard_map/ppermute | solution.py:512
  12.1 2.9 %copy-start.2 = (s32[16,16,16]{2,1,0:T(8,128)S(1)}, s32[16,16,16]{2,1,0:T(8,128)}, u32[]{:S(2)}) copy-start(s32[16,16,16]{2,1,0:T(8,128)} %param.18) | copy-start | bytes 49156
  12.1 2.9 %copy-start.3 = (s32[16,16,16]{2,1,0:T(8,128)S(1)}, s32[16,16,16]{2,1,0:T(8,128)}, u32[]{:S(2)}) copy-start(s32[16,16,16]{2,1,0:T(8,128)} %param.19) | copy-start | bytes 49156
  12.1 2.9 %copy-start.4 = (f32[64,2,256]{2,1,0:T(2,128)S(1)}, f32[64,2,256]{2,1,0:T(2,128)}, u32[]{:S(2)}) copy-start(f32[64,2,256]{2,1,0:T(2,128)} %param.21) | copy-start | bytes 393220
  12.1 2.9 %copy-start.6 = (s32[16,16]{1,0:T(8,128)S(1)}, s32[16,16]{1,0:T(8,128)}, u32[]{:S(2)}) copy-start(s32[16,16]{1,0:T(8,128)} %count_ref) | copy-start | bytes 3076
  20.7 0.9 %copy-start.5 = (bf16[256,256]{1,0:T(8,128)(2,1)S(1)}, bf16[256,256]{1,0:T(8,128)(2,1)}, u32[]{:S(2)}) copy-start(bf16[256,256]{1,0:T(8,128)(2,1)} %refs_8_.1) | copy-start | bytes 393220

commit v13 on v12

--- a/solution.py
+++ b/solution.py
@@ -218,8 +218,8 @@
 
 
 def halos_kernel(
-    tile_x, tile_y, inner_y, outer_y, inner_x, outer_x, agg_ref, near_ref, low_ref, lower_in, field_in, kept_in,
-    lower_ref, field_ref, kept_ref, columns, rims, line_ref,
+    tile_x, tile_y, inner_y, outer_y, inner_x, outer_x, agg_ref, near_ref, low_ref, recv_ref,
+    lower_in, field_in, kept_in, field_ref, kept_ref, columns, rims, line_ref, lower_ref,
 ):
     lanes = lower_in.shape[2]
     width = tile_y + 2 * LEFT
@@ -319,6 +319,11 @@
         value = mm(source, near_ref[2 * end])
         for part in range(2):
             add_row(field_ref, part, tile_x - 1 if end else 0, value[:, part * lanes : (part + 1) * lanes])
+    for child in range(4):
+        total = jnp.concatenate([lower_ref[part, child] for part in range(2)], axis=1).astype(BF16)
+        value = mm(total, recv_ref[...])
+        for part in range(2):
+            field_ref[part, child] = field_ref[part, child] + value[:, part * lanes : (part + 1) * lanes]
 
 
 GROUP = 16
@@ -326,8 +331,11 @@
 
 
 def order_kernel(
-    chunks, kinds, parents_x, parents_y, list_ref, kind_ref, count_ref, table_ref, early_ref, late_ref, table8, words
+    chunks, kinds, parents_x, parents_y, list_ref, kind_ref, count_ref, table_ref, down_ref, recv_ref,
+    early_ref, late_ref, table8, fold_ref, words
 ):
+    for child in range(4):
+        fold_ref[child] = mm(down_ref[child], recv_ref[...]).astype(BF16)
     width = table_ref.shape[1]
     for place, row in enumerate((0, 2, 0, 2, 1, 3, 1, 3)):
         table8[pl.ds(place, kinds, stride=8), :] = table_ref[pl.ds(row, kinds, stride=4), :]
@@ -384,8 +392,8 @@
         at_ref[0:8, :] = head
         at = 8
         for segment in range(0, slots, SEGMENT):
-            for value in (high * 256 + low, kind):
-                for n in range(parents // lanes):
+            for n in range(parents // lanes):
+                for value in (high * 256 + low, kind):
                     at_ref[at : at + SEGMENT, :] = value[segment : segment + SEGMENT, n * lanes : (n + 1) * lanes]
                     at += SEGMENT
 
@@ -403,10 +411,11 @@
 
 
 def load_lists(at_any, at, sems):
-    first = 1024 + (at.shape[0] - 1024) // 2
+    block = 2 * 128 * SEGMENT
+    half = 1024 + (at.shape[0] - 1024) // 2
     loads = []
-    for n, (start, size) in enumerate([(0, first), (first, at.shape[0] - first)]):
-        rows = pl.ds(start, size)
+    for n, (start, end) in enumerate([(0, 1024 + block), (1024 + block, half), (half, at.shape[0])]):
+        rows = pl.ds(start, end - start)
         loads.append(pltpu.make_async_copy(at_any.at[rows], at.at[rows], sems.at[n]))
         loads[-1].start()
     return loads
@@ -414,15 +423,19 @@
 
 def add_lists(parents, slots, loads, at, cells, table8, sums):
     lanes = cells.shape[1]
-    words = parents * SEGMENT
-    per_half = 128 // GROUP
+    words = 128 * SEGMENT
+    per_block = 128 // GROUP
 
     def step(length, n, carry):
-        first = 1024 + (n // per_half) * (128 * SEGMENT) + (n % per_half) * GROUP
+        @pl.when(n == per_block)
+        def _():
+            loads[1].wait()
+
+        first = 1024 + (n // per_block) * (2 * words) + (n % per_block) * GROUP
         for k in range(GROUP):
             total = [None, None]
             for s in range(length):
-                place = first + ((s // SEGMENT) * 2 * words + (s % SEGMENT) * 128 + k)
+                place = first + ((s // SEGMENT) * 2 * parents * SEGMENT + (s % SEGMENT) * 128 + k)
                 source = pl.multiple_of(at[place], 8)
                 kind = pl.multiple_of(at[place + words], 8)
                 term = cells[pl.ds(source, 8), :] * table8[pl.ds(kind, 8), :]
@@ -435,7 +448,7 @@
     start = 0
     for j, length in enumerate(range(0, slots + 1, 2)):
         if length == SEGMENT + 2:
-            loads[1].wait()
+            loads[2].wait()
         end = at[parents + j]
         lax.fori_loop(start, end, functools.partial(step, length), 0)
         start = end
@@ -451,14 +464,12 @@
 
 def late_kernel(count, tile_x, tile_y, slots, *refs):
     sources = refs[:count]
-    (at_any, table8, early_ref, kept_ref, lower_ref, near_ref, recv_ref, down_hbm, out_hbm,
-     cells, sums, lines, at, down_ref, total_ref, out_ref, list_sems, sems) = refs[count:]
+    (at_any, table8, early_ref, kept_ref, field_ref, fold_ref, out_hbm,
+     cells, sums, lines, at, out_ref, list_sems, sems) = refs[count:]
     parents_x, parents_y = tile_x // 2, tile_y // 2
     parents = parents_x * parents_y
     lanes = table8.shape[1]
     loads = load_lists(at_any, at, list_sems)
-    weights = pltpu.make_async_copy(down_hbm, down_ref, sems.at[0])
-    weights.start()
     expand(sources, cells)
     add_lists(parents, slots, loads, at, cells, table8, sums)
     raw = (sums[...] + early_ref[...]).reshape(parents // 2, 2, 8, lanes)
@@ -470,21 +481,16 @@
     lines[...] = (with_real + turned).reshape(4 * parents, lanes)
     ordered = [lines[pl.ds(place, parents, stride=4), :].astype(BF16) for place in range(4)]
     incoming = jnp.concatenate(ordered, axis=1)
-    weights.wait()
-    for child in range(4):
-        down = mm(incoming, down_ref[child])
-        for part in range(2):
-            value = down[:, part * lanes : (part + 1) * lanes] + lower_ref[part, child]
-            total_ref[child, :, part * lanes : (part + 1) * lanes] = value.astype(BF16)
+    fields = [mm(incoming, fold_ref[child]) for child in range(4)]
     stores = []
     for half in range(2):
         first, size = half * parents // 2, parents // 2
         rows = slice(first, first + size)
         for child in range(4):
-            field = mm(total_ref[child, rows, :], recv_ref[...])
             mask = kept_ref[child, rows, :]
             for part in range(2):
-                value = (field[:, part * lanes : (part + 1) * lanes] + near_ref[part, child, rows, :]) * mask
+                value = fields[child][rows, part * lanes : (part + 1) * lanes]
+                value = (value + field_ref[part, child, rows, :]) * mask
                 for p in range(parents_x // 2):
                     line = (2 * (half * parents_x // 2 + p) + child // 2) * tile_y + child % 2
                     out_ref[pl.ds(2 * line + part, parents_y, stride=4), :] = value[
@@ -492,7 +498,7 @@
                     ]
         size = out_ref.shape[0] // 2
         rows = pl.ds(half * size, size)
-        stores.append(pltpu.make_async_copy(out_ref.at[rows], out_hbm.at[rows], sems.at[1 + half]))
+        stores.append(pltpu.make_async_copy(out_ref.at[rows], out_hbm.at[rows], sems.at[half]))
         stores[-1].start()
     for store in stores:
         store.wait()
@@ -612,16 +618,24 @@
 
     table = up_translator.reshape(kinds, 2, 2, half // 2).transpose(0, 2, 1, 3).reshape(4 * kinds, half // 2)
     places = jax.ShapeDtypeStruct((8 + 2 * slots * parents // 128, 128), jnp.int32)
-    early_at, late_at, table8 = pl.pallas_call(
+    early_at, late_at, table8, fold = pl.pallas_call(
         functools.partial(order_kernel, chunks, kinds, parents_x, parents_y),
         name="order",
-        out_shape=[places, places, jax.ShapeDtypeStruct((8 * kinds + 8, half // 2), F32)],
-        in_specs=vmem(4),
-        out_specs=vmem(3),
+        out_shape=[
+            places,
+            places,
+            jax.ShapeDtypeStruct((8 * kinds + 8, half // 2), F32),
+            jax.ShapeDtypeStruct((4, wide, 2 * lanes), BF16),
+        ],
+        in_specs=vmem(6),
+        out_specs=vmem(4),
         scratch_shapes=[pltpu.VMEM((parents, 128), F32)],
         compiler_params=params(10),
         cost_estimate=cost(300 * MIB, MIB),
-    )(coarse_list.reshape(parents, slots), coarse_kind.reshape(parents, slots), coarse_count, table)
+    )(
+        coarse_list.reshape(parents, slots), coarse_kind.reshape(parents, slots), coarse_count, table,
+        parent_to_child, receive_map,
+    )
     early_at, late_at = early_at.reshape(-1), late_at.reshape(-1)
     anywhere = pl.BlockSpec(memory_space=pl.ANY)
     early, late = sources[:2], sources[2:]
@@ -634,48 +648,49 @@
         scratch_shapes=[
             pltpu.VMEM((len(early) * parents * 8, wide // 4), F32),
             pltpu.SMEM(early_at.shape, jnp.int32),
-            pltpu.SemaphoreType.DMA((2,)),
+            pltpu.SemaphoreType.DMA((3,)),
         ],
         compiler_params=params(10),
         cost_estimate=cost(1000 * MIB, 4 * MIB),
     )(*early, early_at, table8)
     lower, near, _ = lax.optimization_barrier((lower, near, early_sums))
-    pair = [jax.ShapeDtypeStruct((2, 4, parents, lanes), F32)] * 2
-    lower, near, kept = pl.pallas_call(
+    field, kept = pl.pallas_call(
         functools.partial(halos_kernel, tile_x, tile_y),
         name="halos",
-        out_shape=pair + [jax.ShapeDtypeStruct((4, parents, lanes), F32)],
-        in_specs=vmem(10),
-        out_specs=vmem(3),
+        out_shape=[
+            jax.ShapeDtypeStruct((2, 4, parents, lanes), F32),
+            jax.ShapeDtypeStruct((4, parents, lanes), F32),
+        ],
+        in_specs=vmem(11),
+        out_specs=vmem(2),
         scratch_shapes=[
             pltpu.VMEM((4, 4, tile_x + 16, lanes), F32),
             pltpu.VMEM((4, 4 * width, lanes), F32),
             pltpu.VMEM((tile_x, lanes), F32),
+            pltpu.VMEM((2, 4, parents, lanes), F32),
         ],
         compiler_params=params(10),
         cost_estimate=cost(100 * MIB, 5 * MIB),
-    )(inner_y, outer_y, inner_x, outer_x, agg_near, near_rows, low_rows, lower, near, kept)
+    )(inner_y, outer_y, inner_x, outer_x, agg_near, near_rows, low_rows, receive_map, lower, near, kept)
 
     out = pl.pallas_call(
         functools.partial(late_kernel, len(late), tile_x, tile_y, slots),
         name="late",
         out_shape=jax.ShapeDtypeStruct((2 * boxes, lanes), F32),
-        in_specs=vmem(len(late)) + [anywhere] + vmem(6) + [in_hbm],
+        in_specs=vmem(len(late)) + [anywhere] + vmem(5),
         out_specs=in_hbm,
         scratch_shapes=[
             pltpu.VMEM((len(late) * parents * 8, wide // 4), F32),
             pltpu.VMEM((8 * parents, wide // 4), F32),
             pltpu.VMEM((4 * parents, wide // 4), F32),
             pltpu.SMEM(late_at.shape, jnp.int32),
-            pltpu.VMEM((4, wide, 2 * lanes), BF16),
-            pltpu.VMEM((4, parents, 2 * lanes), BF16),
             pltpu.VMEM((2 * boxes, lanes), F32),
+            pltpu.SemaphoreType.DMA((3,)),
             pltpu.SemaphoreType.DMA((2,)),
-            pltpu.SemaphoreType.DMA((3,)),
         ],
         compiler_params=params(16 if chunks <= 4 else 40),
         cost_estimate=cost(2000 * MIB, 8 * MIB),
-    )(*late, late_at, table8, early_sums, kept, lower, near, receive_map, hbm(parent_to_child))
+    )(*late, late_at, table8, early_sums, kept, field, fold)
     return out.reshape(tile_x, tile_y, 2, lanes)
 
 

time: 27.1 us -> 26.7 us (0.985)
    ppermute x3, waiting for transfers between devices: 1.16 us -> 0.8 us  [body(): lax.ppermute(coarse, 'gy', [(i, i ^ d) for i in range(chunks)])]
    pallas_call x1, Pallas kernels: 5.37 us -> 5.06 us  [body(): pl.pallas_call(functools.partial(late_kernel, len(late), tile_x, tile_y,...]
    pallas_call x1, Pallas kernels: 0.95 us -> 1.24 us  [body(): pl.pallas_call(functools.partial(order_kernel, chunks, kinds, parents_x,...]
  transfers between devices with their start and end apart: 7 -> 7, of which waited for: 1 -> 2; matrix products, arithmetic and copies ran while one was open for 0% -> 0% of each run, Pallas kernels for 33% -> 34%
where the time goes in v13:
time: 26.7 us; the launch traced here: 26.8 us
  Pallas kernels  15.9 us (60%)
  starting transfers between devices  9.68 us (36%)
  waiting for transfers between devices  0.97 us (4%)
    pallas_call x1, Pallas kernels, body(): pl.pallas_call(functools.partial(late_kernel, len(late), tile_x, tile_y,...  5.06 us
    ppermute x3, starting transfers between devices, body(): lax.ppermute(coarse, 'gy', [(i, i ^ d) for i in range(chunks)])  3.55 us
    pallas_call x1, Pallas kernels, body(): pl.pallas_call(functools.partial(early_kernel, len(early), parents, slots...  3.37 us
    ppermute x2, starting transfers between devices, swap(): lax.ppermute(low, axis, lows)  3.07 us
    ppermute x2, starting transfers between devices, swap(): lax.ppermute(high, axis if other is None else (axis, other), highs)  3.05 us
    pallas_call x1, Pallas kernels, body(): pl.pallas_call(functools.partial(local_kernel, tile_x, tile_y), name='loc...  2.82 us
    pallas_call x1, Pallas kernels, body(): pl.pallas_call(functools.partial(live_kernel, tile_x, tile_y), name='live...  1.61 us
    pallas_call x1, Pallas kernels, body(): pl.pallas_call(functools.partial(order_kernel, chunks, kinds, parents_x,...  1.24 us
  transfers between devices with their start and end apart: 7, of which 2 were waited for; matrix products, arithmetic and copies ran while one was open for 0% of the time, Pallas kernels for 34%

profile of v13, /device:TPU:0, one launch (start us, length us, event | category | flops | bytes accessed | tf_op | source)
XLA Modules:
  0.0 26.8 jit_solution(4345128225950747697)
XLA Ops:
  0.0 0.0 copy-start.2
  0.0 0.0 copy-start
  0.0 1.6 %live.1 = (bf16[1024,256]{1,0:T(8,128)(2,1)S(1)}, f32[1024,128]{1,0:T(8,128)S(1)}, bf16[64,256]{1,0:T(8,128)(2,1)S(1)}, bf16[64,256]{1,0:T(8,128)(2,1)S(1)}, bf1...) custom-call(bf16[2048,128]{1,0:T(8,128)(2,1)} %bitcast.24, s32[32,32]{1,0:T(8,128)} %counts_hbm.1, ...), custom_call_target="tpu_custom_call" | custom-call | flops 209715200 | bytes 3145728 | tf_op jit(solution)/shard_map/live/pallas_call | solution.py:538
  1.6 3.0 %collective-permute-start.2 = (bf16[64,256]{1,0:T(8,128)(2,1)S(1)}, bf16[64,256]{1,0:T(8,128)(2,1)S(1)}, u32[]{:S(2)}, u32[]{:S(2)}) collective-permute-start(bf16[64,256]{1,0:T(8,128)(2,1)S(1)} %get-tuple-element.31), channel_id=1, source_target_pairs={{0,1},{1,0},{2,3},{3,2},{4,5},{5,4},{6,7},{7,6},{8,9},{9,8},{10,11... | collective-permute-start | bytes 98312 | tf_op jit(solution)/shard_map/ppermute | solution.py:518
  4.6 1.5 %collective-permute-start.3 = (bf16[64,256]{1,0:T(8,128)(2,1)S(1)}, bf16[64,256]{1,0:T(8,128)(2,1)S(1)}, u32[]{:S(2)}, u32[]{:S(2)}) collective-permute-start(bf16[64,256]{1,0:T(8,128)(2,1)S(1)} %get-tuple-element.32), channel_id=1, source_target_pairs={{0,3},{1,2},{2,1},{3,0},{4,7},{5,6},{6,5},{7,4},{8,11},{9,10},{10,... | collective-permute-start | bytes 98312 | tf_op jit(solution)/shard_map/ppermute | solution.py:518
  6.1 0.8 %parents.1 = (bf16[1024,128]{1,0:T(8,128)(2,1)S(1)}, f32[3,1536,128]{2,1,0:T(8,128)S(1)}) custom-call(bf16[1024,256]{1,0:T(8,128)(2,1)S(1)} %get-tuple-element.39.live_ref, bf16[256,256]{1,0:T(8,128)(2,1)S(1)} %get-tuple-element.28.agg_ref, bf16[1024,512]{1,0:T(8,128)(2,1)S(1)} %get-tuple-element.29.up_ref), custom_call_target="tpu_custom_call" | custom-call | flops 419430400 | bytes 3145728 | tf_op jit(solution)/shard_map/parents/pallas_call | solution.py:563
  6.9 1.5 %collective-permute-start.4 = (bf16[1024,128]{1,0:T(8,128)(2,1)S(1)}, bf16[1024,128]{1,0:T(8,128)(2,1)S(1)}, u32[]{:S(2)}, u32[]{:S(2)}) collective-permute-start(bf16[1024,128]{1,0:T(8,128)(2,1)S(1)} %get-tuple-element.30.refs_0_), channel_id=1, source_target_pairs={{0,3},{1,2},{2,1},{3,0},{4,7},{5,6},{6,5},{7,4},{8,11},{9,10},{10,... | collective-permute-start | bytes 786440 | tf_op jit(solution)/shard_map/ppermute | solution.py:581
  8.4 1.5 %collective-permute-start.1 = (bf16[1024,128]{1,0:T(8,128)(2,1)S(1)}, bf16[1024,128]{1,0:T(8,128)(2,1)S(1)}, u32[]{:S(2)}, u32[]{:S(2)}) collective-permute-start(bf16[1024,128]{1,0:T(8,128)(2,1)S(1)} %get-tuple-element.30.refs_0_), channel_id=1, source_target_pairs={{0,2},{1,3},{2,0},{3,1},{4,6},{5,7},{6,4},{7,5},{8,10},{9,11},{10,... | collective-permute-start | bytes 786440 | tf_op jit(solution)/shard_map/ppermute | solution.py:581
  9.9 0.5 %collective-permute-start = (bf16[1024,128]{1,0:T(8,128)(2,1)S(1)}, bf16[1024,128]{1,0:T(8,128)(2,1)S(1)}, u32[]{:S(2)}, u32[]{:S(2)}) collective-permute-start(bf16[1024,128]{1,0:T(8,128)(2,1)S(1)} %get-tuple-element.30.refs_0_), channel_id=1, source_target_pairs={{0,1},{1,0},{2,3},{3,2},{4,5},{5,4},{6,7},{7,6},{8,9},{9,8},{10,11... | collective-permute-start | bytes 786440 | tf_op jit(solution)/shard_map/ppermute | solution.py:581
  10.4 0.0 collective-permute-done.2.inner_ref.inner_y
  10.4 0.0 collective-permute-done.3.outer_ref.outer_y
  10.5 0.1 collective-permute-start.5
  10.6 1.6 %collective-permute-start.6 = (bf16[80,256]{1,0:T(8,128)(2,1)S(1)}, bf16[80,256]{1,0:T(8,128)(2,1)S(1)}, u32[]{:S(2)}, u32[]{:S(2)}) collective-permute-start(bf16[80,256]{1,0:T(8,128)(2,1)S(1)} %get-tuple-element.38), channel_id=1, source_target_pairs={{0,1},{1,0},{2,3},{3,2},{4,8},{5,9},{6,10},{7,11},{8,4},{9,5},{10,... | collective-permute-start | bytes 122888 | tf_op jit(solution)/shard_map/ppermute | solution.py:518
  12.1 0.0 copy-done.2
  12.1 0.0 copy-done
  12.1 0.0 copy-start.1
  12.1 0.0 copy-start.3
  12.1 0.0 copy-start.4
  12.2 0.0 copy-start.5
  12.2 0.0 copy-start.6
  12.2 0.0 copy-start.7
  12.2 2.8 %local.1 = (f32[2,1024,128]{2,1,0:T(8,128)S(1)}, f32[2,1024,128]{2,1,0:T(8,128)S(1)}) custom-call(bf16[1024,256]{1,0:T(8,128)(2,1)S(1)} %get-tuple-element.39.live_ref, f32[3,1536,128]{2,1,0:T(8,128)S(1)} %get-tuple-element.40.pats, bf16[3,768,256]{2,1,0:T(8,128)(2,1)S(1)} %bitcast.14, f32[32,128]{1,0:T(8,128)S(1)} %bitcast.16), custom_call_target="tpu_custom_call" | custom-call | flops 4194304000 | bytes 5242880 | tf_op jit(solution)/shard_map/local/pallas_call | solution.py:603
  15.0 0.0 copy-done.1
  15.0 0.0 copy-done.3
  15.0 0.0 copy-done.4
  15.1 0.0 copy-done.5
  15.1 0.0 copy-done.6
  15.1 0.0 copy-done.7
  15.1 1.2 %order.1 = (s32[72,128]{1,0:T(8,128)S(1)}, s32[72,128]{1,0:T(8,128)S(1)}, f32[520,128]{1,0:T(8,128)S(1)}, bf16[4,512,256]{2,1,0:T(8,128)(2,1)S(1)}) custom-call(s32[256,16]{1,0:T(8,128)S(1)} %bitcast.18, s32[256,16]{1,0:T(8,128)S(1)} %bitcast.19, s32[16,16]{1,0:T(8,128)S(1)} %copy-done.7, f32[256,128]{1,0:T(8,128)S(1)} %bitcast.20, ...), custom_call_target="tpu_custom_call" | custom-call | flops 629145600 | bytes 1048576 | tf_op jit(solution)/shard_map/order/pallas_call | solution.py:621
  16.3 0.8 %collective-permute-done.4.refs_1_ = bf16[1024,128]{1,0:T(8,128)(2,1)S(1)} collective-permute-done((bf16[1024,128]{1,0:T(8,128)(2,1)S(1)}, bf16[1024,128]{1,0:T(8,128)(2,1)S(1)}, u32[]{:S(2)}, u32[]{:S(2)}) %collective-permute-start.4) | collective-permute-done | bytes 262176 | tf_op jit(solution)/shard_map/ppermute | solution.py:581
  17.1 3.4 %early.1.refs_4_ = f32[2048,128]{1,0:T(8,128)S(1)} custom-call(bf16[1024,128]{1,0:T(8,128)(2,1)S(1)} %get-tuple-element.30.refs_0_, bf16[1024,128]{1,0:T(8,128)(2,1)S(1)} %collective-permute-done.4.refs_1_, s32[9216]{0:T(1024)S(1)} %bitcast.22, f32[520,128]{1,0:T(8,128)S(1)} %get-tuple-element.36.refs_3_), custom_call_target="tpu_custom_call" | custom-call | flops 2097152000 | bytes 4194304 | tf_op jit(solution)/shard_map/early/pallas_call | solution.py:642
  20.5 0.2 collective-permute-done.6.outer_x
  20.7 0.0 collective-permute-done.5.inner_x
  20.7 1.0 %halos.1 = (f32[2,4,256,128]{3,2,1,0:T(8,128)S(1)}, f32[4,256,128]{2,1,0:T(8,128)S(1)}) custom-call(bf16[64,256]{1,0:T(8,128)(2,1)S(1)} %collective-permute-done.2.inner_ref.inner_y, bf16[64,256]{1,0:T(8,128)(2,1)S(1)} %collective-permute-done.3.outer_ref.outer_y, bf16[80,256]{1,0:T(8,128)(2,1)S(1)} %collective-permute-done.5.inner_x, ...), custom_call_target="tpu_custom_call" | custom-call | flops 209715200 | bytes 5242880 | tf_op jit(solution)/shard_map/halos/pallas_call | solution.py:657
  21.7 0.0 collective-permute-done.1.refs_1_
  21.7 0.0 collective-permute-done.refs_0_
  21.7 5.1 %late.1 = f32[2048,128]{1,0:T(8,128)} custom-call(bf16[1024,128]{1,0:T(8,128)(2,1)S(1)} %collective-permute-done.refs_0_, bf16[1024,128]{1,0:T(8,128)(2,1)S(1)} %collective-permute-done.1.refs_1_, s32[9216]{0:T(1024)S(1)} %bitcast.21, f32[520,128]{1,0:T(8,128)S(1)} %get-tuple-element.36.refs_3_, f32[2048,128]{1,0:T(8,128)S(1)} %early.1.refs_4_, ...), custom_call_target="tpu_custom_call" | custom-call | flops 4194304000 | bytes 8388608 | tf_op jit(solution)/shard_map/late/pallas_call | solution.py:676
  (1 shorter events, 0.0 us)
Async XLA Ops:
  0.0 12.1 %copy-start.2 = (f32[16,2,128]{2,1,0:T(2,128)S(1)}, f32[16,2,128]{2,1,0:T(2,128)}, u32[]{:S(2)}) copy-start(f32[16,2,128]{2,1,0:T(2,128)} %param.16) | copy-start | bytes 49156
  0.0 12.1 %copy-start = (bf16[9,256,256]{2,1,0:T(8,128)(2,1)S(1)}, bf16[9,256,256]{2,1,0:T(8,128)(2,1)}, u32[]{:S(2)}) copy-start(bf16[9,256,256]{2,1,0:T(8,128)(2,1)} %param.15) | copy-start | bytes 3538948
  1.6 8.8 %collective-permute-start.2 = (bf16[64,256]{1,0:T(8,128)(2,1)S(1)}, bf16[64,256]{1,0:T(8,128)(2,1)S(1)}, u32[]{:S(2)}, u32[]{:S(2)}) collective-permute-start(bf16[64,256]{1,0:T(8,128)(2,1)S(1)} %get-tuple-element.31), channel_id=1, source_target_pairs={{0,1},{1,0},{2,3},{3,2},{4,5},{5,4},{6,7},{7,6},{8,9},{9,8},{10,11... | collective-permute-start | bytes 98312 | tf_op jit(solution)/shard_map/ppermute | solution.py:518
  4.6 5.8 %collective-permute-start.3 = (bf16[64,256]{1,0:T(8,128)(2,1)S(1)}, bf16[64,256]{1,0:T(8,128)(2,1)S(1)}, u32[]{:S(2)}, u32[]{:S(2)}) collective-permute-start(bf16[64,256]{1,0:T(8,128)(2,1)S(1)} %get-tuple-element.32), channel_id=1, source_target_pairs={{0,3},{1,2},{2,1},{3,0},{4,7},{5,6},{6,5},{7,4},{8,11},{9,10},{10,... | collective-permute-start | bytes 98312 | tf_op jit(solution)/shard_map/ppermute | solution.py:518
  6.9 10.3 %collective-permute-start.4 = (bf16[1024,128]{1,0:T(8,128)(2,1)S(1)}, bf16[1024,128]{1,0:T(8,128)(2,1)S(1)}, u32[]{:S(2)}, u32[]{:S(2)}) collective-permute-start(bf16[1024,128]{1,0:T(8,128)(2,1)S(1)} %get-tuple-element.30.refs_0_), channel_id=1, source_target_pairs={{0,3},{1,2},{2,1},{3,0},{4,7},{5,6},{6,5},{7,4},{8,11},{9,10},{10,... | collective-permute-start | bytes 786440 | tf_op jit(solution)/shard_map/ppermute | solution.py:581
  8.4 13.3 %collective-permute-start.1 = (bf16[1024,128]{1,0:T(8,128)(2,1)S(1)}, bf16[1024,128]{1,0:T(8,128)(2,1)S(1)}, u32[]{:S(2)}, u32[]{:S(2)}) collective-permute-start(bf16[1024,128]{1,0:T(8,128)(2,1)S(1)} %get-tuple-element.30.refs_0_), channel_id=1, source_target_pairs={{0,2},{1,3},{2,0},{3,1},{4,6},{5,7},{6,4},{7,5},{8,10},{9,11},{10,... | collective-permute-start | bytes 786440 | tf_op jit(solution)/shard_map/ppermute | solution.py:581
  9.9 11.8 %collective-permute-start = (bf16[1024,128]{1,0:T(8,128)(2,1)S(1)}, bf16[1024,128]{1,0:T(8,128)(2,1)S(1)}, u32[]{:S(2)}, u32[]{:S(2)}) collective-permute-start(bf16[1024,128]{1,0:T(8,128)(2,1)S(1)} %get-tuple-element.30.refs_0_), channel_id=1, source_target_pairs={{0,1},{1,0},{2,3},{3,2},{4,5},{5,4},{6,7},{7,6},{8,9},{9,8},{10,11... | collective-permute-start | bytes 786440 | tf_op jit(solution)/shard_map/ppermute | solution.py:581
  10.5 10.2 %collective-permute-start.5 = (bf16[80,256]{1,0:T(8,128)(2,1)S(1)}, bf16[80,256]{1,0:T(8,128)(2,1)S(1)}, u32[]{:S(2)}, u32[]{:S(2)}) collective-permute-start(bf16[80,256]{1,0:T(8,128)(2,1)S(1)} %get-tuple-element.33), channel_id=1, source_target_pairs={{0,4},{4,0},{8,12},{12,8},{16,20},{20,16},{24,28},{28,24},{1,5},{5... | collective-permute-start | bytes 122888 | tf_op jit(solution)/shard_map/ppermute | solution.py:518
  10.6 10.1 %collective-permute-start.6 = (bf16[80,256]{1,0:T(8,128)(2,1)S(1)}, bf16[80,256]{1,0:T(8,128)(2,1)S(1)}, u32[]{:S(2)}, u32[]{:S(2)}) collective-permute-start(bf16[80,256]{1,0:T(8,128)(2,1)S(1)} %get-tuple-element.38), channel_id=1, source_target_pairs={{0,1},{1,0},{2,3},{3,2},{4,8},{5,9},{6,10},{7,11},{8,4},{9,5},{10,... | collective-permute-start | bytes 122888 | tf_op jit(solution)/shard_map/ppermute | solution.py:518
  12.1 2.9 %copy-start.1 = (bf16[256,256]{1,0:T(8,128)(2,1)S(1)}, bf16[256,256]{1,0:T(8,128)(2,1)}, u32[]{:S(2)}) copy-start(bf16[256,256]{1,0:T(8,128)(2,1)} %recv_ref.3) | copy-start | bytes 393220
  12.1 2.9 %copy-start.3 = (bf16[4,512,256]{2,1,0:T(8,128)(2,1)S(1)}, bf16[4,512,256]{2,1,0:T(8,128)(2,1)}, u32[]{:S(2)}) copy-start(bf16[4,512,256]{2,1,0:T(8,128)(2,1)} %down_ref.1) | copy-start | bytes 3145732
  12.1 2.9 %copy-start.4 = (s32[16,16,16]{2,1,0:T(8,128)S(1)}, s32[16,16,16]{2,1,0:T(8,128)}, u32[]{:S(2)}) copy-start(s32[16,16,16]{2,1,0:T(8,128)} %param.18) | copy-start | bytes 49156
  12.2 2.9 %copy-start.5 = (s32[16,16,16]{2,1,0:T(8,128)S(1)}, s32[16,16,16]{2,1,0:T(8,128)}, u32[]{:S(2)}) copy-start(s32[16,16,16]{2,1,0:T(8,128)} %param.19) | copy-start | bytes 49156
  12.2 2.9 %copy-start.6 = (f32[64,2,256]{2,1,0:T(2,128)S(1)}, f32[64,2,256]{2,1,0:T(2,128)}, u32[]{:S(2)}) copy-start(f32[64,2,256]{2,1,0:T(2,128)} %param.21) | copy-start | bytes 393220
  12.2 2.9 %copy-start.7 = (s32[16,16]{1,0:T(8,128)S(1)}, s32[16,16]{1,0:T(8,128)}, u32[]{:S(2)}) copy-start(s32[16,16]{1,0:T(8,128)} %count_ref) | copy-start | bytes 3076

commit v14 on v13

--- a/solution.py
+++ b/solution.py
@@ -382,7 +382,7 @@
         ranked = jnp.where(down.astype(F32) == rank, 1.0, 0.0).astype(BF16)
         moved = lax.dot_general(values, ranked, (((1,), (1,)), ((), ())), preferred_element_type=F32)
         high, low, kind, parent = [
-            moved[n * slots : (n + 1) * slots].astype(jnp.int32) * 8 for n in range(4)
+            moved[n * slots : (n + 1) * slots].astype(jnp.int32) for n in range(4)
         ]
         reach = jnp.sum(jnp.where(column[:, :lanes] <= most, 1.0, 0.0), axis=0, keepdims=True).astype(jnp.int32)
         head = jnp.broadcast_to(reach // GROUP, (8, lanes))
@@ -423,6 +423,7 @@
 
 def add_lists(parents, slots, loads, at, cells, table8, sums):
     lanes = cells.shape[1]
+    tiles, kind_tiles, sum_tiles = [ref.reshape(ref.shape[0] // 8, 8, lanes) for ref in (cells, table8, sums)]
     words = 128 * SEGMENT
     per_block = 128 // GROUP
 
@@ -436,12 +437,10 @@
             total = [None, None]
             for s in range(length):
                 place = first + ((s // SEGMENT) * 2 * parents * SEGMENT + (s % SEGMENT) * 128 + k)
-                source = pl.multiple_of(at[place], 8)
-                kind = pl.multiple_of(at[place + words], 8)
-                term = cells[pl.ds(source, 8), :] * table8[pl.ds(kind, 8), :]
+                term = tiles[at[place]] * kind_tiles[at[place + words]]
                 total[s % 2] = term if total[s % 2] is None else total[s % 2] + term
             total = total[0] + total[1] if length else jnp.zeros((8, lanes), F32)
-            sums[pl.ds(pl.multiple_of(at[n * GROUP + k], 8), 8), :] = total
+            sum_tiles[at[n * GROUP + k]] = total
         return carry
 
     loads[0].wait()

time: 26.7 us -> 28.2 us (1.056)
  Pallas kernels: 15.9 us -> 17.5 us
    pallas_call x1, Pallas kernels: 3.37 us -> 4.35 us  [body(): pl.pallas_call(functools.partial(early_kernel, len(early), parents, slots...]
    pallas_call x1, Pallas kernels: 5.06 us -> 5.71 us  [body(): pl.pallas_call(functools.partial(late_kernel, len(late), tile_x, tile_y,...]
  transfers between devices with their start and end apart: 7 -> 7, of which waited for: 2 -> 1; matrix products, arithmetic and copies ran while one was open for 0% -> 0% of each run, Pallas kernels for 34% -> 36%
where the time goes in v14:
time: 28.2 us
  Pallas kernels  17.5 us (62%)
  starting transfers between devices  9.68 us (34%)
  waiting for transfers between devices  0.81 us (3%)
    pallas_call x1, Pallas kernels, body(): pl.pallas_call(functools.partial(late_kernel, len(late), tile_x, tile_y,...  5.71 us
    pallas_call x1, Pallas kernels, body(): pl.pallas_call(functools.partial(early_kernel, len(early), parents, slots...  4.35 us
    ppermute x3, starting transfers between devices, body(): lax.ppermute(coarse, 'gy', [(i, i ^ d) for i in range(chunks)])  3.55 us
    ppermute x2, starting transfers between devices, swap(): lax.ppermute(low, axis, lows)  3.07 us
    ppermute x2, starting transfers between devices, swap(): lax.ppermute(high, axis if other is None else (axis, other), highs)  3.05 us
    pallas_call x1, Pallas kernels, body(): pl.pallas_call(functools.partial(local_kernel, tile_x, tile_y), name='loc...  2.82 us
    pallas_call x1, Pallas kernels, body(): pl.pallas_call(functools.partial(live_kernel, tile_x, tile_y), name='live...  1.61 us
    pallas_call x1, Pallas kernels, body(): pl.pallas_call(functools.partial(order_kernel, chunks, kinds, parents_x,...  1.24 us
  transfers between devices with their start and end apart: 7, of which 1 were waited for; matrix products, arithmetic and copies ran while one was open for 0% of the time, Pallas kernels for 36%

profile of v14, /device:TPU:0, one launch (start us, length us, event | category | flops | bytes accessed | tf_op | source)
XLA Modules:
  0.0 28.2 jit_solution(12151693840751839076)
XLA Ops:
  0.0 0.0 copy-start.2
  0.0 0.0 copy-start
  0.0 1.6 %live.1 = (bf16[1024,256]{1,0:T(8,128)(2,1)S(1)}, f32[1024,128]{1,0:T(8,128)S(1)}, bf16[64,256]{1,0:T(8,128)(2,1)S(1)}, bf16[64,256]{1,0:T(8,128)(2,1)S(1)}, bf1...) custom-call(bf16[2048,128]{1,0:T(8,128)(2,1)} %bitcast.24, s32[32,32]{1,0:T(8,128)} %counts_hbm.1, ...), custom_call_target="tpu_custom_call" | custom-call | flops 209715200 | bytes 3145728 | tf_op jit(solution)/shard_map/live/pallas_call | solution.py:537
  1.6 3.0 %collective-permute-start.2 = (bf16[64,256]{1,0:T(8,128)(2,1)S(1)}, bf16[64,256]{1,0:T(8,128)(2,1)S(1)}, u32[]{:S(2)}, u32[]{:S(2)}) collective-permute-start(bf16[64,256]{1,0:T(8,128)(2,1)S(1)} %get-tuple-element.31), channel_id=1, source_target_pairs={{0,1},{1,0},{2,3},{3,2},{4,5},{5,4},{6,7},{7,6},{8,9},{9,8},{10,11... | collective-permute-start | bytes 98312 | tf_op jit(solution)/shard_map/ppermute | solution.py:517
  4.6 1.5 %collective-permute-start.3 = (bf16[64,256]{1,0:T(8,128)(2,1)S(1)}, bf16[64,256]{1,0:T(8,128)(2,1)S(1)}, u32[]{:S(2)}, u32[]{:S(2)}) collective-permute-start(bf16[64,256]{1,0:T(8,128)(2,1)S(1)} %get-tuple-element.32), channel_id=1, source_target_pairs={{0,3},{1,2},{2,1},{3,0},{4,7},{5,6},{6,5},{7,4},{8,11},{9,10},{10,... | collective-permute-start | bytes 98312 | tf_op jit(solution)/shard_map/ppermute | solution.py:517
  6.1 0.8 %parents.1 = (bf16[1024,128]{1,0:T(8,128)(2,1)S(1)}, f32[3,1536,128]{2,1,0:T(8,128)S(1)}) custom-call(bf16[1024,256]{1,0:T(8,128)(2,1)S(1)} %get-tuple-element.39.live_ref, bf16[256,256]{1,0:T(8,128)(2,1)S(1)} %get-tuple-element.28.agg_ref, bf16[1024,512]{1,0:T(8,128)(2,1)S(1)} %get-tuple-element.29.up_ref), custom_call_target="tpu_custom_call" | custom-call | flops 419430400 | bytes 3145728 | tf_op jit(solution)/shard_map/parents/pallas_call | solution.py:562
  6.9 1.5 %collective-permute-start.4 = (bf16[1024,128]{1,0:T(8,128)(2,1)S(1)}, bf16[1024,128]{1,0:T(8,128)(2,1)S(1)}, u32[]{:S(2)}, u32[]{:S(2)}) collective-permute-start(bf16[1024,128]{1,0:T(8,128)(2,1)S(1)} %get-tuple-element.30.refs_0_), channel_id=1, source_target_pairs={{0,3},{1,2},{2,1},{3,0},{4,7},{5,6},{6,5},{7,4},{8,11},{9,10},{10,... | collective-permute-start | bytes 786440 | tf_op jit(solution)/shard_map/ppermute | solution.py:580
  8.4 1.5 %collective-permute-start.1 = (bf16[1024,128]{1,0:T(8,128)(2,1)S(1)}, bf16[1024,128]{1,0:T(8,128)(2,1)S(1)}, u32[]{:S(2)}, u32[]{:S(2)}) collective-permute-start(bf16[1024,128]{1,0:T(8,128)(2,1)S(1)} %get-tuple-element.30.refs_0_), channel_id=1, source_target_pairs={{0,2},{1,3},{2,0},{3,1},{4,6},{5,7},{6,4},{7,5},{8,10},{9,11},{10,... | collective-permute-start | bytes 786440 | tf_op jit(solution)/shard_map/ppermute | solution.py:580
  9.9 0.5 %collective-permute-start = (bf16[1024,128]{1,0:T(8,128)(2,1)S(1)}, bf16[1024,128]{1,0:T(8,128)(2,1)S(1)}, u32[]{:S(2)}, u32[]{:S(2)}) collective-permute-start(bf16[1024,128]{1,0:T(8,128)(2,1)S(1)} %get-tuple-element.30.refs_0_), channel_id=1, source_target_pairs={{0,1},{1,0},{2,3},{3,2},{4,5},{5,4},{6,7},{7,6},{8,9},{9,8},{10,11... | collective-permute-start | bytes 786440 | tf_op jit(solution)/shard_map/ppermute | solution.py:580
  10.4 0.0 collective-permute-done.2.inner_ref.inner_y
  10.4 0.0 collective-permute-done.3.outer_ref.outer_y
  10.5 0.1 collective-permute-start.5
  10.6 1.6 %collective-permute-start.6 = (bf16[80,256]{1,0:T(8,128)(2,1)S(1)}, bf16[80,256]{1,0:T(8,128)(2,1)S(1)}, u32[]{:S(2)}, u32[]{:S(2)}) collective-permute-start(bf16[80,256]{1,0:T(8,128)(2,1)S(1)} %get-tuple-element.38), channel_id=1, source_target_pairs={{0,1},{1,0},{2,3},{3,2},{4,8},{5,9},{6,10},{7,11},{8,4},{9,5},{10,... | collective-permute-start | bytes 122888 | tf_op jit(solution)/shard_map/ppermute | solution.py:517
  12.1 0.0 copy-done.2
  12.1 0.0 copy-done
  12.1 0.0 copy-start.1
  12.1 0.0 copy-start.3
  12.1 0.0 copy-start.4
  12.2 0.0 copy-start.5
  12.2 0.0 copy-start.6
  12.2 0.0 copy-start.7
  12.2 2.8 %local.1 = (f32[2,1024,128]{2,1,0:T(8,128)S(1)}, f32[2,1024,128]{2,1,0:T(8,128)S(1)}) custom-call(bf16[1024,256]{1,0:T(8,128)(2,1)S(1)} %get-tuple-element.39.live_ref, f32[3,1536,128]{2,1,0:T(8,128)S(1)} %get-tuple-element.40.pats, bf16[3,768,256]{2,1,0:T(8,128)(2,1)S(1)} %bitcast.14, f32[32,128]{1,0:T(8,128)S(1)} %bitcast.16), custom_call_target="tpu_custom_call" | custom-call | flops 4194304000 | bytes 5242880 | tf_op jit(solution)/shard_map/local/pallas_call | solution.py:602
  15.0 0.0 copy-done.1
  15.0 0.0 copy-done.3
  15.0 0.0 copy-done.4
  15.1 0.0 copy-done.5
  15.1 0.0 copy-done.6
  15.1 0.0 copy-done.7
  15.1 1.2 %order.1 = (s32[72,128]{1,0:T(8,128)S(1)}, s32[72,128]{1,0:T(8,128)S(1)}, f32[520,128]{1,0:T(8,128)S(1)}, bf16[4,512,256]{2,1,0:T(8,128)(2,1)S(1)}) custom-call(s32[256,16]{1,0:T(8,128)S(1)} %bitcast.18, s32[256,16]{1,0:T(8,128)S(1)} %bitcast.19, s32[16,16]{1,0:T(8,128)S(1)} %copy-done.7, f32[256,128]{1,0:T(8,128)S(1)} %bitcast.20, ...), custom_call_target="tpu_custom_call" | custom-call | flops 629145600 | bytes 1048576 | tf_op jit(solution)/shard_map/order/pallas_call | solution.py:620
  16.3 0.8 %collective-permute-done.4.refs_1_ = bf16[1024,128]{1,0:T(8,128)(2,1)S(1)} collective-permute-done((bf16[1024,128]{1,0:T(8,128)(2,1)S(1)}, bf16[1024,128]{1,0:T(8,128)(2,1)S(1)}, u32[]{:S(2)}, u32[]{:S(2)}) %collective-permute-start.4) | collective-permute-done | bytes 262176 | tf_op jit(solution)/shard_map/ppermute | solution.py:580
  17.1 4.3 %early.1.refs_4_ = f32[2048,128]{1,0:T(8,128)S(1)} custom-call(bf16[1024,128]{1,0:T(8,128)(2,1)S(1)} %get-tuple-element.30.refs_0_, bf16[1024,128]{1,0:T(8,128)(2,1)S(1)} %collective-permute-done.4.refs_1_, s32[9216]{0:T(1024)S(1)} %bitcast.22, f32[520,128]{1,0:T(8,128)S(1)} %get-tuple-element.36.refs_3_), custom_call_target="tpu_custom_call" | custom-call | flops 2097152000 | bytes 4194304 | tf_op jit(solution)/shard_map/early/pallas_call | solution.py:641
  21.5 0.0 collective-permute-done.6.outer_x
  21.5 0.0 collective-permute-done.5.inner_x
  21.5 1.0 %halos.1 = (f32[2,4,256,128]{3,2,1,0:T(8,128)S(1)}, f32[4,256,128]{2,1,0:T(8,128)S(1)}) custom-call(bf16[64,256]{1,0:T(8,128)(2,1)S(1)} %collective-permute-done.2.inner_ref.inner_y, bf16[64,256]{1,0:T(8,128)(2,1)S(1)} %collective-permute-done.3.outer_ref.outer_y, bf16[80,256]{1,0:T(8,128)(2,1)S(1)} %collective-permute-done.5.inner_x, ...), custom_call_target="tpu_custom_call" | custom-call | flops 209715200 | bytes 5242880 | tf_op jit(solution)/shard_map/halos/pallas_call | solution.py:656
  22.5 0.0 collective-permute-done.1.refs_1_
  22.5 0.0 collective-permute-done.refs_0_
  22.5 5.7 %late.1 = f32[2048,128]{1,0:T(8,128)} custom-call(bf16[1024,128]{1,0:T(8,128)(2,1)S(1)} %collective-permute-done.refs_0_, bf16[1024,128]{1,0:T(8,128)(2,1)S(1)} %collective-permute-done.1.refs_1_, s32[9216]{0:T(1024)S(1)} %bitcast.21, f32[520,128]{1,0:T(8,128)S(1)} %get-tuple-element.36.refs_3_, f32[2048,128]{1,0:T(8,128)S(1)} %early.1.refs_4_, ...), custom_call_target="tpu_custom_call" | custom-call | flops 4194304000 | bytes 8388608 | tf_op jit(solution)/shard_map/late/pallas_call | solution.py:675
  (1 shorter events, 0.0 us)
Async XLA Ops:
  0.0 12.1 %copy-start.2 = (f32[16,2,128]{2,1,0:T(2,128)S(1)}, f32[16,2,128]{2,1,0:T(2,128)}, u32[]{:S(2)}) copy-start(f32[16,2,128]{2,1,0:T(2,128)} %param.16) | copy-start | bytes 49156
  0.0 12.1 %copy-start = (bf16[9,256,256]{2,1,0:T(8,128)(2,1)S(1)}, bf16[9,256,256]{2,1,0:T(8,128)(2,1)}, u32[]{:S(2)}) copy-start(bf16[9,256,256]{2,1,0:T(8,128)(2,1)} %param.15) | copy-start | bytes 3538948
  1.6 8.8 %collective-permute-start.2 = (bf16[64,256]{1,0:T(8,128)(2,1)S(1)}, bf16[64,256]{1,0:T(8,128)(2,1)S(1)}, u32[]{:S(2)}, u32[]{:S(2)}) collective-permute-start(bf16[64,256]{1,0:T(8,128)(2,1)S(1)} %get-tuple-element.31), channel_id=1, source_target_pairs={{0,1},{1,0},{2,3},{3,2},{4,5},{5,4},{6,7},{7,6},{8,9},{9,8},{10,11... | collective-permute-start | bytes 98312 | tf_op jit(solution)/shard_map/ppermute | solution.py:517
  4.6 5.8 %collective-permute-start.3 = (bf16[64,256]{1,0:T(8,128)(2,1)S(1)}, bf16[64,256]{1,0:T(8,128)(2,1)S(1)}, u32[]{:S(2)}, u32[]{:S(2)}) collective-permute-start(bf16[64,256]{1,0:T(8,128)(2,1)S(1)} %get-tuple-element.32), channel_id=1, source_target_pairs={{0,3},{1,2},{2,1},{3,0},{4,7},{5,6},{6,5},{7,4},{8,11},{9,10},{10,... | collective-permute-start | bytes 98312 | tf_op jit(solution)/shard_map/ppermute | solution.py:517
  6.9 10.3 %collective-permute-start.4 = (bf16[1024,128]{1,0:T(8,128)(2,1)S(1)}, bf16[1024,128]{1,0:T(8,128)(2,1)S(1)}, u32[]{:S(2)}, u32[]{:S(2)}) collective-permute-start(bf16[1024,128]{1,0:T(8,128)(2,1)S(1)} %get-tuple-element.30.refs_0_), channel_id=1, source_target_pairs={{0,3},{1,2},{2,1},{3,0},{4,7},{5,6},{6,5},{7,4},{8,11},{9,10},{10,... | collective-permute-start | bytes 786440 | tf_op jit(solution)/shard_map/ppermute | solution.py:580
  8.4 14.1 %collective-permute-start.1 = (bf16[1024,128]{1,0:T(8,128)(2,1)S(1)}, bf16[1024,128]{1,0:T(8,128)(2,1)S(1)}, u32[]{:S(2)}, u32[]{:S(2)}) collective-permute-start(bf16[1024,128]{1,0:T(8,128)(2,1)S(1)} %get-tuple-element.30.refs_0_), channel_id=1, source_target_pairs={{0,2},{1,3},{2,0},{3,1},{4,6},{5,7},{6,4},{7,5},{8,10},{9,11},{10,... | collective-permute-start | bytes 786440 | tf_op jit(solution)/shard_map/ppermute | solution.py:580
  9.9 12.6 %collective-permute-start = (bf16[1024,128]{1,0:T(8,128)(2,1)S(1)}, bf16[1024,128]{1,0:T(8,128)(2,1)S(1)}, u32[]{:S(2)}, u32[]{:S(2)}) collective-permute-start(bf16[1024,128]{1,0:T(8,128)(2,1)S(1)} %get-tuple-element.30.refs_0_), channel_id=1, source_target_pairs={{0,1},{1,0},{2,3},{3,2},{4,5},{5,4},{6,7},{7,6},{8,9},{9,8},{10,11... | collective-permute-start | bytes 786440 | tf_op jit(solution)/shard_map/ppermute | solution.py:580
  10.5 11.0 %collective-permute-start.5 = (bf16[80,256]{1,0:T(8,128)(2,1)S(1)}, bf16[80,256]{1,0:T(8,128)(2,1)S(1)}, u32[]{:S(2)}, u32[]{:S(2)}) collective-permute-start(bf16[80,256]{1,0:T(8,128)(2,1)S(1)} %get-tuple-element.33), channel_id=1, source_target_pairs={{0,4},{4,0},{8,12},{12,8},{16,20},{20,16},{24,28},{28,24},{1,5},{5... | collective-permute-start | bytes 122888 | tf_op jit(solution)/shard_map/ppermute | solution.py:517
  10.6 10.9 %collective-permute-start.6 = (bf16[80,256]{1,0:T(8,128)(2,1)S(1)}, bf16[80,256]{1,0:T(8,128)(2,1)S(1)}, u32[]{:S(2)}, u32[]{:S(2)}) collective-permute-start(bf16[80,256]{1,0:T(8,128)(2,1)S(1)} %get-tuple-element.38), channel_id=1, source_target_pairs={{0,1},{1,0},{2,3},{3,2},{4,8},{5,9},{6,10},{7,11},{8,4},{9,5},{10,... | collective-permute-start | bytes 122888 | tf_op jit(solution)/shard_map/ppermute | solution.py:517
  12.1 2.9 %copy-start.1 = (bf16[256,256]{1,0:T(8,128)(2,1)S(1)}, bf16[256,256]{1,0:T(8,128)(2,1)}, u32[]{:S(2)}) copy-start(bf16[256,256]{1,0:T(8,128)(2,1)} %recv_ref.3) | copy-start | bytes 393220
  12.1 2.9 %copy-start.3 = (bf16[4,512,256]{2,1,0:T(8,128)(2,1)S(1)}, bf16[4,512,256]{2,1,0:T(8,128)(2,1)}, u32[]{:S(2)}) copy-start(bf16[4,512,256]{2,1,0:T(8,128)(2,1)} %down_ref.1) | copy-start | bytes 3145732
  12.1 2.9 %copy-start.4 = (s32[16,16,16]{2,1,0:T(8,128)S(1)}, s32[16,16,16]{2,1,0:T(8,128)}, u32[]{:S(2)}) copy-start(s32[16,16,16]{2,1,0:T(8,128)} %param.18) | copy-start | bytes 49156
  12.2 2.9 %copy-start.5 = (s32[16,16,16]{2,1,0:T(8,128)S(1)}, s32[16,16,16]{2,1,0:T(8,128)}, u32[]{:S(2)}) copy-start(s32[16,16,16]{2,1,0:T(8,128)} %param.19) | copy-start | bytes 49156
  12.2 2.9 %copy-start.6 = (f32[64,2,256]{2,1,0:T(2,128)S(1)}, f32[64,2,256]{2,1,0:T(2,128)}, u32[]{:S(2)}) copy-start(f32[64,2,256]{2,1,0:T(2,128)} %param.21) | copy-start | bytes 393220
  12.2 2.9 %copy-start.7 = (s32[16,16]{1,0:T(8,128)S(1)}, s32[16,16]{1,0:T(8,128)}, u32[]{:S(2)}) copy-start(s32[16,16]{1,0:T(8,128)} %count_ref) | copy-start | bytes 3076

commit v15 on v13

--- a/solution.py
+++ b/solution.py
@@ -432,6 +432,7 @@
             loads[1].wait()
 
         first = 1024 + (n // per_block) * (2 * words) + (n % per_block) * GROUP
+        totals = []
         for k in range(GROUP):
             total = [None, None]
             for s in range(length):
@@ -440,8 +441,9 @@
                 kind = pl.multiple_of(at[place + words], 8)
                 term = cells[pl.ds(source, 8), :] * table8[pl.ds(kind, 8), :]
                 total[s % 2] = term if total[s % 2] is None else total[s % 2] + term
-            total = total[0] + total[1] if length else jnp.zeros((8, lanes), F32)
-            sums[pl.ds(pl.multiple_of(at[n * GROUP + k], 8), 8), :] = total
+            totals.append(total[0] + total[1] if length else jnp.zeros((8, lanes), F32))
+        for k in range(GROUP):
+            sums[pl.ds(pl.multiple_of(at[n * GROUP + k], 8), 8), :] = totals[k]
         return carry
 
     loads[0].wait()

time: 26.7 us -> 26.9 us (level); the launches traced: 26.8 us -> 26.6 us
  no operation moved by 1% of the time
where the time goes in v15:
time: 26.9 us; the launch traced here: 26.6 us
  Pallas kernels  15.7 us (58%)
  starting transfers between devices  9.68 us (36%)
  waiting for transfers between devices  1.02 us (4%)
    pallas_call x1, Pallas kernels, body(): pl.pallas_call(functools.partial(late_kernel, len(late), tile_x, tile_y,...  4.9 us
    ppermute x3, starting transfers between devices, body(): lax.ppermute(coarse, 'gy', [(i, i ^ d) for i in range(chunks)])  3.55 us
    pallas_call x1, Pallas kernels, body(): pl.pallas_call(functools.partial(early_kernel, len(early), parents, slots...  3.32 us
    ppermute x2, starting transfers between devices, swap(): lax.ppermute(low, axis, lows)  3.07 us
    ppermute x2, starting transfers between devices, swap(): lax.ppermute(high, axis if other is None else (axis, other), highs)  3.05 us
    pallas_call x1, Pallas kernels, body(): pl.pallas_call(functools.partial(local_kernel, tile_x, tile_y), name='loc...  2.82 us
    pallas_call x1, Pallas kernels, body(): pl.pallas_call(functools.partial(live_kernel, tile_x, tile_y), name='live...  1.61 us
    pallas_call x1, Pallas kernels, body(): pl.pallas_call(functools.partial(order_kernel, chunks, kinds, parents_x,...  1.24 us
  transfers between devices with their start and end apart: 7, of which 2 were waited for; matrix products, arithmetic and copies ran while one was open for 0% of the time, Pallas kernels for 34%

profile of v15, /device:TPU:0, one launch (start us, length us, event | category | flops | bytes accessed | tf_op | source)
XLA Modules:
  0.0 26.6 jit_solution(4345128225950747697)
XLA Ops:
  0.0 0.0 copy-start.2
  0.0 0.0 copy-start
  0.0 1.6 %live.1 = (bf16[1024,256]{1,0:T(8,128)(2,1)S(1)}, f32[1024,128]{1,0:T(8,128)S(1)}, bf16[64,256]{1,0:T(8,128)(2,1)S(1)}, bf16[64,256]{1,0:T(8,128)(2,1)S(1)}, bf1...) custom-call(bf16[2048,128]{1,0:T(8,128)(2,1)} %bitcast.24, s32[32,32]{1,0:T(8,128)} %counts_hbm.1, ...), custom_call_target="tpu_custom_call" | custom-call | flops 209715200 | bytes 3145728 | tf_op jit(solution)/shard_map/live/pallas_call | solution.py:540
  1.6 3.0 %collective-permute-start.2 = (bf16[64,256]{1,0:T(8,128)(2,1)S(1)}, bf16[64,256]{1,0:T(8,128)(2,1)S(1)}, u32[]{:S(2)}, u32[]{:S(2)}) collective-permute-start(bf16[64,256]{1,0:T(8,128)(2,1)S(1)} %get-tuple-element.31), channel_id=1, source_target_pairs={{0,1},{1,0},{2,3},{3,2},{4,5},{5,4},{6,7},{7,6},{8,9},{9,8},{10,11... | collective-permute-start | bytes 98312 | tf_op jit(solution)/shard_map/ppermute | solution.py:520
  4.6 1.5 %collective-permute-start.3 = (bf16[64,256]{1,0:T(8,128)(2,1)S(1)}, bf16[64,256]{1,0:T(8,128)(2,1)S(1)}, u32[]{:S(2)}, u32[]{:S(2)}) collective-permute-start(bf16[64,256]{1,0:T(8,128)(2,1)S(1)} %get-tuple-element.32), channel_id=1, source_target_pairs={{0,3},{1,2},{2,1},{3,0},{4,7},{5,6},{6,5},{7,4},{8,11},{9,10},{10,... | collective-permute-start | bytes 98312 | tf_op jit(solution)/shard_map/ppermute | solution.py:520
  6.1 0.8 %parents.1 = (bf16[1024,128]{1,0:T(8,128)(2,1)S(1)}, f32[3,1536,128]{2,1,0:T(8,128)S(1)}) custom-call(bf16[1024,256]{1,0:T(8,128)(2,1)S(1)} %get-tuple-element.39.live_ref, bf16[256,256]{1,0:T(8,128)(2,1)S(1)} %get-tuple-element.28.agg_ref, bf16[1024,512]{1,0:T(8,128)(2,1)S(1)} %get-tuple-element.29.up_ref), custom_call_target="tpu_custom_call" | custom-call | flops 419430400 | bytes 3145728 | tf_op jit(solution)/shard_map/parents/pallas_call | solution.py:565
  6.9 1.5 %collective-permute-start.4 = (bf16[1024,128]{1,0:T(8,128)(2,1)S(1)}, bf16[1024,128]{1,0:T(8,128)(2,1)S(1)}, u32[]{:S(2)}, u32[]{:S(2)}) collective-permute-start(bf16[1024,128]{1,0:T(8,128)(2,1)S(1)} %get-tuple-element.30.refs_0_), channel_id=1, source_target_pairs={{0,3},{1,2},{2,1},{3,0},{4,7},{5,6},{6,5},{7,4},{8,11},{9,10},{10,... | collective-permute-start | bytes 786440 | tf_op jit(solution)/shard_map/ppermute | solution.py:583
  8.4 1.5 %collective-permute-start.1 = (bf16[1024,128]{1,0:T(8,128)(2,1)S(1)}, bf16[1024,128]{1,0:T(8,128)(2,1)S(1)}, u32[]{:S(2)}, u32[]{:S(2)}) collective-permute-start(bf16[1024,128]{1,0:T(8,128)(2,1)S(1)} %get-tuple-element.30.refs_0_), channel_id=1, source_target_pairs={{0,2},{1,3},{2,0},{3,1},{4,6},{5,7},{6,4},{7,5},{8,10},{9,11},{10,... | collective-permute-start | bytes 786440 | tf_op jit(solution)/shard_map/ppermute | solution.py:583
  9.9 0.5 %collective-permute-start = (bf16[1024,128]{1,0:T(8,128)(2,1)S(1)}, bf16[1024,128]{1,0:T(8,128)(2,1)S(1)}, u32[]{:S(2)}, u32[]{:S(2)}) collective-permute-start(bf16[1024,128]{1,0:T(8,128)(2,1)S(1)} %get-tuple-element.30.refs_0_), channel_id=1, source_target_pairs={{0,1},{1,0},{2,3},{3,2},{4,5},{5,4},{6,7},{7,6},{8,9},{9,8},{10,11... | collective-permute-start | bytes 786440 | tf_op jit(solution)/shard_map/ppermute | solution.py:583
  10.4 0.0 collective-permute-done.2.inner_ref.inner_y
  10.4 0.0 collective-permute-done.3.outer_ref.outer_y
  10.5 0.1 collective-permute-start.5
  10.6 1.6 %collective-permute-start.6 = (bf16[80,256]{1,0:T(8,128)(2,1)S(1)}, bf16[80,256]{1,0:T(8,128)(2,1)S(1)}, u32[]{:S(2)}, u32[]{:S(2)}) collective-permute-start(bf16[80,256]{1,0:T(8,128)(2,1)S(1)} %get-tuple-element.38), channel_id=1, source_target_pairs={{0,1},{1,0},{2,3},{3,2},{4,8},{5,9},{6,10},{7,11},{8,4},{9,5},{10,... | collective-permute-start | bytes 122888 | tf_op jit(solution)/shard_map/ppermute | solution.py:520
  12.1 0.0 copy-done.2
  12.1 0.0 copy-done
  12.1 0.0 copy-start.1
  12.1 0.0 copy-start.3
  12.1 0.0 copy-start.4
  12.2 0.0 copy-start.5
  12.2 0.0 copy-start.6
  12.2 0.0 copy-start.7
  12.2 2.8 %local.1 = (f32[2,1024,128]{2,1,0:T(8,128)S(1)}, f32[2,1024,128]{2,1,0:T(8,128)S(1)}) custom-call(bf16[1024,256]{1,0:T(8,128)(2,1)S(1)} %get-tuple-element.39.live_ref, f32[3,1536,128]{2,1,0:T(8,128)S(1)} %get-tuple-element.40.pats, bf16[3,768,256]{2,1,0:T(8,128)(2,1)S(1)} %bitcast.14, f32[32,128]{1,0:T(8,128)S(1)} %bitcast.16), custom_call_target="tpu_custom_call" | custom-call | flops 4194304000 | bytes 5242880 | tf_op jit(solution)/shard_map/local/pallas_call | solution.py:605
  15.0 0.0 copy-done.1
  15.0 0.0 copy-done.3
  15.0 0.0 copy-done.4
  15.1 0.0 copy-done.5
  15.1 0.0 copy-done.6
  15.1 0.0 copy-done.7
  15.1 1.2 %order.1 = (s32[72,128]{1,0:T(8,128)S(1)}, s32[72,128]{1,0:T(8,128)S(1)}, f32[520,128]{1,0:T(8,128)S(1)}, bf16[4,512,256]{2,1,0:T(8,128)(2,1)S(1)}) custom-call(s32[256,16]{1,0:T(8,128)S(1)} %bitcast.18, s32[256,16]{1,0:T(8,128)S(1)} %bitcast.19, s32[16,16]{1,0:T(8,128)S(1)} %copy-done.7, f32[256,128]{1,0:T(8,128)S(1)} %bitcast.20, ...), custom_call_target="tpu_custom_call" | custom-call | flops 629145600 | bytes 1048576 | tf_op jit(solution)/shard_map/order/pallas_call | solution.py:623
  16.3 0.8 %collective-permute-done.4.refs_1_ = bf16[1024,128]{1,0:T(8,128)(2,1)S(1)} collective-permute-done((bf16[1024,128]{1,0:T(8,128)(2,1)S(1)}, bf16[1024,128]{1,0:T(8,128)(2,1)S(1)}, u32[]{:S(2)}, u32[]{:S(2)}) %collective-permute-start.4) | collective-permute-done | bytes 262176 | tf_op jit(solution)/shard_map/ppermute | solution.py:583
  17.1 3.3 %early.1.refs_4_ = f32[2048,128]{1,0:T(8,128)S(1)} custom-call(bf16[1024,128]{1,0:T(8,128)(2,1)S(1)} %get-tuple-element.30.refs_0_, bf16[1024,128]{1,0:T(8,128)(2,1)S(1)} %collective-permute-done.4.refs_1_, s32[9216]{0:T(1024)S(1)} %bitcast.22, f32[520,128]{1,0:T(8,128)S(1)} %get-tuple-element.36.refs_3_), custom_call_target="tpu_custom_call" | custom-call | flops 2097152000 | bytes 4194304 | tf_op jit(solution)/shard_map/early/pallas_call | solution.py:644
  20.5 0.2 collective-permute-done.6.outer_x
  20.7 0.0 collective-permute-done.5.inner_x
  20.7 1.0 %halos.1 = (f32[2,4,256,128]{3,2,1,0:T(8,128)S(1)}, f32[4,256,128]{2,1,0:T(8,128)S(1)}) custom-call(bf16[64,256]{1,0:T(8,128)(2,1)S(1)} %collective-permute-done.2.inner_ref.inner_y, bf16[64,256]{1,0:T(8,128)(2,1)S(1)} %collective-permute-done.3.outer_ref.outer_y, bf16[80,256]{1,0:T(8,128)(2,1)S(1)} %collective-permute-done.5.inner_x, ...), custom_call_target="tpu_custom_call" | custom-call | flops 209715200 | bytes 5242880 | tf_op jit(solution)/shard_map/halos/pallas_call | solution.py:659
  21.7 0.0 collective-permute-done.1.refs_1_
  21.7 0.0 collective-permute-done.refs_0_
  21.7 4.9 %late.1 = f32[2048,128]{1,0:T(8,128)} custom-call(bf16[1024,128]{1,0:T(8,128)(2,1)S(1)} %collective-permute-done.refs_0_, bf16[1024,128]{1,0:T(8,128)(2,1)S(1)} %collective-permute-done.1.refs_1_, s32[9216]{0:T(1024)S(1)} %bitcast.21, f32[520,128]{1,0:T(8,128)S(1)} %get-tuple-element.36.refs_3_, f32[2048,128]{1,0:T(8,128)S(1)} %early.1.refs_4_, ...), custom_call_target="tpu_custom_call" | custom-call | flops 4194304000 | bytes 8388608 | tf_op jit(solution)/shard_map/late/pallas_call | solution.py:678
  (1 shorter events, 0.0 us)
Async XLA Ops:
  0.0 12.1 %copy-start.2 = (f32[16,2,128]{2,1,0:T(2,128)S(1)}, f32[16,2,128]{2,1,0:T(2,128)}, u32[]{:S(2)}) copy-start(f32[16,2,128]{2,1,0:T(2,128)} %param.16) | copy-start | bytes 49156
  0.0 12.1 %copy-start = (bf16[9,256,256]{2,1,0:T(8,128)(2,1)S(1)}, bf16[9,256,256]{2,1,0:T(8,128)(2,1)}, u32[]{:S(2)}) copy-start(bf16[9,256,256]{2,1,0:T(8,128)(2,1)} %param.15) | copy-start | bytes 3538948
  1.6 8.8 %collective-permute-start.2 = (bf16[64,256]{1,0:T(8,128)(2,1)S(1)}, bf16[64,256]{1,0:T(8,128)(2,1)S(1)}, u32[]{:S(2)}, u32[]{:S(2)}) collective-permute-start(bf16[64,256]{1,0:T(8,128)(2,1)S(1)} %get-tuple-element.31), channel_id=1, source_target_pairs={{0,1},{1,0},{2,3},{3,2},{4,5},{5,4},{6,7},{7,6},{8,9},{9,8},{10,11... | collective-permute-start | bytes 98312 | tf_op jit(solution)/shard_map/ppermute | solution.py:520
  4.6 5.8 %collective-permute-start.3 = (bf16[64,256]{1,0:T(8,128)(2,1)S(1)}, bf16[64,256]{1,0:T(8,128)(2,1)S(1)}, u32[]{:S(2)}, u32[]{:S(2)}) collective-permute-start(bf16[64,256]{1,0:T(8,128)(2,1)S(1)} %get-tuple-element.32), channel_id=1, source_target_pairs={{0,3},{1,2},{2,1},{3,0},{4,7},{5,6},{6,5},{7,4},{8,11},{9,10},{10,... | collective-permute-start | bytes 98312 | tf_op jit(solution)/shard_map/ppermute | solution.py:520
  6.9 10.3 %collective-permute-start.4 = (bf16[1024,128]{1,0:T(8,128)(2,1)S(1)}, bf16[1024,128]{1,0:T(8,128)(2,1)S(1)}, u32[]{:S(2)}, u32[]{:S(2)}) collective-permute-start(bf16[1024,128]{1,0:T(8,128)(2,1)S(1)} %get-tuple-element.30.refs_0_), channel_id=1, source_target_pairs={{0,3},{1,2},{2,1},{3,0},{4,7},{5,6},{6,5},{7,4},{8,11},{9,10},{10,... | collective-permute-start | bytes 786440 | tf_op jit(solution)/shard_map/ppermute | solution.py:583
  8.4 13.3 %collective-permute-start.1 = (bf16[1024,128]{1,0:T(8,128)(2,1)S(1)}, bf16[1024,128]{1,0:T(8,128)(2,1)S(1)}, u32[]{:S(2)}, u32[]{:S(2)}) collective-permute-start(bf16[1024,128]{1,0:T(8,128)(2,1)S(1)} %get-tuple-element.30.refs_0_), channel_id=1, source_target_pairs={{0,2},{1,3},{2,0},{3,1},{4,6},{5,7},{6,4},{7,5},{8,10},{9,11},{10,... | collective-permute-start | bytes 786440 | tf_op jit(solution)/shard_map/ppermute | solution.py:583
  9.9 11.8 %collective-permute-start = (bf16[1024,128]{1,0:T(8,128)(2,1)S(1)}, bf16[1024,128]{1,0:T(8,128)(2,1)S(1)}, u32[]{:S(2)}, u32[]{:S(2)}) collective-permute-start(bf16[1024,128]{1,0:T(8,128)(2,1)S(1)} %get-tuple-element.30.refs_0_), channel_id=1, source_target_pairs={{0,1},{1,0},{2,3},{3,2},{4,5},{5,4},{6,7},{7,6},{8,9},{9,8},{10,11... | collective-permute-start | bytes 786440 | tf_op jit(solution)/shard_map/ppermute | solution.py:583
  10.5 10.2 %collective-permute-start.5 = (bf16[80,256]{1,0:T(8,128)(2,1)S(1)}, bf16[80,256]{1,0:T(8,128)(2,1)S(1)}, u32[]{:S(2)}, u32[]{:S(2)}) collective-permute-start(bf16[80,256]{1,0:T(8,128)(2,1)S(1)} %get-tuple-element.33), channel_id=1, source_target_pairs={{0,4},{4,0},{8,12},{12,8},{16,20},{20,16},{24,28},{28,24},{1,5},{5... | collective-permute-start | bytes 122888 | tf_op jit(solution)/shard_map/ppermute | solution.py:520
  10.6 10.1 %collective-permute-start.6 = (bf16[80,256]{1,0:T(8,128)(2,1)S(1)}, bf16[80,256]{1,0:T(8,128)(2,1)S(1)}, u32[]{:S(2)}, u32[]{:S(2)}) collective-permute-start(bf16[80,256]{1,0:T(8,128)(2,1)S(1)} %get-tuple-element.38), channel_id=1, source_target_pairs={{0,1},{1,0},{2,3},{3,2},{4,8},{5,9},{6,10},{7,11},{8,4},{9,5},{10,... | collective-permute-start | bytes 122888 | tf_op jit(solution)/shard_map/ppermute | solution.py:520
  12.1 2.9 %copy-start.1 = (bf16[256,256]{1,0:T(8,128)(2,1)S(1)}, bf16[256,256]{1,0:T(8,128)(2,1)}, u32[]{:S(2)}) copy-start(bf16[256,256]{1,0:T(8,128)(2,1)} %recv_ref.3) | copy-start | bytes 393220
  12.1 2.9 %copy-start.3 = (bf16[4,512,256]{2,1,0:T(8,128)(2,1)S(1)}, bf16[4,512,256]{2,1,0:T(8,128)(2,1)}, u32[]{:S(2)}) copy-start(bf16[4,512,256]{2,1,0:T(8,128)(2,1)} %down_ref.1) | copy-start | bytes 3145732
  12.1 2.9 %copy-start.4 = (s32[16,16,16]{2,1,0:T(8,128)S(1)}, s32[16,16,16]{2,1,0:T(8,128)}, u32[]{:S(2)}) copy-start(s32[16,16,16]{2,1,0:T(8,128)} %param.18) | copy-start | bytes 49156
  12.2 2.9 %copy-start.5 = (s32[16,16,16]{2,1,0:T(8,128)S(1)}, s32[16,16,16]{2,1,0:T(8,128)}, u32[]{:S(2)}) copy-start(s32[16,16,16]{2,1,0:T(8,128)} %param.19) | copy-start | bytes 49156
  12.2 2.9 %copy-start.6 = (f32[64,2,256]{2,1,0:T(2,128)S(1)}, f32[64,2,256]{2,1,0:T(2,128)}, u32[]{:S(2)}) copy-start(f32[64,2,256]{2,1,0:T(2,128)} %param.21) | copy-start | bytes 393220
  12.2 2.9 %copy-start.7 = (s32[16,16]{1,0:T(8,128)S(1)}, s32[16,16]{1,0:T(8,128)}, u32[]{:S(2)}) copy-start(s32[16,16]{1,0:T(8,128)} %count_ref) | copy-start | bytes 3076

commit v16 on v15

--- a/solution.py
+++ b/solution.py
@@ -326,7 +326,7 @@
             field_ref[part, child] = field_ref[part, child] + value[:, part * lanes : (part + 1) * lanes]
 
 
-GROUP = 16
+GROUP = 8
 SEGMENT = 8
 
 

time: 26.9 us -> 26.9 us (level)
  Pallas kernels: 15.7 us -> 16.1 us
  transfers between devices with their start and end apart: 7 -> 7, of which waited for: 2 -> 1; matrix products, arithmetic and copies ran while one was open for 0% -> 0% of each run, Pallas kernels for 34% -> 35%
where the time goes in v16:
time: 26.9 us; the launch traced here: 26.8 us
  Pallas kernels  16.1 us (60%)
  starting transfers between devices  9.68 us (36%)
  waiting for transfers between devices  0.83 us (3%)
    pallas_call x1, Pallas kernels, body(): pl.pallas_call(functools.partial(late_kernel, len(late), tile_x, tile_y,...  5.11 us
    ppermute x3, starting transfers between devices, body(): lax.ppermute(coarse, 'gy', [(i, i ^ d) for i in range(chunks)])  3.55 us
    pallas_call x1, Pallas kernels, body(): pl.pallas_call(functools.partial(early_kernel, len(early), parents, slots...  3.52 us
    ppermute x2, starting transfers between devices, swap(): lax.ppermute(low, axis, lows)  3.07 us
    ppermute x2, starting transfers between devices, swap(): lax.ppermute(high, axis if other is None else (axis, other), highs)  3.05 us
    pallas_call x1, Pallas kernels, body(): pl.pallas_call(functools.partial(local_kernel, tile_x, tile_y), name='loc...  2.82 us
    pallas_call x1, Pallas kernels, body(): pl.pallas_call(functools.partial(live_kernel, tile_x, tile_y), name='live...  1.61 us
    pallas_call x1, Pallas kernels, body(): pl.pallas_call(functools.partial(order_kernel, chunks, kinds, parents_x,...  1.24 us
  transfers between devices with their start and end apart: 7, of which 1 were waited for; matrix products, arithmetic and copies ran while one was open for 0% of the time, Pallas kernels for 35%

profile of v16, /device:TPU:0, one launch (start us, length us, event | category | flops | bytes accessed | tf_op | source)
XLA Modules:
  0.0 26.8 jit_solution(7425029376179777421)
XLA Ops:
  0.0 0.0 copy-start.2
  0.0 0.0 copy-start
  0.0 1.6 %live.1 = (bf16[1024,256]{1,0:T(8,128)(2,1)S(1)}, f32[1024,128]{1,0:T(8,128)S(1)}, bf16[64,256]{1,0:T(8,128)(2,1)S(1)}, bf16[64,256]{1,0:T(8,128)(2,1)S(1)}, bf1...) custom-call(bf16[2048,128]{1,0:T(8,128)(2,1)} %bitcast.24, s32[32,32]{1,0:T(8,128)} %counts_hbm.1, ...), custom_call_target="tpu_custom_call" | custom-call | flops 209715200 | bytes 3145728 | tf_op jit(solution)/shard_map/live/pallas_call | solution.py:540
  1.6 3.0 %collective-permute-start.2 = (bf16[64,256]{1,0:T(8,128)(2,1)S(1)}, bf16[64,256]{1,0:T(8,128)(2,1)S(1)}, u32[]{:S(2)}, u32[]{:S(2)}) collective-permute-start(bf16[64,256]{1,0:T(8,128)(2,1)S(1)} %get-tuple-element.31), channel_id=1, source_target_pairs={{0,1},{1,0},{2,3},{3,2},{4,5},{5,4},{6,7},{7,6},{8,9},{9,8},{10,11... | collective-permute-start | bytes 98312 | tf_op jit(solution)/shard_map/ppermute | solution.py:520
  4.6 1.5 %collective-permute-start.3 = (bf16[64,256]{1,0:T(8,128)(2,1)S(1)}, bf16[64,256]{1,0:T(8,128)(2,1)S(1)}, u32[]{:S(2)}, u32[]{:S(2)}) collective-permute-start(bf16[64,256]{1,0:T(8,128)(2,1)S(1)} %get-tuple-element.32), channel_id=1, source_target_pairs={{0,3},{1,2},{2,1},{3,0},{4,7},{5,6},{6,5},{7,4},{8,11},{9,10},{10,... | collective-permute-start | bytes 98312 | tf_op jit(solution)/shard_map/ppermute | solution.py:520
  6.1 0.8 %parents.1 = (bf16[1024,128]{1,0:T(8,128)(2,1)S(1)}, f32[3,1536,128]{2,1,0:T(8,128)S(1)}) custom-call(bf16[1024,256]{1,0:T(8,128)(2,1)S(1)} %get-tuple-element.39.live_ref, bf16[256,256]{1,0:T(8,128)(2,1)S(1)} %get-tuple-element.28.agg_ref, bf16[1024,512]{1,0:T(8,128)(2,1)S(1)} %get-tuple-element.29.up_ref), custom_call_target="tpu_custom_call" | custom-call | flops 419430400 | bytes 3145728 | tf_op jit(solution)/shard_map/parents/pallas_call | solution.py:565
  6.9 1.5 %collective-permute-start.4 = (bf16[1024,128]{1,0:T(8,128)(2,1)S(1)}, bf16[1024,128]{1,0:T(8,128)(2,1)S(1)}, u32[]{:S(2)}, u32[]{:S(2)}) collective-permute-start(bf16[1024,128]{1,0:T(8,128)(2,1)S(1)} %get-tuple-element.30.refs_0_), channel_id=1, source_target_pairs={{0,3},{1,2},{2,1},{3,0},{4,7},{5,6},{6,5},{7,4},{8,11},{9,10},{10,... | collective-permute-start | bytes 786440 | tf_op jit(solution)/shard_map/ppermute | solution.py:583
  8.4 1.5 %collective-permute-start.1 = (bf16[1024,128]{1,0:T(8,128)(2,1)S(1)}, bf16[1024,128]{1,0:T(8,128)(2,1)S(1)}, u32[]{:S(2)}, u32[]{:S(2)}) collective-permute-start(bf16[1024,128]{1,0:T(8,128)(2,1)S(1)} %get-tuple-element.30.refs_0_), channel_id=1, source_target_pairs={{0,2},{1,3},{2,0},{3,1},{4,6},{5,7},{6,4},{7,5},{8,10},{9,11},{10,... | collective-permute-start | bytes 786440 | tf_op jit(solution)/shard_map/ppermute | solution.py:583
  9.9 0.5 %collective-permute-start = (bf16[1024,128]{1,0:T(8,128)(2,1)S(1)}, bf16[1024,128]{1,0:T(8,128)(2,1)S(1)}, u32[]{:S(2)}, u32[]{:S(2)}) collective-permute-start(bf16[1024,128]{1,0:T(8,128)(2,1)S(1)} %get-tuple-element.30.refs_0_), channel_id=1, source_target_pairs={{0,1},{1,0},{2,3},{3,2},{4,5},{5,4},{6,7},{7,6},{8,9},{9,8},{10,11... | collective-permute-start | bytes 786440 | tf_op jit(solution)/shard_map/ppermute | solution.py:583
  10.4 0.0 collective-permute-done.2.inner_ref.inner_y
  10.4 0.0 collective-permute-done.3.outer_ref.outer_y
  10.5 0.1 collective-permute-start.5
  10.6 1.6 %collective-permute-start.6 = (bf16[80,256]{1,0:T(8,128)(2,1)S(1)}, bf16[80,256]{1,0:T(8,128)(2,1)S(1)}, u32[]{:S(2)}, u32[]{:S(2)}) collective-permute-start(bf16[80,256]{1,0:T(8,128)(2,1)S(1)} %get-tuple-element.38), channel_id=1, source_target_pairs={{0,1},{1,0},{2,3},{3,2},{4,8},{5,9},{6,10},{7,11},{8,4},{9,5},{10,... | collective-permute-start | bytes 122888 | tf_op jit(solution)/shard_map/ppermute | solution.py:520
  12.1 0.0 copy-done.2
  12.1 0.0 copy-done
  12.1 0.0 copy-start.1
  12.1 0.0 copy-start.3
  12.1 0.0 copy-start.4
  12.2 0.0 copy-start.5
  12.2 0.0 copy-start.6
  12.2 0.0 copy-start.7
  12.2 2.8 %local.1 = (f32[2,1024,128]{2,1,0:T(8,128)S(1)}, f32[2,1024,128]{2,1,0:T(8,128)S(1)}) custom-call(bf16[1024,256]{1,0:T(8,128)(2,1)S(1)} %get-tuple-element.39.live_ref, f32[3,1536,128]{2,1,0:T(8,128)S(1)} %get-tuple-element.40.pats, bf16[3,768,256]{2,1,0:T(8,128)(2,1)S(1)} %bitcast.14, f32[32,128]{1,0:T(8,128)S(1)} %bitcast.16), custom_call_target="tpu_custom_call" | custom-call | flops 4194304000 | bytes 5242880 | tf_op jit(solution)/shard_map/local/pallas_call | solution.py:605
  15.0 0.0 copy-done.1
  15.0 0.0 copy-done.3
  15.0 0.0 copy-done.4
  15.1 0.0 copy-done.5
  15.1 0.0 copy-done.6
  15.1 0.0 copy-done.7
  15.1 1.2 %order.1 = (s32[72,128]{1,0:T(8,128)S(1)}, s32[72,128]{1,0:T(8,128)S(1)}, f32[520,128]{1,0:T(8,128)S(1)}, bf16[4,512,256]{2,1,0:T(8,128)(2,1)S(1)}) custom-call(s32[256,16]{1,0:T(8,128)S(1)} %bitcast.18, s32[256,16]{1,0:T(8,128)S(1)} %bitcast.19, s32[16,16]{1,0:T(8,128)S(1)} %copy-done.7, f32[256,128]{1,0:T(8,128)S(1)} %bitcast.20, ...), custom_call_target="tpu_custom_call" | custom-call | flops 629145600 | bytes 1048576 | tf_op jit(solution)/shard_map/order/pallas_call | solution.py:623
  16.3 0.8 %collective-permute-done.4.refs_1_ = bf16[1024,128]{1,0:T(8,128)(2,1)S(1)} collective-permute-done((bf16[1024,128]{1,0:T(8,128)(2,1)S(1)}, bf16[1024,128]{1,0:T(8,128)(2,1)S(1)}, u32[]{:S(2)}, u32[]{:S(2)}) %collective-permute-start.4) | collective-permute-done | bytes 262176 | tf_op jit(solution)/shard_map/ppermute | solution.py:583
  17.1 3.5 %early.1.refs_4_ = f32[2048,128]{1,0:T(8,128)S(1)} custom-call(bf16[1024,128]{1,0:T(8,128)(2,1)S(1)} %get-tuple-element.30.refs_0_, bf16[1024,128]{1,0:T(8,128)(2,1)S(1)} %collective-permute-done.4.refs_1_, s32[9216]{0:T(1024)S(1)} %bitcast.22, f32[520,128]{1,0:T(8,128)S(1)} %get-tuple-element.36.refs_3_), custom_call_target="tpu_custom_call" | custom-call | flops 2097152000 | bytes 4194304 | tf_op jit(solution)/shard_map/early/pallas_call | solution.py:644
  20.7 0.0 collective-permute-done.6.outer_x
  20.7 0.0 collective-permute-done.5.inner_x
  20.7 1.0 %halos.1 = (f32[2,4,256,128]{3,2,1,0:T(8,128)S(1)}, f32[4,256,128]{2,1,0:T(8,128)S(1)}) custom-call(bf16[64,256]{1,0:T(8,128)(2,1)S(1)} %collective-permute-done.2.inner_ref.inner_y, bf16[64,256]{1,0:T(8,128)(2,1)S(1)} %collective-permute-done.3.outer_ref.outer_y, bf16[80,256]{1,0:T(8,128)(2,1)S(1)} %collective-permute-done.5.inner_x, ...), custom_call_target="tpu_custom_call" | custom-call | flops 209715200 | bytes 5242880 | tf_op jit(solution)/shard_map/halos/pallas_call | solution.py:659
  21.7 0.0 collective-permute-done.1.refs_1_
  21.7 0.0 collective-permute-done.refs_0_
  21.7 5.1 %late.1 = f32[2048,128]{1,0:T(8,128)} custom-call(bf16[1024,128]{1,0:T(8,128)(2,1)S(1)} %collective-permute-done.refs_0_, bf16[1024,128]{1,0:T(8,128)(2,1)S(1)} %collective-permute-done.1.refs_1_, s32[9216]{0:T(1024)S(1)} %bitcast.21, f32[520,128]{1,0:T(8,128)S(1)} %get-tuple-element.36.refs_3_, f32[2048,128]{1,0:T(8,128)S(1)} %early.1.refs_4_, ...), custom_call_target="tpu_custom_call" | custom-call | flops 4194304000 | bytes 8388608 | tf_op jit(solution)/shard_map/late/pallas_call | solution.py:678
  (1 shorter events, 0.0 us)
Async XLA Ops:
  0.0 12.1 %copy-start.2 = (f32[16,2,128]{2,1,0:T(2,128)S(1)}, f32[16,2,128]{2,1,0:T(2,128)}, u32[]{:S(2)}) copy-start(f32[16,2,128]{2,1,0:T(2,128)} %param.16) | copy-start | bytes 49156
  0.0 12.1 %copy-start = (bf16[9,256,256]{2,1,0:T(8,128)(2,1)S(1)}, bf16[9,256,256]{2,1,0:T(8,128)(2,1)}, u32[]{:S(2)}) copy-start(bf16[9,256,256]{2,1,0:T(8,128)(2,1)} %param.15) | copy-start | bytes 3538948
  1.6 8.8 %collective-permute-start.2 = (bf16[64,256]{1,0:T(8,128)(2,1)S(1)}, bf16[64,256]{1,0:T(8,128)(2,1)S(1)}, u32[]{:S(2)}, u32[]{:S(2)}) collective-permute-start(bf16[64,256]{1,0:T(8,128)(2,1)S(1)} %get-tuple-element.31), channel_id=1, source_target_pairs={{0,1},{1,0},{2,3},{3,2},{4,5},{5,4},{6,7},{7,6},{8,9},{9,8},{10,11... | collective-permute-start | bytes 98312 | tf_op jit(solution)/shard_map/ppermute | solution.py:520
  4.6 5.8 %collective-permute-start.3 = (bf16[64,256]{1,0:T(8,128)(2,1)S(1)}, bf16[64,256]{1,0:T(8,128)(2,1)S(1)}, u32[]{:S(2)}, u32[]{:S(2)}) collective-permute-start(bf16[64,256]{1,0:T(8,128)(2,1)S(1)} %get-tuple-element.32), channel_id=1, source_target_pairs={{0,3},{1,2},{2,1},{3,0},{4,7},{5,6},{6,5},{7,4},{8,11},{9,10},{10,... | collective-permute-start | bytes 98312 | tf_op jit(solution)/shard_map/ppermute | solution.py:520
  6.9 10.3 %collective-permute-start.4 = (bf16[1024,128]{1,0:T(8,128)(2,1)S(1)}, bf16[1024,128]{1,0:T(8,128)(2,1)S(1)}, u32[]{:S(2)}, u32[]{:S(2)}) collective-permute-start(bf16[1024,128]{1,0:T(8,128)(2,1)S(1)} %get-tuple-element.30.refs_0_), channel_id=1, source_target_pairs={{0,3},{1,2},{2,1},{3,0},{4,7},{5,6},{6,5},{7,4},{8,11},{9,10},{10,... | collective-permute-start | bytes 786440 | tf_op jit(solution)/shard_map/ppermute | solution.py:583
  8.4 13.3 %collective-permute-start.1 = (bf16[1024,128]{1,0:T(8,128)(2,1)S(1)}, bf16[1024,128]{1,0:T(8,128)(2,1)S(1)}, u32[]{:S(2)}, u32[]{:S(2)}) collective-permute-start(bf16[1024,128]{1,0:T(8,128)(2,1)S(1)} %get-tuple-element.30.refs_0_), channel_id=1, source_target_pairs={{0,2},{1,3},{2,0},{3,1},{4,6},{5,7},{6,4},{7,5},{8,10},{9,11},{10,... | collective-permute-start | bytes 786440 | tf_op jit(solution)/shard_map/ppermute | solution.py:583
  9.9 11.8 %collective-permute-start = (bf16[1024,128]{1,0:T(8,128)(2,1)S(1)}, bf16[1024,128]{1,0:T(8,128)(2,1)S(1)}, u32[]{:S(2)}, u32[]{:S(2)}) collective-permute-start(bf16[1024,128]{1,0:T(8,128)(2,1)S(1)} %get-tuple-element.30.refs_0_), channel_id=1, source_target_pairs={{0,1},{1,0},{2,3},{3,2},{4,5},{5,4},{6,7},{7,6},{8,9},{9,8},{10,11... | collective-permute-start | bytes 786440 | tf_op jit(solution)/shard_map/ppermute | solution.py:583
  10.5 10.2 %collective-permute-start.5 = (bf16[80,256]{1,0:T(8,128)(2,1)S(1)}, bf16[80,256]{1,0:T(8,128)(2,1)S(1)}, u32[]{:S(2)}, u32[]{:S(2)}) collective-permute-start(bf16[80,256]{1,0:T(8,128)(2,1)S(1)} %get-tuple-element.33), channel_id=1, source_target_pairs={{0,4},{4,0},{8,12},{12,8},{16,20},{20,16},{24,28},{28,24},{1,5},{5... | collective-permute-start | bytes 122888 | tf_op jit(solution)/shard_map/ppermute | solution.py:520
  10.6 10.1 %collective-permute-start.6 = (bf16[80,256]{1,0:T(8,128)(2,1)S(1)}, bf16[80,256]{1,0:T(8,128)(2,1)S(1)}, u32[]{:S(2)}, u32[]{:S(2)}) collective-permute-start(bf16[80,256]{1,0:T(8,128)(2,1)S(1)} %get-tuple-element.38), channel_id=1, source_target_pairs={{0,1},{1,0},{2,3},{3,2},{4,8},{5,9},{6,10},{7,11},{8,4},{9,5},{10,... | collective-permute-start | bytes 122888 | tf_op jit(solution)/shard_map/ppermute | solution.py:520
  12.1 2.9 %copy-start.1 = (bf16[256,256]{1,0:T(8,128)(2,1)S(1)}, bf16[256,256]{1,0:T(8,128)(2,1)}, u32[]{:S(2)}) copy-start(bf16[256,256]{1,0:T(8,128)(2,1)} %recv_ref.3) | copy-start | bytes 393220
  12.1 2.9 %copy-start.3 = (bf16[4,512,256]{2,1,0:T(8,128)(2,1)S(1)}, bf16[4,512,256]{2,1,0:T(8,128)(2,1)}, u32[]{:S(2)}) copy-start(bf16[4,512,256]{2,1,0:T(8,128)(2,1)} %down_ref.1) | copy-start | bytes 3145732
  12.1 2.9 %copy-start.4 = (s32[16,16,16]{2,1,0:T(8,128)S(1)}, s32[16,16,16]{2,1,0:T(8,128)}, u32[]{:S(2)}) copy-start(s32[16,16,16]{2,1,0:T(8,128)} %param.18) | copy-start | bytes 49156
  12.2 2.9 %copy-start.5 = (s32[16,16,16]{2,1,0:T(8,128)S(1)}, s32[16,16,16]{2,1,0:T(8,128)}, u32[]{:S(2)}) copy-start(s32[16,16,16]{2,1,0:T(8,128)} %param.19) | copy-start | bytes 49156
  12.2 2.9 %copy-start.6 = (f32[64,2,256]{2,1,0:T(2,128)S(1)}, f32[64,2,256]{2,1,0:T(2,128)}, u32[]{:S(2)}) copy-start(f32[64,2,256]{2,1,0:T(2,128)} %param.21) | copy-start | bytes 393220
  12.2 2.9 %copy-start.7 = (s32[16,16]{1,0:T(8,128)S(1)}, s32[16,16]{1,0:T(8,128)}, u32[]{:S(2)}) copy-start(s32[16,16]{1,0:T(8,128)} %count_ref) | copy-start | bytes 3076

commit v17 on v16

--- a/solution.py
+++ b/solution.py
@@ -326,7 +326,7 @@
             field_ref[part, child] = field_ref[part, child] + value[:, part * lanes : (part + 1) * lanes]
 
 
-GROUP = 8
+GROUP = 32
 SEGMENT = 8
 
 

time: 26.9 us -> 27 us (level)
  no operation moved by 1% of the time
where the time goes in v17:
time: 27 us; the launch traced here: 26.7 us
  Pallas kernels  15.9 us (59%)
  starting transfers between devices  9.68 us (36%)
  waiting for transfers between devices  0.84 us (3%)
    pallas_call x1, Pallas kernels, body(): pl.pallas_call(functools.partial(late_kernel, len(late), tile_x, tile_y,...  4.99 us
    ppermute x3, starting transfers between devices, body(): lax.ppermute(coarse, 'gy', [(i, i ^ d) for i in range(chunks)])  3.55 us
    pallas_call x1, Pallas kernels, body(): pl.pallas_call(functools.partial(early_kernel, len(early), parents, slots...  3.5 us
    ppermute x2, starting transfers between devices, swap(): lax.ppermute(low, axis, lows)  3.07 us
    ppermute x2, starting transfers between devices, swap(): lax.ppermute(high, axis if other is None else (axis, other), highs)  3.05 us
    pallas_call x1, Pallas kernels, body(): pl.pallas_call(functools.partial(local_kernel, tile_x, tile_y), name='loc...  2.82 us
    pallas_call x1, Pallas kernels, body(): pl.pallas_call(functools.partial(live_kernel, tile_x, tile_y), name='live...  1.61 us
    pallas_call x1, Pallas kernels, body(): pl.pallas_call(functools.partial(order_kernel, chunks, kinds, parents_x,...  1.24 us
  transfers between devices with their start and end apart: 7, of which 1 were waited for; matrix products, arithmetic and copies ran while one was open for 0% of the time, Pallas kernels for 35%

profile of v17, /device:TPU:0, one launch (start us, length us, event | category | flops | bytes accessed | tf_op | source)
XLA Modules:
  0.0 26.7 jit_solution(13500768242099865828)
XLA Ops:
  0.0 0.0 copy-start.2
  0.0 0.0 copy-start
  0.0 1.6 %live.1 = (bf16[1024,256]{1,0:T(8,128)(2,1)S(1)}, f32[1024,128]{1,0:T(8,128)S(1)}, bf16[64,256]{1,0:T(8,128)(2,1)S(1)}, bf16[64,256]{1,0:T(8,128)(2,1)S(1)}, bf1...) custom-call(bf16[2048,128]{1,0:T(8,128)(2,1)} %bitcast.24, s32[32,32]{1,0:T(8,128)} %counts_hbm.1, ...), custom_call_target="tpu_custom_call" | custom-call | flops 209715200 | bytes 3145728 | tf_op jit(solution)/shard_map/live/pallas_call | solution.py:540
  1.6 3.0 %collective-permute-start.2 = (bf16[64,256]{1,0:T(8,128)(2,1)S(1)}, bf16[64,256]{1,0:T(8,128)(2,1)S(1)}, u32[]{:S(2)}, u32[]{:S(2)}) collective-permute-start(bf16[64,256]{1,0:T(8,128)(2,1)S(1)} %get-tuple-element.31), channel_id=1, source_target_pairs={{0,1},{1,0},{2,3},{3,2},{4,5},{5,4},{6,7},{7,6},{8,9},{9,8},{10,11... | collective-permute-start | bytes 98312 | tf_op jit(solution)/shard_map/ppermute | solution.py:520
  4.6 1.5 %collective-permute-start.3 = (bf16[64,256]{1,0:T(8,128)(2,1)S(1)}, bf16[64,256]{1,0:T(8,128)(2,1)S(1)}, u32[]{:S(2)}, u32[]{:S(2)}) collective-permute-start(bf16[64,256]{1,0:T(8,128)(2,1)S(1)} %get-tuple-element.32), channel_id=1, source_target_pairs={{0,3},{1,2},{2,1},{3,0},{4,7},{5,6},{6,5},{7,4},{8,11},{9,10},{10,... | collective-permute-start | bytes 98312 | tf_op jit(solution)/shard_map/ppermute | solution.py:520
  6.1 0.8 %parents.1 = (bf16[1024,128]{1,0:T(8,128)(2,1)S(1)}, f32[3,1536,128]{2,1,0:T(8,128)S(1)}) custom-call(bf16[1024,256]{1,0:T(8,128)(2,1)S(1)} %get-tuple-element.39.live_ref, bf16[256,256]{1,0:T(8,128)(2,1)S(1)} %get-tuple-element.28.agg_ref, bf16[1024,512]{1,0:T(8,128)(2,1)S(1)} %get-tuple-element.29.up_ref), custom_call_target="tpu_custom_call" | custom-call | flops 419430400 | bytes 3145728 | tf_op jit(solution)/shard_map/parents/pallas_call | solution.py:565
  6.9 1.5 %collective-permute-start.4 = (bf16[1024,128]{1,0:T(8,128)(2,1)S(1)}, bf16[1024,128]{1,0:T(8,128)(2,1)S(1)}, u32[]{:S(2)}, u32[]{:S(2)}) collective-permute-start(bf16[1024,128]{1,0:T(8,128)(2,1)S(1)} %get-tuple-element.30.refs_0_), channel_id=1, source_target_pairs={{0,3},{1,2},{2,1},{3,0},{4,7},{5,6},{6,5},{7,4},{8,11},{9,10},{10,... | collective-permute-start | bytes 786440 | tf_op jit(solution)/shard_map/ppermute | solution.py:583
  8.4 1.5 %collective-permute-start.1 = (bf16[1024,128]{1,0:T(8,128)(2,1)S(1)}, bf16[1024,128]{1,0:T(8,128)(2,1)S(1)}, u32[]{:S(2)}, u32[]{:S(2)}) collective-permute-start(bf16[1024,128]{1,0:T(8,128)(2,1)S(1)} %get-tuple-element.30.refs_0_), channel_id=1, source_target_pairs={{0,2},{1,3},{2,0},{3,1},{4,6},{5,7},{6,4},{7,5},{8,10},{9,11},{10,... | collective-permute-start | bytes 786440 | tf_op jit(solution)/shard_map/ppermute | solution.py:583
  9.9 0.5 %collective-permute-start = (bf16[1024,128]{1,0:T(8,128)(2,1)S(1)}, bf16[1024,128]{1,0:T(8,128)(2,1)S(1)}, u32[]{:S(2)}, u32[]{:S(2)}) collective-permute-start(bf16[1024,128]{1,0:T(8,128)(2,1)S(1)} %get-tuple-element.30.refs_0_), channel_id=1, source_target_pairs={{0,1},{1,0},{2,3},{3,2},{4,5},{5,4},{6,7},{7,6},{8,9},{9,8},{10,11... | collective-permute-start | bytes 786440 | tf_op jit(solution)/shard_map/ppermute | solution.py:583
  10.4 0.0 collective-permute-done.2.inner_ref.inner_y
  10.4 0.0 collective-permute-done.3.outer_ref.outer_y
  10.5 0.1 collective-permute-start.5
  10.6 1.6 %collective-permute-start.6 = (bf16[80,256]{1,0:T(8,128)(2,1)S(1)}, bf16[80,256]{1,0:T(8,128)(2,1)S(1)}, u32[]{:S(2)}, u32[]{:S(2)}) collective-permute-start(bf16[80,256]{1,0:T(8,128)(2,1)S(1)} %get-tuple-element.38), channel_id=1, source_target_pairs={{0,1},{1,0},{2,3},{3,2},{4,8},{5,9},{6,10},{7,11},{8,4},{9,5},{10,... | collective-permute-start | bytes 122888 | tf_op jit(solution)/shard_map/ppermute | solution.py:520
  12.1 0.0 copy-done.2
  12.1 0.0 copy-done
  12.1 0.0 copy-start.1
  12.1 0.0 copy-start.3
  12.1 0.0 copy-start.4
  12.2 0.0 copy-start.5
  12.2 0.0 copy-start.6
  12.2 0.0 copy-start.7
  12.2 2.8 %local.1 = (f32[2,1024,128]{2,1,0:T(8,128)S(1)}, f32[2,1024,128]{2,1,0:T(8,128)S(1)}) custom-call(bf16[1024,256]{1,0:T(8,128)(2,1)S(1)} %get-tuple-element.39.live_ref, f32[3,1536,128]{2,1,0:T(8,128)S(1)} %get-tuple-element.40.pats, bf16[3,768,256]{2,1,0:T(8,128)(2,1)S(1)} %bitcast.14, f32[32,128]{1,0:T(8,128)S(1)} %bitcast.16), custom_call_target="tpu_custom_call" | custom-call | flops 4194304000 | bytes 5242880 | tf_op jit(solution)/shard_map/local/pallas_call | solution.py:605
  15.0 0.0 copy-done.1
  15.0 0.0 copy-done.3
  15.0 0.0 copy-done.4
  15.1 0.0 copy-done.5
  15.1 0.0 copy-done.6
  15.1 0.0 copy-done.7
  15.1 1.2 %order.1 = (s32[72,128]{1,0:T(8,128)S(1)}, s32[72,128]{1,0:T(8,128)S(1)}, f32[520,128]{1,0:T(8,128)S(1)}, bf16[4,512,256]{2,1,0:T(8,128)(2,1)S(1)}) custom-call(s32[256,16]{1,0:T(8,128)S(1)} %bitcast.18, s32[256,16]{1,0:T(8,128)S(1)} %bitcast.19, s32[16,16]{1,0:T(8,128)S(1)} %copy-done.7, f32[256,128]{1,0:T(8,128)S(1)} %bitcast.20, ...), custom_call_target="tpu_custom_call" | custom-call | flops 629145600 | bytes 1048576 | tf_op jit(solution)/shard_map/order/pallas_call | solution.py:623
  16.3 0.8 %collective-permute-done.4.refs_1_ = bf16[1024,128]{1,0:T(8,128)(2,1)S(1)} collective-permute-done((bf16[1024,128]{1,0:T(8,128)(2,1)S(1)}, bf16[1024,128]{1,0:T(8,128)(2,1)S(1)}, u32[]{:S(2)}, u32[]{:S(2)}) %collective-permute-start.4) | collective-permute-done | bytes 262176 | tf_op jit(solution)/shard_map/ppermute | solution.py:583
  17.1 3.5 %early.1.refs_4_ = f32[2048,128]{1,0:T(8,128)S(1)} custom-call(bf16[1024,128]{1,0:T(8,128)(2,1)S(1)} %get-tuple-element.30.refs_0_, bf16[1024,128]{1,0:T(8,128)(2,1)S(1)} %collective-permute-done.4.refs_1_, s32[9216]{0:T(1024)S(1)} %bitcast.22, f32[520,128]{1,0:T(8,128)S(1)} %get-tuple-element.36.refs_3_), custom_call_target="tpu_custom_call" | custom-call | flops 2097152000 | bytes 4194304 | tf_op jit(solution)/shard_map/early/pallas_call | solution.py:644
  20.6 0.0 collective-permute-done.6.outer_x
  20.7 0.0 collective-permute-done.5.inner_x
  20.7 1.0 %halos.1 = (f32[2,4,256,128]{3,2,1,0:T(8,128)S(1)}, f32[4,256,128]{2,1,0:T(8,128)S(1)}) custom-call(bf16[64,256]{1,0:T(8,128)(2,1)S(1)} %collective-permute-done.2.inner_ref.inner_y, bf16[64,256]{1,0:T(8,128)(2,1)S(1)} %collective-permute-done.3.outer_ref.outer_y, bf16[80,256]{1,0:T(8,128)(2,1)S(1)} %collective-permute-done.5.inner_x, ...), custom_call_target="tpu_custom_call" | custom-call | flops 209715200 | bytes 5242880 | tf_op jit(solution)/shard_map/halos/pallas_call | solution.py:659
  21.7 0.0 collective-permute-done.1.refs_1_
  21.7 0.0 collective-permute-done.refs_0_
  21.7 5.0 %late.1 = f32[2048,128]{1,0:T(8,128)} custom-call(bf16[1024,128]{1,0:T(8,128)(2,1)S(1)} %collective-permute-done.refs_0_, bf16[1024,128]{1,0:T(8,128)(2,1)S(1)} %collective-permute-done.1.refs_1_, s32[9216]{0:T(1024)S(1)} %bitcast.21, f32[520,128]{1,0:T(8,128)S(1)} %get-tuple-element.36.refs_3_, f32[2048,128]{1,0:T(8,128)S(1)} %early.1.refs_4_, ...), custom_call_target="tpu_custom_call" | custom-call | flops 4194304000 | bytes 8388608 | tf_op jit(solution)/shard_map/late/pallas_call | solution.py:678
  (1 shorter events, 0.0 us)
Async XLA Ops:
  0.0 12.1 %copy-start.2 = (f32[16,2,128]{2,1,0:T(2,128)S(1)}, f32[16,2,128]{2,1,0:T(2,128)}, u32[]{:S(2)}) copy-start(f32[16,2,128]{2,1,0:T(2,128)} %param.16) | copy-start | bytes 49156
  0.0 12.1 %copy-start = (bf16[9,256,256]{2,1,0:T(8,128)(2,1)S(1)}, bf16[9,256,256]{2,1,0:T(8,128)(2,1)}, u32[]{:S(2)}) copy-start(bf16[9,256,256]{2,1,0:T(8,128)(2,1)} %param.15) | copy-start | bytes 3538948
  1.6 8.8 %collective-permute-start.2 = (bf16[64,256]{1,0:T(8,128)(2,1)S(1)}, bf16[64,256]{1,0:T(8,128)(2,1)S(1)}, u32[]{:S(2)}, u32[]{:S(2)}) collective-permute-start(bf16[64,256]{1,0:T(8,128)(2,1)S(1)} %get-tuple-element.31), channel_id=1, source_target_pairs={{0,1},{1,0},{2,3},{3,2},{4,5},{5,4},{6,7},{7,6},{8,9},{9,8},{10,11... | collective-permute-start | bytes 98312 | tf_op jit(solution)/shard_map/ppermute | solution.py:520
  4.6 5.8 %collective-permute-start.3 = (bf16[64,256]{1,0:T(8,128)(2,1)S(1)}, bf16[64,256]{1,0:T(8,128)(2,1)S(1)}, u32[]{:S(2)}, u32[]{:S(2)}) collective-permute-start(bf16[64,256]{1,0:T(8,128)(2,1)S(1)} %get-tuple-element.32), channel_id=1, source_target_pairs={{0,3},{1,2},{2,1},{3,0},{4,7},{5,6},{6,5},{7,4},{8,11},{9,10},{10,... | collective-permute-start | bytes 98312 | tf_op jit(solution)/shard_map/ppermute | solution.py:520
  6.9 10.3 %collective-permute-start.4 = (bf16[1024,128]{1,0:T(8,128)(2,1)S(1)}, bf16[1024,128]{1,0:T(8,128)(2,1)S(1)}, u32[]{:S(2)}, u32[]{:S(2)}) collective-permute-start(bf16[1024,128]{1,0:T(8,128)(2,1)S(1)} %get-tuple-element.30.refs_0_), channel_id=1, source_target_pairs={{0,3},{1,2},{2,1},{3,0},{4,7},{5,6},{6,5},{7,4},{8,11},{9,10},{10,... | collective-permute-start | bytes 786440 | tf_op jit(solution)/shard_map/ppermute | solution.py:583
  8.4 13.3 %collective-permute-start.1 = (bf16[1024,128]{1,0:T(8,128)(2,1)S(1)}, bf16[1024,128]{1,0:T(8,128)(2,1)S(1)}, u32[]{:S(2)}, u32[]{:S(2)}) collective-permute-start(bf16[1024,128]{1,0:T(8,128)(2,1)S(1)} %get-tuple-element.30.refs_0_), channel_id=1, source_target_pairs={{0,2},{1,3},{2,0},{3,1},{4,6},{5,7},{6,4},{7,5},{8,10},{9,11},{10,... | collective-permute-start | bytes 786440 | tf_op jit(solution)/shard_map/ppermute | solution.py:583
  9.9 11.8 %collective-permute-start = (bf16[1024,128]{1,0:T(8,128)(2,1)S(1)}, bf16[1024,128]{1,0:T(8,128)(2,1)S(1)}, u32[]{:S(2)}, u32[]{:S(2)}) collective-permute-start(bf16[1024,128]{1,0:T(8,128)(2,1)S(1)} %get-tuple-element.30.refs_0_), channel_id=1, source_target_pairs={{0,1},{1,0},{2,3},{3,2},{4,5},{5,4},{6,7},{7,6},{8,9},{9,8},{10,11... | collective-permute-start | bytes 786440 | tf_op jit(solution)/shard_map/ppermute | solution.py:583
  10.5 10.2 %collective-permute-start.5 = (bf16[80,256]{1,0:T(8,128)(2,1)S(1)}, bf16[80,256]{1,0:T(8,128)(2,1)S(1)}, u32[]{:S(2)}, u32[]{:S(2)}) collective-permute-start(bf16[80,256]{1,0:T(8,128)(2,1)S(1)} %get-tuple-element.33), channel_id=1, source_target_pairs={{0,4},{4,0},{8,12},{12,8},{16,20},{20,16},{24,28},{28,24},{1,5},{5... | collective-permute-start | bytes 122888 | tf_op jit(solution)/shard_map/ppermute | solution.py:520
  10.6 10.1 %collective-permute-start.6 = (bf16[80,256]{1,0:T(8,128)(2,1)S(1)}, bf16[80,256]{1,0:T(8,128)(2,1)S(1)}, u32[]{:S(2)}, u32[]{:S(2)}) collective-permute-start(bf16[80,256]{1,0:T(8,128)(2,1)S(1)} %get-tuple-element.38), channel_id=1, source_target_pairs={{0,1},{1,0},{2,3},{3,2},{4,8},{5,9},{6,10},{7,11},{8,4},{9,5},{10,... | collective-permute-start | bytes 122888 | tf_op jit(solution)/shard_map/ppermute | solution.py:520
  12.1 2.9 %copy-start.1 = (bf16[256,256]{1,0:T(8,128)(2,1)S(1)}, bf16[256,256]{1,0:T(8,128)(2,1)}, u32[]{:S(2)}) copy-start(bf16[256,256]{1,0:T(8,128)(2,1)} %recv_ref.3) | copy-start | bytes 393220
  12.1 2.9 %copy-start.3 = (bf16[4,512,256]{2,1,0:T(8,128)(2,1)S(1)}, bf16[4,512,256]{2,1,0:T(8,128)(2,1)}, u32[]{:S(2)}) copy-start(bf16[4,512,256]{2,1,0:T(8,128)(2,1)} %down_ref.1) | copy-start | bytes 3145732
  12.1 2.9 %copy-start.4 = (s32[16,16,16]{2,1,0:T(8,128)S(1)}, s32[16,16,16]{2,1,0:T(8,128)}, u32[]{:S(2)}) copy-start(s32[16,16,16]{2,1,0:T(8,128)} %param.18) | copy-start | bytes 49156
  12.2 2.9 %copy-start.5 = (s32[16,16,16]{2,1,0:T(8,128)S(1)}, s32[16,16,16]{2,1,0:T(8,128)}, u32[]{:S(2)}) copy-start(s32[16,16,16]{2,1,0:T(8,128)} %param.19) | copy-start | bytes 49156
  12.2 2.9 %copy-start.6 = (f32[64,2,256]{2,1,0:T(2,128)S(1)}, f32[64,2,256]{2,1,0:T(2,128)}, u32[]{:S(2)}) copy-start(f32[64,2,256]{2,1,0:T(2,128)} %param.21) | copy-start | bytes 393220
  12.2 2.9 %copy-start.7 = (s32[16,16]{1,0:T(8,128)S(1)}, s32[16,16]{1,0:T(8,128)}, u32[]{:S(2)}) copy-start(s32[16,16]{1,0:T(8,128)} %count_ref) | copy-start | bytes 3076
